TPU v7x, 256 devices: a whole 4x4x8 slice. The times are simulated.
256 devices in a mesh: seq: 4 (over y_lo, core), fsdp: 64 (over x, z, y_hi).
Axes of the slice: x: 4, y: 4 (y_hi: 2, y_lo: 2; y = y_hi * 2 + y_lo), z: 8, core: 2. Of those that a mesh axis runs over, the one named last changes fastest.
Arguments:
- tokens: bfloat16 [2, 2048, 4096], P(None, 'seq'), may hold values from -6 to 6
- out_grad: bfloat16 [2, 2048, 4096], P(None, 'seq', 'fsdp'), may hold values from -6 to 6
- gate_weight: bfloat16 [4096, 8192], P(None, 'fsdp'), may hold values from -0.09375 to 0.09375
- up_weight: bfloat16 [4096, 8192], P(None, 'fsdp'), may hold values from -0.09375 to 0.09375
- down_weight: bfloat16 [8192, 4096], P('fsdp'), may hold values from -0.0625 to 0.0625
- proj_gate_in: bfloat16 [4096, 64], replicated, may hold values from -0.09375 to 0.09375
- proj_gate_out: bfloat16 [8192, 64], P('fsdp'), may hold values from -0.0625 to 0.0625
- proj_up_in: bfloat16 [4096, 64], replicated, may hold values from -0.09375 to 0.09375
- proj_up_out: bfloat16 [8192, 64], P('fsdp'), may hold values from -0.0625 to 0.0625
- proj_down_in: bfloat16 [8192, 64], P('fsdp'), may hold values from -0.0625 to 0.0625
- proj_down_out: bfloat16 [4096, 64], replicated, may hold values from -0.09375 to 0.09375
- lengths: int32 [2], replicated, may hold values from 512 to 2048, as said below
Outputs:
- projected: float32 [2, 3, 4096], P(None, None, 'seq')
Inputs may be any that keep to these rules, and one draw needn't show every extreme that they name: `lengths`: at least one example has all 2048 tokens valid.
All inputs are finite; a program needn't handle non-finite values.
Results may differ from a plain program's by a relative error of at most 0.003.
Values may be sent and summed in bfloat16 or wider, within the bound.
No kernel may reach another device: no remote copies, remote signals or barrier semaphores. Data moves between devices by JAX's collectives and lax.ppermute only.
A program may use at most 128 MiB of HBM per device.

v0:
```python
import jax
import jax.numpy as jnp
from jax import lax
from jax.sharding import PartitionSpec as P


def split_sides(columns, rank_size):
    pieces = [columns[:, k * rank_size : (k + 1) * rank_size] for k in range(6)]
    left_side = jnp.stack([pieces[0], pieces[1], pieces[5]], axis=1)
    right_side = jnp.stack([pieces[3], pieces[4], pieces[2]], axis=1)
    return (left_side, right_side)


def shards(
    tokens,
    out_grad,
    gate_weight,
    up_weight,
    down_weight,
    proj_gate_in,
    proj_gate_out,
    proj_up_in,
    proj_up_out,
    proj_down_in,
    proj_down_out,
    lengths,
):
    examples, seq_dev, model_width = tokens.shape
    row_count = examples * seq_dev
    rank_size = proj_gate_in.shape[1]
    hidden_width = gate_weight.shape[1]
    seq_index = lax.axis_index("seq")
    seq_length = seq_dev * lax.axis_size("seq")
    scale_factor = float(seq_length) ** (-0.5)
    flat_tokens = tokens.reshape(row_count, model_width)
    gate_value = jnp.dot(flat_tokens, gate_weight, preferred_element_type=jnp.float32)
    up_value = jnp.dot(flat_tokens, up_weight, preferred_element_type=jnp.float32)
    sigmoid_gate = jax.nn.sigmoid(gate_value)
    hidden = (gate_value * sigmoid_gate * up_value).astype(jnp.bfloat16)
    initial = (
        jnp.zeros((row_count, hidden_width), jnp.float32),
        jnp.zeros((row_count, rank_size), jnp.float32),
    )
    shard_piece = lax.all_gather(out_grad, "fsdp", axis=2, tiled=True)
    piece_width = shard_piece.shape[2]
    columns_piece = shard_piece.reshape(row_count, piece_width)
    piece_width = shard_piece.shape[2]
    add_columns_piece = shard_piece.reshape(row_count, piece_width)
    grad_total = lax.dot_general(
        add_columns_piece, down_weight, (((1,), (1,)), ((), ())), preferred_element_type=jnp.float32
    )
    grad_total, unused_total = (grad_total, initial[1])
    left_down_full = jnp.dot(columns_piece, proj_down_out, preferred_element_type=jnp.float32)
    derivative = sigmoid_gate * (1.0 + gate_value * (1.0 - sigmoid_gate))
    gate_grad = (grad_total * up_value * derivative).astype(jnp.bfloat16)
    up_grad = (grad_total * gate_value * sigmoid_gate).astype(jnp.bfloat16)
    left_gate = jnp.dot(gate_grad, proj_gate_out, preferred_element_type=jnp.float32)
    left_up = jnp.dot(up_grad, proj_up_out, preferred_element_type=jnp.float32)
    right_down = jnp.dot(hidden, proj_down_in, preferred_element_type=jnp.float32)
    right_gate = jnp.dot(flat_tokens, proj_gate_in, preferred_element_type=jnp.float32)
    right_up = jnp.dot(flat_tokens, proj_up_in, preferred_element_type=jnp.float32)
    partial_terms = jnp.concatenate([left_gate, left_up, right_down], axis=1)
    complete = jnp.concatenate([right_gate, right_up, left_down_full], axis=1)
    summed = lax.psum(partial_terms, "fsdp")
    columns = jnp.concatenate([summed, complete], axis=1)
    left_side, right_side = split_sides(columns, rank_size)
    positions = seq_index * seq_dev + jnp.arange(seq_dev, dtype=jnp.int32)
    valid_mask = (positions[None, :] < lengths[:, None]).astype(jnp.float32)
    left_blocks = left_side.reshape(examples, seq_dev, 3, rank_size) * valid_mask[:, :, None, None]
    right_blocks = right_side.reshape(examples, seq_dev, 3, rank_size)
    products = jnp.einsum(
        "esmi,esmj->emij", left_blocks, right_blocks, precision=lax.Precision.HIGHEST
    )
    products = products.reshape(examples, 3, rank_size * rank_size) * scale_factor
    return lax.psum_scatter(products, "seq", scatter_dimension=2, tiled=True)


def solution(mesh):
    placed = (
        P(None, "seq", None),
        P(None, "seq", "fsdp"),
        P(None, "fsdp"),
        P(None, "fsdp"),
        P("fsdp", None),
        P(),
        P("fsdp", None),
        P(),
        P("fsdp", None),
        P("fsdp", None),
        P(),
        P(),
    )
    return jax.shard_map(
        shards, mesh=mesh, in_specs=placed, out_specs=P(None, None, "seq"), check_vma=False
    )
```

profile of v0, /device:TPU:6, one launch (start us, length us, event | category | flops | bytes accessed | tf_op | source)
XLA Modules:
  0.0 898.0 jit_solution(17858846766450206460)
XLA Ops:
  6.5 0.0 copy-start
  6.5 0.0 copy-start.6
  6.5 0.0 all-gather.2.cloned.1.call-start
  6.5 0.7 all-gather.2.cloned.1.call-update
  7.3 0.0 all-reduce.2.cloned.1.call-start
  7.3 0.0 copy-start.1
  7.3 0.4 copy-done
  7.8 5.9 fusion.14
  13.7 0.0 copy-done.6
  13.7 0.0 copy-done.1
  13.7 0.0 copy-start.11
  13.7 0.0 copy-start.8
  13.7 0.0 copy-start.3
  13.7 2.3 fusion.13
  16.1 0.0 copy-done.8
  16.1 0.0 copy-start.13
  16.1 0.0 copy-start.4
  16.1 0.3 fusion.6
  16.4 0.0 copy-done.3
  16.4 2.7 convolution_bitcast_fusion.2
  19.0 0.0 copy-done.11
  19.1 0.0 copy-done.13
  19.1 0.0 copy-done.4
  19.1 2.7 convolution_bitcast_fusion.1
  21.7 0.0 copy-start.7
  21.7 139.6 %all-gather.2.cloned.1.call-done = bf16[2,512,4096]{1,2,0:T(8,128)(2,1)} async-done(((bf16[2,512,64]{1,2,0:T(8,128)(2,1)}), bf16[2,512,4096]{1,2,0:T(8,128)(2,1)}) %all-gather.2.cloned.1.call-update) | async-done | bytes 8388624 | tf_op jit(solution)/shard_map/all_gather | solution.py:44
  161.3 11.4 %copy.26 = bf16[2,512,4096]{2,1,0:T(8,128)(2,1)} copy(bf16[2,512,4096]{1,2,0:T(8,128)(2,1)} %all-gather.2.cloned.1.call-done) | data formatting | bytes 16777216 | tf_op jit(solution)/shard_map/all_gather | solution.py:44
  172.7 0.0 copy-start.9
  172.7 0.0 copy-start.12
  172.7 0.0 copy-start.10
  172.7 0.0 copy-start.14
  172.7 0.0 copy-done.7
  172.7 0.0 copy-start.5
  172.7 0.0 copy-start.2
  172.7 5.8 fusion.12
  178.6 0.0 copy-done.9
  178.6 0.0 copy-done.12
  178.6 0.3 fusion.5
  178.9 0.0 copy-done.10
  178.9 0.0 copy-done.14
  178.9 0.3 fusion.7
  179.2 0.9 pad_maximum_fusion
  180.2 0.0 all-reduce.2.cloned.1.call-update
  180.2 0.2 reduce-scatter.4.cloned.1.call-start
  180.5 0.0 copy-done.5
  180.5 0.1 compare_convert_fusion
  180.5 0.0 copy-done.2
  180.5 4.9 convolution_bitcast_fusion
  185.4 651.4 %all-reduce.2.cloned.1.call-done = f32[1024,192]{0,1:T(8,128)} async-done(((f32[1024,192]{0,1:T(8,128)}), f32[1024,192]{0,1:T(8,128)}) %all-reduce.2.cloned.1.call-update) | async-done | bytes 786448 | tf_op jit(solution)/shard_map/psum | solution.py:64
  836.9 1.2 fusion.11
  838.0 0.2 stack.18
  838.3 0.1 copy.27
  838.3 0.2 stack.21
  838.5 0.1 copy.29
  838.6 0.2 stack.19
  838.8 0.1 copy.28
  838.9 0.2 maximum_multiply_fusion
  839.1 0.9 convolution_multiply_fusion
  840.0 6.0 copy.37
  846.0 9.0 %reshape.81 = f32[4096,6]{1,0:T(8,128)} reshape(f32[4096,3,2]{2,1,0:T(4,128)} %bitcast.42) | data formatting | bytes 196608
  855.0 0.0 reduce-scatter.4.cloned.1.call-update
  855.0 32.8 %reduce-scatter.4.cloned.1.call-done = f32[1024,6]{1,0:T(8,128)} async-done(((f32[4096,6]{1,0:T(8,128)}), f32[1024,6]{1,0:T(8,128)}) %reduce-scatter.4.cloned.1.call-update) | async-done | bytes 24592
  887.8 2.3 reshape.82
  890.2 1.3 copy.35
  (1 shorter events, 0.0 us)
Async XLA Ops:
  6.5 1.2 copy-start
  6.5 7.1 copy-start.6
  6.5 154.8 %all-gather.2.cloned.1.call-start = ((), (), s32[]{:S(2)}) async-start(), calls=%async_computation.1 | async-start | bytes 8519680 | tf_op jit(solution)/shard_map/all_gather | solution.py:44
  7.3 829.6 %all-reduce.2.cloned.1.call-start = ((), (), s32[]{:S(2)}) async-start(), calls=%async_computation.2 | async-start | bytes 1572864 | tf_op jit(solution)/shard_map/psum | solution.py:64
  7.3 6.4 copy-start.1
  13.7 5.4 copy-start.11
  13.7 2.4 copy-start.8
  13.7 2.7 copy-start.3
  16.1 3.0 copy-start.13
  16.1 3.0 copy-start.4
  21.7 151.0 %copy-start.7 = (bf16[128,4096]{1,0:T(8,128)(2,1)S(1)}, bf16[128,4096]{1,0:T(8,128)(2,1)}, u32[]{:S(2)}) copy-start(bf16[128,4096]{1,0:T(8,128)(2,1)} %param.16) | copy-start | bytes 3145732
  172.7 5.9 copy-start.9
  172.7 5.9 copy-start.12
  172.7 6.2 copy-start.10
  172.7 6.2 copy-start.14
  172.7 7.7 copy-start.5
  172.7 7.8 copy-start.2
  180.2 707.6 %reduce-scatter.4.cloned.1.call-start = ((), (), s32[]{:S(2)}) async-start(), calls=%async_computation.3 | async-start | bytes 2621440
Sparse Core Ops, SparseCore 0:
  10.9 150.3 all-gather.1
  180.3 656.4 all-reduce.1
  855.2 32.6 reduce-scatter.3
where the time goes:
time: 900 us; the launch traced here: 898 us
  waiting for transfers between devices  825 us (92%)
  local copies, waits for them, and re-layouts  32.5 us (4%)
  matrix products  26.1 us (3%)
  between operations  13.4 us (1%)
    psum x1, waiting for transfers between devices, shards(): summed = lax.psum(partial_terms, 'fsdp')  651 us
    all_gather x1, waiting for transfers between devices, shards(): shard_piece = lax.all_gather(out_grad, 'fsdp', axis=2, tiled=True)  140 us
    unnamed x4, waiting for transfers between devices  33.5 us
    unnamed x34, local copies, waits for them, and re-layouts  19.1 us
  transfers between devices with their start and end apart: 3, of which 3 were waited for; matrix products, arithmetic and copies ran while one was open for 2% of the time, Pallas kernels for 0%

commit v1 on v0

v1 whole, which is shorter than its diff:
```python
import jax
import jax.numpy as jnp
from jax import lax
from jax.sharding import Mesh, PartitionSpec as P

SEQ_PARTS = (2, 2)
FSDP_PARTS = (4, 8, 2)
NX, NZ, NY = FSDP_PARTS


def shifted(count, step):
    return [(i, (i + step) % count) for i in range(count)]


def dot32(a, b, dims, precision=None):
    return lax.dot_general(a, b, (dims, ((), ())), preferred_element_type=jnp.float32, precision=precision)


def ring_x(own):
    half = own.shape[0] // 2
    before = lax.ppermute(own, "x", shifted(NX, 1))
    after = lax.ppermute(own, "x", shifted(NX, -1))
    first = lax.ppermute(before[:half], "x", shifted(NX, 1))
    second = lax.ppermute(after[half:], "x", shifted(NX, -1))
    return [own, before, jnp.concatenate([first, second], axis=0), after]


def ring_z(own):
    up, down = [own], [own]
    for _ in range(NZ // 2 - 1):
        up.append(lax.ppermute(up[-1], "z", shifted(NZ, -1)))
        down.append(lax.ppermute(down[-1], "z", shifted(NZ, 1)))
    far = jnp.concatenate(
        [
            lax.ppermute(up[-1][:1], "z", shifted(NZ, -1)),
            lax.ppermute(down[-1][1:], "z", shifted(NZ, 1)),
        ],
        axis=0,
    )
    return up + [far] + down[:0:-1]


def sum_everywhere(partial):
    seq_count = SEQ_PARTS[0] * SEQ_PARTS[1]
    width = partial.shape[1] // (seq_count * NX)
    pieces = partial.reshape(6, seq_count * NX, width).transpose(1, 0, 2)
    pieces = lax.all_to_all(pieces, ("sy", "sc", "x"), 0, 0, tiled=True)
    own = jnp.sum(pieces, axis=0)
    spread = jnp.broadcast_to(own[None], (NZ * NY,) + own.shape)
    own = jnp.sum(lax.all_to_all(spread, ("z", "yh"), 0, 0, tiled=True), axis=0)
    spread = jnp.broadcast_to(own[None], (NX,) + own.shape)
    blocks = lax.all_to_all(spread, "x", 0, 0, tiled=True)
    return blocks.transpose(1, 0, 2).reshape(6, NX * width)


def shards(
    tokens,
    out_grad,
    gate_weight,
    up_weight,
    down_weight,
    proj_gate_in,
    proj_gate_out,
    proj_up_in,
    proj_up_out,
    proj_down_in,
    proj_down_out,
    lengths,
):
    examples, seq_dev, model_width = tokens.shape
    row_count = examples * seq_dev
    rank = proj_gate_in.shape[1]
    hidden = gate_weight.shape[1]
    x_at, z_at, y_at = lax.axis_index("x"), lax.axis_index("z"), lax.axis_index("yh")
    seq_index = lax.axis_index("sy") * SEQ_PARTS[1] + lax.axis_index("sc")
    scale_factor = float(seq_dev * SEQ_PARTS[0] * SEQ_PARTS[1]) ** (-0.5)
    class_width = model_width // NX
    block_width = class_width // NZ

    own_grad = out_grad.transpose(0, 2, 1)
    other_grad = lax.ppermute(own_grad, "yh", shifted(NY, 1))
    first_y = y_at == 0
    pair = jnp.concatenate(
        [jnp.where(first_y, own_grad, other_grad), jnp.where(first_y, other_grad, own_grad)], axis=1
    )
    blocks = ring_z(pair)

    proj_out = jnp.concatenate([proj_gate_out, proj_up_out], axis=1)
    weight_packs = []
    for step in range(NX):
        start = lax.rem(x_at + step, NX) * class_width
        piece = lax.dynamic_slice_in_dim(down_weight, start, class_width, axis=1)
        piece = jnp.concatenate([piece, proj_out], axis=1)
        weight_packs.append(piece if step == 0 else lax.ppermute(piece, "x", shifted(NX, step)))

    flat_tokens = tokens.reshape(row_count, model_width)
    gate_value = dot32(gate_weight, flat_tokens, ((0,), (1,)))
    up_value = dot32(up_weight, flat_tokens, ((0,), (1,)))
    sigmoid_gate = jax.nn.sigmoid(gate_value)
    silu = gate_value * sigmoid_gate
    factor_gate = (up_value * sigmoid_gate * (1.0 + gate_value * (1.0 - sigmoid_gate))).astype(jnp.bfloat16)
    factor_up = silu.astype(jnp.bfloat16)
    hidden_value = (silu * up_value).astype(jnp.bfloat16)
    right_down = dot32(proj_down_in, hidden_value, ((0,), (0,))).astype(jnp.bfloat16)
    factors = ring_x(jnp.concatenate([factor_gate, factor_up, right_down], axis=0))

    positions = seq_index * seq_dev + jnp.arange(seq_dev, dtype=jnp.int32)
    valid = (positions[None, :] < lengths[:, None]).astype(jnp.float32) * scale_factor
    valid = valid.reshape(1, row_count)
    proj_in = jnp.concatenate([proj_gate_in, proj_up_in], axis=1)
    right_both = dot32(proj_in, flat_tokens, ((0,), (1,))) * valid
    right_down_sum = sum(piece[2 * hidden :].astype(jnp.float32) for piece in factors) * valid

    weight = jnp.concatenate([piece[:, :class_width] for piece in weight_packs], axis=0)
    down_out = lax.dynamic_slice_in_dim(proj_down_out, x_at * class_width, class_width, axis=0)
    weight = jnp.concatenate([weight, down_out.T], axis=0)
    twice = jnp.concatenate([weight, weight], axis=1)
    weight = lax.dynamic_slice_in_dim(twice, z_at * block_width, class_width, axis=1)
    grad = jnp.concatenate(blocks, axis=1)
    grad_total = lax.dot_general(weight, grad, (((1,), (1,)), ((), ())), preferred_element_type=jnp.float32)
    grad_total = grad_total.reshape(NX * hidden + rank, row_count)
    left_down = grad_total[NX * hidden :]
    grad_total = grad_total[: NX * hidden]

    def project(factor, proj):
        product = grad_total * factor.astype(jnp.float32)
        high = product.astype(jnp.bfloat16)
        low = (product - high.astype(jnp.float32)).astype(jnp.bfloat16)
        return dot32(proj, high, ((0,), (0,))) + dot32(proj, low, ((0,), (0,)))

    left_gate = project(
        jnp.concatenate([piece[:hidden] for piece in factors], axis=0),
        jnp.concatenate([piece[:, class_width : class_width + rank] for piece in weight_packs], axis=0),
    )
    left_up = project(
        jnp.concatenate([piece[hidden : 2 * hidden] for piece in factors], axis=0),
        jnp.concatenate([piece[:, class_width + rank :] for piece in weight_packs], axis=0),
    )
    left_side = jnp.stack([left_gate, left_up, left_down]).reshape(3, rank, examples, seq_dev)
    right_side = jnp.stack([right_both[:rank], right_both[rank:], right_down_sum])
    right_side = right_side.reshape(3, rank, examples, seq_dev)
    products = jnp.einsum("mies,mjes->emij", left_side, right_side, precision=lax.Precision.HIGHEST)
    total = sum_everywhere(products.reshape(examples * 3, rank * rank))
    return total.reshape(examples, 3, -1)


def solution(mesh):
    fine = Mesh(mesh.devices.reshape(SEQ_PARTS + FSDP_PARTS), ("sy", "sc", "x", "z", "yh"))
    seq, fsdp = ("sy", "sc"), ("x", "z", "yh")
    placed = (
        P(None, seq, None),
        P(None, seq, fsdp),
        P(None, fsdp),
        P(None, fsdp),
        P(fsdp, None),
        P(),
        P(fsdp, None),
        P(),
        P(fsdp, None),
        P(fsdp, None),
        P(),
        P(),
    )
    return jax.shard_map(
        shards, mesh=fine, in_specs=placed, out_specs=P(None, None, seq), check_vma=False
    )
```

time: 900 us -> 143 us (0.16)
  waiting for transfers between devices: 825 us -> 7.56 us
  blocking collectives: 0 us -> 34.8 us
  starting transfers between devices: 0.26 us -> 27.4 us
  between operations: 13.4 us -> 0.58 us
    psum x1 -> x0, waiting for transfers between devices: 651 us -> none  [shards(): summed = lax.psum(partial_terms, 'fsdp')]
    all_gather x1 -> x0, waiting for transfers between devices: 140 us -> none  [shards(): shard_piece = lax.all_gather(out_grad, 'fsdp', axis=2, tiled=True)]
    all_to_all x0 -> x3, blocking collectives: none -> 34.8 us  [the longest x1 17 us: sum_everywhere(): own = jnp.sum(lax.all_to_all(spread, ('z', 'yh'), 0, 0, tiled=True), axis=0)]
    unnamed x4 -> x0, waiting for transfers between devices: 33.5 us -> none
    ppermute x0 -> x16, starting transfers between devices: none -> 27.4 us  [the longest x3 13.6 us: ring_z(): up.append(lax.ppermute(up[-1], 'z', shifted(NZ, -1)))]
    all_gather x1 -> x0, local copies, waits for them, and re-layouts: 11.4 us -> none  [shards(): shard_piece = lax.all_gather(out_grad, 'fsdp', axis=2, tiled=True)]
    slice x1 -> x14, local copies, waits for them, and re-layouts: 1.16 us -> 12.4 us  [the longest x3 3.97 us: shards(): grad_total = grad_total[:NX * hidden]]
    unnamed x34 -> x79, local copies, waits for them, and re-layouts: 19.1 us -> 9.95 us
  transfers between devices with their start and end apart: 3 -> 16, of which waited for: 3 -> 2; matrix products, arithmetic and copies ran while one was open for 2% -> 23% of each run, Pallas kernels for 0% -> 0%
where the time goes in v1:
time: 143 us; the launch traced here: 141 us
  local copies, waits for them, and re-layouts  38.8 us (27%)
  blocking collectives  34.8 us (24%)
  matrix products  28.2 us (20%)
  starting transfers between devices  27.4 us (19%)
  waiting for transfers between devices  7.56 us (5%)
  other arithmetic  3.8 us (3%)
    dot_general x8, matrix products, dot32(): lax.dot_general(a, b, (dims, ((), ())), preferred_element_type=jnp.float3...  23 us
    all_to_all x1, blocking collectives, sum_everywhere(): own = jnp.sum(lax.all_to_all(spread, ('z', 'yh'), 0, 0, tiled=True), axis=0)  17 us
    ppermute x3, starting transfers between devices, ring_z(): up.append(lax.ppermute(up[-1], 'z', shifted(NZ, -1)))  13.6 us
    unnamed x79, local copies, waits for them, and re-layouts  9.95 us
    all_to_all x1, blocking collectives, sum_everywhere(): pieces = lax.all_to_all(pieces, ('sy', 'sc', 'x'), 0, 0, tiled=True)  9.79 us
    all_to_all x1, blocking collectives, sum_everywhere(): blocks = lax.all_to_all(spread, 'x', 0, 0, tiled=True)  8.01 us
    ppermute x3, waiting for transfers between devices, ring_z(): down.append(lax.ppermute(down[-1], 'z', shifted(NZ, 1)))  7.52 us
    concatenate x3, local copies, waits for them, and re-layouts, shards(): piece = jnp.concatenate([piece, proj_out], axis=1)  5.43 us
  transfers between devices with their start and end apart: 16, of which 2 were waited for; matrix products, arithmetic and copies ran while one was open for 23% of the time, Pallas kernels for 0%

profile of v1, /device:TPU:6, one launch (start us, length us, event | category | flops | bytes accessed | tf_op | source)
XLA Modules:
  0.0 141.1 jit_solution(3780945432972404012)
XLA Ops:
  0.0 6.8 %fusion.56 = f32[128,1024]{1,0:T(8,128)S(1)} fusion(bf16[4096,128]{1,0:T(8,128)(2,1)} %param.15, bf16[1024,4096]{1,0:T(8,128)(2,1)} %bitcast.32), kind=kOutput, calls=%fused_computation.89 | convolution fusion | flops 1073741824 | bytes 9961472 | tf_op jit(solution)/shard_map/dot_general | solution.py:16
  6.8 3.0 %multiply_convert_fusion.1 = (bf16[128,1024]{1,0:T(8,128)(2,1)S(1)}, bf16[128,1024]{1,0:T(8,128)(2,1)S(1)}, f32[128,1024]{1,0:T(8,128)S(1)}) fusion(f32[128,1024]{1,0:T(8,128)S(1)} %fusion.56, bf16[4096,128]{1,0:T(8,128)(2,1)S(1)} %copy-done, bf16[1024,4096]{1,0:T(8,128)(2,1)S(1)} %bitcast.34), kind=kOutput, calls=%fused_computation.42 | convolution fusion | flops 1075183616 | bytes 11010048 | tf_op jit(solution)/shard_map/dot_general | solution.py:16
  9.9 0.3 fusion.19
  10.2 0.9 pad_maximum_fusion.2
  11.1 2.2 %collective-permute-start.12 = (bf16[320,1024]{1,0:T(8,128)(2,1)}, bf16[320,1024]{1,0:T(8,128)(2,1)S(1)}, u32[]{:S(2)}, u32[]{:S(2)}) collective-permute-start(bf16[320,1024]{1,0:T(8,128)(2,1)} %pad_maximum_fusion.2), channel_id=1, source_target_pairs={{0,16},{16,32},{32,48},{48,0},{1,17},{17,33},{33,49},{49,1},{2,18}... | collective-permute-start | bytes 1966088 | tf_op jit(solution)/shard_map/ppermute | solution.py:21
  13.4 0.7 copy.84
  14.1 1.4 %copy.89 = bf16[128,64]{1,0:T(8,128)(2,1)} copy(bf16[128,64]{0,1:T(8,128)(2,1)} %param.18) | data formatting | bytes 32768 | tf_op args[6]
  15.6 1.0 constant_dynamic-slice_fusion
  16.6 1.9 %concatenate.52 = bf16[128,1152]{1,0:T(8,128)(2,1)} concatenate(bf16[128,1024]{1,0:T(8,128)(2,1)} %get-tuple-element.11, bf16[128,64]{1,0:T(8,128)(2,1)} %copy.89, bf16[128,64]{1,0:T(8,128)(2,1)} %copy.84), dimensions={1} | concatenate | bytes 589824 | tf_op jit(solution)/shard_map/concatenate | solution.py:93
  18.5 3.2 %collective-permute-start = (bf16[128,1152]{1,0:T(8,128)(2,1)}, bf16[128,1152]{1,0:T(8,128)(2,1)}, u32[]{:S(2)}, u32[]{:S(2)}) collective-permute-start(bf16[128,1152]{1,0:T(8,128)(2,1)} %concatenate.52), channel_id=1, source_target_pairs={{0,16},{16,32},{32,48},{48,0},{1,17},{17,33},{33,49},{49,1},{2,18}... | collective-permute-start | bytes 884744 | tf_op jit(solution)/shard_map/ppermute | solution.py:94
  21.7 1.8 %concatenate.53 = bf16[128,1152]{1,0:T(8,128)(2,1)} concatenate(bf16[128,1024]{1,0:T(8,128)(2,1)} %get-tuple-element.10, bf16[128,64]{1,0:T(8,128)(2,1)} %copy.89, bf16[128,64]{1,0:T(8,128)(2,1)} %copy.84), dimensions={1} | concatenate | bytes 589824 | tf_op jit(solution)/shard_map/concatenate | solution.py:93
  23.5 2.7 %collective-permute-start.3 = (bf16[2,64,512]{2,1,0:T(8,128)(2,1)S(1)}, bf16[2,64,512]{2,1,0:T(8,128)(2,1)}, u32[]{:S(2)}, u32[]{:S(2)}) collective-permute-start(bf16[2,64,512]{2,1,0:T(8,128)(2,1)S(1)} %bitcast.36), channel_id=1, source_target_pairs={{0,1},{1,0},{2,3},{3,2},{4,5},{5,4},{6,7},{7,6},{8,9},{9,8},{10,11... | collective-permute-start | bytes 393224 | tf_op jit(solution)/shard_map/ppermute | solution.py:81
  26.1 1.8 %concatenate.54 = bf16[128,1152]{1,0:T(8,128)(2,1)} concatenate(bf16[128,1024]{1,0:T(8,128)(2,1)} %get-tuple-element.9, bf16[128,64]{1,0:T(8,128)(2,1)} %copy.89, bf16[128,64]{1,0:T(8,128)(2,1)} %copy.84), dimensions={1} | concatenate | bytes 589824 | tf_op jit(solution)/shard_map/concatenate | solution.py:93
  28.0 6.3 %convolution_multiply_fusion = f32[128,1024]{1,0:T(8,128)S(1)} fusion(bf16[1024,4096]{1,0:T(8,128)(2,1)} %bitcast.33, bf16[4096,64]{0,1:T(8,128)(2,1)S(1)} %copy-done.3, bf16[4096,64]{0,1:T(8,128)(2,1)S(1)} %copy-done.4, f32[1024]{0:T(1024)S(1)} %bitcast.39), kind=kOutput, calls=%fused_computation.15 | convolution fusion | flops 1075970048 | bytes 9965568 | tf_op jit(solution)/shard_map/dot_general | solution.py:16
  34.3 0.2 stack.28
  34.5 0.8 copy.96
  35.3 0.2 stack.29
  35.5 0.8 copy.97
  36.3 0.9 constant_dynamic-update-slice_fusion.6
  37.3 6.1 %collective-permute-start.4 = (bf16[2,128,512]{2,1,0:T(8,128)(2,1)S(1)}, bf16[2,128,512]{2,1,0:T(8,128)(2,1)S(1)}, u32[]{:S(2)}, u32[]{:S(2)}) collective-permute-start(bf16[2,128,512]{2,1,0:T(8,128)(2,1)S(1)} %pad_maximum_fusion.3), channel_id=1, source_target_pairs={{0,14},{2,0},{4,2},{6,4},{8,6},{10,8},{12,10},{14,12},{1,15},{3,1}... | collective-permute-start | bytes 786440 | tf_op jit(solution)/shard_map/ppermute | solution.py:31
  43.4 1.7 %slice_dynamic-update-slice_fusion.2 = bf16[576,1024]{1,0:T(8,128)(2,1)} fusion(bf16[576,1024]{1,0:T(8,128)(2,1)} %get-tuple-element.12, bf16[128,1152]{1,0:T(8,128)(2,1)} %collective-permute-done), kind=kLoop, calls=%fused_computation.48 | loop fusion | bytes 524288
  45.1 1.7 %slice_dynamic-update-slice_fusion.1 = bf16[576,1024]{1,0:T(8,128)(2,1)} fusion(bf16[576,1024]{1,0:T(8,128)(2,1)} %slice_dynamic-update-slice_fusion.2, bf16[128,1152]{1,0:T(8,128)(2,1)} %collective-permute-done.1), kind=kLoop, calls=%fused_computation.47 | loop fusion | bytes 524288
  46.8 0.7 slice_dynamic-update-slice_fusion
  47.5 1.5 %fusion.53 = (bf16[128,64]{1,0:T(8,128)(2,1)}, bf16[128,64]{1,0:T(8,128)(2,1)S(1)}) fusion(bf16[128,1152]{1,0:T(8,128)(2,1)} %collective-permute-done), kind=kLoop, calls=%fused_computation.86 | loop fusion | bytes 65536 | tf_op jit(solution)/shard_map/slice | solution.py:133
  48.9 1.5 %fusion.54 = (bf16[128,64]{1,0:T(8,128)(2,1)}, bf16[128,64]{1,0:T(8,128)(2,1)S(1)}) fusion(bf16[128,1152]{1,0:T(8,128)(2,1)} %collective-permute-done.1), kind=kLoop, calls=%fused_computation.87 | loop fusion | bytes 65536 | tf_op jit(solution)/shard_map/slice | solution.py:133
  50.4 4.1 %collective-permute-start.5 = (bf16[2,128,512]{2,1,0:T(8,128)(2,1)S(1)}, bf16[2,128,512]{2,1,0:T(8,128)(2,1)S(1)}, u32[]{:S(2)}, u32[]{:S(2)}) collective-permute-start(bf16[2,128,512]{2,1,0:T(8,128)(2,1)S(1)} %collective-permute-done.4), channel_id=1, source_target_pairs={{0,14},{2,0},{4,2},{6,4},{8,6},{10,8},{12,10},{14,12},{1,15},{3,1}... | collective-permute-start | bytes 786440 | tf_op jit(solution)/shard_map/ppermute | solution.py:31
  54.5 0.7 fusion.55
  55.2 1.6 %bitcast_dynamic-update-slice_fusion = bf16[576,1024]{1,0:T(8,128)(2,1)} fusion(bf16[576,1024]{1,0:T(8,128)(2,1)} %slice_dynamic-update-slice_fusion, bf16[4096,64]{0,1:T(8,128)(2,1)} %param.22, s32[]{:T(128)S(6)} %select_n.34), kind=kLoop, calls=%fused_computation.55 | loop fusion | bytes 262148 | tf_op jit(solution)/shard_map/concatenate | solution.py:116
  56.9 2.4 %collective-permute-start.13 = (bf16[160,1024]{1,0:T(8,128)(2,1)S(1)}, bf16[160,1024]{1,0:T(8,128)(2,1)}, u32[]{:S(2)}, u32[]{:S(2)}) collective-permute-start(bf16[160,1024]{1,0:T(8,128)(2,1)S(1)} %slice.119), channel_id=1, source_target_pairs={{0,16},{16,32},{32,48},{48,0},{1,17},{17,33},{33,49},{49,1},{2,18}... | collective-permute-start | bytes 983048 | tf_op jit(solution)/shard_map/ppermute | solution.py:23
  59.4 3.3 %collective-permute-start.6 = (bf16[2,128,512]{2,1,0:T(8,128)(2,1)S(1)}, bf16[2,128,512]{2,1,0:T(8,128)(2,1)S(1)}, u32[]{:S(2)}, u32[]{:S(2)}) collective-permute-start(bf16[2,128,512]{2,1,0:T(8,128)(2,1)S(1)} %collective-permute-done.5), channel_id=1, source_target_pairs={{0,14},{2,0},{4,2},{6,4},{8,6},{10,8},{12,10},{14,12},{1,15},{3,1}... | collective-permute-start | bytes 786440 | tf_op jit(solution)/shard_map/ppermute | solution.py:31
  62.7 0.8 fusion.50
  63.6 0.9 collective-permute-done.9
  64.5 0.9 fusion.51
  65.4 6.7 %collective-permute-done.10 = bf16[2,128,512]{2,1,0:T(8,128)(2,1)S(1)} collective-permute-done((bf16[2,128,512]{2,1,0:T(8,128)(2,1)S(1)}, bf16[2,128,512]{2,1,0:T(8,128)(2,1)S(1)}, u32[]{:S(2)}, u32[]{:S(2)}) %collective-permute-start.10) | collective-permute-done | bytes 262176 | tf_op jit(solution)/shard_map/ppermute | solution.py:32
  72.0 0.7 slice.116
  72.7 0.7 slice.115
  73.4 3.2 %collective-permute-start.7 = (bf16[1,128,512]{2,1,0:T(8,128)(2,1)}, bf16[1,128,512]{2,1,0:T(8,128)(2,1)}, u32[]{:S(2)}, u32[]{:S(2)}) collective-permute-start(bf16[1,128,512]{2,1,0:T(8,128)(2,1)} %slice.115), channel_id=1, source_target_pairs={{0,14},{2,0},{4,2},{6,4},{8,6},{10,8},{12,10},{14,12},{1,15},{3,1}... | collective-permute-start | bytes 393224 | tf_op jit(solution)/shard_map/ppermute | solution.py:35
  76.7 1.3 copy-done.31
  78.0 0.7 copy-done.23
  78.8 0.2 stack.30
  79.0 0.7 copy.98
  79.8 1.7 %slice.120 = bf16[128,1024]{1,0:T(8,128)(2,1)} slice(bf16[160,1024]{1,0:T(8,128)(2,1)} %collective-permute-done.13), slice={[0:128], [0:1024]} | slice | bytes 524288 | tf_op jit(solution)/shard_map/slice | solution.py:132
  81.5 1.7 %maximum_dynamic-update-slice_fusion = bf16[2,1024,512]{2,1,0:T(8,128)(2,1)} fusion(bf16[2,1024,512]{2,1,0:T(8,128)(2,1)} %copy-done.31, bf16[1,128,512]{2,1,0:T(8,128)(2,1)} %collective-permute-done.11, bf16[1,128,512]{2,1,0:T(8,128)(2,1)} %collective-permute-done.7), kind=kLoop, calls=%fused_computation.50 | loop fusion | flops 524288 | bytes 524288
  83.2 0.7 constant_dynamic-update-slice_fusion.2
  83.9 0.8 constant_dynamic-update-slice_fusion.1
  84.7 0.7 constant_dynamic-update-slice_fusion
  85.4 3.0 %fusion.11 = f32[576,2,512]{2,0,1:T(8,128)S(1)} fusion(bf16[2,1024,512]{2,1,0:T(8,128)(2,1)} %constant_dynamic-update-slice_fusion, s32[]{:T(128)S(6)} %select_n.35, bf16[576,1024]{1,0:T(8,128)(2,1)S(1)} %copy-done.22), kind=kOutput, calls=%fused_computation.18 | convolution fusion | flops 1210318848 | bytes 5636100 | tf_op jit(solution)/shard_map/dot_general | solution.py:120
  88.4 0.2 slice.117
  88.6 0.7 slice_bitcast_fusion
  89.3 1.8 %copy.90 = f32[512,2,512]{0,2,1:T(8,128)} copy(f32[512,2,512]{2,0,1:T(8,128)S(1)} %slice.117) | data formatting | bytes 4194304 | tf_op jit(solution)/shard_map/slice | solution.py:123
  91.2 2.0 %copy.91 = f32[512,1024]{1,0:T(8,128)S(1)} copy(f32[512,1024]{0,1:T(8,128)} %bitcast.35) | data formatting | bytes 4194304 | tf_op jit(solution)/shard_map/slice | solution.py:123
  93.2 1.7 %fusion.23 = f32[64,1024]{1,0:T(8,128)S(1)} fusion(f32[512,1024]{1,0:T(8,128)S(1)} %copy.91, bf16[128,1024]{1,0:T(8,128)(2,1)} %get-tuple-element.15, bf16[128,1024]{1,0:T(8,128)(2,1)} %slice.120, bf16[128,1024]{1,0:T(8,128)(2,1)} %get-tuple-element.13, bf16[128,1024]{1,0:T(8,128)(2,1)S(1)} %copy-done.13, bf16[128,64]{1,0:T(8,128)(2,1)} %get-tuple-element.25, ...), kind=kOutput, calls=%fused_computation.26 | convolution fusion | flops 74186752 | bytes 3473408 | tf_op jit(solution)/shard_map/dot_general | solution.py:16
  95.0 1.1 fusion.16
  96.1 1.2 stack.24
  97.3 0.8 copy.94
  98.1 1.8 %fusion.24 = f32[64,1024]{1,0:T(8,128)S(1)} fusion(f32[512,1024]{1,0:T(8,128)S(1)} %copy.91, bf16[128,64]{1,0:T(8,128)(2,1)S(1)} %copy-done.25, bf16[128,64]{1,0:T(8,128)(2,1)S(1)} %get-tuple-element.24, bf16[128,64]{1,0:T(8,128)(2,1)S(1)} %get-tuple-element.22, bf16[128,64]{1,0:T(8,128)(2,1)S(1)} %copy-done.6, bf16[160,1024]{1,0:T(8,128)(2,1)} %copy-done.23, ...), kind=kOutput, calls=%fused_computation.27 | convolution fusion | flops 77856768 | bytes 3866624 | tf_op jit(solution)/shard_map/dot_general | solution.py:16
  99.9 2.1 %fusion.13 = f32[64,1024]{1,0:T(8,128)} fusion(f32[64,1024]{1,0:T(8,128)S(1)} %fusion.24, f32[512,1024]{1,0:T(8,128)S(1)} %copy.91, bf16[128,64]{1,0:T(8,128)(2,1)S(1)} %copy-done.25, bf16[128,64]{1,0:T(8,128)(2,1)S(1)} %get-tuple-element.24, bf16[128,64]{1,0:T(8,128)(2,1)S(1)} %get-tuple-element.22, bf16[128,64]{1,0:T(8,128)(2,1)S(1)} %copy-done.6, ...), kind=kOutput, calls=%fused_computation.19 | convolution fusion | flops 76349440 | bytes 4128768 | tf_op jit(solution)/shard_map/dot_general | solution.py:16
  102.0 1.2 stack.25
  103.2 2.1 %fusion.28 = f32[2,3,64,64]{3,2,1,0:T(8,128)S(1)} fusion(f32[1,64,2,512]{3,1,0,2:T(8,128)} %copy.98, f32[1,64,2,512]{3,1,0,2:T(8,128)} %copy.97, f32[1,64,2,512]{3,1,0,2:T(8,128)} %copy.96, f32[1,64,2,512]{3,1,2,0:T(8,128)} %slice_bitcast_fusion, f32[1,64,2,512]{3,1,2,0:T(8,128)S(1)} %copy.95, f32[1,64,2,512]{3,1,2,0:T(8,128)} %copy.94), kind=kOutput, calls=%fused_computation.33 | convolution fusion | flops 151781376 | bytes 1671168 | tf_op jit(solution)/shard_map/mies,mjes->emij/dot_general | solution.py:142
  105.3 0.1 reshape_reshape.6
  105.5 9.8 %all_to_all.15 = f32[16,6,256]{2,1,0:T(8,128)S(1)} all-to-all(f32[16,6,256]{2,1,0:T(8,128)S(1)} %bitcast.37), channel_id=1, replica_groups=mesh['sy'=2,'sc'=2,'x'=4,'z'=8,'yh'=2] {'sy','sc','x'}, dimensions={0} | all-to-all | bytes 196608 | tf_op jit(solution)/shard_map/all_to_all | solution.py:47
  115.3 17.0 %all_to_all.16 = f32[16,6,256]{2,1,0:T(8,128)S(1)} all-to-all(f32[16,6,256]{2,1,0:T(8,128)S(1)} %broadcast_in_dim.4), channel_id=1, replica_groups=mesh['sy'=2,'sc'=2,'x'=4,'z'=8,'yh'=2] {'z','yh'}, dimensions={0} | all-to-all | bytes 196608 | tf_op jit(solution)/shard_map/all_to_all | solution.py:50
  132.4 8.0 %all_to_all.17 = f32[4,6,256]{2,1,0:T(8,128)S(1)} all-to-all(f32[4,6,256]{2,1,0:T(8,128)S(1)} %broadcast_in_dim.5), channel_id=1, replica_groups=mesh['sy'=2,'sc'=2,'x'=4,'z'=8,'yh'=2] {'x'}, dimensions={0} | all-to-all | bytes 49152 | tf_op jit(solution)/shard_map/all_to_all | solution.py:52
  140.4 0.6 copy.103
  (108 shorter events, 0.8 us)
Async XLA Ops:
  0.0 6.8 %copy-start = (bf16[4096,128]{1,0:T(8,128)(2,1)S(1)}, bf16[4096,128]{1,0:T(8,128)(2,1)}, u32[]{:S(2)}) copy-start(bf16[4096,128]{1,0:T(8,128)(2,1)} %param.14) | copy-start | bytes 3145732
  0.0 6.8 %copy-start.1 = (bf16[2,512,4096]{2,1,0:T(8,128)(2,1)S(1)}, bf16[2,512,4096]{2,1,0:T(8,128)(2,1)}, u32[]{:S(2)}) copy-start(bf16[2,512,4096]{2,1,0:T(8,128)(2,1)} %param.12) | copy-start | bytes 25165828
  6.8 3.1 %copy-start.33 = (bf16[128,64]{0,1:T(8,128)(2,1)S(1)}, bf16[128,64]{0,1:T(8,128)(2,1)}, u32[]{:S(2)}) copy-start(bf16[128,64]{0,1:T(8,128)(2,1)} %param.21) | copy-start | bytes 49156
  9.9 3.5 %copy-start.10 = (bf16[128,1024]{1,0:T(8,128)(2,1)}, bf16[128,1024]{1,0:T(8,128)(2,1)S(1)}, u32[]{:S(2)}) copy-start(bf16[128,1024]{1,0:T(8,128)(2,1)S(1)} %get-tuple-element.20) | copy-start | bytes 786436
  9.9 3.5 %copy-start.12 = (bf16[128,1024]{1,0:T(8,128)(2,1)}, bf16[128,1024]{1,0:T(8,128)(2,1)S(1)}, u32[]{:S(2)}) copy-start(bf16[128,1024]{1,0:T(8,128)(2,1)S(1)} %get-tuple-element.19) | copy-start | bytes 786436
  9.9 3.5 %copy-start.30 = (bf16[128,64]{0,1:T(8,128)(2,1)S(1)}, bf16[128,64]{0,1:T(8,128)(2,1)}, u32[]{:S(2)}) copy-start(bf16[128,64]{0,1:T(8,128)(2,1)} %param.20) | copy-start | bytes 49156
  9.9 5.7 %copy-start.2 = (bf16[128,4096]{1,0:T(8,128)(2,1)S(1)}, bf16[128,4096]{1,0:T(8,128)(2,1)}, u32[]{:S(2)}) copy-start(bf16[128,4096]{1,0:T(8,128)(2,1)} %param.16) | copy-start | bytes 3145732
  10.2 0.9 copy-start.8
  11.1 12.3 %copy-start.5 = (bf16[2,512,64]{1,2,0:T(8,128)(2,1)S(1)}, bf16[2,512,64]{1,2,0:T(8,128)(2,1)}, u32[]{:S(2)}) copy-start(bf16[2,512,64]{1,2,0:T(8,128)(2,1)} %param.13) | copy-start | bytes 393220
  11.1 45.7 %collective-permute-start.12 = (bf16[320,1024]{1,0:T(8,128)(2,1)}, bf16[320,1024]{1,0:T(8,128)(2,1)S(1)}, u32[]{:S(2)}, u32[]{:S(2)}) collective-permute-start(bf16[320,1024]{1,0:T(8,128)(2,1)} %pad_maximum_fusion.2), channel_id=1, source_target_pairs={{0,16},{16,32},{32,48},{48,0},{1,17},{17,33},{33,49},{49,1},{2,18}... | collective-permute-start | bytes 1966088 | tf_op jit(solution)/shard_map/ppermute | solution.py:21
  13.3 46.0 %collective-permute-start.14 = (bf16[320,1024]{1,0:T(8,128)(2,1)}, bf16[320,1024]{1,0:T(8,128)(2,1)S(1)}, u32[]{:S(2)}, u32[]{:S(2)}) collective-permute-start(bf16[320,1024]{1,0:T(8,128)(2,1)} %pad_maximum_fusion.2), channel_id=1, source_target_pairs={{0,48},{16,0},{32,16},{48,32},{1,49},{17,1},{33,17},{49,33},{2,50}... | collective-permute-start | bytes 1966088 | tf_op jit(solution)/shard_map/ppermute | solution.py:22
  14.1 13.8 %copy-start.32 = (s32[2]{0:T(128)S(1)}, s32[2]{0:T(128)}, u32[]{:S(2)}) copy-start(s32[2]{0:T(128)} %param.23) | copy-start | bytes 28
  16.6 11.4 %copy-start.3 = (bf16[4096,64]{0,1:T(8,128)(2,1)S(1)}, bf16[4096,64]{0,1:T(8,128)(2,1)}, u32[]{:S(2)}) copy-start(bf16[4096,64]{0,1:T(8,128)(2,1)} %param.19) | copy-start | bytes 1572868
  16.6 11.4 %copy-start.4 = (bf16[4096,64]{0,1:T(8,128)(2,1)S(1)}, bf16[4096,64]{0,1:T(8,128)(2,1)}, u32[]{:S(2)}) copy-start(bf16[4096,64]{0,1:T(8,128)(2,1)} %param.17) | copy-start | bytes 1572868
  18.5 18.8 %collective-permute-start = (bf16[128,1152]{1,0:T(8,128)(2,1)}, bf16[128,1152]{1,0:T(8,128)(2,1)}, u32[]{:S(2)}, u32[]{:S(2)}) collective-permute-start(bf16[128,1152]{1,0:T(8,128)(2,1)} %concatenate.52), channel_id=1, source_target_pairs={{0,16},{16,32},{32,48},{48,0},{1,17},{17,33},{33,49},{49,1},{2,18}... | collective-permute-start | bytes 884744 | tf_op jit(solution)/shard_map/ppermute | solution.py:94
  23.5 21.6 %collective-permute-start.1 = (bf16[128,1152]{1,0:T(8,128)(2,1)}, bf16[128,1152]{1,0:T(8,128)(2,1)}, u32[]{:S(2)}, u32[]{:S(2)}) collective-permute-start(bf16[128,1152]{1,0:T(8,128)(2,1)} %concatenate.53), channel_id=1, source_target_pairs={{0,32},{16,48},{32,0},{48,16},{1,33},{17,49},{33,1},{49,17},{2,34}... | collective-permute-start | bytes 884744 | tf_op jit(solution)/shard_map/ppermute | solution.py:94
  23.5 12.8 %collective-permute-start.3 = (bf16[2,64,512]{2,1,0:T(8,128)(2,1)S(1)}, bf16[2,64,512]{2,1,0:T(8,128)(2,1)}, u32[]{:S(2)}, u32[]{:S(2)}) collective-permute-start(bf16[2,64,512]{2,1,0:T(8,128)(2,1)S(1)} %bitcast.36), channel_id=1, source_target_pairs={{0,1},{1,0},{2,3},{3,2},{4,5},{5,4},{6,7},{7,6},{8,9},{9,8},{10,11... | collective-permute-start | bytes 393224 | tf_op jit(solution)/shard_map/ppermute | solution.py:81
  36.3 10.5 %collective-permute-start.2 = (bf16[128,1152]{1,0:T(8,128)(2,1)}, bf16[128,1152]{1,0:T(8,128)(2,1)S(1)}, u32[]{:S(2)}, u32[]{:S(2)}) collective-permute-start(bf16[128,1152]{1,0:T(8,128)(2,1)} %concatenate.54), channel_id=1, source_target_pairs={{0,48},{16,0},{32,16},{48,32},{1,49},{17,1},{33,17},{49,33},{2,50}... | collective-permute-start | bytes 884744 | tf_op jit(solution)/shard_map/ppermute | solution.py:94
  37.3 13.1 %collective-permute-start.4 = (bf16[2,128,512]{2,1,0:T(8,128)(2,1)S(1)}, bf16[2,128,512]{2,1,0:T(8,128)(2,1)S(1)}, u32[]{:S(2)}, u32[]{:S(2)}) collective-permute-start(bf16[2,128,512]{2,1,0:T(8,128)(2,1)S(1)} %pad_maximum_fusion.3), channel_id=1, source_target_pairs={{0,14},{2,0},{4,2},{6,4},{8,6},{10,8},{12,10},{14,12},{1,15},{3,1}... | collective-permute-start | bytes 786440 | tf_op jit(solution)/shard_map/ppermute | solution.py:31
  45.1 11.7 %collective-permute-start.8 = (bf16[2,128,512]{2,1,0:T(8,128)(2,1)S(1)}, bf16[2,128,512]{2,1,0:T(8,128)(2,1)S(1)}, u32[]{:S(2)}, u32[]{:S(2)}) collective-permute-start(bf16[2,128,512]{2,1,0:T(8,128)(2,1)S(1)} %pad_maximum_fusion.3), channel_id=1, source_target_pairs={{0,2},{2,4},{4,6},{6,8},{8,10},{10,12},{12,14},{14,0},{1,3},{3,5},... | collective-permute-start | bytes 786440 | tf_op jit(solution)/shard_map/ppermute | solution.py:32
  50.4 9.0 %collective-permute-start.5 = (bf16[2,128,512]{2,1,0:T(8,128)(2,1)S(1)}, bf16[2,128,512]{2,1,0:T(8,128)(2,1)S(1)}, u32[]{:S(2)}, u32[]{:S(2)}) collective-permute-start(bf16[2,128,512]{2,1,0:T(8,128)(2,1)S(1)} %collective-permute-done.4), channel_id=1, source_target_pairs={{0,14},{2,0},{4,2},{6,4},{8,6},{10,8},{12,10},{14,12},{1,15},{3,1}... | collective-permute-start | bytes 786440 | tf_op jit(solution)/shard_map/ppermute | solution.py:31
  56.8 7.6 %collective-permute-start.9 = (bf16[2,128,512]{2,1,0:T(8,128)(2,1)S(1)}, bf16[2,128,512]{2,1,0:T(8,128)(2,1)S(1)}, u32[]{:S(2)}, u32[]{:S(2)}) collective-permute-start(bf16[2,128,512]{2,1,0:T(8,128)(2,1)S(1)} %collective-permute-done.8), channel_id=1, source_target_pairs={{0,2},{2,4},{4,6},{6,8},{8,10},{10,12},{12,14},{14,0},{1,3},{3,5},... | collective-permute-start | bytes 786440 | tf_op jit(solution)/shard_map/ppermute | solution.py:32
  56.9 21.8 %copy-start.9 = (bf16[64,1024]{1,0:T(8,128)(2,1)S(1)}, bf16[64,1024]{1,0:T(8,128)(2,1)}, u32[]{:S(2)}) copy-start(bf16[64,1024]{1,0:T(8,128)(2,1)} %copy-done.8) | copy-start | bytes 393220
  56.9 22.9 %collective-permute-start.13 = (bf16[160,1024]{1,0:T(8,128)(2,1)S(1)}, bf16[160,1024]{1,0:T(8,128)(2,1)}, u32[]{:S(2)}, u32[]{:S(2)}) collective-permute-start(bf16[160,1024]{1,0:T(8,128)(2,1)S(1)} %slice.119), channel_id=1, source_target_pairs={{0,16},{16,32},{32,48},{48,0},{1,17},{17,33},{33,49},{49,1},{2,18}... | collective-permute-start | bytes 983048 | tf_op jit(solution)/shard_map/ppermute | solution.py:23
  59.3 17.3 %collective-permute-start.15 = (bf16[160,1024]{1,0:T(8,128)(2,1)S(1)}, bf16[160,1024]{1,0:T(8,128)(2,1)S(1)}, u32[]{:S(2)}, u32[]{:S(2)}) collective-permute-start(bf16[160,1024]{1,0:T(8,128)(2,1)S(1)} %slice.126), channel_id=1, source_target_pairs={{0,48},{16,0},{32,16},{48,32},{1,49},{17,1},{33,17},{49,33},{2,50}... | collective-permute-start | bytes 983048 | tf_op jit(solution)/shard_map/ppermute | solution.py:24
  59.4 13.3 %collective-permute-start.6 = (bf16[2,128,512]{2,1,0:T(8,128)(2,1)S(1)}, bf16[2,128,512]{2,1,0:T(8,128)(2,1)S(1)}, u32[]{:S(2)}, u32[]{:S(2)}) collective-permute-start(bf16[2,128,512]{2,1,0:T(8,128)(2,1)S(1)} %collective-permute-done.5), channel_id=1, source_target_pairs={{0,14},{2,0},{4,2},{6,4},{8,6},{10,8},{12,10},{14,12},{1,15},{3,1}... | collective-permute-start | bytes 786440 | tf_op jit(solution)/shard_map/ppermute | solution.py:31
  64.4 12.2 %copy-start.15 = (bf16[2,128,512]{2,1,0:T(8,128)(2,1)}, bf16[2,128,512]{2,1,0:T(8,128)(2,1)S(1)}, u32[]{:S(2)}) copy-start(bf16[2,128,512]{2,1,0:T(8,128)(2,1)S(1)} %collective-permute-done.9) | copy-start | bytes 786436
  64.5 7.6 %collective-permute-start.10 = (bf16[2,128,512]{2,1,0:T(8,128)(2,1)S(1)}, bf16[2,128,512]{2,1,0:T(8,128)(2,1)S(1)}, u32[]{:S(2)}, u32[]{:S(2)}) collective-permute-start(bf16[2,128,512]{2,1,0:T(8,128)(2,1)S(1)} %collective-permute-done.9), channel_id=1, source_target_pairs={{0,2},{2,4},{4,6},{6,8},{8,10},{10,12},{12,14},{14,0},{1,3},{3,5},... | collective-permute-start | bytes 786440 | tf_op jit(solution)/shard_map/ppermute | solution.py:32
  72.7 8.8 %collective-permute-start.11 = (bf16[1,128,512]{2,1,0:T(8,128)(2,1)}, bf16[1,128,512]{2,1,0:T(8,128)(2,1)}, u32[]{:S(2)}, u32[]{:S(2)}) collective-permute-start(bf16[1,128,512]{2,1,0:T(8,128)(2,1)} %slice.116), channel_id=1, source_target_pairs={{0,2},{2,4},{4,6},{6,8},{8,10},{10,12},{12,14},{14,0},{1,3},{3,5},... | collective-permute-start | bytes 393224 | tf_op jit(solution)/shard_map/ppermute | solution.py:36
  73.4 8.1 %collective-permute-start.7 = (bf16[1,128,512]{2,1,0:T(8,128)(2,1)}, bf16[1,128,512]{2,1,0:T(8,128)(2,1)}, u32[]{:S(2)}, u32[]{:S(2)}) collective-permute-start(bf16[1,128,512]{2,1,0:T(8,128)(2,1)} %slice.115), channel_id=1, source_target_pairs={{0,14},{2,0},{4,2},{6,4},{8,6},{10,8},{12,10},{14,12},{1,15},{3,1}... | collective-permute-start | bytes 393224 | tf_op jit(solution)/shard_map/ppermute | solution.py:35
  76.6 1.3 copy-start.31
  78.0 0.7 copy-start.23
  78.8 5.1 %copy-start.16 = (bf16[2,128,512]{2,1,0:T(8,128)(2,1)S(1)}, bf16[2,128,512]{2,1,0:T(8,128)(2,1)}, u32[]{:S(2)}) copy-start(bf16[2,128,512]{2,1,0:T(8,128)(2,1)} %copy-done.15) | copy-start | bytes 786436
  79.0 6.3 %copy-start.22 = (bf16[576,1024]{1,0:T(8,128)(2,1)S(1)}, bf16[576,1024]{1,0:T(8,128)(2,1)}, u32[]{:S(2)}) copy-start(bf16[576,1024]{1,0:T(8,128)(2,1)} %bitcast_dynamic-update-slice_fusion) | copy-start | bytes 3538948
  91.1 2.0 %copy-start.7 = (bf16[128,64]{1,0:T(8,128)(2,1)S(1)}, bf16[128,64]{1,0:T(8,128)(2,1)}, u32[]{:S(2)}) copy-start(bf16[128,64]{1,0:T(8,128)(2,1)} %copy.89) | copy-start | bytes 49156
  91.1 2.0 %copy-start.13 = (bf16[128,1024]{1,0:T(8,128)(2,1)S(1)}, bf16[128,1024]{1,0:T(8,128)(2,1)}, u32[]{:S(2)}) copy-start(bf16[128,1024]{1,0:T(8,128)(2,1)} %copy-done.12) | copy-start | bytes 786436
  91.1 2.0 %copy-start.26 = (bf16[128,64]{1,0:T(8,128)(2,1)S(1)}, bf16[128,64]{1,0:T(8,128)(2,1)}, u32[]{:S(2)}) copy-start(bf16[128,64]{1,0:T(8,128)(2,1)} %get-tuple-element.21) | copy-start | bytes 49156
  93.2 1.7 %copy-start.14 = (bf16[128,1024]{1,0:T(8,128)(2,1)S(1)}, bf16[128,1024]{1,0:T(8,128)(2,1)}, u32[]{:S(2)}) copy-start(bf16[128,1024]{1,0:T(8,128)(2,1)} %copy-done.12) | copy-start | bytes 786436
  93.2 1.7 %copy-start.17 = (bf16[128,1024]{1,0:T(8,128)(2,1)S(1)}, bf16[128,1024]{1,0:T(8,128)(2,1)}, u32[]{:S(2)}) copy-start(bf16[128,1024]{1,0:T(8,128)(2,1)} %slice.120) | copy-start | bytes 786436
  93.2 1.7 %copy-start.20 = (bf16[128,1024]{1,0:T(8,128)(2,1)S(1)}, bf16[128,1024]{1,0:T(8,128)(2,1)}, u32[]{:S(2)}) copy-start(bf16[128,1024]{1,0:T(8,128)(2,1)} %get-tuple-element.13) | copy-start | bytes 786436
  93.2 1.7 %copy-start.21 = (bf16[128,1024]{1,0:T(8,128)(2,1)S(1)}, bf16[128,1024]{1,0:T(8,128)(2,1)}, u32[]{:S(2)}) copy-start(bf16[128,1024]{1,0:T(8,128)(2,1)} %get-tuple-element.15) | copy-start | bytes 786436
  93.2 1.7 %copy-start.27 = (bf16[128,64]{1,0:T(8,128)(2,1)S(1)}, bf16[128,64]{1,0:T(8,128)(2,1)}, u32[]{:S(2)}) copy-start(bf16[128,64]{1,0:T(8,128)(2,1)} %get-tuple-element.21) | copy-start | bytes 49156
  93.2 1.7 %copy-start.28 = (bf16[128,64]{1,0:T(8,128)(2,1)S(1)}, bf16[128,64]{1,0:T(8,128)(2,1)}, u32[]{:S(2)}) copy-start(bf16[128,64]{1,0:T(8,128)(2,1)} %get-tuple-element.23) | copy-start | bytes 49156
  93.2 1.7 %copy-start.29 = (bf16[128,64]{1,0:T(8,128)(2,1)S(1)}, bf16[128,64]{1,0:T(8,128)(2,1)}, u32[]{:S(2)}) copy-start(bf16[128,64]{1,0:T(8,128)(2,1)} %get-tuple-element.25) | copy-start | bytes 49156
  94.9 3.1 %copy-start.6 = (bf16[128,64]{1,0:T(8,128)(2,1)S(1)}, bf16[128,64]{1,0:T(8,128)(2,1)}, u32[]{:S(2)}) copy-start(bf16[128,64]{1,0:T(8,128)(2,1)} %copy.84) | copy-start | bytes 49156
  95.0 3.1 %copy-start.25 = (bf16[128,64]{1,0:T(8,128)(2,1)S(1)}, bf16[128,64]{1,0:T(8,128)(2,1)}, u32[]{:S(2)}) copy-start(bf16[128,64]{1,0:T(8,128)(2,1)} %get-tuple-element.26) | copy-start | bytes 49156
  98.0 1.9 %copy-start.11 = (bf16[128,1024]{1,0:T(8,128)(2,1)S(1)}, bf16[128,1024]{1,0:T(8,128)(2,1)}, u32[]{:S(2)}) copy-start(bf16[128,1024]{1,0:T(8,128)(2,1)} %copy-done.10) | copy-start | bytes 786436
  98.0 1.9 %copy-start.18 = (bf16[128,1024]{1,0:T(8,128)(2,1)S(1)}, bf16[128,1024]{1,0:T(8,128)(2,1)}, u32[]{:S(2)}) copy-start(bf16[128,1024]{1,0:T(8,128)(2,1)} %get-tuple-element.14) | copy-start | bytes 786436
  98.0 1.9 %copy-start.19 = (bf16[128,1024]{1,0:T(8,128)(2,1)S(1)}, bf16[128,1024]{1,0:T(8,128)(2,1)}, u32[]{:S(2)}) copy-start(bf16[128,1024]{1,0:T(8,128)(2,1)} %get-tuple-element.16) | copy-start | bytes 786436
  98.0 1.9 %copy-start.24 = (bf16[160,1024]{1,0:T(8,128)(2,1)S(1)}, bf16[160,1024]{1,0:T(8,128)(2,1)}, u32[]{:S(2)}) copy-start(bf16[160,1024]{1,0:T(8,128)(2,1)} %copy-done.23) | copy-start | bytes 983044

commit v2 on v1

v2 whole, which is shorter than its diff:
```python
import jax
import jax.numpy as jnp
from jax import lax
from jax.experimental import pallas as pl
from jax.experimental.pallas import tpu as pltpu
from jax.sharding import Mesh, PartitionSpec as P

SEQ_PARTS = (2, 2)
FSDP_PARTS = (4, 8, 2)
NX, NZ, NY = FSDP_PARTS
MIB = 1024 * 1024
VMEM = pl.BlockSpec(memory_space=pltpu.VMEM)


def shifted(count, step):
    return [(i, (i + step) % count) for i in range(count)]


def dot32(a, b, dims, precision=None):
    return lax.dot_general(a, b, (dims, ((), ())), preferred_element_type=jnp.float32, precision=precision)


def pack_kernel(weight_ref, gate_ref, up_ref, *outs):
    width = weight_ref.shape[1] // NX
    rank = gate_ref.shape[0]
    x_at = lax.axis_index("x")
    for step, out in enumerate(outs, 1):
        start = pl.multiple_of(lax.rem(x_at + step, NX) * width, width)
        out[:, :width] = weight_ref[:, pl.ds(start, width)]
        out[:rank, width:] = gate_ref[...]
        out[rank:, width:] = up_ref[...]


def pack_weights(down_weight, gate_out, up_out):
    hidden, width = down_weight.shape
    shape = jax.ShapeDtypeStruct((hidden, width // NX + hidden), jnp.bfloat16)
    return pl.pallas_call(
        pack_kernel,
        out_shape=[shape] * (NX - 1),
        in_specs=[VMEM] * 3,
        out_specs=[VMEM] * (NX - 1),
        compiler_params=pltpu.CompilerParams(vmem_limit_bytes=16 * MIB),
        name="pack_weights",
    )(down_weight, gate_out, up_out)


def token_kernel(tile, seq_dev, scale, lengths_ref, tokens_ref, gate_ref, up_ref, gate_in_ref, up_in_ref, down_in_ref, factors_ref, right_ref):
    hidden = gate_ref.shape[1]
    rank = gate_in_ref.shape[0]
    step = pl.program_id(0)
    tokens = tokens_ref[...]
    gate = jnp.dot(tokens, gate_ref[...], preferred_element_type=jnp.float32)
    up = jnp.dot(tokens, up_ref[...], preferred_element_type=jnp.float32)
    sigmoid = 1.0 / (1.0 + jnp.exp(-gate))
    silu = gate * sigmoid
    factor_gate = up * sigmoid * (1.0 + gate * (1.0 - sigmoid))
    hidden_value = (silu * up).astype(jnp.bfloat16)
    factors_ref[:hidden, :] = factor_gate.T.astype(jnp.bfloat16)
    factors_ref[hidden : 2 * hidden, :] = silu.T.astype(jnp.bfloat16)

    per_example = seq_dev // tile
    seq_index = lax.axis_index("sy") * SEQ_PARTS[1] + lax.axis_index("sc")
    first = seq_index * seq_dev + lax.rem(step, per_example) * tile
    limit = lengths_ref[step // per_example]
    columns = first + lax.broadcasted_iota(jnp.int32, (rank, tile), 1)
    right_down = dot32(down_in_ref[...], hidden_value, ((1,), (1,)))
    right_down = jnp.where(columns < limit, right_down * scale, 0.0)
    factors_ref[2 * hidden :, :] = right_down.astype(jnp.bfloat16)
    rows = first + lax.broadcasted_iota(jnp.int32, (tile, rank), 0)
    valid = rows < limit
    right_gate = dot32(tokens, gate_in_ref[...], ((1,), (1,)))
    right_up = dot32(tokens, up_in_ref[...], ((1,), (1,)))
    right_ref[:, :rank] = jnp.where(valid, right_gate * scale, 0.0)
    right_ref[:, rank:] = jnp.where(valid, right_up * scale, 0.0)


def token_stage(tokens, gate_weight, up_weight, gate_in, up_in, down_in, lengths, seq_dev, scale):
    rows, width = tokens.shape
    hidden = gate_weight.shape[1]
    rank = gate_in.shape[0]
    tile = 256
    return pl.pallas_call(
        lambda *refs: token_kernel(tile, seq_dev, scale, *refs),
        grid=(rows // tile,),
        out_shape=[
            jax.ShapeDtypeStruct((2 * hidden + rank, rows), jnp.bfloat16),
            jax.ShapeDtypeStruct((rows, 2 * rank), jnp.float32),
        ],
        in_specs=[
            pl.BlockSpec(memory_space=pltpu.SMEM),
            pl.BlockSpec((tile, width), lambda i: (i, 0)),
            VMEM,
            VMEM,
            VMEM,
            VMEM,
            VMEM,
        ],
        out_specs=[
            pl.BlockSpec((2 * hidden + rank, tile), lambda i: (0, i)),
            pl.BlockSpec((tile, 2 * rank), lambda i: (i, 0)),
        ],
        compiler_params=pltpu.CompilerParams(vmem_limit_bytes=40 * MIB),
        cost_estimate=pl.CostEstimate(flops=2 * rows * width * 384, bytes_accessed=12 * MIB, transcendentals=rows * hidden),
        name="token_stage",
    )(lengths, tokens, gate_weight, up_weight, gate_in, up_in, down_in)


def tail_kernel(weight_ref, gate_out_ref, up_out_ref, down_out_ref, right_ref, *refs):
    packs, factors, own, other = refs[:3], refs[3:7], refs[7:15], refs[15:23]
    out_ref, weights, projs, grads = refs[23:]
    hidden, model_width = weight_ref.shape
    rank = gate_out_ref.shape[0]
    width = model_width // NX
    examples, piece, seq_dev = own[0].shape
    x_at, z_at, y_at = lax.axis_index("x"), lax.axis_index("z"), lax.axis_index("yh")

    start = pl.multiple_of(x_at * width, width)
    weights[:hidden, :] = weight_ref[:, pl.ds(start, width)]
    projs[:rank, :hidden] = gate_out_ref[...]
    projs[rank:, :hidden] = up_out_ref[...]
    for step, pack in enumerate(packs, 1):
        weights[step * hidden : (step + 1) * hidden, :] = pack[:, :width]
        projs[:, step * hidden : (step + 1) * hidden] = pack[:, width:]
    weights[NX * hidden :, :] = down_out_ref[:, pl.ds(start, width)]
    for example in range(examples):
        for step in range(NZ):
            block = lax.rem(z_at + step, NZ) * (NY * piece)
            grads[pl.ds(pl.multiple_of(block + y_at * piece, piece), piece), :] = own[step][example]
            grads[pl.ds(pl.multiple_of(block + (1 - y_at) * piece, piece), piece), :] = other[step][example]
        columns = slice(example * seq_dev, (example + 1) * seq_dev)
        total = jnp.dot(weights[...], grads[...], preferred_element_type=jnp.float32)
        left = []
        for kind in range(2):
            proj = projs[kind * rank : (kind + 1) * rank, :]
            factor = jnp.concatenate(
                [part[kind * hidden : (kind + 1) * hidden, columns] for part in factors], axis=0
            )
            product = total[: NX * hidden] * factor.astype(jnp.float32)
            high = product.astype(jnp.bfloat16)
            low = (product - high.astype(jnp.float32)).astype(jnp.bfloat16)
            left.append(
                jnp.dot(proj, high, preferred_element_type=jnp.float32)
                + jnp.dot(proj, low, preferred_element_type=jnp.float32)
            )
        both = jnp.dot(
            jnp.concatenate(left, axis=0),
            right_ref[columns, :],
            precision=lax.Precision.HIGHEST,
            preferred_element_type=jnp.float32,
        )
        right_down = factors[0][2 * hidden :, columns].astype(jnp.float32)
        for part in factors[1:]:
            right_down = right_down + part[2 * hidden :, columns].astype(jnp.float32)
        out_ref[3 * example] = both[:rank, :rank]
        out_ref[3 * example + 1] = both[rank:, rank:]
        out_ref[3 * example + 2] = dot32(
            total[NX * hidden :], right_down, ((1,), (1,)), precision=lax.Precision.HIGHEST
        )


def tail_stage(down_weight, gate_out, up_out, down_out, right, packs, factors, own, other):
    hidden, model_width = down_weight.shape
    rank = gate_out.shape[0]
    examples, piece, seq_dev = own[0].shape
    width = model_width // NX
    operands = [down_weight, gate_out, up_out, down_out, right, *packs, *factors, *own, *other]
    return pl.pallas_call(
        tail_kernel,
        out_shape=jax.ShapeDtypeStruct((examples * 3, rank, rank), jnp.float32),
        in_specs=[VMEM] * len(operands),
        out_specs=VMEM,
        scratch_shapes=[
            pltpu.VMEM((NX * hidden + rank, width), jnp.bfloat16),
            pltpu.VMEM((2 * rank, NX * hidden), jnp.bfloat16),
            pltpu.VMEM((width, seq_dev), jnp.bfloat16),
        ],
        compiler_params=pltpu.CompilerParams(vmem_limit_bytes=40 * MIB),
        cost_estimate=pl.CostEstimate(flops=4 * 10**9, bytes_accessed=8 * MIB, transcendentals=0),
        name="tail_stage",
    )(*operands)


def ring_z(own, far_step):
    up, down = [own], [own]
    for _ in range(NZ // 2 - 1):
        up.append(lax.ppermute(up[-1], "z", shifted(NZ, -1)))
        down.append(lax.ppermute(down[-1], "z", shifted(NZ, 1)))
    last = up[-1] if far_step < 0 else down[-1]
    return up + [lax.ppermute(last, "z", shifted(NZ, far_step))] + down[:0:-1]


def sum_everywhere(partial):
    seq_count = SEQ_PARTS[0] * SEQ_PARTS[1]
    width = partial.shape[1] // (seq_count * NX)
    pieces = partial.reshape(6, seq_count * NX, width).transpose(1, 0, 2)
    pieces = lax.all_to_all(pieces, ("sy", "sc", "x"), 0, 0, tiled=True)
    own = jnp.sum(pieces, axis=0)
    spread = jnp.broadcast_to(own[None], (NZ * NY,) + own.shape)
    own = jnp.sum(lax.all_to_all(spread, ("z", "yh"), 0, 0, tiled=True), axis=0)
    spread = jnp.broadcast_to(own[None], (NX,) + own.shape)
    blocks = lax.all_to_all(spread, "x", 0, 0, tiled=True)
    return blocks.transpose(1, 0, 2).reshape(6, NX * width)


def shards(
    tokens,
    out_grad,
    gate_weight,
    up_weight,
    down_weight,
    proj_gate_in,
    proj_gate_out,
    proj_up_in,
    proj_up_out,
    proj_down_in,
    proj_down_out,
    lengths,
):
    examples, seq_dev, model_width = tokens.shape
    scale = float(seq_dev * SEQ_PARTS[0] * SEQ_PARTS[1]) ** (-0.5)
    gate_out, up_out = proj_gate_out.T, proj_up_out.T

    own_grad = out_grad.transpose(0, 2, 1)
    other_grad = lax.ppermute(own_grad, "yh", shifted(NY, 1))
    own = ring_z(own_grad, -1)
    other = ring_z(other_grad, 1)

    sent = pack_weights(down_weight, gate_out, up_out)
    packs = [lax.ppermute(piece, "x", shifted(NX, step)) for step, piece in enumerate(sent, 1)]

    flat_tokens = tokens.reshape(examples * seq_dev, model_width)
    factors, right = token_stage(
        flat_tokens, gate_weight, up_weight, proj_gate_in.T, proj_up_in.T, proj_down_in.T, lengths, seq_dev, scale
    )
    factors = [factors] + [lax.ppermute(factors, "x", shifted(NX, step)) for step in range(1, NX)]

    products = tail_stage(
        down_weight, gate_out, up_out, proj_down_out.T, right, packs, factors, own, other
    )
    total = sum_everywhere(products.reshape(examples * 3, -1))
    return total.reshape(examples, 3, -1)


def solution(mesh):
    fine = Mesh(mesh.devices.reshape(SEQ_PARTS + FSDP_PARTS), ("sy", "sc", "x", "z", "yh"))
    seq, fsdp = ("sy", "sc"), ("x", "z", "yh")
    placed = (
        P(None, seq, None),
        P(None, seq, fsdp),
        P(None, fsdp),
        P(None, fsdp),
        P(fsdp, None),
        P(),
        P(fsdp, None),
        P(),
        P(fsdp, None),
        P(fsdp, None),
        P(),
        P(),
    )
    return jax.shard_map(
        shards, mesh=fine, in_specs=placed, out_specs=P(None, None, seq), check_vma=False
    )
```

time: 143 us -> 118 us (0.83)
  matrix products: 28.2 us -> 0 us
  local copies, waits for them, and re-layouts: 38.8 us -> 12.8 us
  Pallas kernels: 0 us -> 14.3 us
  starting transfers between devices: 27.4 us -> 37 us
  waiting for transfers between devices: 7.56 us -> 15.2 us
  other arithmetic: 3.8 us -> 0.05 us
  blocking collectives: 34.8 us -> 37 us
    dot_general x10 -> x0, matrix products: 28.2 us -> none  [the longest x8 23 us: dot32(): lax.dot_general(a, b, (dims, ((), ())), preferred_element_type=jnp.float3...]
    pallas_call x0 -> x3, Pallas kernels: none -> 14.3 us  [the longest x1 10.7 us: token_stage(): pl.pallas_call(lambda *refs: token_kernel(tile, seq_dev, scale, *refs), g...]
    slice x14 -> x0, local copies, waits for them, and re-layouts: 12.4 us -> none  [the longest x3 3.97 us: shards(): grad_total = grad_total[:NX * hidden]]
    concatenate x5 -> x0, local copies, waits for them, and re-layouts: 7.72 us -> none  [the longest x3 5.43 us: shards(): piece = jnp.concatenate([piece, proj_out], axis=1)]
    ppermute x3 -> x6, starting transfers between devices: 13.6 us -> 20.9 us  [ring_z(): up.append(lax.ppermute(up[-1], 'z', shifted(NZ, -1)))]
    another operation x11 -> x0, local copies, waits for them, and re-layouts: 6.8 us -> none  [the longest x5 3.89 us: shards(): jnp.stack([left_gate, left_up, left_down])]
    ppermute x6 -> x5, waiting for transfers between devices: 0.02 us -> 4.16 us  [the longest x2 4.16 us: ring_z(): return up + [lax.ppermute(last, 'z', shifted(NZ, far_step))] + down[:0:-1]]
    ppermute x3 -> x6, waiting for transfers between devices: 7.52 us -> 11 us  [ring_z(): down.append(lax.ppermute(down[-1], 'z', shifted(NZ, 1)))]
  transfers between devices with their start and end apart: 16 -> 21, of which waited for: 2 -> 5; matrix products, arithmetic and copies ran while one was open for 23% -> 0% of each run, Pallas kernels for 0% -> 9%
where the time goes in v2:
time: 118 us; the launch traced here: 116 us
  starting transfers between devices  37 us (31%)
  blocking collectives  37 us (31%)
  waiting for transfers between devices  15.2 us (13%)
  Pallas kernels  14.3 us (12%)
  local copies, waits for them, and re-layouts  12.8 us (11%)
    ppermute x6, starting transfers between devices, ring_z(): up.append(lax.ppermute(up[-1], 'z', shifted(NZ, -1)))  20.9 us
    all_to_all x1, blocking collectives, sum_everywhere(): own = jnp.sum(lax.all_to_all(spread, ('z', 'yh'), 0, 0, tiled=True), axis=0)  19.2 us
    unnamed x30, local copies, waits for them, and re-layouts  12 us
    ppermute x6, waiting for transfers between devices, ring_z(): down.append(lax.ppermute(down[-1], 'z', shifted(NZ, 1)))  11 us
    pallas_call x1, Pallas kernels, token_stage(): pl.pallas_call(lambda *refs: token_kernel(tile, seq_dev, scale, *refs), g...  10.7 us
    all_to_all x1, blocking collectives, sum_everywhere(): pieces = lax.all_to_all(pieces, ('sy', 'sc', 'x'), 0, 0, tiled=True)  9.72 us
    all_to_all x1, blocking collectives, sum_everywhere(): blocks = lax.all_to_all(spread, 'x', 0, 0, tiled=True)  8.01 us
    ppermute x3, starting transfers between devices, shards(): lax.ppermute(factors, 'x', shifted(NX, step))  5.89 us
  transfers between devices with their start and end apart: 21, of which 5 were waited for; matrix products, arithmetic and copies ran while one was open for 0% of the time, Pallas kernels for 9%

profile of v2, /device:TPU:6, one launch (start us, length us, event | category | flops | bytes accessed | tf_op | source)
XLA Modules:
  0.0 116.4 jit_solution(10909614397749033910)
XLA Ops:
  0.0 3.2 %collective-permute-start.13 = (bf16[2,64,512]{2,1,0:T(8,128)(2,1)}, bf16[2,64,512]{2,1,0:T(8,128)(2,1)S(1)}, u32[]{:S(2)}, u32[]{:S(2)}) collective-permute-start(bf16[2,64,512]{2,1,0:T(8,128)(2,1)} %bitcast.20), channel_id=1, source_target_pairs={{0,1},{1,0},{2,3},{3,2},{4,5},{5,4},{6,7},{7,6},{8,9},{9,8},{10,11... | collective-permute-start | bytes 393224 | tf_op jit(solution)/shard_map/ppermute | solution.py:224
  3.2 1.9 %collective-permute-start.10 = (bf16[2,64,512]{2,1,0:T(8,128)(2,1)}, bf16[2,64,512]{2,1,0:T(8,128)(2,1)S(1)}, u32[]{:S(2)}, u32[]{:S(2)}) collective-permute-start(bf16[2,64,512]{2,1,0:T(8,128)(2,1)} %bitcast.21), channel_id=1, source_target_pairs={{0,2},{2,4},{4,6},{6,8},{8,10},{10,12},{12,14},{14,0},{1,3},{3,5},... | collective-permute-start | bytes 393224 | tf_op jit(solution)/shard_map/ppermute | solution.py:187
  5.1 3.9 %collective-permute-start.6 = (bf16[2,64,512]{2,1,0:T(8,128)(2,1)}, bf16[2,64,512]{2,1,0:T(8,128)(2,1)S(1)}, u32[]{:S(2)}, u32[]{:S(2)}) collective-permute-start(bf16[2,64,512]{2,1,0:T(8,128)(2,1)} %bitcast.22), channel_id=1, source_target_pairs={{0,14},{2,0},{4,2},{6,4},{8,6},{10,8},{12,10},{14,12},{1,15},{3,1}... | collective-permute-start | bytes 393224 | tf_op jit(solution)/shard_map/ppermute | solution.py:186
  9.1 0.0 collective-permute-done.13.refs_15_
  9.1 0.0 collective-permute-start.17
  9.1 3.8 %collective-permute-start.14 = (bf16[2,64,512]{2,1,0:T(8,128)(2,1)S(1)}, bf16[2,64,512]{2,1,0:T(8,128)(2,1)S(1)}, u32[]{:S(2)}, u32[]{:S(2)}) collective-permute-start(bf16[2,64,512]{2,1,0:T(8,128)(2,1)S(1)} %collective-permute-done.13.refs_15_), channel_id=1, source_target_pairs={{0,14},{2,0},{4,2},{6,4},{8,6},{10,8},{12,10},{14,12},{1,15},{3,1}... | collective-permute-start | bytes 393224 | tf_op jit(solution)/shard_map/ppermute | solution.py:186
  12.8 1.2 %copy-done = bf16[128,4096]{1,0:T(8,128)(2,1)S(1)} copy-done((bf16[128,4096]{1,0:T(8,128)(2,1)S(1)}, bf16[128,4096]{1,0:T(8,128)(2,1)}, u32[]{:S(2)}) %copy-start) | copy-done | bytes 1048600
  14.0 0.7 copy-done.2
  14.8 0.7 copy-done.4
  15.5 0.1 pack_weights.1
  15.6 0.6 collective-permute-start
  16.1 0.0 collective-permute-done.10.refs_14_
  16.1 2.4 %collective-permute-start.1 = (bf16[128,1152]{1,0:T(8,128)(2,1)S(1)}, bf16[128,1152]{1,0:T(8,128)(2,1)S(1)}, u32[]{:S(2)}, u32[]{:S(2)}) collective-permute-start(bf16[128,1152]{1,0:T(8,128)(2,1)S(1)} %get-tuple-element.12), channel_id=1, source_target_pairs={{0,32},{16,48},{32,0},{48,16},{1,33},{17,49},{33,1},{49,17},{2,34}... | collective-permute-start | bytes 884744 | tf_op jit(solution)/shard_map/ppermute | solution.py:229
  18.5 0.0 collective-permute-done.6.refs_8_
  18.5 0.0 collective-permute-start.2
  18.5 0.0 collective-permute-done.17.refs_22_
  18.5 0.1 collective-permute-start.11
  18.6 0.0 collective-permute-done.14.refs_16_
  18.6 3.2 %collective-permute-start.7 = (bf16[2,64,512]{2,1,0:T(8,128)(2,1)S(1)}, bf16[2,64,512]{2,1,0:T(8,128)(2,1)S(1)}, u32[]{:S(2)}, u32[]{:S(2)}) collective-permute-start(bf16[2,64,512]{2,1,0:T(8,128)(2,1)S(1)} %collective-permute-done.6.refs_8_), channel_id=1, source_target_pairs={{0,14},{2,0},{4,2},{6,4},{8,6},{10,8},{12,10},{14,12},{1,15},{3,1}... | collective-permute-start | bytes 393224 | tf_op jit(solution)/shard_map/ppermute | solution.py:186
  21.9 3.4 %copy-done.6 = bf16[2,512,4096]{2,1,0:T(8,128)(2,1)S(1)} copy-done((bf16[2,512,4096]{2,1,0:T(8,128)(2,1)S(1)}, bf16[2,512,4096]{2,1,0:T(8,128)(2,1)}, u32[]{:S(2)}) %copy-start.6) | copy-done | bytes 8388632
  25.2 1.2 %copy-done.7 = bf16[4096,128]{1,0:T(8,128)(2,1)S(1)} copy-done((bf16[4096,128]{1,0:T(8,128)(2,1)S(1)}, bf16[4096,128]{1,0:T(8,128)(2,1)}, u32[]{:S(2)}) %copy-start.7) | copy-done | bytes 1048600
  26.5 1.2 %copy-done.8 = bf16[4096,128]{1,0:T(8,128)(2,1)S(1)} copy-done((bf16[4096,128]{1,0:T(8,128)(2,1)S(1)}, bf16[4096,128]{1,0:T(8,128)(2,1)}, u32[]{:S(2)}) %copy-start.8) | copy-done | bytes 1048600
  27.7 1.0 copy-done.9
  28.7 1.0 copy-done.10
  29.8 0.7 copy-done.13
  30.5 0.7 copy-done.14
  31.2 10.7 %token_stage.1 = (bf16[320,1024]{1,0:T(8,128)(2,1)S(1)}, f32[1024,128]{1,0:T(8,128)S(1)}) custom-call(s32[2]{0:T(128)S(1)} %copy-done.14, bf16[1024,4096]{1,0:T(8,128)(2,1)S(1)} %bitcast.16, bf16[4096,128]{1,0:T(8,128)(2,1)S(1)} %copy-done.7, bf16[4096,128]{1,0:T(8,128)(2,1)S(1)} %copy-done.8, bf16[64,4096]{1,0:T(8,128)(2,1)S(1)} %bitcast.17, ...), custom_call_target="tpu_custom_call" | custom-call | flops 3221225472 | bytes 12582912 | tf_op jit(solution)/shard_map/token_stage/pallas_call | solution.py:82
  41.9 0.0 collective-permute-done.11.refs_13_
  41.9 1.1 collective-permute-start.5
  43.0 0.0 collective-permute-done.7.refs_9_
  43.0 3.6 %collective-permute-start.4 = (bf16[320,1024]{1,0:T(8,128)(2,1)S(1)}, bf16[320,1024]{1,0:T(8,128)(2,1)S(1)}, u32[]{:S(2)}, u32[]{:S(2)}) collective-permute-start(bf16[320,1024]{1,0:T(8,128)(2,1)S(1)} %get-tuple-element.14.refs_3_), channel_id=1, source_target_pairs={{0,32},{16,48},{32,0},{48,16},{1,33},{17,49},{33,1},{49,17},{2,34}... | collective-permute-start | bytes 1966088 | tf_op jit(solution)/shard_map/ppermute | solution.py:235
  46.6 0.0 collective-permute-done.refs_0_
  46.6 1.2 %collective-permute-start.3 = (bf16[320,1024]{1,0:T(8,128)(2,1)S(1)}, bf16[320,1024]{1,0:T(8,128)(2,1)S(1)}, u32[]{:S(2)}, u32[]{:S(2)}) collective-permute-start(bf16[320,1024]{1,0:T(8,128)(2,1)S(1)} %get-tuple-element.14.refs_3_), channel_id=1, source_target_pairs={{0,16},{16,32},{32,48},{48,0},{1,17},{17,33},{33,49},{49,1},{2,18}... | collective-permute-start | bytes 1966088 | tf_op jit(solution)/shard_map/ppermute | solution.py:235
  47.8 0.0 collective-permute-done.1.refs_1_
  47.8 0.0 collective-permute-start.18
  47.8 0.0 collective-permute-done.2.refs_2_
  47.8 3.2 %collective-permute-start.15 = (bf16[2,64,512]{2,1,0:T(8,128)(2,1)S(1)}, bf16[2,64,512]{2,1,0:T(8,128)(2,1)S(1)}, u32[]{:S(2)}, u32[]{:S(2)}) collective-permute-start(bf16[2,64,512]{2,1,0:T(8,128)(2,1)S(1)} %collective-permute-done.14.refs_16_), channel_id=1, source_target_pairs={{0,14},{2,0},{4,2},{6,4},{8,6},{10,8},{12,10},{14,12},{1,15},{3,1}... | collective-permute-start | bytes 393224 | tf_op jit(solution)/shard_map/ppermute | solution.py:186
  51.1 3.6 %collective-permute-done.18.refs_21_ = bf16[2,64,512]{2,1,0:T(8,128)(2,1)S(1)} collective-permute-done((bf16[2,64,512]{2,1,0:T(8,128)(2,1)S(1)}, bf16[2,64,512]{2,1,0:T(8,128)(2,1)S(1)}, u32[]{:S(2)}, u32[]{:S(2)}) %collective-permute-start.18) | collective-permute-done | bytes 131104 | tf_op jit(solution)/shard_map/ppermute | solution.py:187
  54.6 0.0 collective-permute-start.12
  54.6 0.0 collective-permute-done.15.refs_17_
  54.6 3.6 %collective-permute-start.8 = (bf16[2,64,512]{2,1,0:T(8,128)(2,1)S(1)}, bf16[2,64,512]{2,1,0:T(8,128)(2,1)S(1)}, u32[]{:S(2)}, u32[]{:S(2)}) collective-permute-start(bf16[2,64,512]{2,1,0:T(8,128)(2,1)S(1)} %collective-permute-done.7.refs_9_), channel_id=1, source_target_pairs={{0,14},{2,0},{4,2},{6,4},{8,6},{10,8},{12,10},{14,12},{1,15},{3,1}... | collective-permute-start | bytes 393224 | tf_op jit(solution)/shard_map/ppermute | solution.py:186
  58.2 3.9 %collective-permute-done.12.refs_12_ = bf16[2,64,512]{2,1,0:T(8,128)(2,1)S(1)} collective-permute-done((bf16[2,64,512]{2,1,0:T(8,128)(2,1)S(1)}, bf16[2,64,512]{2,1,0:T(8,128)(2,1)S(1)}, u32[]{:S(2)}, u32[]{:S(2)}) %collective-permute-start.12) | collective-permute-done | bytes 131104 | tf_op jit(solution)/shard_map/ppermute | solution.py:187
  62.1 0.0 collective-permute-start.19
  62.1 0.0 collective-permute-done.8.refs_10_
  62.1 3.2 %collective-permute-start.16 = (bf16[2,64,512]{2,1,0:T(8,128)(2,1)S(1)}, bf16[2,64,512]{2,1,0:T(8,128)(2,1)S(1)}, u32[]{:S(2)}, u32[]{:S(2)}) collective-permute-start(bf16[2,64,512]{2,1,0:T(8,128)(2,1)S(1)} %collective-permute-done.15.refs_17_), channel_id=1, source_target_pairs={{0,14},{2,0},{4,2},{6,4},{8,6},{10,8},{12,10},{14,12},{1,15},{3,1}... | collective-permute-start | bytes 393224 | tf_op jit(solution)/shard_map/ppermute | solution.py:186
  65.4 3.5 %collective-permute-done.19.refs_20_ = bf16[2,64,512]{2,1,0:T(8,128)(2,1)S(1)} collective-permute-done((bf16[2,64,512]{2,1,0:T(8,128)(2,1)S(1)}, bf16[2,64,512]{2,1,0:T(8,128)(2,1)S(1)}, u32[]{:S(2)}, u32[]{:S(2)}) %collective-permute-start.19) | collective-permute-done | bytes 131104 | tf_op jit(solution)/shard_map/ppermute | solution.py:187
  68.8 0.0 collective-permute-start.9
  68.8 0.0 collective-permute-done.16.refs_18_
  68.8 2.0 %collective-permute-start.20 = (bf16[2,64,512]{2,1,0:T(8,128)(2,1)S(1)}, bf16[2,64,512]{2,1,0:T(8,128)(2,1)S(1)}, u32[]{:S(2)}, u32[]{:S(2)}) collective-permute-start(bf16[2,64,512]{2,1,0:T(8,128)(2,1)S(1)} %collective-permute-done.19.refs_20_), channel_id=1, source_target_pairs={{0,2},{2,4},{4,6},{6,8},{8,10},{10,12},{12,14},{14,0},{1,3},{3,5},... | collective-permute-start | bytes 393224 | tf_op jit(solution)/shard_map/ppermute | solution.py:189
  70.9 2.9 %collective-permute-done.9.refs_11_ = bf16[2,64,512]{2,1,0:T(8,128)(2,1)S(1)} collective-permute-done((bf16[2,64,512]{2,1,0:T(8,128)(2,1)S(1)}, bf16[2,64,512]{2,1,0:T(8,128)(2,1)S(1)}, u32[]{:S(2)}, u32[]{:S(2)}) %collective-permute-start.9) | collective-permute-done | bytes 131104 | tf_op jit(solution)/shard_map/ppermute | solution.py:189
  73.8 1.2 %collective-permute-done.20.refs_19_ = bf16[2,64,512]{2,1,0:T(8,128)(2,1)S(1)} collective-permute-done((bf16[2,64,512]{2,1,0:T(8,128)(2,1)S(1)}, bf16[2,64,512]{2,1,0:T(8,128)(2,1)S(1)}, u32[]{:S(2)}, u32[]{:S(2)}) %collective-permute-start.20) | collective-permute-done | bytes 131104 | tf_op jit(solution)/shard_map/ppermute | solution.py:189
  75.0 0.0 collective-permute-done.5.refs_6_
  75.0 0.0 collective-permute-done.4.refs_5_
  75.0 0.0 collective-permute-done.3.refs_4_
  75.0 0.0 copy-done.1
  75.0 0.0 copy-done.3
  75.0 0.0 copy-done.5
  75.1 3.5 %tail_stage.1 = f32[6,64,64]{2,1,0:T(8,128)S(1)} custom-call(bf16[128,4096]{1,0:T(8,128)(2,1)S(1)} %copy-done.1, bf16[64,128]{1,0:T(8,128)(2,1)S(1)} %bitcast.13, bf16[64,128]{1,0:T(8,128)(2,1)S(1)} %bitcast.15, bf16[64,4096]{1,0:T(8,128)(2,1)S(1)} %bitcast.19, f32[1024,128]{1,0:T(8,128)S(1)} %get-tuple-element.10.right_ref, ...), custom_call_target="tpu_custom_call" | custom-call | flops 4000000000 | bytes 8388608 | tf_op jit(solution)/shard_map/tail_stage/pallas_call | solution.py:167
  78.5 0.1 reshape_reshape.6
  78.7 0.1 copy.26
  78.7 9.7 %all_to_all.15 = f32[16,6,256]{2,1,0:T(8,128)S(1)} all-to-all(f32[16,6,256]{2,1,0:T(8,128)S(1)} %bitcast.25), channel_id=1, replica_groups=mesh['sy'=2,'sc'=2,'x'=4,'z'=8,'yh'=2] {'sy','sc','x'}, dimensions={0} | all-to-all | bytes 196608 | tf_op jit(solution)/shard_map/all_to_all | solution.py:196
  88.5 19.2 %all_to_all.16 = f32[16,6,256]{2,1,0:T(8,128)S(1)} all-to-all(f32[16,6,256]{2,1,0:T(8,128)S(1)} %broadcast_in_dim.4), channel_id=1, replica_groups=mesh['sy'=2,'sc'=2,'x'=4,'z'=8,'yh'=2] {'z','yh'}, dimensions={0} | all-to-all | bytes 196608 | tf_op jit(solution)/shard_map/all_to_all | solution.py:199
  107.7 8.0 %all_to_all.17 = f32[4,6,256]{2,1,0:T(8,128)S(1)} all-to-all(f32[4,6,256]{2,1,0:T(8,128)S(1)} %broadcast_in_dim.5), channel_id=1, replica_groups=mesh['sy'=2,'sc'=2,'x'=4,'z'=8,'yh'=2] {'x'}, dimensions={0} | all-to-all | bytes 49152 | tf_op jit(solution)/shard_map/all_to_all | solution.py:201
  115.8 0.6 copy.23
  (23 shorter events, 0.1 us)
Async XLA Ops:
  0.0 9.1 %collective-permute-start.13 = (bf16[2,64,512]{2,1,0:T(8,128)(2,1)}, bf16[2,64,512]{2,1,0:T(8,128)(2,1)S(1)}, u32[]{:S(2)}, u32[]{:S(2)}) collective-permute-start(bf16[2,64,512]{2,1,0:T(8,128)(2,1)} %bitcast.20), channel_id=1, source_target_pairs={{0,1},{1,0},{2,3},{3,2},{4,5},{5,4},{6,7},{7,6},{8,9},{9,8},{10,11... | collective-permute-start | bytes 393224 | tf_op jit(solution)/shard_map/ppermute | solution.py:224
  3.2 12.9 %collective-permute-start.10 = (bf16[2,64,512]{2,1,0:T(8,128)(2,1)}, bf16[2,64,512]{2,1,0:T(8,128)(2,1)S(1)}, u32[]{:S(2)}, u32[]{:S(2)}) collective-permute-start(bf16[2,64,512]{2,1,0:T(8,128)(2,1)} %bitcast.21), channel_id=1, source_target_pairs={{0,2},{2,4},{4,6},{6,8},{8,10},{10,12},{12,14},{14,0},{1,3},{3,5},... | collective-permute-start | bytes 393224 | tf_op jit(solution)/shard_map/ppermute | solution.py:187
  5.1 13.4 %collective-permute-start.6 = (bf16[2,64,512]{2,1,0:T(8,128)(2,1)}, bf16[2,64,512]{2,1,0:T(8,128)(2,1)S(1)}, u32[]{:S(2)}, u32[]{:S(2)}) collective-permute-start(bf16[2,64,512]{2,1,0:T(8,128)(2,1)} %bitcast.22), channel_id=1, source_target_pairs={{0,14},{2,0},{4,2},{6,4},{8,6},{10,8},{12,10},{14,12},{1,15},{3,1}... | collective-permute-start | bytes 393224 | tf_op jit(solution)/shard_map/ppermute | solution.py:186
  9.1 9.5 %collective-permute-start.17 = (bf16[2,64,512]{2,1,0:T(8,128)(2,1)S(1)}, bf16[2,64,512]{2,1,0:T(8,128)(2,1)S(1)}, u32[]{:S(2)}, u32[]{:S(2)}) collective-permute-start(bf16[2,64,512]{2,1,0:T(8,128)(2,1)S(1)} %collective-permute-done.13.refs_15_), channel_id=1, source_target_pairs={{0,2},{2,4},{4,6},{6,8},{8,10},{10,12},{12,14},{14,0},{1,3},{3,5},... | collective-permute-start | bytes 393224 | tf_op jit(solution)/shard_map/ppermute | solution.py:187
  9.1 9.6 %collective-permute-start.14 = (bf16[2,64,512]{2,1,0:T(8,128)(2,1)S(1)}, bf16[2,64,512]{2,1,0:T(8,128)(2,1)S(1)}, u32[]{:S(2)}, u32[]{:S(2)}) collective-permute-start(bf16[2,64,512]{2,1,0:T(8,128)(2,1)S(1)} %collective-permute-done.13.refs_15_), channel_id=1, source_target_pairs={{0,14},{2,0},{4,2},{6,4},{8,6},{10,8},{12,10},{14,12},{1,15},{3,1}... | collective-permute-start | bytes 393224 | tf_op jit(solution)/shard_map/ppermute | solution.py:186
  12.8 1.2 %copy-start = (bf16[128,4096]{1,0:T(8,128)(2,1)S(1)}, bf16[128,4096]{1,0:T(8,128)(2,1)}, u32[]{:S(2)}) copy-start(bf16[128,4096]{1,0:T(8,128)(2,1)} %weight_ref.3) | copy-start | bytes 3145732
  14.0 0.7 copy-start.2
  14.8 0.7 copy-start.4
  15.5 59.5 %copy-start.1 = (bf16[128,4096]{1,0:T(8,128)(2,1)S(1)}, bf16[128,4096]{1,0:T(8,128)(2,1)}, u32[]{:S(2)}) copy-start(bf16[128,4096]{1,0:T(8,128)(2,1)} %weight_ref.3) | copy-start | bytes 3145732
  15.5 59.6 %copy-start.3 = (bf16[128,64]{0,1:T(8,128)(2,1)S(1)}, bf16[128,64]{0,1:T(8,128)(2,1)}, u32[]{:S(2)}) copy-start(bf16[128,64]{0,1:T(8,128)(2,1)} %param.18) | copy-start | bytes 49156
  15.5 59.6 %copy-start.5 = (bf16[128,64]{0,1:T(8,128)(2,1)S(1)}, bf16[128,64]{0,1:T(8,128)(2,1)}, u32[]{:S(2)}) copy-start(bf16[128,64]{0,1:T(8,128)(2,1)} %param.20) | copy-start | bytes 49156
  15.6 31.1 %collective-permute-start = (bf16[128,1152]{1,0:T(8,128)(2,1)S(1)}, bf16[128,1152]{1,0:T(8,128)(2,1)S(1)}, u32[]{:S(2)}, u32[]{:S(2)}) collective-permute-start(bf16[128,1152]{1,0:T(8,128)(2,1)S(1)} %get-tuple-element.11), channel_id=1, source_target_pairs={{0,16},{16,32},{32,48},{48,0},{1,17},{17,33},{33,49},{49,1},{2,18}... | collective-permute-start | bytes 884744 | tf_op jit(solution)/shard_map/ppermute | solution.py:229
  16.1 31.7 %collective-permute-start.1 = (bf16[128,1152]{1,0:T(8,128)(2,1)S(1)}, bf16[128,1152]{1,0:T(8,128)(2,1)S(1)}, u32[]{:S(2)}, u32[]{:S(2)}) collective-permute-start(bf16[128,1152]{1,0:T(8,128)(2,1)S(1)} %get-tuple-element.12), channel_id=1, source_target_pairs={{0,32},{16,48},{32,0},{48,16},{1,33},{17,49},{33,1},{49,17},{2,34}... | collective-permute-start | bytes 884744 | tf_op jit(solution)/shard_map/ppermute | solution.py:229
  18.5 29.3 %collective-permute-start.2 = (bf16[128,1152]{1,0:T(8,128)(2,1)S(1)}, bf16[128,1152]{1,0:T(8,128)(2,1)S(1)}, u32[]{:S(2)}, u32[]{:S(2)}) collective-permute-start(bf16[128,1152]{1,0:T(8,128)(2,1)S(1)} %get-tuple-element.13), channel_id=1, source_target_pairs={{0,48},{16,0},{32,16},{48,32},{1,49},{17,1},{33,17},{49,33},{2,50}... | collective-permute-start | bytes 884744 | tf_op jit(solution)/shard_map/ppermute | solution.py:229
  18.5 23.4 %collective-permute-start.11 = (bf16[2,64,512]{2,1,0:T(8,128)(2,1)S(1)}, bf16[2,64,512]{2,1,0:T(8,128)(2,1)S(1)}, u32[]{:S(2)}, u32[]{:S(2)}) collective-permute-start(bf16[2,64,512]{2,1,0:T(8,128)(2,1)S(1)} %collective-permute-done.10.refs_14_), channel_id=1, source_target_pairs={{0,2},{2,4},{4,6},{6,8},{8,10},{10,12},{12,14},{14,0},{1,3},{3,5},... | collective-permute-start | bytes 393224 | tf_op jit(solution)/shard_map/ppermute | solution.py:187
  18.6 24.3 %collective-permute-start.7 = (bf16[2,64,512]{2,1,0:T(8,128)(2,1)S(1)}, bf16[2,64,512]{2,1,0:T(8,128)(2,1)S(1)}, u32[]{:S(2)}, u32[]{:S(2)}) collective-permute-start(bf16[2,64,512]{2,1,0:T(8,128)(2,1)S(1)} %collective-permute-done.6.refs_8_), channel_id=1, source_target_pairs={{0,14},{2,0},{4,2},{6,4},{8,6},{10,8},{12,10},{14,12},{1,15},{3,1}... | collective-permute-start | bytes 393224 | tf_op jit(solution)/shard_map/ppermute | solution.py:186
  21.9 3.4 %copy-start.6 = (bf16[2,512,4096]{2,1,0:T(8,128)(2,1)S(1)}, bf16[2,512,4096]{2,1,0:T(8,128)(2,1)}, u32[]{:S(2)}) copy-start(bf16[2,512,4096]{2,1,0:T(8,128)(2,1)} %param.12) | copy-start | bytes 25165828
  25.2 1.2 %copy-start.7 = (bf16[4096,128]{1,0:T(8,128)(2,1)S(1)}, bf16[4096,128]{1,0:T(8,128)(2,1)}, u32[]{:S(2)}) copy-start(bf16[4096,128]{1,0:T(8,128)(2,1)} %refs_2_.1) | copy-start | bytes 3145732
  26.5 1.2 %copy-start.8 = (bf16[4096,128]{1,0:T(8,128)(2,1)S(1)}, bf16[4096,128]{1,0:T(8,128)(2,1)}, u32[]{:S(2)}) copy-start(bf16[4096,128]{1,0:T(8,128)(2,1)} %refs_3_.1) | copy-start | bytes 3145732
  27.7 1.0 copy-start.9
  28.7 1.0 copy-start.10
  29.8 0.7 copy-start.13
  30.5 0.7 copy-start.14
  31.2 43.9 %copy-start.11 = (bf16[4096,64]{0,1:T(8,128)(2,1)S(1)}, bf16[4096,64]{0,1:T(8,128)(2,1)}, u32[]{:S(2)}) copy-start(bf16[4096,64]{0,1:T(8,128)(2,1)} %param.22) | copy-start | bytes 1572868
  31.2 43.9 %copy-start.12 = (bf16[2,512,64]{1,2,0:T(8,128)(2,1)S(1)}, bf16[2,512,64]{1,2,0:T(8,128)(2,1)}, u32[]{:S(2)}) copy-start(bf16[2,512,64]{1,2,0:T(8,128)(2,1)} %param.13) | copy-start | bytes 393220
  41.9 33.1 %collective-permute-start.5 = (bf16[320,1024]{1,0:T(8,128)(2,1)S(1)}, bf16[320,1024]{1,0:T(8,128)(2,1)S(1)}, u32[]{:S(2)}, u32[]{:S(2)}) collective-permute-start(bf16[320,1024]{1,0:T(8,128)(2,1)S(1)} %get-tuple-element.14.refs_3_), channel_id=1, source_target_pairs={{0,48},{16,0},{32,16},{48,32},{1,49},{17,1},{33,17},{49,33},{2,50}... | collective-permute-start | bytes 1966088 | tf_op jit(solution)/shard_map/ppermute | solution.py:235
  43.0 32.0 %collective-permute-start.4 = (bf16[320,1024]{1,0:T(8,128)(2,1)S(1)}, bf16[320,1024]{1,0:T(8,128)(2,1)S(1)}, u32[]{:S(2)}, u32[]{:S(2)}) collective-permute-start(bf16[320,1024]{1,0:T(8,128)(2,1)S(1)} %get-tuple-element.14.refs_3_), channel_id=1, source_target_pairs={{0,32},{16,48},{32,0},{48,16},{1,33},{17,49},{33,1},{49,17},{2,34}... | collective-permute-start | bytes 1966088 | tf_op jit(solution)/shard_map/ppermute | solution.py:235
  46.6 28.4 %collective-permute-start.3 = (bf16[320,1024]{1,0:T(8,128)(2,1)S(1)}, bf16[320,1024]{1,0:T(8,128)(2,1)S(1)}, u32[]{:S(2)}, u32[]{:S(2)}) collective-permute-start(bf16[320,1024]{1,0:T(8,128)(2,1)S(1)} %get-tuple-element.14.refs_3_), channel_id=1, source_target_pairs={{0,16},{16,32},{32,48},{48,0},{1,17},{17,33},{33,49},{49,1},{2,18}... | collective-permute-start | bytes 1966088 | tf_op jit(solution)/shard_map/ppermute | solution.py:235
  47.8 6.8 %collective-permute-start.18 = (bf16[2,64,512]{2,1,0:T(8,128)(2,1)S(1)}, bf16[2,64,512]{2,1,0:T(8,128)(2,1)S(1)}, u32[]{:S(2)}, u32[]{:S(2)}) collective-permute-start(bf16[2,64,512]{2,1,0:T(8,128)(2,1)S(1)} %collective-permute-done.17.refs_22_), channel_id=1, source_target_pairs={{0,2},{2,4},{4,6},{6,8},{8,10},{10,12},{12,14},{14,0},{1,3},{3,5},... | collective-permute-start | bytes 393224 | tf_op jit(solution)/shard_map/ppermute | solution.py:187
  47.8 6.8 %collective-permute-start.15 = (bf16[2,64,512]{2,1,0:T(8,128)(2,1)S(1)}, bf16[2,64,512]{2,1,0:T(8,128)(2,1)S(1)}, u32[]{:S(2)}, u32[]{:S(2)}) collective-permute-start(bf16[2,64,512]{2,1,0:T(8,128)(2,1)S(1)} %collective-permute-done.14.refs_16_), channel_id=1, source_target_pairs={{0,14},{2,0},{4,2},{6,4},{8,6},{10,8},{12,10},{14,12},{1,15},{3,1}... | collective-permute-start | bytes 393224 | tf_op jit(solution)/shard_map/ppermute | solution.py:186
  54.6 7.5 %collective-permute-start.12 = (bf16[2,64,512]{2,1,0:T(8,128)(2,1)S(1)}, bf16[2,64,512]{2,1,0:T(8,128)(2,1)S(1)}, u32[]{:S(2)}, u32[]{:S(2)}) collective-permute-start(bf16[2,64,512]{2,1,0:T(8,128)(2,1)S(1)} %collective-permute-done.11.refs_13_), channel_id=1, source_target_pairs={{0,2},{2,4},{4,6},{6,8},{8,10},{10,12},{12,14},{14,0},{1,3},{3,5},... | collective-permute-start | bytes 393224 | tf_op jit(solution)/shard_map/ppermute | solution.py:187
  54.6 7.5 %collective-permute-start.8 = (bf16[2,64,512]{2,1,0:T(8,128)(2,1)S(1)}, bf16[2,64,512]{2,1,0:T(8,128)(2,1)S(1)}, u32[]{:S(2)}, u32[]{:S(2)}) collective-permute-start(bf16[2,64,512]{2,1,0:T(8,128)(2,1)S(1)} %collective-permute-done.7.refs_9_), channel_id=1, source_target_pairs={{0,14},{2,0},{4,2},{6,4},{8,6},{10,8},{12,10},{14,12},{1,15},{3,1}... | collective-permute-start | bytes 393224 | tf_op jit(solution)/shard_map/ppermute | solution.py:186
  62.1 6.7 %collective-permute-start.19 = (bf16[2,64,512]{2,1,0:T(8,128)(2,1)S(1)}, bf16[2,64,512]{2,1,0:T(8,128)(2,1)S(1)}, u32[]{:S(2)}, u32[]{:S(2)}) collective-permute-start(bf16[2,64,512]{2,1,0:T(8,128)(2,1)S(1)} %collective-permute-done.18.refs_21_), channel_id=1, source_target_pairs={{0,2},{2,4},{4,6},{6,8},{8,10},{10,12},{12,14},{14,0},{1,3},{3,5},... | collective-permute-start | bytes 393224 | tf_op jit(solution)/shard_map/ppermute | solution.py:187
  62.1 6.7 %collective-permute-start.16 = (bf16[2,64,512]{2,1,0:T(8,128)(2,1)S(1)}, bf16[2,64,512]{2,1,0:T(8,128)(2,1)S(1)}, u32[]{:S(2)}, u32[]{:S(2)}) collective-permute-start(bf16[2,64,512]{2,1,0:T(8,128)(2,1)S(1)} %collective-permute-done.15.refs_17_), channel_id=1, source_target_pairs={{0,14},{2,0},{4,2},{6,4},{8,6},{10,8},{12,10},{14,12},{1,15},{3,1}... | collective-permute-start | bytes 393224 | tf_op jit(solution)/shard_map/ppermute | solution.py:186
  68.8 5.0 %collective-permute-start.9 = (bf16[2,64,512]{2,1,0:T(8,128)(2,1)S(1)}, bf16[2,64,512]{2,1,0:T(8,128)(2,1)S(1)}, u32[]{:S(2)}, u32[]{:S(2)}) collective-permute-start(bf16[2,64,512]{2,1,0:T(8,128)(2,1)S(1)} %collective-permute-done.8.refs_10_), channel_id=1, source_target_pairs={{0,14},{2,0},{4,2},{6,4},{8,6},{10,8},{12,10},{14,12},{1,15},{3,1}... | collective-permute-start | bytes 393224 | tf_op jit(solution)/shard_map/ppermute | solution.py:189
  68.8 6.2 %collective-permute-start.20 = (bf16[2,64,512]{2,1,0:T(8,128)(2,1)S(1)}, bf16[2,64,512]{2,1,0:T(8,128)(2,1)S(1)}, u32[]{:S(2)}, u32[]{:S(2)}) collective-permute-start(bf16[2,64,512]{2,1,0:T(8,128)(2,1)S(1)} %collective-permute-done.19.refs_20_), channel_id=1, source_target_pairs={{0,2},{2,4},{4,6},{6,8},{8,10},{10,12},{12,14},{14,0},{1,3},{3,5},... | collective-permute-start | bytes 393224 | tf_op jit(solution)/shard_map/ppermute | solution.py:189

commit v3 on v2

--- a/solution.py
+++ b/solution.py
@@ -10,6 +10,7 @@
 NX, NZ, NY = FSDP_PARTS
 MIB = 1024 * 1024
 VMEM = pl.BlockSpec(memory_space=pltpu.VMEM)
+HBM = pl.BlockSpec(memory_space=pltpu.HBM)
 
 
 def shifted(count, step):
@@ -20,15 +21,24 @@
     return lax.dot_general(a, b, (dims, ((), ())), preferred_element_type=jnp.float32, precision=precision)
 
 
-def pack_kernel(weight_ref, gate_ref, up_ref, *outs):
-    width = weight_ref.shape[1] // NX
-    rank = gate_ref.shape[0]
+def pack_kernel(weight_hbm, gate_hbm, up_hbm, *refs):
+    outs, sems = refs[: NX - 1], refs[NX - 1]
+    width = weight_hbm.shape[1] // NX
+    rank = gate_hbm.shape[0]
     x_at = lax.axis_index("x")
+    copies = []
     for step, out in enumerate(outs, 1):
         start = pl.multiple_of(lax.rem(x_at + step, NX) * width, width)
-        out[:, :width] = weight_ref[:, pl.ds(start, width)]
-        out[:rank, width:] = gate_ref[...]
-        out[rank:, width:] = up_ref[...]
+        copies += [
+            (weight_hbm.at[:, pl.ds(start, width)], out.at[:, pl.ds(0, width)]),
+            (gate_hbm, out.at[pl.ds(0, rank), pl.ds(width, weight_hbm.shape[0])]),
+            (up_hbm, out.at[pl.ds(rank, rank), pl.ds(width, weight_hbm.shape[0])]),
+        ]
+    copies = [pltpu.make_async_copy(a, b, sems.at[k]) for k, (a, b) in enumerate(copies)]
+    for copy in copies:
+        copy.start()
+    for copy in copies:
+        copy.wait()
 
 
 def pack_weights(down_weight, gate_out, up_out):
@@ -37,81 +47,119 @@
     return pl.pallas_call(
         pack_kernel,
         out_shape=[shape] * (NX - 1),
-        in_specs=[VMEM] * 3,
+        in_specs=[HBM] * 3,
         out_specs=[VMEM] * (NX - 1),
-        compiler_params=pltpu.CompilerParams(vmem_limit_bytes=16 * MIB),
+        scratch_shapes=[pltpu.SemaphoreType.DMA((3 * (NX - 1),))],
+        compiler_params=pltpu.CompilerParams(vmem_limit_bytes=62 * MIB),
+        cost_estimate=pl.CostEstimate(flops=0, bytes_accessed=2 * MIB, transcendentals=0),
         name="pack_weights",
     )(down_weight, gate_out, up_out)
 
 
-def token_kernel(tile, seq_dev, scale, lengths_ref, tokens_ref, gate_ref, up_ref, gate_in_ref, up_in_ref, down_in_ref, factors_ref, right_ref):
-    hidden = gate_ref.shape[1]
-    rank = gate_in_ref.shape[0]
-    step = pl.program_id(0)
-    tokens = tokens_ref[...]
-    gate = jnp.dot(tokens, gate_ref[...], preferred_element_type=jnp.float32)
-    up = jnp.dot(tokens, up_ref[...], preferred_element_type=jnp.float32)
-    sigmoid = 1.0 / (1.0 + jnp.exp(-gate))
-    silu = gate * sigmoid
-    factor_gate = up * sigmoid * (1.0 + gate * (1.0 - sigmoid))
-    hidden_value = (silu * up).astype(jnp.bfloat16)
-    factors_ref[:hidden, :] = factor_gate.T.astype(jnp.bfloat16)
-    factors_ref[hidden : 2 * hidden, :] = silu.T.astype(jnp.bfloat16)
-
+def pair_kernel(own_ref, other_ref, after_ref, out_ref):
+    piece = own_ref.shape[1]
+    out_ref[:, :piece, :] = own_ref[...]
+    out_ref[:, piece:, :] = other_ref[...]
+
+
+def pair_up(own, other, after):
+    examples, piece, seq_dev = own.shape
+    return pl.pallas_call(
+        pair_kernel,
+        out_shape=jax.ShapeDtypeStruct((examples, NY * piece, seq_dev), own.dtype),
+        in_specs=[VMEM, VMEM, HBM],
+        out_specs=VMEM,
+        compiler_params=pltpu.CompilerParams(vmem_limit_bytes=4 * MIB),
+        name="pair_up",
+    )(own, other, after)
+
+
+def token_kernel(tile, seq_dev, scale, lengths_ref, tokens_hbm, gate_hbm, up_hbm, gate_in_hbm, up_in_hbm, down_in_hbm, after_ref, factors_ref, right_ref, tokens_ref, weight_ref, in_ref, down_in_ref, sems):
+    model_width, hidden = gate_hbm.shape
+    rank = gate_in_hbm.shape[0]
+    tiles = tokens_hbm.shape[0] // tile
+    pairs = [
+        (gate_hbm, weight_ref.at[:, pl.ds(0, hidden)]),
+        (up_hbm, weight_ref.at[:, pl.ds(hidden, hidden)]),
+        (down_in_hbm, down_in_ref),
+        (tokens_hbm.at[pl.ds(0, tile)], tokens_ref.at[pl.ds(0, tile)]),
+        (gate_in_hbm, in_ref.at[pl.ds(0, rank)]),
+        (up_in_hbm, in_ref.at[pl.ds(rank, rank)]),
+    ]
+    pairs += [
+        (tokens_hbm.at[pl.ds(k * tile, tile)], tokens_ref.at[pl.ds(k * tile, tile)]) for k in range(1, tiles)
+    ]
+    copies = [pltpu.make_async_copy(a, b, sems.at[k]) for k, (a, b) in enumerate(pairs)]
+    for copy in copies:
+        copy.start()
+    for copy in copies[:4]:
+        copy.wait()
     per_example = seq_dev // tile
     seq_index = lax.axis_index("sy") * SEQ_PARTS[1] + lax.axis_index("sc")
-    first = seq_index * seq_dev + lax.rem(step, per_example) * tile
-    limit = lengths_ref[step // per_example]
-    columns = first + lax.broadcasted_iota(jnp.int32, (rank, tile), 1)
-    right_down = dot32(down_in_ref[...], hidden_value, ((1,), (1,)))
-    right_down = jnp.where(columns < limit, right_down * scale, 0.0)
-    factors_ref[2 * hidden :, :] = right_down.astype(jnp.bfloat16)
-    rows = first + lax.broadcasted_iota(jnp.int32, (tile, rank), 0)
-    valid = rows < limit
-    right_gate = dot32(tokens, gate_in_ref[...], ((1,), (1,)))
-    right_up = dot32(tokens, up_in_ref[...], ((1,), (1,)))
-    right_ref[:, :rank] = jnp.where(valid, right_gate * scale, 0.0)
-    right_ref[:, rank:] = jnp.where(valid, right_up * scale, 0.0)
-
-
-def token_stage(tokens, gate_weight, up_weight, gate_in, up_in, down_in, lengths, seq_dev, scale):
+    for step in range(tiles):
+        if step > 0:
+            copies[5 + step].wait()
+        span = slice(step * tile, (step + 1) * tile)
+        tokens = tokens_ref[span, :]
+        values = jnp.dot(tokens, weight_ref[...], preferred_element_type=jnp.float32)
+        gate, up = values[:, :hidden], values[:, hidden:]
+        sigmoid = 1.0 / (1.0 + jnp.exp(-gate))
+        silu = gate * sigmoid
+        factor_gate = up * sigmoid * (1.0 + gate * (1.0 - sigmoid))
+        hidden_value = (silu * up).astype(jnp.bfloat16)
+        factors_ref[:hidden, span] = factor_gate.T.astype(jnp.bfloat16)
+        factors_ref[hidden : 2 * hidden, span] = silu.T.astype(jnp.bfloat16)
+
+        first = seq_index * seq_dev + (step % per_example) * tile
+        limit = lengths_ref[step // per_example]
+        columns = first + lax.broadcasted_iota(jnp.int32, (rank, tile), 1)
+        right_down = dot32(down_in_ref[...], hidden_value, ((1,), (1,)))
+        right_down = jnp.where(columns < limit, right_down * scale, 0.0)
+        factors_ref[2 * hidden :, span] = right_down.astype(jnp.bfloat16)
+        if step == 0:
+            copies[4].wait()
+            copies[5].wait()
+        rows = first + lax.broadcasted_iota(jnp.int32, (tile, 2 * rank), 0)
+        right = dot32(tokens, in_ref[...], ((1,), (1,)))
+        right_ref[span, :] = jnp.where(rows < limit, right * scale, 0.0)
+
+
+def token_stage(tokens, gate_weight, up_weight, gate_in, up_in, down_in, lengths, after, seq_dev, scale):
     rows, width = tokens.shape
     hidden = gate_weight.shape[1]
     rank = gate_in.shape[0]
     tile = 256
     return pl.pallas_call(
         lambda *refs: token_kernel(tile, seq_dev, scale, *refs),
-        grid=(rows // tile,),
         out_shape=[
             jax.ShapeDtypeStruct((2 * hidden + rank, rows), jnp.bfloat16),
             jax.ShapeDtypeStruct((rows, 2 * rank), jnp.float32),
         ],
-        in_specs=[
-            pl.BlockSpec(memory_space=pltpu.SMEM),
-            pl.BlockSpec((tile, width), lambda i: (i, 0)),
-            VMEM,
-            VMEM,
-            VMEM,
-            VMEM,
-            VMEM,
+        in_specs=[pl.BlockSpec(memory_space=pltpu.SMEM)] + [HBM] * 7,
+        out_specs=[VMEM, VMEM],
+        scratch_shapes=[
+            pltpu.VMEM((rows, width), jnp.bfloat16),
+            pltpu.VMEM((width, 2 * hidden), jnp.bfloat16),
+            pltpu.VMEM((2 * rank, width), jnp.bfloat16),
+            pltpu.VMEM((rank, hidden), jnp.bfloat16),
+            pltpu.SemaphoreType.DMA((5 + rows // tile,)),
         ],
-        out_specs=[
-            pl.BlockSpec((2 * hidden + rank, tile), lambda i: (0, i)),
-            pl.BlockSpec((tile, 2 * rank), lambda i: (i, 0)),
-        ],
-        compiler_params=pltpu.CompilerParams(vmem_limit_bytes=40 * MIB),
-        cost_estimate=pl.CostEstimate(flops=2 * rows * width * 384, bytes_accessed=12 * MIB, transcendentals=rows * hidden),
+        compiler_params=pltpu.CompilerParams(vmem_limit_bytes=62 * MIB),
+        cost_estimate=pl.CostEstimate(
+            flops=2 * rows * width * 512, bytes_accessed=16 * MIB, transcendentals=rows * hidden
+        ),
         name="token_stage",
-    )(lengths, tokens, gate_weight, up_weight, gate_in, up_in, down_in)
+    )(lengths, tokens, gate_weight, up_weight, gate_in, up_in, down_in, after)
 
 
 def tail_kernel(weight_ref, gate_out_ref, up_out_ref, down_out_ref, right_ref, *refs):
-    packs, factors, own, other = refs[:3], refs[3:7], refs[7:15], refs[15:23]
-    out_ref, weights, projs, grads = refs[23:]
+    packs, factors, blocks = refs[:3], refs[3:7], refs[7:15]
+    out_ref, weights, projs, grads = refs[15:]
     hidden, model_width = weight_ref.shape
     rank = gate_out_ref.shape[0]
     width = model_width // NX
-    examples, piece, seq_dev = own[0].shape
+    examples, piece, seq_dev = blocks[0].shape
+    piece = piece // NY
     x_at, z_at, y_at = lax.axis_index("x"), lax.axis_index("z"), lax.axis_index("yh")
 
     start = pl.multiple_of(x_at * width, width)
@@ -125,8 +173,8 @@
     for example in range(examples):
         for step in range(NZ):
             block = lax.rem(z_at + step, NZ) * (NY * piece)
-            grads[pl.ds(pl.multiple_of(block + y_at * piece, piece), piece), :] = own[step][example]
-            grads[pl.ds(pl.multiple_of(block + (1 - y_at) * piece, piece), piece), :] = other[step][example]
+            grads[pl.ds(pl.multiple_of(block + y_at * piece, piece), piece), :] = blocks[step][example, :piece]
+            grads[pl.ds(pl.multiple_of(block + (1 - y_at) * piece, piece), piece), :] = blocks[step][example, piece:]
         columns = slice(example * seq_dev, (example + 1) * seq_dev)
         total = jnp.dot(weights[...], grads[...], preferred_element_type=jnp.float32)
         left = []
@@ -158,12 +206,12 @@
         )
 
 
-def tail_stage(down_weight, gate_out, up_out, down_out, right, packs, factors, own, other):
+def tail_stage(down_weight, gate_out, up_out, down_out, right, packs, factors, blocks):
     hidden, model_width = down_weight.shape
     rank = gate_out.shape[0]
-    examples, piece, seq_dev = own[0].shape
+    examples, piece, seq_dev = blocks[0].shape
     width = model_width // NX
-    operands = [down_weight, gate_out, up_out, down_out, right, *packs, *factors, *own, *other]
+    operands = [down_weight, gate_out, up_out, down_out, right, *packs, *factors, *blocks]
     return pl.pallas_call(
         tail_kernel,
         out_shape=jax.ShapeDtypeStruct((examples * 3, rank, rank), jnp.float32),
@@ -180,13 +228,12 @@
     )(*operands)
 
 
-def ring_z(own, far_step):
+def ring_z(own):
     up, down = [own], [own]
     for _ in range(NZ // 2 - 1):
         up.append(lax.ppermute(up[-1], "z", shifted(NZ, -1)))
         down.append(lax.ppermute(down[-1], "z", shifted(NZ, 1)))
-    last = up[-1] if far_step < 0 else down[-1]
-    return up + [lax.ppermute(last, "z", shifted(NZ, far_step))] + down[:0:-1]
+    return up + [lax.ppermute(up[-1], "z", shifted(NZ, -1))] + down[:0:-1]
 
 
 def sum_everywhere(partial):
@@ -222,20 +269,28 @@
 
     own_grad = out_grad.transpose(0, 2, 1)
     other_grad = lax.ppermute(own_grad, "yh", shifted(NY, 1))
-    own = ring_z(own_grad, -1)
-    other = ring_z(other_grad, 1)
-
     sent = pack_weights(down_weight, gate_out, up_out)
     packs = [lax.ppermute(piece, "x", shifted(NX, step)) for step, piece in enumerate(sent, 1)]
+    pair = pair_up(own_grad, other_grad, sent[0])
+    blocks = ring_z(pair)
 
     flat_tokens = tokens.reshape(examples * seq_dev, model_width)
     factors, right = token_stage(
-        flat_tokens, gate_weight, up_weight, proj_gate_in.T, proj_up_in.T, proj_down_in.T, lengths, seq_dev, scale
+        flat_tokens,
+        gate_weight,
+        up_weight,
+        proj_gate_in.T,
+        proj_up_in.T,
+        proj_down_in.T,
+        lengths,
+        pair,
+        seq_dev,
+        scale,
     )
     factors = [factors] + [lax.ppermute(factors, "x", shifted(NX, step)) for step in range(1, NX)]
 
     products = tail_stage(
-        down_weight, gate_out, up_out, proj_down_out.T, right, packs, factors, own, other
+        down_weight, gate_out, up_out, proj_down_out.T, right, packs, factors, blocks
     )
     total = sum_everywhere(products.reshape(examples * 3, -1))
     return total.reshape(examples, 3, -1)

time: 118 us -> 111 us (0.941)
  starting transfers between devices: 37 us -> 26.7 us
  local copies, waits for them, and re-layouts: 12.8 us -> 4.85 us
  waiting for transfers between devices: 15.2 us -> 23 us
  Pallas kernels: 14.3 us -> 21 us
  blocking collectives: 37 us -> 34.6 us
    ppermute x3, waiting for transfers between devices: 0.01 us -> 15.1 us  [shards(): lax.ppermute(factors, 'x', shifted(NX, step))]
    ppermute x6 -> x3, starting transfers between devices: 20.9 us -> 13 us  [ring_z(): up.append(lax.ppermute(up[-1], 'z', shifted(NZ, -1)))]
    unnamed x30 -> x18, local copies, waits for them, and re-layouts: 12 us -> 4 us
    ppermute x6 -> x3, waiting for transfers between devices: 11 us -> 4.61 us  [ring_z(): down.append(lax.ppermute(down[-1], 'z', shifted(NZ, 1)))]
    pallas_call x2 -> x3, Pallas kernels: 10.8 us -> 16.2 us  [the longest x1 13.9 us: token_stage(): pl.pallas_call(lambda *refs: token_kernel(tile, seq_dev, scale, *refs), o...]
    ppermute x2 -> x1, waiting for transfers between devices: 4.16 us -> 0.01 us  [ring_z(): return up + [lax.ppermute(up[-1], 'z', shifted(NZ, -1))] + down[:0:-1]]
    all_to_all x1, blocking collectives: 19.2 us -> 16.7 us  [sum_everywhere(): own = jnp.sum(lax.all_to_all(spread, ('z', 'yh'), 0, 0, tiled=True), axis=0)]
    ppermute x6 -> x3, starting transfers between devices: 2.01 us -> 0.01 us  [ring_z(): down.append(lax.ppermute(down[-1], 'z', shifted(NZ, 1)))]
  transfers between devices with their start and end apart: 21 -> 14, of which waited for: 5 -> 5; matrix products, arithmetic and copies ran while one was open for 0% -> 0% of each run, Pallas kernels for 9% -> 15%
where the time goes in v3:
time: 111 us; the launch traced here: 110 us
  blocking collectives  34.6 us (31%)
  starting transfers between devices  26.7 us (24%)
  waiting for transfers between devices  23 us (21%)
  Pallas kernels  21 us (19%)
  local copies, waits for them, and re-layouts  4.85 us (4%)
    all_to_all x1, blocking collectives, sum_everywhere(): own = jnp.sum(lax.all_to_all(spread, ('z', 'yh'), 0, 0, tiled=True), axis=0)  16.7 us
    ppermute x3, waiting for transfers between devices, shards(): lax.ppermute(factors, 'x', shifted(NX, step))  15.1 us
    pallas_call x1, Pallas kernels, token_stage(): pl.pallas_call(lambda *refs: token_kernel(tile, seq_dev, scale, *refs), o...  13.9 us
    ppermute x3, starting transfers between devices, ring_z(): up.append(lax.ppermute(up[-1], 'z', shifted(NZ, -1)))  13 us
    all_to_all x1, blocking collectives, sum_everywhere(): pieces = lax.all_to_all(pieces, ('sy', 'sc', 'x'), 0, 0, tiled=True)  9.91 us
    all_to_all x1, blocking collectives, sum_everywhere(): blocks = lax.all_to_all(spread, 'x', 0, 0, tiled=True)  8.01 us
    pallas_call x1, Pallas kernels, tail_stage(): pl.pallas_call(tail_kernel, out_shape=jax.ShapeDtypeStruct((examples * 3,...  4.77 us
    ppermute x3, waiting for transfers between devices, ring_z(): down.append(lax.ppermute(down[-1], 'z', shifted(NZ, 1)))  4.61 us
  transfers between devices with their start and end apart: 14, of which 5 were waited for; matrix products, arithmetic and copies ran while one was open for 0% of the time, Pallas kernels for 15%

profile of v3, /device:TPU:6, one launch (start us, length us, event | category | flops | bytes accessed | tf_op | source)
XLA Modules:
  0.0 110.3 jit_solution(10255759841667392063)
XLA Ops:
  0.0 3.2 %collective-permute-start = (bf16[2,64,512]{2,1,0:T(8,128)(2,1)}, bf16[2,64,512]{2,1,0:T(8,128)(2,1)S(1)}, u32[]{:S(2)}, u32[]{:S(2)}) collective-permute-start(bf16[2,64,512]{2,1,0:T(8,128)(2,1)} %bitcast.12), channel_id=1, source_target_pairs={{0,1},{1,0},{2,3},{3,2},{4,5},{5,4},{6,7},{7,6},{8,9},{9,8},{10,11... | collective-permute-start | bytes 393224 | tf_op jit(solution)/shard_map/ppermute | solution.py:271
  3.2 0.0 copy-start.4
  3.2 0.0 copy-start.5
  3.2 0.0 copy-start.7
  3.2 2.3 %pack_weights.1 = (bf16[128,1152]{1,0:T(8,128)(2,1)}, bf16[128,1152]{1,0:T(8,128)(2,1)}, bf16[128,1152]{1,0:T(8,128)(2,1)}) custom-call(bf16[128,4096]{1,0:T(8,128)(2,1)} %weight_ref.1, bf16[64,128]{1,0:T(8,128)(2,1)} %bitcast.14, bf16[64,128]{1,0:T(8,128)(2,1)} %bitcast.16), custom_call_target="tpu_custom_call" | custom-call | bytes 2097152 | tf_op jit(solution)/shard_map/pack_weights/pallas_call | solution.py:47
  5.5 0.0 copy-start
  5.5 1.5 %collective-permute-done.other_ref = bf16[2,64,512]{2,1,0:T(8,128)(2,1)S(1)} collective-permute-done((bf16[2,64,512]{2,1,0:T(8,128)(2,1)}, bf16[2,64,512]{2,1,0:T(8,128)(2,1)S(1)}, u32[]{:S(2)}, u32[]{:S(2)}) %collective-permute-start) | collective-permute-done | bytes 131104 | tf_op jit(solution)/shard_map/ppermute | solution.py:271
  7.0 0.0 copy-start.3
  7.0 0.9 copy-done.3
  7.9 0.0 copy-start.1
  7.9 5.9 %collective-permute-start.7 = (bf16[2,128,512]{2,1,0:T(8,128)(2,1)S(1)}, bf16[2,128,512]{2,1,0:T(8,128)(2,1)}, u32[]{:S(2)}, u32[]{:S(2)}) collective-permute-start(bf16[2,128,512]{2,1,0:T(8,128)(2,1)S(1)} %pair_up.1.refs_7_), channel_id=1, source_target_pairs={{0,14},{2,0},{4,2},{6,4},{8,6},{10,8},{12,10},{14,12},{1,15},{3,1}... | collective-permute-start | bytes 786440 | tf_op jit(solution)/shard_map/ppermute | solution.py:234
  13.8 0.5 collective-permute-start.1
  14.3 2.4 %collective-permute-start.2 = (bf16[128,1152]{1,0:T(8,128)(2,1)}, bf16[128,1152]{1,0:T(8,128)(2,1)}, u32[]{:S(2)}, u32[]{:S(2)}) collective-permute-start(bf16[128,1152]{1,0:T(8,128)(2,1)} %get-tuple-element.12), channel_id=1, source_target_pairs={{0,32},{16,48},{32,0},{48,16},{1,33},{17,49},{33,1},{49,17},{2,34}... | collective-permute-start | bytes 884744 | tf_op jit(solution)/shard_map/ppermute | solution.py:273
  16.7 0.0 collective-permute-start.3
  16.7 0.0 collective-permute-start.11
  16.7 1.8 %collective-permute-done.7.refs_8_ = bf16[2,128,512]{2,1,0:T(8,128)(2,1)} collective-permute-done((bf16[2,128,512]{2,1,0:T(8,128)(2,1)S(1)}, bf16[2,128,512]{2,1,0:T(8,128)(2,1)}, u32[]{:S(2)}, u32[]{:S(2)}) %collective-permute-start.7) | collective-permute-done | bytes 262176 | tf_op jit(solution)/shard_map/ppermute | solution.py:234
  18.5 3.8 %collective-permute-start.8 = (bf16[2,128,512]{2,1,0:T(8,128)(2,1)}, bf16[2,128,512]{2,1,0:T(8,128)(2,1)}, u32[]{:S(2)}, u32[]{:S(2)}) collective-permute-start(bf16[2,128,512]{2,1,0:T(8,128)(2,1)} %collective-permute-done.7.refs_8_), channel_id=1, source_target_pairs={{0,14},{2,0},{4,2},{6,4},{8,6},{10,8},{12,10},{14,12},{1,15},{3,1}... | collective-permute-start | bytes 786440 | tf_op jit(solution)/shard_map/ppermute | solution.py:234
  22.3 0.0 copy-done.1
  22.3 13.9 %token_stage.1 = (bf16[320,1024]{1,0:T(8,128)(2,1)}, f32[1024,128]{1,0:T(8,128)}) custom-call(s32[2]{0:T(128)} %refs_0_.1, bf16[1024,4096]{1,0:T(8,128)(2,1)} %bitcast.21, bf16[4096,128]{1,0:T(8,128)(2,1)} %refs_2_.1, bf16[4096,128]{1,0:T(8,128)(2,1)} %refs_3_.1, bf16[64,4096]{1,0:T(8,128)(2,1)} %bitcast.22, bf16[64,4096]{1,0:T(8,128)(2,1)} %bitcast.23, ...), custom_call_target="tpu_custom_call" | custom-call | flops 4294967296 | bytes 16777216 | tf_op jit(solution)/shard_map/token_stage/pallas_call | solution.py:132
  36.2 0.0 collective-permute-done.2.refs_1_
  36.2 0.9 collective-permute-start.6
  37.1 0.0 collective-permute-done.3.refs_2_
  37.2 1.5 %collective-permute-start.5 = (bf16[320,1024]{1,0:T(8,128)(2,1)}, bf16[320,1024]{1,0:T(8,128)(2,1)S(1)}, u32[]{:S(2)}, u32[]{:S(2)}) collective-permute-start(bf16[320,1024]{1,0:T(8,128)(2,1)} %get-tuple-element.14.refs_3_), channel_id=1, source_target_pairs={{0,32},{16,48},{32,0},{48,16},{1,33},{17,49},{33,1},{49,17},{2,34}... | collective-permute-start | bytes 1966088 | tf_op jit(solution)/shard_map/ppermute | solution.py:290
  38.7 0.0 collective-permute-done.1.refs_0_
  38.7 1.7 %collective-permute-start.4 = (bf16[320,1024]{1,0:T(8,128)(2,1)}, bf16[320,1024]{1,0:T(8,128)(2,1)S(1)}, u32[]{:S(2)}, u32[]{:S(2)}) collective-permute-start(bf16[320,1024]{1,0:T(8,128)(2,1)} %get-tuple-element.14.refs_3_), channel_id=1, source_target_pairs={{0,16},{16,32},{32,48},{48,0},{1,17},{17,33},{33,49},{49,1},{2,18}... | collective-permute-start | bytes 1966088 | tf_op jit(solution)/shard_map/ppermute | solution.py:290
  40.4 0.0 collective-permute-done.11.refs_14_
  40.4 0.0 collective-permute-start.12
  40.4 0.0 collective-permute-done.8.refs_9_
  40.4 3.2 %collective-permute-start.9 = (bf16[2,128,512]{2,1,0:T(8,128)(2,1)}, bf16[2,128,512]{2,1,0:T(8,128)(2,1)S(1)}, u32[]{:S(2)}, u32[]{:S(2)}) collective-permute-start(bf16[2,128,512]{2,1,0:T(8,128)(2,1)} %collective-permute-done.8.refs_9_), channel_id=1, source_target_pairs={{0,14},{2,0},{4,2},{6,4},{8,6},{10,8},{12,10},{14,12},{1,15},{3,1}... | collective-permute-start | bytes 786440 | tf_op jit(solution)/shard_map/ppermute | solution.py:234
  43.6 4.6 %collective-permute-done.12.refs_13_ = bf16[2,128,512]{2,1,0:T(8,128)(2,1)S(1)} collective-permute-done((bf16[2,128,512]{2,1,0:T(8,128)(2,1)}, bf16[2,128,512]{2,1,0:T(8,128)(2,1)S(1)}, u32[]{:S(2)}, u32[]{:S(2)}) %collective-permute-start.12) | collective-permute-done | bytes 262176 | tf_op jit(solution)/shard_map/ppermute | solution.py:235
  48.2 0.0 collective-permute-start.13
  48.2 0.0 collective-permute-done.9.refs_10_
  48.2 3.5 %collective-permute-start.10 = (bf16[2,128,512]{2,1,0:T(8,128)(2,1)S(1)}, bf16[2,128,512]{2,1,0:T(8,128)(2,1)S(1)}, u32[]{:S(2)}, u32[]{:S(2)}) collective-permute-start(bf16[2,128,512]{2,1,0:T(8,128)(2,1)S(1)} %collective-permute-done.9.refs_10_), channel_id=1, source_target_pairs={{0,14},{2,0},{4,2},{6,4},{8,6},{10,8},{12,10},{14,12},{1,15},{3,1}... | collective-permute-start | bytes 786440 | tf_op jit(solution)/shard_map/ppermute | solution.py:236
  51.7 14.4 %collective-permute-done.6.refs_6_ = bf16[320,1024]{1,0:T(8,128)(2,1)S(1)} collective-permute-done((bf16[320,1024]{1,0:T(8,128)(2,1)}, bf16[320,1024]{1,0:T(8,128)(2,1)S(1)}, u32[]{:S(2)}, u32[]{:S(2)}) %collective-permute-start.6) | collective-permute-done | bytes 655392 | tf_op jit(solution)/shard_map/ppermute | solution.py:290
  66.2 0.0 collective-permute-done.5.refs_5_
  66.2 0.6 collective-permute-done.4.refs_4_
  66.8 0.0 collective-permute-done.13.refs_12_
  66.8 0.0 collective-permute-done.10.refs_11_
  66.8 0.0 copy-done.4
  66.8 0.0 copy-done.5
  66.8 0.0 copy-done.7
  66.8 0.0 copy-done
  66.9 0.0 copy-start.2
  66.9 0.9 copy-done.2
  67.8 0.0 copy-start.6
  67.8 1.1 copy-done.6
  68.9 0.0 copy-start.8
  68.9 1.0 copy-done.8
  69.9 4.8 %tail_stage.1 = f32[6,64,64]{2,1,0:T(8,128)S(1)} custom-call(bf16[128,4096]{1,0:T(8,128)(2,1)S(1)} %copy-done, bf16[64,128]{1,0:T(8,128)(2,1)S(1)} %bitcast.15, bf16[64,128]{1,0:T(8,128)(2,1)S(1)} %bitcast.17, bf16[64,4096]{1,0:T(8,128)(2,1)S(1)} %bitcast.18, f32[1024,128]{1,0:T(8,128)S(1)} %copy-done.8, bf16[128,1152]{1,0:T(8,128)(2,1)} %collective-permute-done.1.refs_0_, ...), custom_call_target="tpu_custom_call" | custom-call | flops 4000000000 | bytes 8388608 | tf_op jit(solution)/shard_map/tail_stage/pallas_call | solution.py:215
  74.7 0.1 reshape_reshape.6
  74.8 0.1 copy.26
  74.9 9.9 %all_to_all.15 = f32[16,6,256]{2,1,0:T(8,128)S(1)} all-to-all(f32[16,6,256]{2,1,0:T(8,128)S(1)} %bitcast.19), channel_id=1, replica_groups=mesh['sy'=2,'sc'=2,'x'=4,'z'=8,'yh'=2] {'sy','sc','x'}, dimensions={0} | all-to-all | bytes 196608 | tf_op jit(solution)/shard_map/all_to_all | solution.py:243
  84.8 16.7 %all_to_all.16 = f32[16,6,256]{2,1,0:T(8,128)S(1)} all-to-all(f32[16,6,256]{2,1,0:T(8,128)S(1)} %broadcast_in_dim.4), channel_id=1, replica_groups=mesh['sy'=2,'sc'=2,'x'=4,'z'=8,'yh'=2] {'z','yh'}, dimensions={0} | all-to-all | bytes 196608 | tf_op jit(solution)/shard_map/all_to_all | solution.py:246
  101.6 8.0 %all_to_all.17 = f32[4,6,256]{2,1,0:T(8,128)S(1)} all-to-all(f32[4,6,256]{2,1,0:T(8,128)S(1)} %broadcast_in_dim.5), channel_id=1, replica_groups=mesh['sy'=2,'sc'=2,'x'=4,'z'=8,'yh'=2] {'x'}, dimensions={0} | all-to-all | bytes 49152 | tf_op jit(solution)/shard_map/all_to_all | solution.py:248
  109.6 0.6 copy.23
  (7 shorter events, 0.1 us)
Async XLA Ops:
  0.0 7.0 %collective-permute-start = (bf16[2,64,512]{2,1,0:T(8,128)(2,1)}, bf16[2,64,512]{2,1,0:T(8,128)(2,1)S(1)}, u32[]{:S(2)}, u32[]{:S(2)}) collective-permute-start(bf16[2,64,512]{2,1,0:T(8,128)(2,1)} %bitcast.12), channel_id=1, source_target_pairs={{0,1},{1,0},{2,3},{3,2},{4,5},{5,4},{6,7},{7,6},{8,9},{9,8},{10,11... | collective-permute-start | bytes 393224 | tf_op jit(solution)/shard_map/ppermute | solution.py:271
  3.2 63.6 %copy-start.4 = (bf16[128,64]{0,1:T(8,128)(2,1)S(1)}, bf16[128,64]{0,1:T(8,128)(2,1)}, u32[]{:S(2)}) copy-start(bf16[128,64]{0,1:T(8,128)(2,1)} %param.18) | copy-start | bytes 49156
  3.2 63.6 %copy-start.5 = (bf16[128,64]{0,1:T(8,128)(2,1)S(1)}, bf16[128,64]{0,1:T(8,128)(2,1)}, u32[]{:S(2)}) copy-start(bf16[128,64]{0,1:T(8,128)(2,1)} %param.20) | copy-start | bytes 49156
  3.2 63.6 %copy-start.7 = (bf16[4096,64]{0,1:T(8,128)(2,1)S(1)}, bf16[4096,64]{0,1:T(8,128)(2,1)}, u32[]{:S(2)}) copy-start(bf16[4096,64]{0,1:T(8,128)(2,1)} %param.22) | copy-start | bytes 1572868
  5.5 61.4 %copy-start = (bf16[128,4096]{1,0:T(8,128)(2,1)S(1)}, bf16[128,4096]{1,0:T(8,128)(2,1)}, u32[]{:S(2)}) copy-start(bf16[128,4096]{1,0:T(8,128)(2,1)} %weight_ref.1) | copy-start | bytes 3145732
  7.0 0.9 copy-start.3
  7.9 14.4 %copy-start.1 = (bf16[2,128,512]{2,1,0:T(8,128)(2,1)}, bf16[2,128,512]{2,1,0:T(8,128)(2,1)S(1)}, u32[]{:S(2)}) copy-start(bf16[2,128,512]{2,1,0:T(8,128)(2,1)S(1)} %pair_up.1.refs_7_) | copy-start | bytes 786436
  7.9 10.6 %collective-permute-start.7 = (bf16[2,128,512]{2,1,0:T(8,128)(2,1)S(1)}, bf16[2,128,512]{2,1,0:T(8,128)(2,1)}, u32[]{:S(2)}, u32[]{:S(2)}) collective-permute-start(bf16[2,128,512]{2,1,0:T(8,128)(2,1)S(1)} %pair_up.1.refs_7_), channel_id=1, source_target_pairs={{0,14},{2,0},{4,2},{6,4},{8,6},{10,8},{12,10},{14,12},{1,15},{3,1}... | collective-permute-start | bytes 786440 | tf_op jit(solution)/shard_map/ppermute | solution.py:234
  13.8 24.9 %collective-permute-start.1 = (bf16[128,1152]{1,0:T(8,128)(2,1)}, bf16[128,1152]{1,0:T(8,128)(2,1)}, u32[]{:S(2)}, u32[]{:S(2)}) collective-permute-start(bf16[128,1152]{1,0:T(8,128)(2,1)} %get-tuple-element.10.after_ref), channel_id=1, source_target_pairs={{0,16},{16,32},{32,48},{48,0},{1,17},{17,33},{33,49},{49,1},{2,18}... | collective-permute-start | bytes 884744 | tf_op jit(solution)/shard_map/ppermute | solution.py:273
  14.3 21.9 %collective-permute-start.2 = (bf16[128,1152]{1,0:T(8,128)(2,1)}, bf16[128,1152]{1,0:T(8,128)(2,1)}, u32[]{:S(2)}, u32[]{:S(2)}) collective-permute-start(bf16[128,1152]{1,0:T(8,128)(2,1)} %get-tuple-element.12), channel_id=1, source_target_pairs={{0,32},{16,48},{32,0},{48,16},{1,33},{17,49},{33,1},{49,17},{2,34}... | collective-permute-start | bytes 884744 | tf_op jit(solution)/shard_map/ppermute | solution.py:273
  16.7 20.4 %collective-permute-start.3 = (bf16[128,1152]{1,0:T(8,128)(2,1)}, bf16[128,1152]{1,0:T(8,128)(2,1)}, u32[]{:S(2)}, u32[]{:S(2)}) collective-permute-start(bf16[128,1152]{1,0:T(8,128)(2,1)} %get-tuple-element.13), channel_id=1, source_target_pairs={{0,48},{16,0},{32,16},{48,32},{1,49},{17,1},{33,17},{49,33},{2,50}... | collective-permute-start | bytes 884744 | tf_op jit(solution)/shard_map/ppermute | solution.py:273
  16.7 23.6 %collective-permute-start.11 = (bf16[2,128,512]{2,1,0:T(8,128)(2,1)S(1)}, bf16[2,128,512]{2,1,0:T(8,128)(2,1)}, u32[]{:S(2)}, u32[]{:S(2)}) collective-permute-start(bf16[2,128,512]{2,1,0:T(8,128)(2,1)S(1)} %pair_up.1.refs_7_), channel_id=1, source_target_pairs={{0,2},{2,4},{4,6},{6,8},{8,10},{10,12},{12,14},{14,0},{1,3},{3,5},... | collective-permute-start | bytes 786440 | tf_op jit(solution)/shard_map/ppermute | solution.py:235
  18.5 21.9 %collective-permute-start.8 = (bf16[2,128,512]{2,1,0:T(8,128)(2,1)}, bf16[2,128,512]{2,1,0:T(8,128)(2,1)}, u32[]{:S(2)}, u32[]{:S(2)}) collective-permute-start(bf16[2,128,512]{2,1,0:T(8,128)(2,1)} %collective-permute-done.7.refs_8_), channel_id=1, source_target_pairs={{0,14},{2,0},{4,2},{6,4},{8,6},{10,8},{12,10},{14,12},{1,15},{3,1}... | collective-permute-start | bytes 786440 | tf_op jit(solution)/shard_map/ppermute | solution.py:234
  36.2 29.9 %collective-permute-start.6 = (bf16[320,1024]{1,0:T(8,128)(2,1)}, bf16[320,1024]{1,0:T(8,128)(2,1)S(1)}, u32[]{:S(2)}, u32[]{:S(2)}) collective-permute-start(bf16[320,1024]{1,0:T(8,128)(2,1)} %get-tuple-element.14.refs_3_), channel_id=1, source_target_pairs={{0,48},{16,0},{32,16},{48,32},{1,49},{17,1},{33,17},{49,33},{2,50}... | collective-permute-start | bytes 1966088 | tf_op jit(solution)/shard_map/ppermute | solution.py:290
  37.2 29.0 %collective-permute-start.5 = (bf16[320,1024]{1,0:T(8,128)(2,1)}, bf16[320,1024]{1,0:T(8,128)(2,1)S(1)}, u32[]{:S(2)}, u32[]{:S(2)}) collective-permute-start(bf16[320,1024]{1,0:T(8,128)(2,1)} %get-tuple-element.14.refs_3_), channel_id=1, source_target_pairs={{0,32},{16,48},{32,0},{48,16},{1,33},{17,49},{33,1},{49,17},{2,34}... | collective-permute-start | bytes 1966088 | tf_op jit(solution)/shard_map/ppermute | solution.py:290
  38.7 28.1 %collective-permute-start.4 = (bf16[320,1024]{1,0:T(8,128)(2,1)}, bf16[320,1024]{1,0:T(8,128)(2,1)S(1)}, u32[]{:S(2)}, u32[]{:S(2)}) collective-permute-start(bf16[320,1024]{1,0:T(8,128)(2,1)} %get-tuple-element.14.refs_3_), channel_id=1, source_target_pairs={{0,16},{16,32},{32,48},{48,0},{1,17},{17,33},{33,49},{49,1},{2,18}... | collective-permute-start | bytes 1966088 | tf_op jit(solution)/shard_map/ppermute | solution.py:290
  40.4 7.8 %collective-permute-start.12 = (bf16[2,128,512]{2,1,0:T(8,128)(2,1)}, bf16[2,128,512]{2,1,0:T(8,128)(2,1)S(1)}, u32[]{:S(2)}, u32[]{:S(2)}) collective-permute-start(bf16[2,128,512]{2,1,0:T(8,128)(2,1)} %collective-permute-done.11.refs_14_), channel_id=1, source_target_pairs={{0,2},{2,4},{4,6},{6,8},{8,10},{10,12},{12,14},{14,0},{1,3},{3,5},... | collective-permute-start | bytes 786440 | tf_op jit(solution)/shard_map/ppermute | solution.py:235
  40.4 7.8 %collective-permute-start.9 = (bf16[2,128,512]{2,1,0:T(8,128)(2,1)}, bf16[2,128,512]{2,1,0:T(8,128)(2,1)S(1)}, u32[]{:S(2)}, u32[]{:S(2)}) collective-permute-start(bf16[2,128,512]{2,1,0:T(8,128)(2,1)} %collective-permute-done.8.refs_9_), channel_id=1, source_target_pairs={{0,14},{2,0},{4,2},{6,4},{8,6},{10,8},{12,10},{14,12},{1,15},{3,1}... | collective-permute-start | bytes 786440 | tf_op jit(solution)/shard_map/ppermute | solution.py:234
  48.2 18.6 %collective-permute-start.13 = (bf16[2,128,512]{2,1,0:T(8,128)(2,1)S(1)}, bf16[2,128,512]{2,1,0:T(8,128)(2,1)S(1)}, u32[]{:S(2)}, u32[]{:S(2)}) collective-permute-start(bf16[2,128,512]{2,1,0:T(8,128)(2,1)S(1)} %collective-permute-done.12.refs_13_), channel_id=1, source_target_pairs={{0,2},{2,4},{4,6},{6,8},{8,10},{10,12},{12,14},{14,0},{1,3},{3,5},... | collective-permute-start | bytes 786440 | tf_op jit(solution)/shard_map/ppermute | solution.py:235
  48.2 18.6 %collective-permute-start.10 = (bf16[2,128,512]{2,1,0:T(8,128)(2,1)S(1)}, bf16[2,128,512]{2,1,0:T(8,128)(2,1)S(1)}, u32[]{:S(2)}, u32[]{:S(2)}) collective-permute-start(bf16[2,128,512]{2,1,0:T(8,128)(2,1)S(1)} %collective-permute-done.9.refs_10_), channel_id=1, source_target_pairs={{0,14},{2,0},{4,2},{6,4},{8,6},{10,8},{12,10},{14,12},{1,15},{3,1}... | collective-permute-start | bytes 786440 | tf_op jit(solution)/shard_map/ppermute | solution.py:236
  66.9 1.0 copy-start.2
  67.8 1.1 copy-start.6
  68.9 1.0 copy-start.8

commit v4 on v3

v4 whole, which is shorter than its diff:
```python
import jax
import jax.numpy as jnp
from jax import lax
from jax.experimental import pallas as pl
from jax.experimental.pallas import tpu as pltpu
from jax.sharding import Mesh, PartitionSpec as P

SEQ_PARTS = (2, 2)
FSDP_PARTS = (4, 8, 2)
NX, NZ, NY = FSDP_PARTS
FOLD = 16
MIB = 1024 * 1024
VMEM = pl.BlockSpec(memory_space=pltpu.VMEM)
HBM = pl.BlockSpec(memory_space=pltpu.HBM)


def shifted(count, step):
    return [(i, (i + step) % count) for i in range(count)]


def dot32(a, b, dims, precision=None):
    return lax.dot_general(a, b, (dims, ((), ())), preferred_element_type=jnp.float32, precision=precision)


def pair_kernel(own_ref, other_ref, after_ref, out_ref):
    piece = own_ref.shape[1]
    out_ref[:, :piece, :] = own_ref[...]
    out_ref[:, piece:, :] = other_ref[...]


def pair_up(own, other, after):
    examples, piece, seq_dev = own.shape
    return pl.pallas_call(
        pair_kernel,
        out_shape=jax.ShapeDtypeStruct((examples, NY * piece, seq_dev), own.dtype),
        in_specs=[VMEM, VMEM, HBM],
        out_specs=VMEM,
        compiler_params=pltpu.CompilerParams(vmem_limit_bytes=4 * MIB),
        name="pair_up",
    )(own, other, after)


def token_kernel(chunk, scale, lengths_ref, tokens_hbm, gate_hbm, up_hbm, gate_in_hbm, up_in_hbm, down_in_hbm, down_hbm, gate_out_hbm, up_out_hbm, *refs):
    messages, (right_ref, done_ref) = refs[: NX - 1], refs[NX - 1 : NX + 1]
    tokens_ref, weight_ref, in_ref, down_in_ref, out_ref, total_ref, sems = refs[NX + 1 :]
    rows, model_width = tokens_hbm.shape
    hidden = gate_hbm.shape[1]
    rank = gate_in_hbm.shape[0]
    examples = lengths_ref.shape[0]
    seq_dev = rows // examples
    groups, count = [], 0
    for start in range(0, model_width, chunk):
        part = pl.ds(start, chunk)
        pairs = [
            (tokens_hbm.at[:, part], tokens_ref.at[:, part]),
            (gate_hbm.at[part], weight_ref.at[part, pl.ds(0, hidden)]),
            (up_hbm.at[part], weight_ref.at[part, pl.ds(hidden, hidden)]),
            (gate_in_hbm.at[:, part], in_ref.at[pl.ds(0, rank), part]),
            (up_in_hbm.at[:, part], in_ref.at[pl.ds(rank, rank), part]),
        ]
        if start + chunk == model_width:
            pairs.append((down_in_hbm, down_in_ref))
        groups.append([pltpu.make_async_copy(a, b, sems.at[count + k]) for k, (a, b) in enumerate(pairs)])
        count += len(pairs)
        for copy in groups[-1]:
            copy.start()
    top = 2 * hidden + rank
    width = model_width // NX
    pairs = [(gate_out_hbm, out_ref.at[pl.ds(0, rank)]), (up_out_hbm, out_ref.at[pl.ds(rank, rank)])]
    for step, message in enumerate(messages, 1):
        start = pl.multiple_of(lax.rem(lax.axis_index("x") + step, NX) * width, width)
        pairs.append((down_hbm.at[:, pl.ds(start, width)], message.at[pl.ds(top, hidden)]))
    extra = [pltpu.make_async_copy(a, b, sems.at[count + k]) for k, (a, b) in enumerate(pairs)]
    for copy in extra:
        copy.start()
    for index, group in enumerate(groups):
        for copy in group:
            copy.wait()
        part = slice(index * chunk, (index + 1) * chunk)
        values = jnp.dot(tokens_ref[:, part], weight_ref[part, :], preferred_element_type=jnp.float32)
        right = dot32(tokens_ref[:, part], in_ref[:, part], ((1,), (1,)))
        if index == 0:
            total_ref[...] = values
            right_ref[...] = right
        else:
            total_ref[...] += values
            right_ref[...] += right

    done_ref[...] = jnp.zeros_like(done_ref)
    tile = min(256, seq_dev)
    seq_index = lax.axis_index("sy") * SEQ_PARTS[1] + lax.axis_index("sc")
    for step in range(rows // tile):
        span = slice(step * tile, (step + 1) * tile)
        gate, up = total_ref[span, :hidden], total_ref[span, hidden:]
        sigmoid = 1.0 / (1.0 + jnp.exp(-gate))
        silu = gate * sigmoid
        factor_gate = up * sigmoid * (1.0 + gate * (1.0 - sigmoid))
        hidden_value = (silu * up).astype(jnp.bfloat16)
        factor_gate = factor_gate.T.astype(jnp.bfloat16)
        factor_up = silu.T.astype(jnp.bfloat16)

        first = seq_index * seq_dev + step * tile % seq_dev
        limit = lengths_ref[step * tile // seq_dev]
        columns = first + lax.broadcasted_iota(jnp.int32, (rank, tile), 1)
        right_down = dot32(down_in_ref[...], hidden_value, ((1,), (1,)))
        right_down = jnp.where(columns < limit, right_down * scale, 0.0).astype(jnp.bfloat16)
        for message in messages:
            message[:hidden, span] = factor_gate
            message[hidden : 2 * hidden, span] = factor_up
            message[2 * hidden : top, span] = right_down
        rows_at = first + lax.broadcasted_iota(jnp.int32, (tile, 2 * rank), 0)
        right_ref[span, :] = jnp.where(rows_at < limit, right_ref[span, :] * scale, 0.0)
    for copy in extra:
        copy.wait()
    for message in messages:
        for block in range(2 * rank // FOLD):
            rows_of = slice(block * FOLD, (block + 1) * FOLD)
            message[top + hidden :, block * hidden : (block + 1) * hidden] = out_ref[rows_of, :]


def token_stage(tokens, gate_weight, up_weight, gate_in, up_in, down_in, down_weight, gate_out, up_out, lengths, scale):
    rows, width = tokens.shape
    hidden = gate_weight.shape[1]
    rank = gate_in.shape[0]
    chunk = 512
    return pl.pallas_call(
        lambda *refs: token_kernel(chunk, scale, *refs),
        out_shape=[
            *[jax.ShapeDtypeStruct((3 * hidden + rank + FOLD, rows), jnp.bfloat16)] * (NX - 1),
            jax.ShapeDtypeStruct((rows, 2 * rank), jnp.float32),
            jax.ShapeDtypeStruct((8, 128), jnp.float32),
        ],
        in_specs=[pl.BlockSpec(memory_space=pltpu.SMEM)] + [HBM] * 9,
        out_specs=[VMEM] * (NX + 1),
        scratch_shapes=[
            pltpu.VMEM((rows, width), jnp.bfloat16),
            pltpu.VMEM((width, 2 * hidden), jnp.bfloat16),
            pltpu.VMEM((2 * rank, width), jnp.bfloat16),
            pltpu.VMEM((rank, hidden), jnp.bfloat16),
            pltpu.VMEM((2 * rank, hidden), jnp.bfloat16),
            pltpu.VMEM((rows, 2 * hidden), jnp.float32),
            pltpu.SemaphoreType.DMA((5 * (width // chunk) + 2 + NX,)),
        ],
        compiler_params=pltpu.CompilerParams(vmem_limit_bytes=61 * MIB),
        cost_estimate=pl.CostEstimate(
            flops=2 * rows * width * 512, bytes_accessed=16 * MIB, transcendentals=rows * hidden
        ),
        name="token_stage",
    )(lengths, tokens, gate_weight, up_weight, gate_in, up_in, down_in, down_weight, gate_out, up_out)


def tail_kernel(weight_hbm, gate_out_ref, up_out_ref, down_out_hbm, right_ref, *refs):
    messages, blocks = refs[:NX], refs[NX : NX + NZ]
    out_ref, weights, projs, grads, total, sems = refs[NX + NZ :]
    hidden, model_width = weight_hbm.shape
    rank = gate_out_ref.shape[0]
    width = model_width // NX
    examples, both, seq_dev = blocks[0].shape
    piece = both // NY
    top = 2 * hidden + rank
    x_at, z_at, y_at = lax.axis_index("x"), lax.axis_index("z"), lax.axis_index("yh")

    start = pl.multiple_of(x_at * width, width)
    pairs = [
        (weight_hbm.at[:, pl.ds(start, width)], weights.at[pl.ds(0, hidden)]),
        (down_out_hbm.at[:, pl.ds(start, width)], weights.at[pl.ds(NX * hidden, rank)]),
    ]
    for step in range(1, NX):
        pairs.append((messages[step].at[pl.ds(top, hidden)], weights.at[pl.ds(step * hidden, hidden)]))
    for step, block in enumerate(blocks):
        base = lax.rem(z_at + step, NZ) * both
        for kind, y_of in enumerate((y_at, 1 - y_at)):
            rows = pl.ds(pl.multiple_of(base + y_of * piece, piece), piece)
            pairs.append((block.at[:, pl.ds(kind * piece, piece)], grads.at[:, rows]))
    copies = [pltpu.make_async_copy(a, b, sems.at[k]) for k, (a, b) in enumerate(pairs)]
    for copy in copies:
        copy.start()
    projs[:rank, :hidden] = gate_out_ref[...]
    projs[rank:, :hidden] = up_out_ref[...]
    for step in range(1, NX):
        columns = slice(step * hidden, (step + 1) * hidden)
        for block in range(2 * rank // FOLD):
            folded = messages[step][top + hidden :, block * hidden : (block + 1) * hidden]
            projs[block * FOLD : (block + 1) * FOLD, columns] = folded
    for copy in copies:
        copy.wait()
    for example in range(examples):
        total[example] = jnp.dot(weights[...], grads[example], preferred_element_type=jnp.float32)
    for example in range(examples):
        columns = slice(example * seq_dev, (example + 1) * seq_dev)
        left = []
        for kind in range(2):
            products = []
            for step in range(NX):
                factor = messages[step][kind * hidden : (kind + 1) * hidden, columns].astype(jnp.float32)
                products.append(total[example, step * hidden : (step + 1) * hidden] * factor)
            product = jnp.concatenate(products, axis=0)
            high = product.astype(jnp.bfloat16)
            low = (product - high.astype(jnp.float32)).astype(jnp.bfloat16)
            proj = projs[kind * rank : (kind + 1) * rank, :]
            left.append(
                jnp.dot(proj, high, preferred_element_type=jnp.float32)
                + jnp.dot(proj, low, preferred_element_type=jnp.float32)
            )
        sides = jnp.dot(
            jnp.concatenate(left, axis=0),
            right_ref[columns, :],
            precision=lax.Precision.HIGHEST,
            preferred_element_type=jnp.float32,
        )
        right_down = messages[0][2 * hidden : top, columns].astype(jnp.float32)
        for step in range(1, NX):
            right_down = right_down + messages[step][2 * hidden : top, columns].astype(jnp.float32)
        out_ref[3 * example] = sides[:rank, :rank]
        out_ref[3 * example + 1] = sides[rank:, rank:]
        out_ref[3 * example + 2] = dot32(
            total[example, NX * hidden :], right_down, ((1,), (1,)), precision=lax.Precision.HIGHEST
        )


def tail_stage(down_weight, gate_out, up_out, down_out, right, messages, blocks):
    hidden, model_width = down_weight.shape
    rank = gate_out.shape[0]
    examples, _, seq_dev = blocks[0].shape
    width = model_width // NX
    operands = [down_weight, gate_out, up_out, down_out, right, *messages, *blocks]
    return pl.pallas_call(
        tail_kernel,
        out_shape=jax.ShapeDtypeStruct((examples * 3, rank, rank), jnp.float32),
        in_specs=[HBM, VMEM, VMEM, HBM, VMEM] + [VMEM] * NX + [HBM] * NZ,
        out_specs=VMEM,
        scratch_shapes=[
            pltpu.VMEM((NX * hidden + rank, width), jnp.bfloat16),
            pltpu.VMEM((2 * rank, NX * hidden), jnp.bfloat16),
            pltpu.VMEM((examples, width, seq_dev), jnp.bfloat16),
            pltpu.VMEM((examples, NX * hidden + rank, seq_dev), jnp.float32),
            pltpu.SemaphoreType.DMA((1 + NX + NZ * NY,)),
        ],
        compiler_params=pltpu.CompilerParams(vmem_limit_bytes=16 * MIB),
        cost_estimate=pl.CostEstimate(flops=4 * 10**9, bytes_accessed=8 * MIB, transcendentals=0),
        name="tail_stage",
    )(*operands)


def ring_z(own):
    up, down = [own], [own]
    for _ in range(NZ // 2 - 1):
        up.append(lax.ppermute(up[-1], "z", shifted(NZ, -1)))
        down.append(lax.ppermute(down[-1], "z", shifted(NZ, 1)))
    return up + [lax.ppermute(up[-1], "z", shifted(NZ, -1))] + down[:0:-1]


def sum_everywhere(partial):
    count, size = partial.shape
    parts = SEQ_PARTS[0] * SEQ_PARTS[1] * NZ
    width = size // parts
    pieces = partial.reshape(count, parts, width).transpose(1, 0, 2)
    pieces = lax.all_to_all(pieces, ("sy", "sc", "z"), 0, 0, tiled=True)
    own = jnp.sum(pieces, axis=0)
    spread = jnp.broadcast_to(own[None], (NX * NZ * NY,) + own.shape)
    blocks = lax.all_to_all(spread, ("x", "z", "yh"), 0, 0, tiled=True)
    blocks = blocks.reshape(NX, NZ, NY, count, width).sum(axis=(0, 2))
    return blocks.transpose(1, 0, 2).reshape(count, NZ * width)


def shards(
    tokens,
    out_grad,
    gate_weight,
    up_weight,
    down_weight,
    proj_gate_in,
    proj_gate_out,
    proj_up_in,
    proj_up_out,
    proj_down_in,
    proj_down_out,
    lengths,
):
    examples, seq_dev, model_width = tokens.shape
    scale = float(seq_dev * SEQ_PARTS[0] * SEQ_PARTS[1]) ** (-0.5)
    gate_out, up_out = proj_gate_out.T, proj_up_out.T

    own_grad = out_grad.transpose(0, 2, 1)
    other_grad = lax.ppermute(own_grad, "yh", shifted(NY, 1))
    flat_tokens = tokens.reshape(examples * seq_dev, model_width)
    sent = token_stage(
        flat_tokens,
        gate_weight,
        up_weight,
        proj_gate_in.T,
        proj_up_in.T,
        proj_down_in.T,
        down_weight,
        gate_out,
        up_out,
        lengths,
        scale,
    )
    sent, (right, done) = sent[: NX - 1], sent[NX - 1 :]
    messages = [sent[0]] + [lax.ppermute(piece, "x", shifted(NX, step)) for step, piece in enumerate(sent, 1)]
    pair = pair_up(own_grad, other_grad, done)
    blocks = ring_z(pair)
    products = tail_stage(down_weight, gate_out, up_out, proj_down_out.T, right, messages, blocks)
    total = sum_everywhere(products.reshape(examples * 3, -1))
    return total.reshape(examples, 3, -1)


def solution(mesh):
    fine = Mesh(mesh.devices.reshape(SEQ_PARTS + FSDP_PARTS), ("sy", "sc", "x", "z", "yh"))
    seq, fsdp = ("sy", "sc"), ("x", "z", "yh")
    placed = (
        P(None, seq, None),
        P(None, seq, fsdp),
        P(None, fsdp),
        P(None, fsdp),
        P(fsdp, None),
        P(),
        P(fsdp, None),
        P(),
        P(fsdp, None),
        P(fsdp, None),
        P(),
        P(),
    )
    return jax.shard_map(
        shards, mesh=fine, in_specs=placed, out_specs=P(None, None, seq), check_vma=False
    )
```

time: 111 us -> 106 us (0.955)
  Pallas kernels: 21 us -> 14.2 us
  waiting for transfers between devices: 23 us -> 28.6 us
  starting transfers between devices: 26.7 us -> 24.9 us
    ppermute x3, waiting for transfers between devices: 0.01 us -> 16.6 us  [shards(): lax.ppermute(piece, 'x', shifted(NX, step))]
    ppermute x3 -> x0, waiting for transfers between devices: 15.1 us -> none  [shards(): lax.ppermute(factors, 'x', shifted(NX, step))]
    pallas_call x2 -> x1, Pallas kernels: 16.2 us -> 9.23 us  [token_stage(): pl.pallas_call(lambda *refs: token_kernel(chunk, scale, *refs), out_shape...]
    ppermute x3, waiting for transfers between devices: 4.61 us -> 9.59 us  [ring_z(): down.append(lax.ppermute(down[-1], 'z', shifted(NZ, 1)))]
    ppermute x3 -> x0, starting transfers between devices: 4.11 us -> none  [shards(): lax.ppermute(factors, 'x', shifted(NX, step))]
    ppermute x3, starting transfers between devices: 2.9 us -> 4.64 us  [shards(): lax.ppermute(piece, 'x', shifted(NX, step))]
    ppermute x1, waiting for transfers between devices: 1.48 us -> 0.01 us  [shards(): other_grad = lax.ppermute(own_grad, 'yh', shifted(NY, 1))]
    unnamed x18 -> x17, local copies, waits for them, and re-layouts: 4 us -> 2.93 us
  transfers between devices with their start and end apart: 14 -> 11, of which waited for: 5 -> 7; matrix products, arithmetic and copies ran while one was open for 0% -> 0% of each run, Pallas kernels for 15% -> 9%
where the time goes in v4:
time: 106 us; the launch traced here: 105 us
  blocking collectives  33.7 us (32%)
  waiting for transfers between devices  28.6 us (27%)
  starting transfers between devices  24.9 us (23%)
  Pallas kernels  14.2 us (13%)
  local copies, waits for them, and re-layouts  3.75 us (4%)
    all_to_all x1, blocking collectives, sum_everywhere(): blocks = lax.all_to_all(spread, ('x', 'z', 'yh'), 0, 0, tiled=True)  20.4 us
    ppermute x3, waiting for transfers between devices, shards(): lax.ppermute(piece, 'x', shifted(NX, step))  16.6 us
    ppermute x3, starting transfers between devices, ring_z(): up.append(lax.ppermute(up[-1], 'z', shifted(NZ, -1)))  13.3 us
    all_to_all x1, blocking collectives, sum_everywhere(): pieces = lax.all_to_all(pieces, ('sy', 'sc', 'z'), 0, 0, tiled=True)  13.3 us
    ppermute x3, waiting for transfers between devices, ring_z(): down.append(lax.ppermute(down[-1], 'z', shifted(NZ, 1)))  9.59 us
    pallas_call x1, Pallas kernels, token_stage(): pl.pallas_call(lambda *refs: token_kernel(chunk, scale, *refs), out_shape...  9.23 us
    pallas_call x1, Pallas kernels, tail_stage(): pl.pallas_call(tail_kernel, out_shape=jax.ShapeDtypeStruct((examples * 3,...  4.97 us
    ppermute x3, starting transfers between devices, shards(): lax.ppermute(piece, 'x', shifted(NX, step))  4.64 us
  transfers between devices with their start and end apart: 11, of which 7 were waited for; matrix products, arithmetic and copies ran while one was open for 0% of the time, Pallas kernels for 9%

profile of v4, /device:TPU:6, one launch (start us, length us, event | category | flops | bytes accessed | tf_op | source)
XLA Modules:
  0.0 105.4 jit_solution(7192085681759337050)
XLA Ops:
  0.0 0.0 copy-start
  0.0 0.0 copy-start.2
  0.0 0.0 copy-start.6
  0.0 0.0 copy-start.5
  0.0 0.0 copy-start.4
  0.0 3.3 %collective-permute-start.3 = (bf16[2,64,512]{2,1,0:T(8,128)(2,1)}, bf16[2,64,512]{2,1,0:T(8,128)(2,1)S(1)}, u32[]{:S(2)}, u32[]{:S(2)}) collective-permute-start(bf16[2,64,512]{2,1,0:T(8,128)(2,1)} %bitcast.15), channel_id=1, source_target_pairs={{0,1},{1,0},{2,3},{3,2},{4,5},{5,4},{6,7},{7,6},{8,9},{9,8},{10,11... | collective-permute-start | bytes 393224 | tf_op jit(solution)/shard_map/ppermute | solution.py:285
  3.3 9.2 %token_stage.1 = (bf16[464,1024]{1,0:T(8,128)(2,1)}, bf16[464,1024]{1,0:T(8,128)(2,1)}, bf16[464,1024]{1,0:T(8,128)(2,1)}, f32[1024,128]{1,0:T(8,128)}, f32[8,128]{1,0:T(8,128)}) custom-call(s32[2]{0:T(128)} %refs_0_.1, bf16[1024,4096]{1,0:T(8,128)(2,1)} %bitcast.25, bf16[4096,128]{1,0:T(8,128)(2,1)} %refs_2_.1, bf16[4096,128]{1,0:T(8,128)(2,1)} %refs_3_.1, ...), custom_call_target="tpu_custom_call" | custom-call | flops 4294967296 | bytes 16777216 | tf_op jit(solution)/shard_map/token_stage/pallas_call | solution.py:126
  12.6 0.0 collective-permute-done.3.other_ref
  12.6 0.0 copy-done
  12.6 0.0 copy-start.1
  12.6 0.7 copy-done.1
  13.3 5.9 %collective-permute-start.4 = (bf16[2,128,512]{2,1,0:T(8,128)(2,1)S(1)}, bf16[2,128,512]{2,1,0:T(8,128)(2,1)S(1)}, u32[]{:S(2)}, u32[]{:S(2)}) collective-permute-start(bf16[2,128,512]{2,1,0:T(8,128)(2,1)S(1)} %pair_up.1.refs_4_), channel_id=1, source_target_pairs={{0,14},{2,0},{4,2},{6,4},{8,6},{10,8},{12,10},{14,12},{1,15},{3,1}... | collective-permute-start | bytes 786440 | tf_op jit(solution)/shard_map/ppermute | solution.py:248
  19.2 1.4 %collective-permute-start.1 = (bf16[464,1024]{1,0:T(8,128)(2,1)}, bf16[464,1024]{1,0:T(8,128)(2,1)S(1)}, u32[]{:S(2)}, u32[]{:S(2)}) collective-permute-start(bf16[464,1024]{1,0:T(8,128)(2,1)} %get-tuple-element.12), channel_id=1, source_target_pairs={{0,32},{16,48},{32,0},{48,16},{1,33},{17,49},{33,1},{49,17},{2,34}... | collective-permute-start | bytes 2850824 | tf_op jit(solution)/shard_map/ppermute | solution.py:301
  20.6 0.0 collective-permute-start.2
  20.6 3.2 %collective-permute-start = (bf16[464,1024]{1,0:T(8,128)(2,1)}, bf16[464,1024]{1,0:T(8,128)(2,1)S(1)}, u32[]{:S(2)}, u32[]{:S(2)}) collective-permute-start(bf16[464,1024]{1,0:T(8,128)(2,1)} %get-tuple-element.11.refs_0_), channel_id=1, source_target_pairs={{0,16},{16,32},{32,48},{48,0},{1,17},{17,33},{33,49},{49,1},{2,18}... | collective-permute-start | bytes 2850824 | tf_op jit(solution)/shard_map/ppermute | solution.py:301
  23.9 0.0 collective-permute-start.8
  23.9 0.6 collective-permute-done.4.refs_5_
  24.5 3.7 %collective-permute-start.5 = (bf16[2,128,512]{2,1,0:T(8,128)(2,1)S(1)}, bf16[2,128,512]{2,1,0:T(8,128)(2,1)S(1)}, u32[]{:S(2)}, u32[]{:S(2)}) collective-permute-start(bf16[2,128,512]{2,1,0:T(8,128)(2,1)S(1)} %collective-permute-done.4.refs_5_), channel_id=1, source_target_pairs={{0,14},{2,0},{4,2},{6,4},{8,6},{10,8},{12,10},{14,12},{1,15},{3,1}... | collective-permute-start | bytes 786440 | tf_op jit(solution)/shard_map/ppermute | solution.py:248
  28.2 3.5 %collective-permute-done.8.refs_11_ = bf16[2,128,512]{2,1,0:T(8,128)(2,1)S(1)} collective-permute-done((bf16[2,128,512]{2,1,0:T(8,128)(2,1)S(1)}, bf16[2,128,512]{2,1,0:T(8,128)(2,1)S(1)}, u32[]{:S(2)}, u32[]{:S(2)}) %collective-permute-start.8) | collective-permute-done | bytes 262176 | tf_op jit(solution)/shard_map/ppermute | solution.py:249
  31.7 0.0 collective-permute-start.9
  31.7 0.9 collective-permute-done.5.refs_6_
  32.6 3.7 %collective-permute-start.6 = (bf16[2,128,512]{2,1,0:T(8,128)(2,1)S(1)}, bf16[2,128,512]{2,1,0:T(8,128)(2,1)S(1)}, u32[]{:S(2)}, u32[]{:S(2)}) collective-permute-start(bf16[2,128,512]{2,1,0:T(8,128)(2,1)S(1)} %collective-permute-done.5.refs_6_), channel_id=1, source_target_pairs={{0,14},{2,0},{4,2},{6,4},{8,6},{10,8},{12,10},{14,12},{1,15},{3,1}... | collective-permute-start | bytes 786440 | tf_op jit(solution)/shard_map/ppermute | solution.py:248
  36.3 3.0 %collective-permute-done.9.refs_10_ = bf16[2,128,512]{2,1,0:T(8,128)(2,1)S(1)} collective-permute-done((bf16[2,128,512]{2,1,0:T(8,128)(2,1)S(1)}, bf16[2,128,512]{2,1,0:T(8,128)(2,1)S(1)}, u32[]{:S(2)}, u32[]{:S(2)}) %collective-permute-start.9) | collective-permute-done | bytes 262176 | tf_op jit(solution)/shard_map/ppermute | solution.py:249
  39.3 0.0 collective-permute-start.10
  39.3 0.9 collective-permute-done.6.refs_7_
  40.2 3.7 %collective-permute-start.7 = (bf16[2,128,512]{2,1,0:T(8,128)(2,1)S(1)}, bf16[2,128,512]{2,1,0:T(8,128)(2,1)S(1)}, u32[]{:S(2)}, u32[]{:S(2)}) collective-permute-start(bf16[2,128,512]{2,1,0:T(8,128)(2,1)S(1)} %collective-permute-done.6.refs_7_), channel_id=1, source_target_pairs={{0,14},{2,0},{4,2},{6,4},{8,6},{10,8},{12,10},{14,12},{1,15},{3,1}... | collective-permute-start | bytes 786440 | tf_op jit(solution)/shard_map/ppermute | solution.py:250
  43.9 3.0 %collective-permute-done.10.refs_9_ = bf16[2,128,512]{2,1,0:T(8,128)(2,1)S(1)} collective-permute-done((bf16[2,128,512]{2,1,0:T(8,128)(2,1)S(1)}, bf16[2,128,512]{2,1,0:T(8,128)(2,1)S(1)}, u32[]{:S(2)}, u32[]{:S(2)}) %collective-permute-start.10) | collective-permute-done | bytes 262176 | tf_op jit(solution)/shard_map/ppermute | solution.py:249
  46.9 0.0 collective-permute-done.1.refs_2_
  46.9 16.6 %collective-permute-done.2.refs_3_ = bf16[464,1024]{1,0:T(8,128)(2,1)S(1)} collective-permute-done((bf16[464,1024]{1,0:T(8,128)(2,1)}, bf16[464,1024]{1,0:T(8,128)(2,1)S(1)}, u32[]{:S(2)}, u32[]{:S(2)}) %collective-permute-start.2) | collective-permute-done | bytes 950304 | tf_op jit(solution)/shard_map/ppermute | solution.py:301
  63.5 0.0 collective-permute-done.refs_1_
  63.5 0.0 collective-permute-done.7.refs_8_
  63.5 0.0 copy-done.2
  63.6 0.0 copy-done.6
  63.6 0.0 copy-done.5
  63.6 0.0 copy-done.4
  63.6 0.0 copy-start.3
  63.6 1.2 %copy-done.3 = bf16[464,1024]{1,0:T(8,128)(2,1)S(1)} copy-done((bf16[464,1024]{1,0:T(8,128)(2,1)S(1)}, bf16[464,1024]{1,0:T(8,128)(2,1)}, u32[]{:S(2)}) %copy-start.3) | copy-done | bytes 950296
  64.8 0.0 copy-start.7
  64.8 1.0 copy-done.7
  65.8 5.0 %tail_stage.1 = f32[6,64,64]{2,1,0:T(8,128)S(1)} custom-call(bf16[128,4096]{1,0:T(8,128)(2,1)S(1)} %copy-done.2, bf16[64,128]{1,0:T(8,128)(2,1)S(1)} %bitcast.19, bf16[64,128]{1,0:T(8,128)(2,1)S(1)} %bitcast.21, bf16[64,4096]{1,0:T(8,128)(2,1)S(1)} %bitcast.17, f32[1024,128]{1,0:T(8,128)S(1)} %copy-done.7, bf16[464,1024]{1,0:T(8,128)(2,1)S(1)} %copy-done.3, ...), custom_call_target="tpu_custom_call" | custom-call | flops 4000000000 | bytes 8388608 | tf_op jit(solution)/shard_map/tail_stage/pallas_call | solution.py:227
  70.8 0.1 reshape_reshape.6
  70.9 0.1 copy.30
  71.0 13.3 %all_to_all.10 = f32[32,6,128]{2,1,0:T(8,128)S(1)} all-to-all(f32[32,6,128]{2,1,0:T(8,128)S(1)} %bitcast.23), channel_id=1, replica_groups=mesh['sy'=2,'sc'=2,'x'=4,'z'=8,'yh'=2] {'sy','sc','z'}, dimensions={0} | all-to-all | bytes 196608 | tf_op jit(solution)/shard_map/all_to_all | solution.py:258
  84.3 20.4 %all_to_all.11 = f32[64,6,128]{2,1,0:T(8,128)S(1)} all-to-all(f32[64,6,128]{2,1,0:T(8,128)S(1)} %broadcast_in_dim.2), channel_id=1, replica_groups=mesh['sy'=2,'sc'=2,'x'=4,'z'=8,'yh'=2] {'x','z','yh'}, dimensions={0} | all-to-all | bytes 393216 | tf_op jit(solution)/shard_map/all_to_all | solution.py:261
  104.8 0.6 copy.24
  (6 shorter events, 0.1 us)
Async XLA Ops:
  0.0 12.6 %copy-start = (bf16[2,512,64]{1,2,0:T(8,128)(2,1)S(1)}, bf16[2,512,64]{1,2,0:T(8,128)(2,1)}, u32[]{:S(2)}) copy-start(bf16[2,512,64]{1,2,0:T(8,128)(2,1)} %param.13) | copy-start | bytes 393220
  0.0 63.5 %copy-start.2 = (bf16[128,4096]{1,0:T(8,128)(2,1)S(1)}, bf16[128,4096]{1,0:T(8,128)(2,1)}, u32[]{:S(2)}) copy-start(bf16[128,4096]{1,0:T(8,128)(2,1)} %weight_hbm.1) | copy-start | bytes 3145732
  0.0 63.5 %copy-start.6 = (bf16[128,64]{0,1:T(8,128)(2,1)S(1)}, bf16[128,64]{0,1:T(8,128)(2,1)}, u32[]{:S(2)}) copy-start(bf16[128,64]{0,1:T(8,128)(2,1)} %param.20) | copy-start | bytes 49156
  0.0 63.6 %copy-start.5 = (bf16[128,64]{0,1:T(8,128)(2,1)S(1)}, bf16[128,64]{0,1:T(8,128)(2,1)}, u32[]{:S(2)}) copy-start(bf16[128,64]{0,1:T(8,128)(2,1)} %param.18) | copy-start | bytes 49156
  0.0 63.6 %copy-start.4 = (bf16[4096,64]{0,1:T(8,128)(2,1)S(1)}, bf16[4096,64]{0,1:T(8,128)(2,1)}, u32[]{:S(2)}) copy-start(bf16[4096,64]{0,1:T(8,128)(2,1)} %param.22) | copy-start | bytes 1572868
  0.0 12.5 %collective-permute-start.3 = (bf16[2,64,512]{2,1,0:T(8,128)(2,1)}, bf16[2,64,512]{2,1,0:T(8,128)(2,1)S(1)}, u32[]{:S(2)}, u32[]{:S(2)}) collective-permute-start(bf16[2,64,512]{2,1,0:T(8,128)(2,1)} %bitcast.15), channel_id=1, source_target_pairs={{0,1},{1,0},{2,3},{3,2},{4,5},{5,4},{6,7},{7,6},{8,9},{9,8},{10,11... | collective-permute-start | bytes 393224 | tf_op jit(solution)/shard_map/ppermute | solution.py:285
  12.6 0.7 copy-start.1
  13.3 11.2 %collective-permute-start.4 = (bf16[2,128,512]{2,1,0:T(8,128)(2,1)S(1)}, bf16[2,128,512]{2,1,0:T(8,128)(2,1)S(1)}, u32[]{:S(2)}, u32[]{:S(2)}) collective-permute-start(bf16[2,128,512]{2,1,0:T(8,128)(2,1)S(1)} %pair_up.1.refs_4_), channel_id=1, source_target_pairs={{0,14},{2,0},{4,2},{6,4},{8,6},{10,8},{12,10},{14,12},{1,15},{3,1}... | collective-permute-start | bytes 786440 | tf_op jit(solution)/shard_map/ppermute | solution.py:248
  19.2 27.7 %collective-permute-start.1 = (bf16[464,1024]{1,0:T(8,128)(2,1)}, bf16[464,1024]{1,0:T(8,128)(2,1)S(1)}, u32[]{:S(2)}, u32[]{:S(2)}) collective-permute-start(bf16[464,1024]{1,0:T(8,128)(2,1)} %get-tuple-element.12), channel_id=1, source_target_pairs={{0,32},{16,48},{32,0},{48,16},{1,33},{17,49},{33,1},{49,17},{2,34}... | collective-permute-start | bytes 2850824 | tf_op jit(solution)/shard_map/ppermute | solution.py:301
  20.6 42.9 %collective-permute-start.2 = (bf16[464,1024]{1,0:T(8,128)(2,1)}, bf16[464,1024]{1,0:T(8,128)(2,1)S(1)}, u32[]{:S(2)}, u32[]{:S(2)}) collective-permute-start(bf16[464,1024]{1,0:T(8,128)(2,1)} %get-tuple-element.13), channel_id=1, source_target_pairs={{0,48},{16,0},{32,16},{48,32},{1,49},{17,1},{33,17},{49,33},{2,50}... | collective-permute-start | bytes 2850824 | tf_op jit(solution)/shard_map/ppermute | solution.py:301
  20.6 42.9 %collective-permute-start = (bf16[464,1024]{1,0:T(8,128)(2,1)}, bf16[464,1024]{1,0:T(8,128)(2,1)S(1)}, u32[]{:S(2)}, u32[]{:S(2)}) collective-permute-start(bf16[464,1024]{1,0:T(8,128)(2,1)} %get-tuple-element.11.refs_0_), channel_id=1, source_target_pairs={{0,16},{16,32},{32,48},{48,0},{1,17},{17,33},{33,49},{49,1},{2,18}... | collective-permute-start | bytes 2850824 | tf_op jit(solution)/shard_map/ppermute | solution.py:301
  23.9 7.9 %collective-permute-start.8 = (bf16[2,128,512]{2,1,0:T(8,128)(2,1)S(1)}, bf16[2,128,512]{2,1,0:T(8,128)(2,1)S(1)}, u32[]{:S(2)}, u32[]{:S(2)}) collective-permute-start(bf16[2,128,512]{2,1,0:T(8,128)(2,1)S(1)} %pair_up.1.refs_4_), channel_id=1, source_target_pairs={{0,2},{2,4},{4,6},{6,8},{8,10},{10,12},{12,14},{14,0},{1,3},{3,5},... | collective-permute-start | bytes 786440 | tf_op jit(solution)/shard_map/ppermute | solution.py:249
  24.5 8.1 %collective-permute-start.5 = (bf16[2,128,512]{2,1,0:T(8,128)(2,1)S(1)}, bf16[2,128,512]{2,1,0:T(8,128)(2,1)S(1)}, u32[]{:S(2)}, u32[]{:S(2)}) collective-permute-start(bf16[2,128,512]{2,1,0:T(8,128)(2,1)S(1)} %collective-permute-done.4.refs_5_), channel_id=1, source_target_pairs={{0,14},{2,0},{4,2},{6,4},{8,6},{10,8},{12,10},{14,12},{1,15},{3,1}... | collective-permute-start | bytes 786440 | tf_op jit(solution)/shard_map/ppermute | solution.py:248
  31.7 7.6 %collective-permute-start.9 = (bf16[2,128,512]{2,1,0:T(8,128)(2,1)S(1)}, bf16[2,128,512]{2,1,0:T(8,128)(2,1)S(1)}, u32[]{:S(2)}, u32[]{:S(2)}) collective-permute-start(bf16[2,128,512]{2,1,0:T(8,128)(2,1)S(1)} %collective-permute-done.8.refs_11_), channel_id=1, source_target_pairs={{0,2},{2,4},{4,6},{6,8},{8,10},{10,12},{12,14},{14,0},{1,3},{3,5},... | collective-permute-start | bytes 786440 | tf_op jit(solution)/shard_map/ppermute | solution.py:249
  32.6 7.6 %collective-permute-start.6 = (bf16[2,128,512]{2,1,0:T(8,128)(2,1)S(1)}, bf16[2,128,512]{2,1,0:T(8,128)(2,1)S(1)}, u32[]{:S(2)}, u32[]{:S(2)}) collective-permute-start(bf16[2,128,512]{2,1,0:T(8,128)(2,1)S(1)} %collective-permute-done.5.refs_6_), channel_id=1, source_target_pairs={{0,14},{2,0},{4,2},{6,4},{8,6},{10,8},{12,10},{14,12},{1,15},{3,1}... | collective-permute-start | bytes 786440 | tf_op jit(solution)/shard_map/ppermute | solution.py:248
  39.3 7.6 %collective-permute-start.10 = (bf16[2,128,512]{2,1,0:T(8,128)(2,1)S(1)}, bf16[2,128,512]{2,1,0:T(8,128)(2,1)S(1)}, u32[]{:S(2)}, u32[]{:S(2)}) collective-permute-start(bf16[2,128,512]{2,1,0:T(8,128)(2,1)S(1)} %collective-permute-done.9.refs_10_), channel_id=1, source_target_pairs={{0,2},{2,4},{4,6},{6,8},{8,10},{10,12},{12,14},{14,0},{1,3},{3,5},... | collective-permute-start | bytes 786440 | tf_op jit(solution)/shard_map/ppermute | solution.py:249
  40.2 23.4 %collective-permute-start.7 = (bf16[2,128,512]{2,1,0:T(8,128)(2,1)S(1)}, bf16[2,128,512]{2,1,0:T(8,128)(2,1)S(1)}, u32[]{:S(2)}, u32[]{:S(2)}) collective-permute-start(bf16[2,128,512]{2,1,0:T(8,128)(2,1)S(1)} %collective-permute-done.6.refs_7_), channel_id=1, source_target_pairs={{0,14},{2,0},{4,2},{6,4},{8,6},{10,8},{12,10},{14,12},{1,15},{3,1}... | collective-permute-start | bytes 786440 | tf_op jit(solution)/shard_map/ppermute | solution.py:250
  63.6 1.2 %copy-start.3 = (bf16[464,1024]{1,0:T(8,128)(2,1)S(1)}, bf16[464,1024]{1,0:T(8,128)(2,1)}, u32[]{:S(2)}) copy-start(bf16[464,1024]{1,0:T(8,128)(2,1)} %get-tuple-element.11.refs_0_) | copy-start | bytes 2850820
  64.8 1.0 copy-start.7

commit v5 on v4

--- a/solution.py
+++ b/solution.py
@@ -69,7 +69,8 @@
     pairs = [(gate_out_hbm, out_ref.at[pl.ds(0, rank)]), (up_out_hbm, out_ref.at[pl.ds(rank, rank)])]
     for step, message in enumerate(messages, 1):
         start = pl.multiple_of(lax.rem(lax.axis_index("x") + step, NX) * width, width)
-        pairs.append((down_hbm.at[:, pl.ds(start, width)], message.at[pl.ds(top, hidden)]))
+        bottom = message.shape[0] - hidden - FOLD
+        pairs.append((down_hbm.at[:, pl.ds(start, width)], message.at[pl.ds(bottom, hidden)]))
     extra = [pltpu.make_async_copy(a, b, sems.at[count + k]) for k, (a, b) in enumerate(pairs)]
     for copy in extra:
         copy.start()
@@ -104,7 +105,7 @@
         columns = first + lax.broadcasted_iota(jnp.int32, (rank, tile), 1)
         right_down = dot32(down_in_ref[...], hidden_value, ((1,), (1,)))
         right_down = jnp.where(columns < limit, right_down * scale, 0.0).astype(jnp.bfloat16)
-        for message in messages:
+        for message in messages[::2]:
             message[:hidden, span] = factor_gate
             message[hidden : 2 * hidden, span] = factor_up
             message[2 * hidden : top, span] = right_down
@@ -115,7 +116,7 @@
     for message in messages:
         for block in range(2 * rank // FOLD):
             rows_of = slice(block * FOLD, (block + 1) * FOLD)
-            message[top + hidden :, block * hidden : (block + 1) * hidden] = out_ref[rows_of, :]
+            message[-FOLD:, block * hidden : (block + 1) * hidden] = out_ref[rows_of, :]
 
 
 def token_stage(tokens, gate_weight, up_weight, gate_in, up_in, down_in, down_weight, gate_out, up_out, lengths, scale):
@@ -126,7 +127,9 @@
     return pl.pallas_call(
         lambda *refs: token_kernel(chunk, scale, *refs),
         out_shape=[
-            *[jax.ShapeDtypeStruct((3 * hidden + rank + FOLD, rows), jnp.bfloat16)] * (NX - 1),
+            jax.ShapeDtypeStruct((3 * hidden + rank + FOLD, rows), jnp.bfloat16),
+            jax.ShapeDtypeStruct((hidden + FOLD, rows), jnp.bfloat16),
+            jax.ShapeDtypeStruct((3 * hidden + rank + FOLD, rows), jnp.bfloat16),
             jax.ShapeDtypeStruct((rows, 2 * rank), jnp.float32),
             jax.ShapeDtypeStruct((8, 128), jnp.float32),
         ],
@@ -149,9 +152,28 @@
     )(lengths, tokens, gate_weight, up_weight, gate_in, up_in, down_in, down_weight, gate_out, up_out)
 
 
+def forward_kernel(before_ref, after_ref, first_ref, second_ref):
+    half = first_ref.shape[0]
+    first_ref[...] = before_ref[:half, :]
+    second_ref[...] = after_ref[half : 2 * half, :]
+
+
+def halves(before, after, half):
+    shape = jax.ShapeDtypeStruct((half, before.shape[1]), before.dtype)
+    return pl.pallas_call(
+        forward_kernel,
+        out_shape=[shape] * 2,
+        in_specs=[VMEM] * 2,
+        out_specs=[VMEM] * 2,
+        compiler_params=pltpu.CompilerParams(vmem_limit_bytes=8 * MIB),
+        name="halves",
+    )(before, after)
+
+
 def tail_kernel(weight_hbm, gate_out_ref, up_out_ref, down_out_hbm, right_ref, *refs):
-    messages, blocks = refs[:NX], refs[NX : NX + NZ]
-    out_ref, weights, projs, grads, total, sems = refs[NX + NZ :]
+    messages, far_halves, blocks = refs[:NX], refs[NX : NX + 2], refs[NX + 2 : NX + 2 + NZ]
+    out_ref, weights, projs, grads, far_ref, total, sems = refs[NX + 2 + NZ :]
+    factors = [messages[0], messages[1], far_ref, messages[3]]
     hidden, model_width = weight_hbm.shape
     rank = gate_out_ref.shape[0]
     width = model_width // NX
@@ -166,7 +188,10 @@
         (down_out_hbm.at[:, pl.ds(start, width)], weights.at[pl.ds(NX * hidden, rank)]),
     ]
     for step in range(1, NX):
-        pairs.append((messages[step].at[pl.ds(top, hidden)], weights.at[pl.ds(step * hidden, hidden)]))
+        bottom = messages[step].shape[0] - hidden - FOLD
+        pairs.append((messages[step].at[pl.ds(bottom, hidden)], weights.at[pl.ds(step * hidden, hidden)]))
+    for index, part in enumerate(far_halves):
+        pairs.append((part, far_ref.at[pl.ds(index * part.shape[0], part.shape[0])]))
     for step, block in enumerate(blocks):
         base = lax.rem(z_at + step, NZ) * both
         for kind, y_of in enumerate((y_at, 1 - y_at)):
@@ -180,7 +205,7 @@
     for step in range(1, NX):
         columns = slice(step * hidden, (step + 1) * hidden)
         for block in range(2 * rank // FOLD):
-            folded = messages[step][top + hidden :, block * hidden : (block + 1) * hidden]
+            folded = messages[step][-FOLD:, block * hidden : (block + 1) * hidden]
             projs[block * FOLD : (block + 1) * FOLD, columns] = folded
     for copy in copies:
         copy.wait()
@@ -192,7 +217,7 @@
         for kind in range(2):
             products = []
             for step in range(NX):
-                factor = messages[step][kind * hidden : (kind + 1) * hidden, columns].astype(jnp.float32)
+                factor = factors[step][kind * hidden : (kind + 1) * hidden, columns].astype(jnp.float32)
                 products.append(total[example, step * hidden : (step + 1) * hidden] * factor)
             product = jnp.concatenate(products, axis=0)
             high = product.astype(jnp.bfloat16)
@@ -208,9 +233,9 @@
             precision=lax.Precision.HIGHEST,
             preferred_element_type=jnp.float32,
         )
-        right_down = messages[0][2 * hidden : top, columns].astype(jnp.float32)
+        right_down = factors[0][2 * hidden : top, columns].astype(jnp.float32)
         for step in range(1, NX):
-            right_down = right_down + messages[step][2 * hidden : top, columns].astype(jnp.float32)
+            right_down = right_down + factors[step][2 * hidden : top, columns].astype(jnp.float32)
         out_ref[3 * example] = sides[:rank, :rank]
         out_ref[3 * example + 1] = sides[rank:, rank:]
         out_ref[3 * example + 2] = dot32(
@@ -218,23 +243,24 @@
         )
 
 
-def tail_stage(down_weight, gate_out, up_out, down_out, right, messages, blocks):
+def tail_stage(down_weight, gate_out, up_out, down_out, right, messages, far, blocks):
     hidden, model_width = down_weight.shape
     rank = gate_out.shape[0]
     examples, _, seq_dev = blocks[0].shape
     width = model_width // NX
-    operands = [down_weight, gate_out, up_out, down_out, right, *messages, *blocks]
+    operands = [down_weight, gate_out, up_out, down_out, right, *messages, *far, *blocks]
     return pl.pallas_call(
         tail_kernel,
         out_shape=jax.ShapeDtypeStruct((examples * 3, rank, rank), jnp.float32),
-        in_specs=[HBM, VMEM, VMEM, HBM, VMEM] + [VMEM] * NX + [HBM] * NZ,
+        in_specs=[HBM, VMEM, VMEM, HBM, VMEM] + [VMEM] * NX + [HBM] * (2 + NZ),
         out_specs=VMEM,
         scratch_shapes=[
             pltpu.VMEM((NX * hidden + rank, width), jnp.bfloat16),
             pltpu.VMEM((2 * rank, NX * hidden), jnp.bfloat16),
             pltpu.VMEM((examples, width, seq_dev), jnp.bfloat16),
+            pltpu.VMEM((2 * far[0].shape[0], examples * seq_dev), jnp.bfloat16),
             pltpu.VMEM((examples, NX * hidden + rank, seq_dev), jnp.float32),
-            pltpu.SemaphoreType.DMA((1 + NX + NZ * NY,)),
+            pltpu.SemaphoreType.DMA((3 + NX + NZ * NY,)),
         ],
         compiler_params=pltpu.CompilerParams(vmem_limit_bytes=16 * MIB),
         cost_estimate=pl.CostEstimate(flops=4 * 10**9, bytes_accessed=8 * MIB, transcendentals=0),
@@ -299,9 +325,11 @@
     )
     sent, (right, done) = sent[: NX - 1], sent[NX - 1 :]
     messages = [sent[0]] + [lax.ppermute(piece, "x", shifted(NX, step)) for step, piece in enumerate(sent, 1)]
+    first, second = halves(messages[1], messages[3], gate_weight.shape[1] + gate_out.shape[0] // 2)
+    far = [lax.ppermute(first, "x", shifted(NX, 1)), lax.ppermute(second, "x", shifted(NX, -1))]
     pair = pair_up(own_grad, other_grad, done)
     blocks = ring_z(pair)
-    products = tail_stage(down_weight, gate_out, up_out, proj_down_out.T, right, messages, blocks)
+    products = tail_stage(down_weight, gate_out, up_out, proj_down_out.T, right, messages, far, blocks)
     total = sum_everywhere(products.reshape(examples * 3, -1))
     return total.reshape(examples, 3, -1)
 

time: 106 us -> 99.4 us (0.938)
  waiting for transfers between devices: 28.6 us -> 18.5 us
  blocking collectives: 33.7 us -> 36.3 us
    ppermute x3, waiting for transfers between devices: 16.6 us -> 5.13 us  [shards(): lax.ppermute(piece, 'x', shifted(NX, step))]
    ppermute x3, waiting for transfers between devices: 9.59 us -> 0.01 us  [ring_z(): down.append(lax.ppermute(down[-1], 'z', shifted(NZ, 1)))]
    ppermute x3, waiting for transfers between devices: 2.35 us -> 8.67 us  [ring_z(): up.append(lax.ppermute(up[-1], 'z', shifted(NZ, -1)))]
    ppermute x1, waiting for transfers between devices: 0.01 us -> 3.46 us  [shards(): other_grad = lax.ppermute(own_grad, 'yh', shifted(NY, 1))]
    ppermute x0 -> x2, starting transfers between devices: none -> 2.1 us  [the longest x1 1.76 us: shards(): lax.ppermute(first, 'x', shifted(NX, 1))]
    all_to_all x1, blocking collectives: 13.3 us -> 15.2 us  [sum_everywhere(): pieces = lax.all_to_all(pieces, ('sy', 'sc', 'z'), 0, 0, tiled=True)]
    ppermute x0 -> x2, waiting for transfers between devices: none -> 1.24 us  [the longest x1 1.24 us: shards(): lax.ppermute(second, 'x', shifted(NX, -1))]
  transfers between devices with their start and end apart: 11 -> 13, of which waited for: 7 -> 6; matrix products, arithmetic and copies ran while one was open for 0% -> 0% of each run, Pallas kernels for 9% -> 0%
where the time goes in v5:
time: 99.4 us; the launch traced here: 99.1 us
  blocking collectives  36.3 us (37%)
  starting transfers between devices  25.9 us (26%)
  waiting for transfers between devices  18.5 us (19%)
  Pallas kernels  14.4 us (14%)
  local copies, waits for them, and re-layouts  3.75 us (4%)
    all_to_all x1, blocking collectives, sum_everywhere(): blocks = lax.all_to_all(spread, ('x', 'z', 'yh'), 0, 0, tiled=True)  21.2 us
    all_to_all x1, blocking collectives, sum_everywhere(): pieces = lax.all_to_all(pieces, ('sy', 'sc', 'z'), 0, 0, tiled=True)  15.2 us
    ppermute x3, starting transfers between devices, ring_z(): up.append(lax.ppermute(up[-1], 'z', shifted(NZ, -1)))  13.1 us
    pallas_call x1, Pallas kernels, token_stage(): pl.pallas_call(lambda *refs: token_kernel(chunk, scale, *refs), out_shape...  9.17 us
    ppermute x3, waiting for transfers between devices, ring_z(): up.append(lax.ppermute(up[-1], 'z', shifted(NZ, -1)))  8.67 us
    pallas_call x1, Pallas kernels, tail_stage(): pl.pallas_call(tail_kernel, out_shape=jax.ShapeDtypeStruct((examples * 3,...  5.19 us
    ppermute x3, waiting for transfers between devices, shards(): lax.ppermute(piece, 'x', shifted(NX, step))  5.13 us
    ppermute x3, starting transfers between devices, shards(): lax.ppermute(piece, 'x', shifted(NX, step))  3.98 us
  transfers between devices with their start and end apart: 13, of which 6 were waited for; matrix products, arithmetic and copies ran while one was open for 0% of the time, Pallas kernels for 0%

profile of v5, /device:TPU:6, one launch (start us, length us, event | category | flops | bytes accessed | tf_op | source)
XLA Modules:
  0.0 99.1 jit_solution(430919442522882600)
XLA Ops:
  0.0 0.0 copy-start
  0.0 0.0 copy-start.2
  0.0 0.0 copy-start.4
  0.0 0.0 copy-start.5
  0.0 0.0 copy-start.6
  0.0 9.2 %token_stage.1 = (bf16[464,1024]{1,0:T(8,128)(2,1)}, bf16[144,1024]{1,0:T(8,128)(2,1)}, bf16[464,1024]{1,0:T(8,128)(2,1)}, f32[1024,128]{1,0:T(8,128)}, f32[8,128]{1,0:T(8,128)}) custom-call(s32[2]{0:T(128)} %refs_0_.1, bf16[1024,4096]{1,0:T(8,128)(2,1)} %bitcast.25, bf16[4096,128]{1,0:T(8,128)(2,1)} %refs_2_.1, bf16[4096,128]{1,0:T(8,128)(2,1)} %refs_3_.1, ...), custom_call_target="tpu_custom_call" | custom-call | flops 4294967296 | bytes 16777216 | tf_op jit(solution)/shard_map/token_stage/pallas_call | solution.py:127
  9.2 2.3 %collective-permute-start = (bf16[464,1024]{1,0:T(8,128)(2,1)}, bf16[464,1024]{1,0:T(8,128)(2,1)S(1)}, u32[]{:S(2)}, u32[]{:S(2)}) collective-permute-start(bf16[464,1024]{1,0:T(8,128)(2,1)} %get-tuple-element.13.refs_0_), channel_id=1, source_target_pairs={{0,16},{16,32},{32,48},{48,0},{1,17},{17,33},{33,49},{49,1},{2,18}... | collective-permute-start | bytes 2850824 | tf_op jit(solution)/shard_map/ppermute | solution.py:327
  11.5 0.0 collective-permute-start.2
  11.5 0.0 copy-done
  11.5 3.0 %collective-permute-start.5 = (bf16[2,64,512]{2,1,0:T(8,128)(2,1)S(1)}, bf16[2,64,512]{2,1,0:T(8,128)(2,1)S(1)}, u32[]{:S(2)}, u32[]{:S(2)}) collective-permute-start(bf16[2,64,512]{2,1,0:T(8,128)(2,1)S(1)} %bitcast.15), channel_id=1, source_target_pairs={{0,1},{1,0},{2,3},{3,2},{4,5},{5,4},{6,7},{7,6},{8,9},{9,8},{10,11... | collective-permute-start | bytes 393224 | tf_op jit(solution)/shard_map/ppermute | solution.py:311
  14.5 3.5 %collective-permute-done.5.other_ref = bf16[2,64,512]{2,1,0:T(8,128)(2,1)S(1)} collective-permute-done((bf16[2,64,512]{2,1,0:T(8,128)(2,1)S(1)}, bf16[2,64,512]{2,1,0:T(8,128)(2,1)S(1)}, u32[]{:S(2)}, u32[]{:S(2)}) %collective-permute-start.5) | collective-permute-done | bytes 131104 | tf_op jit(solution)/shard_map/ppermute | solution.py:311
  18.0 0.0 copy-start.1
  18.0 0.7 copy-done.1
  18.7 5.7 %collective-permute-start.6 = (bf16[2,128,512]{2,1,0:T(8,128)(2,1)S(1)}, bf16[2,128,512]{2,1,0:T(8,128)(2,1)S(1)}, u32[]{:S(2)}, u32[]{:S(2)}) collective-permute-start(bf16[2,128,512]{2,1,0:T(8,128)(2,1)S(1)} %pair_up.1.refs_6_), channel_id=1, source_target_pairs={{0,14},{2,0},{4,2},{6,4},{8,6},{10,8},{12,10},{14,12},{1,15},{3,1}... | collective-permute-start | bytes 786440 | tf_op jit(solution)/shard_map/ppermute | solution.py:274
  24.4 0.0 collective-permute-start.10
  24.4 3.9 %collective-permute-done.6.refs_7_ = bf16[2,128,512]{2,1,0:T(8,128)(2,1)S(1)} collective-permute-done((bf16[2,128,512]{2,1,0:T(8,128)(2,1)S(1)}, bf16[2,128,512]{2,1,0:T(8,128)(2,1)S(1)}, u32[]{:S(2)}, u32[]{:S(2)}) %collective-permute-start.6) | collective-permute-done | bytes 262176 | tf_op jit(solution)/shard_map/ppermute | solution.py:274
  28.3 3.7 %collective-permute-start.7 = (bf16[2,128,512]{2,1,0:T(8,128)(2,1)S(1)}, bf16[2,128,512]{2,1,0:T(8,128)(2,1)S(1)}, u32[]{:S(2)}, u32[]{:S(2)}) collective-permute-start(bf16[2,128,512]{2,1,0:T(8,128)(2,1)S(1)} %collective-permute-done.6.refs_7_), channel_id=1, source_target_pairs={{0,14},{2,0},{4,2},{6,4},{8,6},{10,8},{12,10},{14,12},{1,15},{3,1}... | collective-permute-start | bytes 786440 | tf_op jit(solution)/shard_map/ppermute | solution.py:274
  32.0 0.0 collective-permute-done.10.refs_13_
  32.0 0.0 collective-permute-start.11
  32.0 3.9 %collective-permute-done.7.refs_8_ = bf16[2,128,512]{2,1,0:T(8,128)(2,1)S(1)} collective-permute-done((bf16[2,128,512]{2,1,0:T(8,128)(2,1)S(1)}, bf16[2,128,512]{2,1,0:T(8,128)(2,1)S(1)}, u32[]{:S(2)}, u32[]{:S(2)}) %collective-permute-start.7) | collective-permute-done | bytes 262176 | tf_op jit(solution)/shard_map/ppermute | solution.py:274
  35.9 3.7 %collective-permute-start.8 = (bf16[2,128,512]{2,1,0:T(8,128)(2,1)S(1)}, bf16[2,128,512]{2,1,0:T(8,128)(2,1)S(1)}, u32[]{:S(2)}, u32[]{:S(2)}) collective-permute-start(bf16[2,128,512]{2,1,0:T(8,128)(2,1)S(1)} %collective-permute-done.7.refs_8_), channel_id=1, source_target_pairs={{0,14},{2,0},{4,2},{6,4},{8,6},{10,8},{12,10},{14,12},{1,15},{3,1}... | collective-permute-start | bytes 786440 | tf_op jit(solution)/shard_map/ppermute | solution.py:274
  39.6 0.0 collective-permute-done.before_ref.refs_1_
  39.6 0.0 collective-permute-done.2.after_ref.refs_3_
  39.7 1.8 %collective-permute-start.3 = (bf16[160,1024]{1,0:T(8,128)(2,1)S(1)}, bf16[160,1024]{1,0:T(8,128)(2,1)S(1)}, u32[]{:S(2)}, u32[]{:S(2)}) collective-permute-start(bf16[160,1024]{1,0:T(8,128)(2,1)S(1)} %get-tuple-element.16), channel_id=1, source_target_pairs={{0,16},{16,32},{32,48},{48,0},{1,17},{17,33},{33,49},{49,1},{2,18}... | collective-permute-start | bytes 983048 | tf_op jit(solution)/shard_map/ppermute | solution.py:329
  41.4 0.3 collective-permute-start.4
  41.8 1.7 %collective-permute-start.1 = (bf16[144,1024]{1,0:T(8,128)(2,1)}, bf16[144,1024]{1,0:T(8,128)(2,1)S(1)}, u32[]{:S(2)}, u32[]{:S(2)}) collective-permute-start(bf16[144,1024]{1,0:T(8,128)(2,1)} %get-tuple-element.14), channel_id=1, source_target_pairs={{0,32},{16,48},{32,0},{48,16},{1,33},{17,49},{33,1},{49,17},{2,34}... | collective-permute-start | bytes 884744 | tf_op jit(solution)/shard_map/ppermute | solution.py:327
  43.4 0.0 collective-permute-done.11.refs_12_
  43.5 0.0 collective-permute-start.12
  43.5 0.9 collective-permute-done.8.refs_9_
  44.4 3.7 %collective-permute-start.9 = (bf16[2,128,512]{2,1,0:T(8,128)(2,1)S(1)}, bf16[2,128,512]{2,1,0:T(8,128)(2,1)S(1)}, u32[]{:S(2)}, u32[]{:S(2)}) collective-permute-start(bf16[2,128,512]{2,1,0:T(8,128)(2,1)S(1)} %collective-permute-done.8.refs_9_), channel_id=1, source_target_pairs={{0,14},{2,0},{4,2},{6,4},{8,6},{10,8},{12,10},{14,12},{1,15},{3,1}... | collective-permute-start | bytes 786440 | tf_op jit(solution)/shard_map/ppermute | solution.py:276
  48.0 5.1 %collective-permute-done.1.refs_2_ = bf16[144,1024]{1,0:T(8,128)(2,1)S(1)} collective-permute-done((bf16[144,1024]{1,0:T(8,128)(2,1)}, bf16[144,1024]{1,0:T(8,128)(2,1)S(1)}, u32[]{:S(2)}, u32[]{:S(2)}) %collective-permute-start.1) | collective-permute-done | bytes 294944 | tf_op jit(solution)/shard_map/ppermute | solution.py:327
  53.2 0.0 collective-permute-done.12.refs_11_
  53.2 0.0 collective-permute-done.9.refs_10_
  53.2 0.0 collective-permute-done.3.refs_4_
  53.2 1.2 %collective-permute-done.4.refs_5_ = bf16[160,1024]{1,0:T(8,128)(2,1)S(1)} collective-permute-done((bf16[160,1024]{1,0:T(8,128)(2,1)S(1)}, bf16[160,1024]{1,0:T(8,128)(2,1)S(1)}, u32[]{:S(2)}, u32[]{:S(2)}) %collective-permute-start.4) | collective-permute-done | bytes 327712 | tf_op jit(solution)/shard_map/ppermute | solution.py:329
  54.4 0.0 copy-done.2
  54.4 0.0 copy-done.4
  54.4 0.0 copy-done.5
  54.4 0.0 copy-done.6
  54.4 0.0 copy-start.3
  54.5 1.2 %copy-done.3 = bf16[464,1024]{1,0:T(8,128)(2,1)S(1)} copy-done((bf16[464,1024]{1,0:T(8,128)(2,1)S(1)}, bf16[464,1024]{1,0:T(8,128)(2,1)}, u32[]{:S(2)}) %copy-start.3) | copy-done | bytes 950296
  55.6 0.0 copy-start.7
  55.6 1.0 %copy-done.7 = f32[1024,128]{1,0:T(8,128)S(1)} copy-done((f32[1024,128]{1,0:T(8,128)S(1)}, f32[1024,128]{1,0:T(8,128)}, u32[]{:S(2)}) %copy-start.7) | copy-done | bytes 524312
  56.7 5.2 %tail_stage.1 = f32[6,64,64]{2,1,0:T(8,128)S(1)} custom-call(bf16[128,4096]{1,0:T(8,128)(2,1)S(1)} %copy-done.2, bf16[64,128]{1,0:T(8,128)(2,1)S(1)} %bitcast.19, bf16[64,128]{1,0:T(8,128)(2,1)S(1)} %bitcast.21, bf16[64,4096]{1,0:T(8,128)(2,1)S(1)} %bitcast.17, f32[1024,128]{1,0:T(8,128)S(1)} %copy-done.7, bf16[464,1024]{1,0:T(8,128)(2,1)S(1)} %copy-done.3, ...), custom_call_target="tpu_custom_call" | custom-call | flops 4000000000 | bytes 8388608 | tf_op jit(solution)/shard_map/tail_stage/pallas_call | solution.py:252
  61.9 0.1 reshape_reshape.6
  62.0 0.1 copy.30
  62.0 15.2 %all_to_all.10 = f32[32,6,128]{2,1,0:T(8,128)S(1)} all-to-all(f32[32,6,128]{2,1,0:T(8,128)S(1)} %bitcast.23), channel_id=1, replica_groups=mesh['sy'=2,'sc'=2,'x'=4,'z'=8,'yh'=2] {'sy','sc','z'}, dimensions={0} | all-to-all | bytes 196608 | tf_op jit(solution)/shard_map/all_to_all | solution.py:284
  77.3 21.2 %all_to_all.11 = f32[64,6,128]{2,1,0:T(8,128)S(1)} all-to-all(f32[64,6,128]{2,1,0:T(8,128)S(1)} %broadcast_in_dim.2), channel_id=1, replica_groups=mesh['sy'=2,'sc'=2,'x'=4,'z'=8,'yh'=2] {'x','z','yh'}, dimensions={0} | all-to-all | bytes 393216 | tf_op jit(solution)/shard_map/all_to_all | solution.py:287
  98.5 0.6 copy.24
  (7 shorter events, 0.2 us)
Async XLA Ops:
  0.0 11.5 %copy-start = (bf16[2,512,64]{1,2,0:T(8,128)(2,1)S(1)}, bf16[2,512,64]{1,2,0:T(8,128)(2,1)}, u32[]{:S(2)}) copy-start(bf16[2,512,64]{1,2,0:T(8,128)(2,1)} %param.13) | copy-start | bytes 393220
  0.0 54.4 %copy-start.2 = (bf16[128,4096]{1,0:T(8,128)(2,1)S(1)}, bf16[128,4096]{1,0:T(8,128)(2,1)}, u32[]{:S(2)}) copy-start(bf16[128,4096]{1,0:T(8,128)(2,1)} %weight_hbm.1) | copy-start | bytes 3145732
  0.0 54.4 %copy-start.4 = (bf16[4096,64]{0,1:T(8,128)(2,1)S(1)}, bf16[4096,64]{0,1:T(8,128)(2,1)}, u32[]{:S(2)}) copy-start(bf16[4096,64]{0,1:T(8,128)(2,1)} %param.22) | copy-start | bytes 1572868
  0.0 54.4 %copy-start.5 = (bf16[128,64]{0,1:T(8,128)(2,1)S(1)}, bf16[128,64]{0,1:T(8,128)(2,1)}, u32[]{:S(2)}) copy-start(bf16[128,64]{0,1:T(8,128)(2,1)} %param.18) | copy-start | bytes 49156
  0.0 54.4 %copy-start.6 = (bf16[128,64]{0,1:T(8,128)(2,1)S(1)}, bf16[128,64]{0,1:T(8,128)(2,1)}, u32[]{:S(2)}) copy-start(bf16[128,64]{0,1:T(8,128)(2,1)} %param.20) | copy-start | bytes 49156
  9.2 30.4 %collective-permute-start = (bf16[464,1024]{1,0:T(8,128)(2,1)}, bf16[464,1024]{1,0:T(8,128)(2,1)S(1)}, u32[]{:S(2)}, u32[]{:S(2)}) collective-permute-start(bf16[464,1024]{1,0:T(8,128)(2,1)} %get-tuple-element.13.refs_0_), channel_id=1, source_target_pairs={{0,16},{16,32},{32,48},{48,0},{1,17},{17,33},{33,49},{49,1},{2,18}... | collective-permute-start | bytes 2850824 | tf_op jit(solution)/shard_map/ppermute | solution.py:327
  11.5 28.1 %collective-permute-start.2 = (bf16[464,1024]{1,0:T(8,128)(2,1)}, bf16[464,1024]{1,0:T(8,128)(2,1)S(1)}, u32[]{:S(2)}, u32[]{:S(2)}) collective-permute-start(bf16[464,1024]{1,0:T(8,128)(2,1)} %get-tuple-element.15), channel_id=1, source_target_pairs={{0,48},{16,0},{32,16},{48,32},{1,49},{17,1},{33,17},{49,33},{2,50}... | collective-permute-start | bytes 2850824 | tf_op jit(solution)/shard_map/ppermute | solution.py:327
  11.5 6.5 %collective-permute-start.5 = (bf16[2,64,512]{2,1,0:T(8,128)(2,1)S(1)}, bf16[2,64,512]{2,1,0:T(8,128)(2,1)S(1)}, u32[]{:S(2)}, u32[]{:S(2)}) collective-permute-start(bf16[2,64,512]{2,1,0:T(8,128)(2,1)S(1)} %bitcast.15), channel_id=1, source_target_pairs={{0,1},{1,0},{2,3},{3,2},{4,5},{5,4},{6,7},{7,6},{8,9},{9,8},{10,11... | collective-permute-start | bytes 393224 | tf_op jit(solution)/shard_map/ppermute | solution.py:311
  18.0 0.7 copy-start.1
  18.7 9.6 %collective-permute-start.6 = (bf16[2,128,512]{2,1,0:T(8,128)(2,1)S(1)}, bf16[2,128,512]{2,1,0:T(8,128)(2,1)S(1)}, u32[]{:S(2)}, u32[]{:S(2)}) collective-permute-start(bf16[2,128,512]{2,1,0:T(8,128)(2,1)S(1)} %pair_up.1.refs_6_), channel_id=1, source_target_pairs={{0,14},{2,0},{4,2},{6,4},{8,6},{10,8},{12,10},{14,12},{1,15},{3,1}... | collective-permute-start | bytes 786440 | tf_op jit(solution)/shard_map/ppermute | solution.py:274
  24.4 7.6 %collective-permute-start.10 = (bf16[2,128,512]{2,1,0:T(8,128)(2,1)S(1)}, bf16[2,128,512]{2,1,0:T(8,128)(2,1)S(1)}, u32[]{:S(2)}, u32[]{:S(2)}) collective-permute-start(bf16[2,128,512]{2,1,0:T(8,128)(2,1)S(1)} %pair_up.1.refs_6_), channel_id=1, source_target_pairs={{0,2},{2,4},{4,6},{6,8},{8,10},{10,12},{12,14},{14,0},{1,3},{3,5},... | collective-permute-start | bytes 786440 | tf_op jit(solution)/shard_map/ppermute | solution.py:275
  28.3 7.6 %collective-permute-start.7 = (bf16[2,128,512]{2,1,0:T(8,128)(2,1)S(1)}, bf16[2,128,512]{2,1,0:T(8,128)(2,1)S(1)}, u32[]{:S(2)}, u32[]{:S(2)}) collective-permute-start(bf16[2,128,512]{2,1,0:T(8,128)(2,1)S(1)} %collective-permute-done.6.refs_7_), channel_id=1, source_target_pairs={{0,14},{2,0},{4,2},{6,4},{8,6},{10,8},{12,10},{14,12},{1,15},{3,1}... | collective-permute-start | bytes 786440 | tf_op jit(solution)/shard_map/ppermute | solution.py:274
  32.0 11.4 %collective-permute-start.11 = (bf16[2,128,512]{2,1,0:T(8,128)(2,1)S(1)}, bf16[2,128,512]{2,1,0:T(8,128)(2,1)S(1)}, u32[]{:S(2)}, u32[]{:S(2)}) collective-permute-start(bf16[2,128,512]{2,1,0:T(8,128)(2,1)S(1)} %collective-permute-done.10.refs_13_), channel_id=1, source_target_pairs={{0,2},{2,4},{4,6},{6,8},{8,10},{10,12},{12,14},{14,0},{1,3},{3,5},... | collective-permute-start | bytes 786440 | tf_op jit(solution)/shard_map/ppermute | solution.py:275
  35.9 8.4 %collective-permute-start.8 = (bf16[2,128,512]{2,1,0:T(8,128)(2,1)S(1)}, bf16[2,128,512]{2,1,0:T(8,128)(2,1)S(1)}, u32[]{:S(2)}, u32[]{:S(2)}) collective-permute-start(bf16[2,128,512]{2,1,0:T(8,128)(2,1)S(1)} %collective-permute-done.7.refs_8_), channel_id=1, source_target_pairs={{0,14},{2,0},{4,2},{6,4},{8,6},{10,8},{12,10},{14,12},{1,15},{3,1}... | collective-permute-start | bytes 786440 | tf_op jit(solution)/shard_map/ppermute | solution.py:274
  39.7 13.5 %collective-permute-start.3 = (bf16[160,1024]{1,0:T(8,128)(2,1)S(1)}, bf16[160,1024]{1,0:T(8,128)(2,1)S(1)}, u32[]{:S(2)}, u32[]{:S(2)}) collective-permute-start(bf16[160,1024]{1,0:T(8,128)(2,1)S(1)} %get-tuple-element.16), channel_id=1, source_target_pairs={{0,16},{16,32},{32,48},{48,0},{1,17},{17,33},{33,49},{49,1},{2,18}... | collective-permute-start | bytes 983048 | tf_op jit(solution)/shard_map/ppermute | solution.py:329
  41.4 13.0 %collective-permute-start.4 = (bf16[160,1024]{1,0:T(8,128)(2,1)S(1)}, bf16[160,1024]{1,0:T(8,128)(2,1)S(1)}, u32[]{:S(2)}, u32[]{:S(2)}) collective-permute-start(bf16[160,1024]{1,0:T(8,128)(2,1)S(1)} %get-tuple-element.17), channel_id=1, source_target_pairs={{0,48},{16,0},{32,16},{48,32},{1,49},{17,1},{33,17},{49,33},{2,50}... | collective-permute-start | bytes 983048 | tf_op jit(solution)/shard_map/ppermute | solution.py:329
  41.8 11.4 %collective-permute-start.1 = (bf16[144,1024]{1,0:T(8,128)(2,1)}, bf16[144,1024]{1,0:T(8,128)(2,1)S(1)}, u32[]{:S(2)}, u32[]{:S(2)}) collective-permute-start(bf16[144,1024]{1,0:T(8,128)(2,1)} %get-tuple-element.14), channel_id=1, source_target_pairs={{0,32},{16,48},{32,0},{48,16},{1,33},{17,49},{33,1},{49,17},{2,34}... | collective-permute-start | bytes 884744 | tf_op jit(solution)/shard_map/ppermute | solution.py:327
  43.5 9.7 %collective-permute-start.12 = (bf16[2,128,512]{2,1,0:T(8,128)(2,1)S(1)}, bf16[2,128,512]{2,1,0:T(8,128)(2,1)S(1)}, u32[]{:S(2)}, u32[]{:S(2)}) collective-permute-start(bf16[2,128,512]{2,1,0:T(8,128)(2,1)S(1)} %collective-permute-done.11.refs_12_), channel_id=1, source_target_pairs={{0,2},{2,4},{4,6},{6,8},{8,10},{10,12},{12,14},{14,0},{1,3},{3,5},... | collective-permute-start | bytes 786440 | tf_op jit(solution)/shard_map/ppermute | solution.py:275
  44.4 8.8 %collective-permute-start.9 = (bf16[2,128,512]{2,1,0:T(8,128)(2,1)S(1)}, bf16[2,128,512]{2,1,0:T(8,128)(2,1)S(1)}, u32[]{:S(2)}, u32[]{:S(2)}) collective-permute-start(bf16[2,128,512]{2,1,0:T(8,128)(2,1)S(1)} %collective-permute-done.8.refs_9_), channel_id=1, source_target_pairs={{0,14},{2,0},{4,2},{6,4},{8,6},{10,8},{12,10},{14,12},{1,15},{3,1}... | collective-permute-start | bytes 786440 | tf_op jit(solution)/shard_map/ppermute | solution.py:276
  54.4 1.2 %copy-start.3 = (bf16[464,1024]{1,0:T(8,128)(2,1)S(1)}, bf16[464,1024]{1,0:T(8,128)(2,1)}, u32[]{:S(2)}) copy-start(bf16[464,1024]{1,0:T(8,128)(2,1)} %get-tuple-element.13.refs_0_) | copy-start | bytes 2850820
  55.6 1.0 %copy-start.7 = (f32[1024,128]{1,0:T(8,128)S(1)}, f32[1024,128]{1,0:T(8,128)}, u32[]{:S(2)}) copy-start(f32[1024,128]{1,0:T(8,128)} %get-tuple-element.12.right_ref) | copy-start | bytes 1572868

commit v6 on v5

--- a/solution.py
+++ b/solution.py
@@ -22,27 +22,33 @@
     return lax.dot_general(a, b, (dims, ((), ())), preferred_element_type=jnp.float32, precision=precision)
 
 
-def pair_kernel(own_ref, other_ref, after_ref, out_ref):
+def pair_kernel(own_ref, other_ref, *refs):
+    out_ref = refs[-1]
     piece = own_ref.shape[1]
     out_ref[:, :piece, :] = own_ref[...]
     out_ref[:, piece:, :] = other_ref[...]
 
 
-def pair_up(own, other, after):
+def pair_up(own, other, messages):
     examples, piece, seq_dev = own.shape
-    return pl.pallas_call(
+    *messages, pair = pl.pallas_call(
         pair_kernel,
-        out_shape=jax.ShapeDtypeStruct((examples, NY * piece, seq_dev), own.dtype),
-        in_specs=[VMEM, VMEM, HBM],
-        out_specs=VMEM,
-        compiler_params=pltpu.CompilerParams(vmem_limit_bytes=4 * MIB),
+        out_shape=[
+            *[jax.ShapeDtypeStruct(message.shape, message.dtype) for message in messages],
+            jax.ShapeDtypeStruct((examples, NY * piece, seq_dev), own.dtype),
+        ],
+        in_specs=[VMEM, VMEM] + [HBM] * len(messages),
+        out_specs=[HBM] * len(messages) + [VMEM],
+        input_output_aliases={2 + index: index for index in range(len(messages))},
+        compiler_params=pltpu.CompilerParams(vmem_limit_bytes=62 * MIB),
         name="pair_up",
-    )(own, other, after)
+    )(own, other, *messages)
+    return pair, messages
 
 
 def token_kernel(chunk, scale, lengths_ref, tokens_hbm, gate_hbm, up_hbm, gate_in_hbm, up_in_hbm, down_in_hbm, down_hbm, gate_out_hbm, up_out_hbm, *refs):
-    messages, (right_ref, done_ref) = refs[: NX - 1], refs[NX - 1 : NX + 1]
-    tokens_ref, weight_ref, in_ref, down_in_ref, out_ref, total_ref, sems = refs[NX + 1 :]
+    messages, right_ref = refs[: NX - 1], refs[NX - 1]
+    tokens_ref, weight_ref, in_ref, down_in_ref, out_ref, total_ref, sems = refs[NX:]
     rows, model_width = tokens_hbm.shape
     hidden = gate_hbm.shape[1]
     rank = gate_in_hbm.shape[0]
@@ -65,12 +71,13 @@
         for copy in groups[-1]:
             copy.start()
     top = 2 * hidden + rank
-    width = model_width // NX
+    width, half = model_width // NX, hidden // 2
+    core = lax.axis_index("sc")
     pairs = [(gate_out_hbm, out_ref.at[pl.ds(0, rank)]), (up_out_hbm, out_ref.at[pl.ds(rank, rank)])]
     for step, message in enumerate(messages, 1):
         start = pl.multiple_of(lax.rem(lax.axis_index("x") + step, NX) * width, width)
-        bottom = message.shape[0] - hidden - FOLD
-        pairs.append((down_hbm.at[:, pl.ds(start, width)], message.at[pl.ds(bottom, hidden)]))
+        bottom = message.shape[0] - half - FOLD
+        pairs.append((down_hbm.at[pl.ds(core * half, half), pl.ds(start, width)], message.at[pl.ds(bottom, half)]))
     extra = [pltpu.make_async_copy(a, b, sems.at[count + k]) for k, (a, b) in enumerate(pairs)]
     for copy in extra:
         copy.start()
@@ -87,7 +94,6 @@
             total_ref[...] += values
             right_ref[...] += right
 
-    done_ref[...] = jnp.zeros_like(done_ref)
     tile = min(256, seq_dev)
     seq_index = lax.axis_index("sy") * SEQ_PARTS[1] + lax.axis_index("sc")
     for step in range(rows // tile):
@@ -127,14 +133,13 @@
     return pl.pallas_call(
         lambda *refs: token_kernel(chunk, scale, *refs),
         out_shape=[
-            jax.ShapeDtypeStruct((3 * hidden + rank + FOLD, rows), jnp.bfloat16),
-            jax.ShapeDtypeStruct((hidden + FOLD, rows), jnp.bfloat16),
-            jax.ShapeDtypeStruct((3 * hidden + rank + FOLD, rows), jnp.bfloat16),
+            jax.ShapeDtypeStruct((2 * hidden + hidden // 2 + rank + FOLD, rows), jnp.bfloat16),
+            jax.ShapeDtypeStruct((hidden // 2 + FOLD, rows), jnp.bfloat16),
+            jax.ShapeDtypeStruct((2 * hidden + hidden // 2 + rank + FOLD, rows), jnp.bfloat16),
             jax.ShapeDtypeStruct((rows, 2 * rank), jnp.float32),
-            jax.ShapeDtypeStruct((8, 128), jnp.float32),
         ],
         in_specs=[pl.BlockSpec(memory_space=pltpu.SMEM)] + [HBM] * 9,
-        out_specs=[VMEM] * (NX + 1),
+        out_specs=[VMEM] * NX,
         scratch_shapes=[
             pltpu.VMEM((rows, width), jnp.bfloat16),
             pltpu.VMEM((width, 2 * hidden), jnp.bfloat16),
@@ -152,34 +157,38 @@
     )(lengths, tokens, gate_weight, up_weight, gate_in, up_in, down_in, down_weight, gate_out, up_out)
 
 
-def forward_kernel(before_ref, after_ref, first_ref, second_ref):
-    half = first_ref.shape[0]
-    first_ref[...] = before_ref[:half, :]
-    second_ref[...] = after_ref[half : 2 * half, :]
-
-
-def halves(before, after, half):
-    shape = jax.ShapeDtypeStruct((half, before.shape[1]), before.dtype)
+def forward_kernel(before_ref, after_ref, first_ref, second_ref, swap_ref):
+    rows = first_ref.shape[0]
+    half = swap_ref.shape[0] // 2
+    first_ref[...] = before_ref[:rows, :]
+    second_ref[...] = after_ref[rows : 2 * rows, :]
+    swap_ref[:half, :] = before_ref[2 * rows : 2 * rows + half, :]
+    swap_ref[half:, :] = after_ref[2 * rows : 2 * rows + half, :]
+
+
+def halves(before, after, rows, half):
+    shape = jax.ShapeDtypeStruct((rows, before.shape[1]), before.dtype)
+    swap = jax.ShapeDtypeStruct((2 * half, before.shape[1]), before.dtype)
     return pl.pallas_call(
         forward_kernel,
-        out_shape=[shape] * 2,
+        out_shape=[shape, shape, swap],
         in_specs=[VMEM] * 2,
-        out_specs=[VMEM] * 2,
-        compiler_params=pltpu.CompilerParams(vmem_limit_bytes=8 * MIB),
+        out_specs=[VMEM] * 3,
+        compiler_params=pltpu.CompilerParams(vmem_limit_bytes=12 * MIB),
         name="halves",
     )(before, after)
 
 
 def tail_kernel(weight_hbm, gate_out_ref, up_out_ref, down_out_hbm, right_ref, *refs):
-    messages, far_halves, blocks = refs[:NX], refs[NX : NX + 2], refs[NX + 2 : NX + 2 + NZ]
-    out_ref, weights, projs, grads, far_ref, total, sems = refs[NX + 2 + NZ :]
+    messages, far_halves, swaps, blocks = refs[:NX], refs[NX : NX + 2], refs[NX + 2 : NX + 4], refs[NX + 4 : NX + 4 + NZ]
+    out_ref, weights, projs, grads, far_ref, total, sems = refs[NX + 4 + NZ :]
     factors = [messages[0], messages[1], far_ref, messages[3]]
     hidden, model_width = weight_hbm.shape
     rank = gate_out_ref.shape[0]
     width = model_width // NX
     examples, both, seq_dev = blocks[0].shape
     piece = both // NY
-    top = 2 * hidden + rank
+    top, half, core = 2 * hidden + rank, hidden // 2, lax.axis_index("sc")
     x_at, z_at, y_at = lax.axis_index("x"), lax.axis_index("z"), lax.axis_index("yh")
 
     start = pl.multiple_of(x_at * width, width)
@@ -188,8 +197,12 @@
         (down_out_hbm.at[:, pl.ds(start, width)], weights.at[pl.ds(NX * hidden, rank)]),
     ]
     for step in range(1, NX):
-        bottom = messages[step].shape[0] - hidden - FOLD
-        pairs.append((messages[step].at[pl.ds(bottom, hidden)], weights.at[pl.ds(step * hidden, hidden)]))
+        bottom = messages[step].shape[0] - half - FOLD
+        mine = pl.ds(pl.multiple_of(step * hidden + core * half, half), half)
+        pairs.append((messages[step].at[pl.ds(bottom, half)], weights.at[mine]))
+        theirs = pl.ds(pl.multiple_of(step * hidden + (1 - core) * half, half), half)
+        swapped = swaps[1].at[pl.ds(0, half)] if step == 2 else swaps[0].at[pl.ds(step // 2 * half, half)]
+        pairs.append((swapped, weights.at[theirs]))
     for index, part in enumerate(far_halves):
         pairs.append((part, far_ref.at[pl.ds(index * part.shape[0], part.shape[0])]))
     for step, block in enumerate(blocks):
@@ -243,16 +256,16 @@
         )
 
 
-def tail_stage(down_weight, gate_out, up_out, down_out, right, messages, far, blocks):
+def tail_stage(down_weight, gate_out, up_out, down_out, right, messages, far, swaps, blocks):
     hidden, model_width = down_weight.shape
     rank = gate_out.shape[0]
     examples, _, seq_dev = blocks[0].shape
     width = model_width // NX
-    operands = [down_weight, gate_out, up_out, down_out, right, *messages, *far, *blocks]
+    operands = [down_weight, gate_out, up_out, down_out, right, *messages, *far, *swaps, *blocks]
     return pl.pallas_call(
         tail_kernel,
         out_shape=jax.ShapeDtypeStruct((examples * 3, rank, rank), jnp.float32),
-        in_specs=[HBM, VMEM, VMEM, HBM, VMEM] + [VMEM] * NX + [HBM] * (2 + NZ),
+        in_specs=[HBM, VMEM, VMEM, HBM, VMEM] + [VMEM] * NX + [HBM] * (4 + NZ),
         out_specs=VMEM,
         scratch_shapes=[
             pltpu.VMEM((NX * hidden + rank, width), jnp.bfloat16),
@@ -260,7 +273,7 @@
             pltpu.VMEM((examples, width, seq_dev), jnp.bfloat16),
             pltpu.VMEM((2 * far[0].shape[0], examples * seq_dev), jnp.bfloat16),
             pltpu.VMEM((examples, NX * hidden + rank, seq_dev), jnp.float32),
-            pltpu.SemaphoreType.DMA((3 + NX + NZ * NY,)),
+            pltpu.SemaphoreType.DMA((2 + 2 * NX + NZ * NY,)),
         ],
         compiler_params=pltpu.CompilerParams(vmem_limit_bytes=16 * MIB),
         cost_estimate=pl.CostEstimate(flops=4 * 10**9, bytes_accessed=8 * MIB, transcendentals=0),
@@ -323,13 +336,15 @@
         lengths,
         scale,
     )
-    sent, (right, done) = sent[: NX - 1], sent[NX - 1 :]
+    sent, right = sent[: NX - 1], sent[NX - 1]
+    pair, sent = pair_up(own_grad, other_grad, sent)
     messages = [sent[0]] + [lax.ppermute(piece, "x", shifted(NX, step)) for step, piece in enumerate(sent, 1)]
-    first, second = halves(messages[1], messages[3], gate_weight.shape[1] + gate_out.shape[0] // 2)
+    hidden, rank = gate_weight.shape[1], gate_out.shape[0]
+    first, second, swap = halves(messages[1], messages[3], hidden + rank // 2, hidden // 2)
     far = [lax.ppermute(first, "x", shifted(NX, 1)), lax.ppermute(second, "x", shifted(NX, -1))]
-    pair = pair_up(own_grad, other_grad, done)
+    swaps = [lax.ppermute(piece, "sc", shifted(SEQ_PARTS[1], 1)) for piece in (swap, messages[2])]
     blocks = ring_z(pair)
-    products = tail_stage(down_weight, gate_out, up_out, proj_down_out.T, right, messages, far, blocks)
+    products = tail_stage(down_weight, gate_out, up_out, proj_down_out.T, right, messages, far, swaps, blocks)
     total = sum_everywhere(products.reshape(examples * 3, -1))
     return total.reshape(examples, 3, -1)
 

time: 99.4 us -> 101 us (1.016)
  waiting for transfers between devices: 18.5 us -> 14.4 us
  Pallas kernels: 14.4 us -> 17 us
  starting transfers between devices: 25.9 us -> 27.8 us
    ppermute x3, waiting for transfers between devices: 0.01 us -> 6.15 us  [ring_z(): down.append(lax.ppermute(down[-1], 'z', shifted(NZ, 1)))]
    ppermute x3, waiting for transfers between devices: 5.13 us -> 0.74 us  [shards(): lax.ppermute(piece, 'x', shifted(NX, step))]
    ppermute x1, waiting for transfers between devices: 3.46 us -> 0.01 us  [shards(): other_grad = lax.ppermute(own_grad, 'yh', shifted(NY, 1))]
    ppermute x3, starting transfers between devices: 0.01 us -> 1.92 us  [ring_z(): down.append(lax.ppermute(down[-1], 'z', shifted(NZ, 1)))]
    pallas_call x2, Pallas kernels: 0.06 us -> 1.74 us  [the longest x1 1.68 us: pair_up(): pl.pallas_call(pair_kernel, out_shape=[*[jax.ShapeDtypeStruct(message.sha...]
    all_to_all x1, blocking collectives: 15.2 us -> 16.7 us  [sum_everywhere(): pieces = lax.all_to_all(pieces, ('sy', 'sc', 'z'), 0, 0, tiled=True)]
    ppermute x1, waiting for transfers between devices: 1.24 us -> 0.01 us  [shards(): lax.ppermute(second, 'x', shifted(NX, -1))]
    ppermute x3, waiting for transfers between devices: 8.67 us -> 7.52 us  [ring_z(): up.append(lax.ppermute(up[-1], 'z', shifted(NZ, -1)))]
  transfers between devices with their start and end apart: 13 -> 15, of which waited for: 6 -> 5; matrix products, arithmetic and copies ran while one was open for 0% -> 0% of each run, Pallas kernels for 0% -> 9%
where the time goes in v6:
time: 101 us
  blocking collectives  36.9 us (37%)
  starting transfers between devices  27.8 us (28%)
  Pallas kernels  17 us (17%)
  waiting for transfers between devices  14.4 us (14%)
  local copies, waits for them, and re-layouts  4.61 us (5%)
    all_to_all x1, blocking collectives, sum_everywhere(): blocks = lax.all_to_all(spread, ('x', 'z', 'yh'), 0, 0, tiled=True)  20.2 us
    all_to_all x1, blocking collectives, sum_everywhere(): pieces = lax.all_to_all(pieces, ('sy', 'sc', 'z'), 0, 0, tiled=True)  16.7 us
    ppermute x3, starting transfers between devices, ring_z(): up.append(lax.ppermute(up[-1], 'z', shifted(NZ, -1)))  13.1 us
    pallas_call x1, Pallas kernels, token_stage(): pl.pallas_call(lambda *refs: token_kernel(chunk, scale, *refs), out_shape...  9.02 us
    ppermute x3, waiting for transfers between devices, ring_z(): up.append(lax.ppermute(up[-1], 'z', shifted(NZ, -1)))  7.52 us
    pallas_call x1, Pallas kernels, tail_stage(): pl.pallas_call(tail_kernel, out_shape=jax.ShapeDtypeStruct((examples * 3,...  6.26 us
    ppermute x3, waiting for transfers between devices, ring_z(): down.append(lax.ppermute(down[-1], 'z', shifted(NZ, 1)))  6.15 us
    ppermute x1, starting transfers between devices, ring_z(): return up + [lax.ppermute(up[-1], 'z', shifted(NZ, -1))] + down[:0:-1]  4.02 us
  transfers between devices with their start and end apart: 15, of which 5 were waited for; matrix products, arithmetic and copies ran while one was open for 0% of the time, Pallas kernels for 9%

profile of v6, /device:TPU:6, one launch (start us, length us, event | category | flops | bytes accessed | tf_op | source)
XLA Modules:
  0.0 101.0 jit_solution(8327118989683214958)
XLA Ops:
  0.0 3.2 %collective-permute-start = (bf16[2,64,512]{2,1,0:T(8,128)(2,1)}, bf16[2,64,512]{2,1,0:T(8,128)(2,1)S(1)}, u32[]{:S(2)}, u32[]{:S(2)}) collective-permute-start(bf16[2,64,512]{2,1,0:T(8,128)(2,1)} %bitcast.22), channel_id=1, source_target_pairs={{0,1},{1,0},{2,3},{3,2},{4,5},{5,4},{6,7},{7,6},{8,9},{9,8},{10,11... | collective-permute-start | bytes 393224 | tf_op jit(solution)/shard_map/ppermute | solution.py:324
  3.2 0.0 copy-start.1
  3.2 0.0 copy-start.2
  3.2 0.0 copy-start.4
  3.2 0.0 copy-start.5
  3.2 9.0 %token_stage.1 = (bf16[400,1024]{1,0:T(8,128)(2,1)}, bf16[80,1024]{1,0:T(8,128)(2,1)}, bf16[400,1024]{1,0:T(8,128)(2,1)}, f32[1024,128]{1,0:T(8,128)}) custom-call(s32[2]{0:T(128)} %refs_0_.1, bf16[1024,4096]{1,0:T(8,128)(2,1)} %bitcast.25, bf16[4096,128]{1,0:T(8,128)(2,1)} %refs_2_.1, bf16[4096,128]{1,0:T(8,128)(2,1)} %refs_3_.1, ...), custom_call_target="tpu_custom_call" | custom-call | flops 4294967296 | bytes 16777216 | tf_op jit(solution)/shard_map/token_stage/pallas_call | solution.py:133
  12.2 0.0 collective-permute-done.other_ref
  12.2 0.0 copy-start.7
  12.3 0.6 copy-done.7
  12.9 1.7 %pair_up.1 = (bf16[400,1024]{1,0:T(8,128)(2,1)}, bf16[80,1024]{1,0:T(8,128)(2,1)}, bf16[400,1024]{1,0:T(8,128)(2,1)}, bf16[2,128,512]{2,1,0:T(8,128)(2,1)}) custom-call(bf16[2,64,512]{2,1,0:T(8,128)(2,1)} %bitcast.23, bf16[2,64,512]{2,1,0:T(8,128)(2,1)} %copy-done.7, ...), custom_call_target="tpu_custom_call", output_to_operand_aliasing={{0}: (2, {}), {1}: (3, {}), {2}: (4, {})} | custom-call | tf_op jit(solution)/shard_map/pair_up/pallas_call | solution.py:34
  14.6 0.5 collective-permute-start.1
  15.0 1.6 %collective-permute-start.3 = (bf16[400,1024]{1,0:T(8,128)(2,1)}, bf16[400,1024]{1,0:T(8,128)(2,1)S(1)}, u32[]{:S(2)}, u32[]{:S(2)}) collective-permute-start(bf16[400,1024]{1,0:T(8,128)(2,1)} %get-tuple-element.22), channel_id=1, source_target_pairs={{0,48},{16,0},{32,16},{48,32},{1,49},{17,1},{33,17},{49,33},{2,50}... | collective-permute-start | bytes 2457608 | tf_op jit(solution)/shard_map/ppermute | solution.py:341
  16.6 5.9 %collective-permute-start.8 = (bf16[2,128,512]{2,1,0:T(8,128)(2,1)}, bf16[2,128,512]{2,1,0:T(8,128)(2,1)S(1)}, u32[]{:S(2)}, u32[]{:S(2)}) collective-permute-start(bf16[2,128,512]{2,1,0:T(8,128)(2,1)} %get-tuple-element.26.refs_8_), channel_id=1, source_target_pairs={{0,14},{2,0},{4,2},{6,4},{8,6},{10,8},{12,10},{14,12},{1,15},{3,1}... | collective-permute-start | bytes 786440 | tf_op jit(solution)/shard_map/ppermute | solution.py:287
  22.5 0.0 collective-permute-start.12
  22.5 5.0 %collective-permute-done.8.refs_9_ = bf16[2,128,512]{2,1,0:T(8,128)(2,1)S(1)} collective-permute-done((bf16[2,128,512]{2,1,0:T(8,128)(2,1)}, bf16[2,128,512]{2,1,0:T(8,128)(2,1)S(1)}, u32[]{:S(2)}, u32[]{:S(2)}) %collective-permute-start.8) | collective-permute-done | bytes 262176 | tf_op jit(solution)/shard_map/ppermute | solution.py:287
  27.5 3.6 %collective-permute-start.9 = (bf16[2,128,512]{2,1,0:T(8,128)(2,1)S(1)}, bf16[2,128,512]{2,1,0:T(8,128)(2,1)S(1)}, u32[]{:S(2)}, u32[]{:S(2)}) collective-permute-start(bf16[2,128,512]{2,1,0:T(8,128)(2,1)S(1)} %collective-permute-done.8.refs_9_), channel_id=1, source_target_pairs={{0,14},{2,0},{4,2},{6,4},{8,6},{10,8},{12,10},{14,12},{1,15},{3,1}... | collective-permute-start | bytes 786440 | tf_op jit(solution)/shard_map/ppermute | solution.py:287
  31.1 1.4 %collective-permute-start.2 = (bf16[80,1024]{1,0:T(8,128)(2,1)}, bf16[80,1024]{1,0:T(8,128)(2,1)S(1)}, u32[]{:S(2)}, u32[]{:S(2)}) collective-permute-start(bf16[80,1024]{1,0:T(8,128)(2,1)} %get-tuple-element.21), channel_id=1, source_target_pairs={{0,32},{16,48},{32,0},{48,16},{1,33},{17,49},{33,1},{49,17},{2,34}... | collective-permute-start | bytes 491528 | tf_op jit(solution)/shard_map/ppermute | solution.py:341
  32.5 0.0 collective-permute-done.12.refs_15_
  32.5 0.0 collective-permute-start.13
  32.5 2.5 %collective-permute-done.9.refs_10_ = bf16[2,128,512]{2,1,0:T(8,128)(2,1)S(1)} collective-permute-done((bf16[2,128,512]{2,1,0:T(8,128)(2,1)S(1)}, bf16[2,128,512]{2,1,0:T(8,128)(2,1)S(1)}, u32[]{:S(2)}, u32[]{:S(2)}) %collective-permute-start.9) | collective-permute-done | bytes 262176 | tf_op jit(solution)/shard_map/ppermute | solution.py:287
  35.0 3.7 %collective-permute-start.10 = (bf16[2,128,512]{2,1,0:T(8,128)(2,1)S(1)}, bf16[2,128,512]{2,1,0:T(8,128)(2,1)S(1)}, u32[]{:S(2)}, u32[]{:S(2)}) collective-permute-start(bf16[2,128,512]{2,1,0:T(8,128)(2,1)S(1)} %collective-permute-done.9.refs_10_), channel_id=1, source_target_pairs={{0,14},{2,0},{4,2},{6,4},{8,6},{10,8},{12,10},{14,12},{1,15},{3,1}... | collective-permute-start | bytes 786440 | tf_op jit(solution)/shard_map/ppermute | solution.py:287
  38.7 0.6 collective-permute-done.2.refs_2_
  39.2 0.0 collective-permute-start.7
  39.2 0.0 collective-permute-done.1.before_ref.refs_1_
  39.2 0.2 collective-permute-done.3.after_ref.refs_3_
  39.4 0.1 halves.1
  39.5 1.4 %collective-permute-start.4 = (bf16[160,1024]{1,0:T(8,128)(2,1)S(1)}, bf16[160,1024]{1,0:T(8,128)(2,1)S(1)}, u32[]{:S(2)}, u32[]{:S(2)}) collective-permute-start(bf16[160,1024]{1,0:T(8,128)(2,1)S(1)} %get-tuple-element.23), channel_id=1, source_target_pairs={{0,16},{16,32},{32,48},{48,0},{1,17},{17,33},{33,49},{49,1},{2,18}... | collective-permute-start | bytes 983048 | tf_op jit(solution)/shard_map/ppermute | solution.py:344
  40.8 0.8 collective-permute-start.5
  41.6 0.0 collective-permute-done.13.refs_14_
  41.6 1.9 %collective-permute-start.14 = (bf16[2,128,512]{2,1,0:T(8,128)(2,1)S(1)}, bf16[2,128,512]{2,1,0:T(8,128)(2,1)S(1)}, u32[]{:S(2)}, u32[]{:S(2)}) collective-permute-start(bf16[2,128,512]{2,1,0:T(8,128)(2,1)S(1)} %collective-permute-done.13.refs_14_), channel_id=1, source_target_pairs={{0,2},{2,4},{4,6},{6,8},{8,10},{10,12},{12,14},{14,0},{1,3},{3,5},... | collective-permute-start | bytes 786440 | tf_op jit(solution)/shard_map/ppermute | solution.py:288
  43.5 0.0 collective-permute-done.10.refs_11_
  43.5 4.0 %collective-permute-start.11 = (bf16[2,128,512]{2,1,0:T(8,128)(2,1)S(1)}, bf16[2,128,512]{2,1,0:T(8,128)(2,1)S(1)}, u32[]{:S(2)}, u32[]{:S(2)}) collective-permute-start(bf16[2,128,512]{2,1,0:T(8,128)(2,1)S(1)} %collective-permute-done.10.refs_11_), channel_id=1, source_target_pairs={{0,14},{2,0},{4,2},{6,4},{8,6},{10,8},{12,10},{14,12},{1,15},{3,1}... | collective-permute-start | bytes 786440 | tf_op jit(solution)/shard_map/ppermute | solution.py:289
  47.5 0.0 collective-permute-done.7.refs_7_
  47.5 0.0 collective-permute-start.6
  47.5 6.1 %collective-permute-done.14.refs_13_ = bf16[2,128,512]{2,1,0:T(8,128)(2,1)S(1)} collective-permute-done((bf16[2,128,512]{2,1,0:T(8,128)(2,1)S(1)}, bf16[2,128,512]{2,1,0:T(8,128)(2,1)S(1)}, u32[]{:S(2)}, u32[]{:S(2)}) %collective-permute-start.14) | collective-permute-done | bytes 262176 | tf_op jit(solution)/shard_map/ppermute | solution.py:288
  53.7 0.0 collective-permute-done.11.refs_12_
  53.7 0.0 collective-permute-done.6.refs_6_
  53.7 0.0 collective-permute-done.4.refs_4_
  53.7 0.0 collective-permute-done.5.refs_5_
  53.7 0.0 copy-done.1
  53.7 0.0 copy-done.2
  53.7 0.0 copy-done.4
  53.7 0.0 copy-done.5
  53.7 0.0 copy-start
  53.8 1.1 %copy-done = bf16[400,1024]{1,0:T(8,128)(2,1)S(1)} copy-done((bf16[400,1024]{1,0:T(8,128)(2,1)S(1)}, bf16[400,1024]{1,0:T(8,128)(2,1)}, u32[]{:S(2)}) %copy-start) | copy-done | bytes 819224
  54.9 0.0 copy-start.3
  54.9 0.9 copy-done.3
  55.8 0.0 copy-start.6
  55.8 1.0 %copy-done.6 = f32[1024,128]{1,0:T(8,128)S(1)} copy-done((f32[1024,128]{1,0:T(8,128)S(1)}, f32[1024,128]{1,0:T(8,128)}, u32[]{:S(2)}) %copy-start.6) | copy-done | bytes 524312
  56.9 6.3 %tail_stage.1 = f32[6,64,64]{2,1,0:T(8,128)S(1)} custom-call(bf16[128,4096]{1,0:T(8,128)(2,1)S(1)} %copy-done.1, bf16[64,128]{1,0:T(8,128)(2,1)S(1)} %bitcast.17, bf16[64,128]{1,0:T(8,128)(2,1)S(1)} %bitcast.19, bf16[64,4096]{1,0:T(8,128)(2,1)S(1)} %bitcast.15, f32[1024,128]{1,0:T(8,128)S(1)} %copy-done.6, bf16[400,1024]{1,0:T(8,128)(2,1)S(1)} %copy-done, ...), custom_call_target="tpu_custom_call" | custom-call | flops 4000000000 | bytes 8388608 | tf_op jit(solution)/shard_map/tail_stage/pallas_call | solution.py:265
  63.2 0.1 reshape_reshape.6
  63.2 0.1 copy.33
  63.3 16.7 %all_to_all.10 = f32[32,6,128]{2,1,0:T(8,128)S(1)} all-to-all(f32[32,6,128]{2,1,0:T(8,128)S(1)} %bitcast.21), channel_id=1, replica_groups=mesh['sy'=2,'sc'=2,'x'=4,'z'=8,'yh'=2] {'sy','sc','z'}, dimensions={0} | all-to-all | bytes 196608 | tf_op jit(solution)/shard_map/all_to_all | solution.py:297
  80.1 20.2 %all_to_all.11 = f32[64,6,128]{2,1,0:T(8,128)S(1)} all-to-all(f32[64,6,128]{2,1,0:T(8,128)S(1)} %broadcast_in_dim.2), channel_id=1, replica_groups=mesh['sy'=2,'sc'=2,'x'=4,'z'=8,'yh'=2] {'x','z','yh'}, dimensions={0} | all-to-all | bytes 393216 | tf_op jit(solution)/shard_map/all_to_all | solution.py:300
  100.4 0.6 copy.27
  (5 shorter events, 0.1 us)
Async XLA Ops:
  0.0 12.2 %collective-permute-start = (bf16[2,64,512]{2,1,0:T(8,128)(2,1)}, bf16[2,64,512]{2,1,0:T(8,128)(2,1)S(1)}, u32[]{:S(2)}, u32[]{:S(2)}) collective-permute-start(bf16[2,64,512]{2,1,0:T(8,128)(2,1)} %bitcast.22), channel_id=1, source_target_pairs={{0,1},{1,0},{2,3},{3,2},{4,5},{5,4},{6,7},{7,6},{8,9},{9,8},{10,11... | collective-permute-start | bytes 393224 | tf_op jit(solution)/shard_map/ppermute | solution.py:324
  3.2 50.5 %copy-start.1 = (bf16[128,4096]{1,0:T(8,128)(2,1)S(1)}, bf16[128,4096]{1,0:T(8,128)(2,1)}, u32[]{:S(2)}) copy-start(bf16[128,4096]{1,0:T(8,128)(2,1)} %weight_hbm.1) | copy-start | bytes 3145732
  3.2 50.5 %copy-start.2 = (bf16[4096,64]{0,1:T(8,128)(2,1)S(1)}, bf16[4096,64]{0,1:T(8,128)(2,1)}, u32[]{:S(2)}) copy-start(bf16[4096,64]{0,1:T(8,128)(2,1)} %param.22) | copy-start | bytes 1572868
  3.2 50.5 %copy-start.4 = (bf16[128,64]{0,1:T(8,128)(2,1)S(1)}, bf16[128,64]{0,1:T(8,128)(2,1)}, u32[]{:S(2)}) copy-start(bf16[128,64]{0,1:T(8,128)(2,1)} %param.18) | copy-start | bytes 49156
  3.2 50.5 %copy-start.5 = (bf16[128,64]{0,1:T(8,128)(2,1)S(1)}, bf16[128,64]{0,1:T(8,128)(2,1)}, u32[]{:S(2)}) copy-start(bf16[128,64]{0,1:T(8,128)(2,1)} %param.20) | copy-start | bytes 49156
  12.2 0.7 copy-start.7
  14.6 24.7 %collective-permute-start.1 = (bf16[400,1024]{1,0:T(8,128)(2,1)}, bf16[400,1024]{1,0:T(8,128)(2,1)S(1)}, u32[]{:S(2)}, u32[]{:S(2)}) collective-permute-start(bf16[400,1024]{1,0:T(8,128)(2,1)} %get-tuple-element.20.refs_0_), channel_id=1, source_target_pairs={{0,16},{16,32},{32,48},{48,0},{1,17},{17,33},{33,49},{49,1},{2,18}... | collective-permute-start | bytes 2457608 | tf_op jit(solution)/shard_map/ppermute | solution.py:341
  15.0 24.4 %collective-permute-start.3 = (bf16[400,1024]{1,0:T(8,128)(2,1)}, bf16[400,1024]{1,0:T(8,128)(2,1)S(1)}, u32[]{:S(2)}, u32[]{:S(2)}) collective-permute-start(bf16[400,1024]{1,0:T(8,128)(2,1)} %get-tuple-element.22), channel_id=1, source_target_pairs={{0,48},{16,0},{32,16},{48,32},{1,49},{17,1},{33,17},{49,33},{2,50}... | collective-permute-start | bytes 2457608 | tf_op jit(solution)/shard_map/ppermute | solution.py:341
  16.6 10.9 %collective-permute-start.8 = (bf16[2,128,512]{2,1,0:T(8,128)(2,1)}, bf16[2,128,512]{2,1,0:T(8,128)(2,1)S(1)}, u32[]{:S(2)}, u32[]{:S(2)}) collective-permute-start(bf16[2,128,512]{2,1,0:T(8,128)(2,1)} %get-tuple-element.26.refs_8_), channel_id=1, source_target_pairs={{0,14},{2,0},{4,2},{6,4},{8,6},{10,8},{12,10},{14,12},{1,15},{3,1}... | collective-permute-start | bytes 786440 | tf_op jit(solution)/shard_map/ppermute | solution.py:287
  22.5 10.0 %collective-permute-start.12 = (bf16[2,128,512]{2,1,0:T(8,128)(2,1)}, bf16[2,128,512]{2,1,0:T(8,128)(2,1)S(1)}, u32[]{:S(2)}, u32[]{:S(2)}) collective-permute-start(bf16[2,128,512]{2,1,0:T(8,128)(2,1)} %get-tuple-element.26.refs_8_), channel_id=1, source_target_pairs={{0,2},{2,4},{4,6},{6,8},{8,10},{10,12},{12,14},{14,0},{1,3},{3,5},... | collective-permute-start | bytes 786440 | tf_op jit(solution)/shard_map/ppermute | solution.py:288
  27.5 7.5 %collective-permute-start.9 = (bf16[2,128,512]{2,1,0:T(8,128)(2,1)S(1)}, bf16[2,128,512]{2,1,0:T(8,128)(2,1)S(1)}, u32[]{:S(2)}, u32[]{:S(2)}) collective-permute-start(bf16[2,128,512]{2,1,0:T(8,128)(2,1)S(1)} %collective-permute-done.8.refs_9_), channel_id=1, source_target_pairs={{0,14},{2,0},{4,2},{6,4},{8,6},{10,8},{12,10},{14,12},{1,15},{3,1}... | collective-permute-start | bytes 786440 | tf_op jit(solution)/shard_map/ppermute | solution.py:287
  31.1 8.1 %collective-permute-start.2 = (bf16[80,1024]{1,0:T(8,128)(2,1)}, bf16[80,1024]{1,0:T(8,128)(2,1)S(1)}, u32[]{:S(2)}, u32[]{:S(2)}) collective-permute-start(bf16[80,1024]{1,0:T(8,128)(2,1)} %get-tuple-element.21), channel_id=1, source_target_pairs={{0,32},{16,48},{32,0},{48,16},{1,33},{17,49},{33,1},{49,17},{2,34}... | collective-permute-start | bytes 491528 | tf_op jit(solution)/shard_map/ppermute | solution.py:341
  32.5 9.1 %collective-permute-start.13 = (bf16[2,128,512]{2,1,0:T(8,128)(2,1)S(1)}, bf16[2,128,512]{2,1,0:T(8,128)(2,1)S(1)}, u32[]{:S(2)}, u32[]{:S(2)}) collective-permute-start(bf16[2,128,512]{2,1,0:T(8,128)(2,1)S(1)} %collective-permute-done.12.refs_15_), channel_id=1, source_target_pairs={{0,2},{2,4},{4,6},{6,8},{8,10},{10,12},{12,14},{14,0},{1,3},{3,5},... | collective-permute-start | bytes 786440 | tf_op jit(solution)/shard_map/ppermute | solution.py:288
  35.0 8.5 %collective-permute-start.10 = (bf16[2,128,512]{2,1,0:T(8,128)(2,1)S(1)}, bf16[2,128,512]{2,1,0:T(8,128)(2,1)S(1)}, u32[]{:S(2)}, u32[]{:S(2)}) collective-permute-start(bf16[2,128,512]{2,1,0:T(8,128)(2,1)S(1)} %collective-permute-done.9.refs_10_), channel_id=1, source_target_pairs={{0,14},{2,0},{4,2},{6,4},{8,6},{10,8},{12,10},{14,12},{1,15},{3,1}... | collective-permute-start | bytes 786440 | tf_op jit(solution)/shard_map/ppermute | solution.py:287
  39.2 8.3 %collective-permute-start.7 = (bf16[80,1024]{1,0:T(8,128)(2,1)S(1)}, bf16[80,1024]{1,0:T(8,128)(2,1)S(1)}, u32[]{:S(2)}, u32[]{:S(2)}) collective-permute-start(bf16[80,1024]{1,0:T(8,128)(2,1)S(1)} %collective-permute-done.2.refs_2_), channel_id=1, source_target_pairs={{0,64},{64,0},{1,65},{65,1},{2,66},{66,2},{3,67},{67,3},{4,68},{68... | collective-permute-start | bytes 491528 | tf_op jit(solution)/shard_map/ppermute | solution.py:345
  39.5 14.2 %collective-permute-start.4 = (bf16[160,1024]{1,0:T(8,128)(2,1)S(1)}, bf16[160,1024]{1,0:T(8,128)(2,1)S(1)}, u32[]{:S(2)}, u32[]{:S(2)}) collective-permute-start(bf16[160,1024]{1,0:T(8,128)(2,1)S(1)} %get-tuple-element.23), channel_id=1, source_target_pairs={{0,16},{16,32},{32,48},{48,0},{1,17},{17,33},{33,49},{49,1},{2,18}... | collective-permute-start | bytes 983048 | tf_op jit(solution)/shard_map/ppermute | solution.py:344
  40.8 12.9 %collective-permute-start.5 = (bf16[160,1024]{1,0:T(8,128)(2,1)S(1)}, bf16[160,1024]{1,0:T(8,128)(2,1)S(1)}, u32[]{:S(2)}, u32[]{:S(2)}) collective-permute-start(bf16[160,1024]{1,0:T(8,128)(2,1)S(1)} %get-tuple-element.24), channel_id=1, source_target_pairs={{0,48},{16,0},{32,16},{48,32},{1,49},{17,1},{33,17},{49,33},{2,50}... | collective-permute-start | bytes 983048 | tf_op jit(solution)/shard_map/ppermute | solution.py:344
  41.6 12.1 %collective-permute-start.14 = (bf16[2,128,512]{2,1,0:T(8,128)(2,1)S(1)}, bf16[2,128,512]{2,1,0:T(8,128)(2,1)S(1)}, u32[]{:S(2)}, u32[]{:S(2)}) collective-permute-start(bf16[2,128,512]{2,1,0:T(8,128)(2,1)S(1)} %collective-permute-done.13.refs_14_), channel_id=1, source_target_pairs={{0,2},{2,4},{4,6},{6,8},{8,10},{10,12},{12,14},{14,0},{1,3},{3,5},... | collective-permute-start | bytes 786440 | tf_op jit(solution)/shard_map/ppermute | solution.py:288
  43.5 10.2 %collective-permute-start.11 = (bf16[2,128,512]{2,1,0:T(8,128)(2,1)S(1)}, bf16[2,128,512]{2,1,0:T(8,128)(2,1)S(1)}, u32[]{:S(2)}, u32[]{:S(2)}) collective-permute-start(bf16[2,128,512]{2,1,0:T(8,128)(2,1)S(1)} %collective-permute-done.10.refs_11_), channel_id=1, source_target_pairs={{0,14},{2,0},{4,2},{6,4},{8,6},{10,8},{12,10},{14,12},{1,15},{3,1}... | collective-permute-start | bytes 786440 | tf_op jit(solution)/shard_map/ppermute | solution.py:289
  47.5 6.2 %collective-permute-start.6 = (bf16[128,1024]{1,0:T(8,128)(2,1)S(1)}, bf16[128,1024]{1,0:T(8,128)(2,1)S(1)}, u32[]{:S(2)}, u32[]{:S(2)}) collective-permute-start(bf16[128,1024]{1,0:T(8,128)(2,1)S(1)} %get-tuple-element.25), channel_id=1, source_target_pairs={{0,64},{64,0},{1,65},{65,1},{2,66},{66,2},{3,67},{67,3},{4,68},{68... | collective-permute-start | bytes 786440 | tf_op jit(solution)/shard_map/ppermute | solution.py:345
  53.7 1.1 %copy-start = (bf16[400,1024]{1,0:T(8,128)(2,1)S(1)}, bf16[400,1024]{1,0:T(8,128)(2,1)}, u32[]{:S(2)}) copy-start(bf16[400,1024]{1,0:T(8,128)(2,1)} %get-tuple-element.20.refs_0_) | copy-start | bytes 2457604
  54.9 0.9 copy-start.3
  55.8 1.0 %copy-start.6 = (f32[1024,128]{1,0:T(8,128)S(1)}, f32[1024,128]{1,0:T(8,128)}, u32[]{:S(2)}) copy-start(f32[1024,128]{1,0:T(8,128)} %get-tuple-element.16.right_ref) | copy-start | bytes 1572868

commit v7 on v6

--- a/solution.py
+++ b/solution.py
@@ -20,6 +20,22 @@
 
 def dot32(a, b, dims, precision=None):
     return lax.dot_general(a, b, (dims, ((), ())), preferred_element_type=jnp.float32, precision=precision)
+
+
+def hold_kernel(*refs):
+    pass
+
+
+def hold(arrays):
+    return pl.pallas_call(
+        hold_kernel,
+        out_shape=[jax.ShapeDtypeStruct(array.shape, array.dtype) for array in arrays],
+        in_specs=[HBM] * len(arrays),
+        out_specs=[HBM] * len(arrays),
+        input_output_aliases={index: index for index in range(len(arrays))},
+        compiler_params=pltpu.CompilerParams(vmem_limit_bytes=62 * MIB),
+        name="hold",
+    )(*arrays)
 
 
 def pair_kernel(own_ref, other_ref, *refs):
@@ -179,12 +195,12 @@
     )(before, after)
 
 
-def tail_kernel(weight_hbm, gate_out_ref, up_out_ref, down_out_hbm, right_ref, *refs):
-    messages, far_halves, swaps, blocks = refs[:NX], refs[NX : NX + 2], refs[NX + 2 : NX + 4], refs[NX + 4 : NX + 4 + NZ]
-    out_ref, weights, projs, grads, far_ref, total, sems = refs[NX + 4 + NZ :]
-    factors = [messages[0], messages[1], far_ref, messages[3]]
+def tail_kernel(weight_hbm, gate_out_hbm, up_out_hbm, down_out_hbm, right_hbm, *refs):
+    messages, far_halves, swaps = refs[:NX], refs[NX : NX + 2], refs[NX + 2 : NX + 4]
+    blocks, far_block = refs[NX + 4 : NX + 3 + NZ], refs[NX + 3 + NZ : NX + 5 + NZ]
+    out_ref, weights, projs, folds, grads, factors, right_ref, total, sems = refs[NX + 5 + NZ :]
     hidden, model_width = weight_hbm.shape
-    rank = gate_out_ref.shape[0]
+    rank = gate_out_hbm.shape[0]
     width = model_width // NX
     examples, both, seq_dev = blocks[0].shape
     piece = both // NY
@@ -203,34 +219,45 @@
         theirs = pl.ds(pl.multiple_of(step * hidden + (1 - core) * half, half), half)
         swapped = swaps[1].at[pl.ds(0, half)] if step == 2 else swaps[0].at[pl.ds(step // 2 * half, half)]
         pairs.append((swapped, weights.at[theirs]))
-    for index, part in enumerate(far_halves):
-        pairs.append((part, far_ref.at[pl.ds(index * part.shape[0], part.shape[0])]))
-    for step, block in enumerate(blocks):
+    count = examples // 2
+    slots = [(slice(0, examples), step, blocks[step if step < NZ // 2 else step - 1]) for step in range(NZ) if step != NZ // 2]
+    slots += [(slice(0, count), NZ // 2, far_block[0]), (slice(count, examples), NZ // 2, far_block[1])]
+    for span, step, block in slots:
         base = lax.rem(z_at + step, NZ) * both
         for kind, y_of in enumerate((y_at, 1 - y_at)):
             rows = pl.ds(pl.multiple_of(base + y_of * piece, piece), piece)
-            pairs.append((block.at[:, pl.ds(kind * piece, piece)], grads.at[:, rows]))
+            pairs.append((block.at[:, pl.ds(kind * piece, piece)], grads.at[span, rows]))
+    early = len(pairs)
+    pairs += [(gate_out_hbm, projs.at[pl.ds(0, rank), pl.ds(0, hidden)])]
+    pairs += [(up_out_hbm, projs.at[pl.ds(rank, rank), pl.ds(0, hidden)])]
+    for step, message in enumerate(messages):
+        if step > 0:
+            pairs.append((message.at[pl.ds(message.shape[0] - FOLD, FOLD)], folds.at[step - 1]))
+        if step != 2:
+            pairs.append((message.at[pl.ds(0, top)], factors.at[step]))
+    for index, part in enumerate(far_halves):
+        pairs.append((part, factors.at[2, pl.ds(index * part.shape[0], part.shape[0])]))
+    pairs.append((right_hbm, right_ref))
     copies = [pltpu.make_async_copy(a, b, sems.at[k]) for k, (a, b) in enumerate(pairs)]
     for copy in copies:
         copy.start()
-    projs[:rank, :hidden] = gate_out_ref[...]
-    projs[rank:, :hidden] = up_out_ref[...]
+    for copy in copies[:early]:
+        copy.wait()
+    for example in range(examples):
+        total[example] = jnp.dot(weights[...], grads[example], preferred_element_type=jnp.float32)
+    for copy in copies[early:]:
+        copy.wait()
     for step in range(1, NX):
         columns = slice(step * hidden, (step + 1) * hidden)
         for block in range(2 * rank // FOLD):
-            folded = messages[step][-FOLD:, block * hidden : (block + 1) * hidden]
-            projs[block * FOLD : (block + 1) * FOLD, columns] = folded
-    for copy in copies:
-        copy.wait()
-    for example in range(examples):
-        total[example] = jnp.dot(weights[...], grads[example], preferred_element_type=jnp.float32)
+            projs[block * FOLD : (block + 1) * FOLD, columns] = folds[step - 1, :, block * hidden : (block + 1) * hidden]
     for example in range(examples):
         columns = slice(example * seq_dev, (example + 1) * seq_dev)
         left = []
         for kind in range(2):
             products = []
             for step in range(NX):
-                factor = factors[step][kind * hidden : (kind + 1) * hidden, columns].astype(jnp.float32)
+                factor = factors[step, kind * hidden : (kind + 1) * hidden, columns].astype(jnp.float32)
                 products.append(total[example, step * hidden : (step + 1) * hidden] * factor)
             product = jnp.concatenate(products, axis=0)
             high = product.astype(jnp.bfloat16)
@@ -246,9 +273,9 @@
             precision=lax.Precision.HIGHEST,
             preferred_element_type=jnp.float32,
         )
-        right_down = factors[0][2 * hidden : top, columns].astype(jnp.float32)
+        right_down = factors[0, 2 * hidden : top, columns].astype(jnp.float32)
         for step in range(1, NX):
-            right_down = right_down + factors[step][2 * hidden : top, columns].astype(jnp.float32)
+            right_down = right_down + factors[step, 2 * hidden : top, columns].astype(jnp.float32)
         out_ref[3 * example] = sides[:rank, :rank]
         out_ref[3 * example + 1] = sides[rank:, rank:]
         out_ref[3 * example + 2] = dot32(
@@ -256,29 +283,48 @@
         )
 
 
-def tail_stage(down_weight, gate_out, up_out, down_out, right, messages, far, swaps, blocks):
+def tail_stage(down_weight, gate_out, up_out, down_out, right, messages, far, swaps, blocks, far_block):
     hidden, model_width = down_weight.shape
     rank = gate_out.shape[0]
     examples, _, seq_dev = blocks[0].shape
     width = model_width // NX
-    operands = [down_weight, gate_out, up_out, down_out, right, *messages, *far, *swaps, *blocks]
+    operands = [down_weight, gate_out, up_out, down_out, right, *messages, *far, *swaps, *blocks, *far_block]
     return pl.pallas_call(
         tail_kernel,
         out_shape=jax.ShapeDtypeStruct((examples * 3, rank, rank), jnp.float32),
-        in_specs=[HBM, VMEM, VMEM, HBM, VMEM] + [VMEM] * NX + [HBM] * (4 + NZ),
+        in_specs=[HBM] * len(operands),
         out_specs=VMEM,
         scratch_shapes=[
             pltpu.VMEM((NX * hidden + rank, width), jnp.bfloat16),
             pltpu.VMEM((2 * rank, NX * hidden), jnp.bfloat16),
+            pltpu.VMEM((NX - 1, FOLD, examples * seq_dev), jnp.bfloat16),
             pltpu.VMEM((examples, width, seq_dev), jnp.bfloat16),
-            pltpu.VMEM((2 * far[0].shape[0], examples * seq_dev), jnp.bfloat16),
+            pltpu.VMEM((NX, 2 * hidden + rank, examples * seq_dev), jnp.bfloat16),
+            pltpu.VMEM(right.shape, jnp.float32),
             pltpu.VMEM((examples, NX * hidden + rank, seq_dev), jnp.float32),
-            pltpu.SemaphoreType.DMA((2 + 2 * NX + NZ * NY,)),
+            pltpu.SemaphoreType.DMA((2 + 2 * (NX - 1) + (NZ + 1) * NY + 2 + 2 * NX + 2,)),
         ],
-        compiler_params=pltpu.CompilerParams(vmem_limit_bytes=16 * MIB),
+        compiler_params=pltpu.CompilerParams(vmem_limit_bytes=62 * MIB),
         cost_estimate=pl.CostEstimate(flops=4 * 10**9, bytes_accessed=8 * MIB, transcendentals=0),
         name="tail_stage",
     )(*operands)
+
+
+def cut_kernel(up_ref, down_ref, first_ref, second_ref):
+    first_ref[...] = up_ref[: first_ref.shape[0]]
+    second_ref[...] = down_ref[first_ref.shape[0] :]
+
+
+def cut(up, down):
+    shape = jax.ShapeDtypeStruct((up.shape[0] // 2,) + up.shape[1:], up.dtype)
+    return pl.pallas_call(
+        cut_kernel,
+        out_shape=[shape] * 2,
+        in_specs=[VMEM] * 2,
+        out_specs=[VMEM] * 2,
+        compiler_params=pltpu.CompilerParams(vmem_limit_bytes=4 * MIB),
+        name="cut",
+    )(up, down)
 
 
 def ring_z(own):
@@ -286,7 +332,9 @@
     for _ in range(NZ // 2 - 1):
         up.append(lax.ppermute(up[-1], "z", shifted(NZ, -1)))
         down.append(lax.ppermute(down[-1], "z", shifted(NZ, 1)))
-    return up + [lax.ppermute(up[-1], "z", shifted(NZ, -1))] + down[:0:-1]
+    first, second = cut(up[-1], down[-1])
+    far = [lax.ppermute(first, "z", shifted(NZ, -1)), lax.ppermute(second, "z", shifted(NZ, 1))]
+    return up + down[:0:-1], far
 
 
 def sum_everywhere(partial):
@@ -343,8 +391,8 @@
     first, second, swap = halves(messages[1], messages[3], hidden + rank // 2, hidden // 2)
     far = [lax.ppermute(first, "x", shifted(NX, 1)), lax.ppermute(second, "x", shifted(NX, -1))]
     swaps = [lax.ppermute(piece, "sc", shifted(SEQ_PARTS[1], 1)) for piece in (swap, messages[2])]
-    blocks = ring_z(pair)
-    products = tail_stage(down_weight, gate_out, up_out, proj_down_out.T, right, messages, far, swaps, blocks)
+    blocks, far_block = ring_z(pair)
+    products = tail_stage(down_weight, gate_out, up_out, proj_down_out.T, right, messages, far, swaps, blocks, far_block)
     total = sum_everywhere(products.reshape(examples * 3, -1))
     return total.reshape(examples, 3, -1)
 

time: 101 us -> 99.1 us (0.981)
  waiting for transfers between devices: 14.4 us -> 18.5 us
  starting transfers between devices: 27.8 us -> 24.5 us
  blocking collectives: 36.9 us -> 34.1 us
    ppermute x3, waiting for transfers between devices: 6.15 us -> 0.11 us  [ring_z(): down.append(lax.ppermute(down[-1], 'z', shifted(NZ, 1)))]
    ppermute x1 -> x2, waiting for transfers between devices: 0.01 us -> 4.77 us  [the longest x1 3.37 us: ring_z(): lax.ppermute(first, 'z', shifted(NZ, -1))]
    ppermute x3, waiting for transfers between devices: 0.74 us -> 4.66 us  [shards(): lax.ppermute(piece, 'x', shifted(NX, step))]
    all_to_all x1, blocking collectives: 16.7 us -> 13.4 us  [sum_everywhere(): pieces = lax.all_to_all(pieces, ('sy', 'sc', 'z'), 0, 0, tiled=True)]
    ppermute x1 -> x2, starting transfers between devices: 4.02 us -> 2.03 us  [the longest x1 1.98 us: ring_z(): lax.ppermute(second, 'z', shifted(NZ, 1))]
    ppermute x3, starting transfers between devices: 1.92 us -> 0.01 us  [ring_z(): down.append(lax.ppermute(down[-1], 'z', shifted(NZ, 1)))]
    ppermute x3, waiting for transfers between devices: 7.52 us -> 8.91 us  [ring_z(): up.append(lax.ppermute(up[-1], 'z', shifted(NZ, -1)))]
    unnamed x17 -> x33, local copies, waits for them, and re-layouts: 3.79 us -> 2.88 us
  transfers between devices with their start and end apart: 15 -> 16, of which waited for: 5 -> 6; matrix products, arithmetic and copies ran while one was open for 0% -> 0% of each run, Pallas kernels for 9% -> 9%
where the time goes in v7:
time: 99.1 us; the launch traced here: 98.9 us
  blocking collectives  34.1 us (34%)
  starting transfers between devices  24.5 us (25%)
  waiting for transfers between devices  18.5 us (19%)
  Pallas kernels  17 us (17%)
  local copies, waits for them, and re-layouts  4.63 us (5%)
    all_to_all x1, blocking collectives, sum_everywhere(): blocks = lax.all_to_all(spread, ('x', 'z', 'yh'), 0, 0, tiled=True)  20.7 us
    all_to_all x1, blocking collectives, sum_everywhere(): pieces = lax.all_to_all(pieces, ('sy', 'sc', 'z'), 0, 0, tiled=True)  13.4 us
    ppermute x3, starting transfers between devices, ring_z(): up.append(lax.ppermute(up[-1], 'z', shifted(NZ, -1)))  13.1 us
    ppermute x3, waiting for transfers between devices, ring_z(): up.append(lax.ppermute(up[-1], 'z', shifted(NZ, -1)))  8.91 us
    pallas_call x1, Pallas kernels, token_stage(): pl.pallas_call(lambda *refs: token_kernel(chunk, scale, *refs), out_shape...  8.89 us
    pallas_call x1, Pallas kernels, tail_stage(): pl.pallas_call(tail_kernel, out_shape=jax.ShapeDtypeStruct((examples * 3,...  6.33 us
    ppermute x3, waiting for transfers between devices, shards(): lax.ppermute(piece, 'x', shifted(NX, step))  4.66 us
    ppermute x3, starting transfers between devices, shards(): lax.ppermute(piece, 'x', shifted(NX, step))  3.44 us
  transfers between devices with their start and end apart: 16, of which 6 were waited for; matrix products, arithmetic and copies ran while one was open for 0% of the time, Pallas kernels for 9%

profile of v7, /device:TPU:6, one launch (start us, length us, event | category | flops | bytes accessed | tf_op | source)
XLA Modules:
  0.0 98.9 jit_solution(10802418253155032455)
XLA Ops:
  0.0 3.2 %collective-permute-start = (bf16[2,64,512]{2,1,0:T(8,128)(2,1)}, bf16[2,64,512]{2,1,0:T(8,128)(2,1)S(1)}, u32[]{:S(2)}, u32[]{:S(2)}) collective-permute-start(bf16[2,64,512]{2,1,0:T(8,128)(2,1)} %bitcast.17), channel_id=1, source_target_pairs={{0,1},{1,0},{2,3},{3,2},{4,5},{5,4},{6,7},{7,6},{8,9},{9,8},{10,11... | collective-permute-start | bytes 393224 | tf_op jit(solution)/shard_map/ppermute | solution.py:372
  3.2 8.9 %token_stage.1 = (bf16[400,1024]{1,0:T(8,128)(2,1)}, bf16[80,1024]{1,0:T(8,128)(2,1)}, bf16[400,1024]{1,0:T(8,128)(2,1)}, f32[1024,128]{1,0:T(8,128)}) custom-call(s32[2]{0:T(128)} %refs_0_.1, bf16[1024,4096]{1,0:T(8,128)(2,1)} %bitcast.20, bf16[4096,128]{1,0:T(8,128)(2,1)} %refs_2_.1, bf16[4096,128]{1,0:T(8,128)(2,1)} %refs_3_.1, ...), custom_call_target="tpu_custom_call" | custom-call | flops 4294967296 | bytes 16777216 | tf_op jit(solution)/shard_map/token_stage/pallas_call | solution.py:149
  12.1 0.0 collective-permute-done.other_ref
  12.1 0.0 copy-start.4
  12.1 0.6 copy-done.4
  12.8 1.7 %pair_up.1 = (bf16[400,1024]{1,0:T(8,128)(2,1)}, bf16[80,1024]{1,0:T(8,128)(2,1)}, bf16[400,1024]{1,0:T(8,128)(2,1)}, bf16[2,128,512]{2,1,0:T(8,128)(2,1)}) custom-call(bf16[2,64,512]{2,1,0:T(8,128)(2,1)} %bitcast.18, bf16[2,64,512]{2,1,0:T(8,128)(2,1)} %copy-done.4, ...), custom_call_target="tpu_custom_call", output_to_operand_aliasing={{0}: (2, {}), {1}: (3, {}), {2}: (4, {})} | custom-call | tf_op jit(solution)/shard_map/pair_up/pallas_call | solution.py:50
  14.4 0.5 collective-permute-start.1
  14.9 1.6 %collective-permute-start.3 = (bf16[400,1024]{1,0:T(8,128)(2,1)}, bf16[400,1024]{1,0:T(8,128)(2,1)S(1)}, u32[]{:S(2)}, u32[]{:S(2)}) collective-permute-start(bf16[400,1024]{1,0:T(8,128)(2,1)} %get-tuple-element.24), channel_id=1, source_target_pairs={{0,48},{16,0},{32,16},{48,32},{1,49},{17,1},{33,17},{49,33},{2,50}... | collective-permute-start | bytes 2457608 | tf_op jit(solution)/shard_map/ppermute | solution.py:389
  16.4 5.9 %collective-permute-start.8 = (bf16[2,128,512]{2,1,0:T(8,128)(2,1)}, bf16[2,128,512]{2,1,0:T(8,128)(2,1)S(1)}, u32[]{:S(2)}, u32[]{:S(2)}) collective-permute-start(bf16[2,128,512]{2,1,0:T(8,128)(2,1)} %get-tuple-element.28.refs_8_), channel_id=1, source_target_pairs={{0,14},{2,0},{4,2},{6,4},{8,6},{10,8},{12,10},{14,12},{1,15},{3,1}... | collective-permute-start | bytes 786440 | tf_op jit(solution)/shard_map/ppermute | solution.py:333
  22.3 0.0 collective-permute-start.11
  22.3 5.0 %collective-permute-done.8.refs_9_ = bf16[2,128,512]{2,1,0:T(8,128)(2,1)S(1)} collective-permute-done((bf16[2,128,512]{2,1,0:T(8,128)(2,1)}, bf16[2,128,512]{2,1,0:T(8,128)(2,1)S(1)}, u32[]{:S(2)}, u32[]{:S(2)}) %collective-permute-start.8) | collective-permute-done | bytes 262176 | tf_op jit(solution)/shard_map/ppermute | solution.py:333
  27.3 0.0 copy-start.7
  27.3 3.6 %collective-permute-start.9 = (bf16[2,128,512]{2,1,0:T(8,128)(2,1)S(1)}, bf16[2,128,512]{2,1,0:T(8,128)(2,1)S(1)}, u32[]{:S(2)}, u32[]{:S(2)}) collective-permute-start(bf16[2,128,512]{2,1,0:T(8,128)(2,1)S(1)} %collective-permute-done.8.refs_9_), channel_id=1, source_target_pairs={{0,14},{2,0},{4,2},{6,4},{8,6},{10,8},{12,10},{14,12},{1,15},{3,1}... | collective-permute-start | bytes 786440 | tf_op jit(solution)/shard_map/ppermute | solution.py:333
  30.9 0.0 collective-permute-done.11.refs_14_
  30.9 0.0 collective-permute-start.12
  30.9 3.9 %collective-permute-done.9.refs_10_ = bf16[2,128,512]{2,1,0:T(8,128)(2,1)S(1)} collective-permute-done((bf16[2,128,512]{2,1,0:T(8,128)(2,1)S(1)}, bf16[2,128,512]{2,1,0:T(8,128)(2,1)S(1)}, u32[]{:S(2)}, u32[]{:S(2)}) %collective-permute-start.9) | collective-permute-done | bytes 262176 | tf_op jit(solution)/shard_map/ppermute | solution.py:333
  34.8 3.7 %collective-permute-start.10 = (bf16[2,128,512]{2,1,0:T(8,128)(2,1)S(1)}, bf16[2,128,512]{2,1,0:T(8,128)(2,1)S(1)}, u32[]{:S(2)}, u32[]{:S(2)}) collective-permute-start(bf16[2,128,512]{2,1,0:T(8,128)(2,1)S(1)} %collective-permute-done.9.refs_10_), channel_id=1, source_target_pairs={{0,14},{2,0},{4,2},{6,4},{8,6},{10,8},{12,10},{14,12},{1,15},{3,1}... | collective-permute-start | bytes 786440 | tf_op jit(solution)/shard_map/ppermute | solution.py:333
  38.5 1.4 %collective-permute-start.2 = (bf16[80,1024]{1,0:T(8,128)(2,1)}, bf16[80,1024]{1,0:T(8,128)(2,1)S(1)}, u32[]{:S(2)}, u32[]{:S(2)}) collective-permute-start(bf16[80,1024]{1,0:T(8,128)(2,1)} %get-tuple-element.23), channel_id=1, source_target_pairs={{0,32},{16,48},{32,0},{48,16},{1,33},{17,49},{33,1},{49,17},{2,34}... | collective-permute-start | bytes 491528 | tf_op jit(solution)/shard_map/ppermute | solution.py:389
  39.9 0.0 collective-permute-done.12.refs_13_
  39.9 0.0 collective-permute-start.13
  39.9 0.0 collective-permute-done.1.before_ref.refs_1_
  39.9 0.0 copy-done.7
  40.0 0.0 copy-done.8
  40.0 0.0 copy-start
  40.0 0.0 collective-permute-done.3.after_ref.refs_3_
  40.0 0.0 copy-start.1
  40.0 0.1 halves.1
  40.1 2.2 %collective-permute-start.4 = (bf16[160,1024]{1,0:T(8,128)(2,1)S(1)}, bf16[160,1024]{1,0:T(8,128)(2,1)S(1)}, u32[]{:S(2)}, u32[]{:S(2)}) collective-permute-start(bf16[160,1024]{1,0:T(8,128)(2,1)S(1)} %get-tuple-element.25), channel_id=1, source_target_pairs={{0,16},{16,32},{32,48},{48,0},{1,17},{17,33},{33,49},{49,1},{2,18}... | collective-permute-start | bytes 983048 | tf_op jit(solution)/shard_map/ppermute | solution.py:392
  42.2 0.0 collective-permute-start.5
  42.2 4.7 %collective-permute-done.2.refs_2_ = bf16[80,1024]{1,0:T(8,128)(2,1)S(1)} collective-permute-done((bf16[80,1024]{1,0:T(8,128)(2,1)}, bf16[80,1024]{1,0:T(8,128)(2,1)S(1)}, u32[]{:S(2)}, u32[]{:S(2)}) %collective-permute-start.2) | collective-permute-done | bytes 163872 | tf_op jit(solution)/shard_map/ppermute | solution.py:389
  46.9 0.0 collective-permute-start.7
  46.9 0.0 collective-permute-done.10.up_ref.refs_11_
  46.9 0.0 copy-start.2
  46.9 0.5 collective-permute-start.6
  47.4 0.1 collective-permute-done.13.down_ref.refs_12_
  47.5 0.0 copy-start.3
  47.5 0.7 copy-done.3
  48.2 0.0 collective-permute-start.14
  48.3 0.0 collective-permute-done.7.refs_7_
  48.3 2.0 %collective-permute-start.15 = (bf16[1,128,512]{2,1,0:T(8,128)(2,1)S(1)}, bf16[1,128,512]{2,1,0:T(8,128)(2,1)S(1)}, u32[]{:S(2)}, u32[]{:S(2)}) collective-permute-start(bf16[1,128,512]{2,1,0:T(8,128)(2,1)S(1)} %get-tuple-element.30), channel_id=1, source_target_pairs={{0,2},{2,4},{4,6},{6,8},{8,10},{10,12},{12,14},{14,0},{1,3},{3,5},... | collective-permute-start | bytes 393224 | tf_op jit(solution)/shard_map/ppermute | solution.py:336
  50.3 3.4 %collective-permute-done.14.refs_15_ = bf16[1,128,512]{2,1,0:T(8,128)(2,1)S(1)} collective-permute-done((bf16[1,128,512]{2,1,0:T(8,128)(2,1)S(1)}, bf16[1,128,512]{2,1,0:T(8,128)(2,1)S(1)}, u32[]{:S(2)}, u32[]{:S(2)}) %collective-permute-start.14) | collective-permute-done | bytes 131104 | tf_op jit(solution)/shard_map/ppermute | solution.py:336
  53.6 1.4 %collective-permute-done.15.refs_16_ = bf16[1,128,512]{2,1,0:T(8,128)(2,1)S(1)} collective-permute-done((bf16[1,128,512]{2,1,0:T(8,128)(2,1)S(1)}, bf16[1,128,512]{2,1,0:T(8,128)(2,1)S(1)}, u32[]{:S(2)}, u32[]{:S(2)}) %collective-permute-start.15) | collective-permute-done | bytes 131104 | tf_op jit(solution)/shard_map/ppermute | solution.py:336
  55.0 0.0 collective-permute-done.6.refs_6_
  55.1 0.0 collective-permute-done.4.refs_4_
  55.1 0.0 copy-start.5
  55.1 0.0 collective-permute-done.5.refs_5_
  55.1 0.8 copy-done.5
  55.9 0.0 copy-done.9
  55.9 0.0 copy-done.10
  55.9 0.0 copy-done.12
  55.9 0.0 copy-done.13
  55.9 0.0 copy-done.15
  55.9 0.1 copy-done.11
  56.0 0.6 copy-done.6
  56.6 0.0 copy-done
  56.6 0.0 copy-done.1
  56.6 0.0 copy-done.2
  56.6 0.0 copy-done.14
  56.6 6.3 %tail_stage.1 = f32[6,64,64]{2,1,0:T(8,128)} custom-call(bf16[128,4096]{1,0:T(8,128)(2,1)} %weight_hbm.1, bf16[64,128]{1,0:T(8,128)(2,1)} %bitcast.26, bf16[64,128]{1,0:T(8,128)(2,1)} %bitcast.28, bf16[64,4096]{1,0:T(8,128)(2,1)} %bitcast.23, f32[1024,128]{1,0:T(8,128)} %get-tuple-element.18.right_hbm, bf16[400,1024]{1,0:T(8,128)(2,1)} %get-tuple-element.22.refs_0_, ...), custom_call_target="tpu_custom_call" | custom-call | flops 4000000000 | bytes 8388608 | tf_op jit(solution)/shard_map/tail_stage/pallas_call | solution.py:292
  63.0 1.0 %reshape_reshape.6 = f32[6,32,128]{2,1,0:T(8,128)S(1)} reshape(f32[6,64,64]{2,1,0:T(8,128)} %tail_stage.1) | data formatting | bytes 196608 | tf_op jit(solution)/shard_map/reshape;reshape | solution.py:344
  64.0 0.1 copy.33
  64.0 13.4 %all_to_all.10 = f32[32,6,128]{2,1,0:T(8,128)S(1)} all-to-all(f32[32,6,128]{2,1,0:T(8,128)S(1)} %bitcast.16), channel_id=1, replica_groups=mesh['sy'=2,'sc'=2,'x'=4,'z'=8,'yh'=2] {'sy','sc','z'}, dimensions={0} | all-to-all | bytes 196608 | tf_op jit(solution)/shard_map/all_to_all | solution.py:345
  77.6 20.7 %all_to_all.11 = f32[64,6,128]{2,1,0:T(8,128)S(1)} all-to-all(f32[64,6,128]{2,1,0:T(8,128)S(1)} %broadcast_in_dim.2), channel_id=1, replica_groups=mesh['sy'=2,'sc'=2,'x'=4,'z'=8,'yh'=2] {'x','z','yh'}, dimensions={0} | all-to-all | bytes 393216 | tf_op jit(solution)/shard_map/all_to_all | solution.py:348
  98.3 0.6 copy.27
  (15 shorter events, 0.1 us)
Async XLA Ops:
  0.0 12.1 %collective-permute-start = (bf16[2,64,512]{2,1,0:T(8,128)(2,1)}, bf16[2,64,512]{2,1,0:T(8,128)(2,1)S(1)}, u32[]{:S(2)}, u32[]{:S(2)}) collective-permute-start(bf16[2,64,512]{2,1,0:T(8,128)(2,1)} %bitcast.17), channel_id=1, source_target_pairs={{0,1},{1,0},{2,3},{3,2},{4,5},{5,4},{6,7},{7,6},{8,9},{9,8},{10,11... | collective-permute-start | bytes 393224 | tf_op jit(solution)/shard_map/ppermute | solution.py:372
  12.1 0.6 copy-start.4
  14.4 25.5 %collective-permute-start.1 = (bf16[400,1024]{1,0:T(8,128)(2,1)}, bf16[400,1024]{1,0:T(8,128)(2,1)S(1)}, u32[]{:S(2)}, u32[]{:S(2)}) collective-permute-start(bf16[400,1024]{1,0:T(8,128)(2,1)} %get-tuple-element.22.refs_0_), channel_id=1, source_target_pairs={{0,16},{16,32},{32,48},{48,0},{1,17},{17,33},{33,49},{49,1},{2,18}... | collective-permute-start | bytes 2457608 | tf_op jit(solution)/shard_map/ppermute | solution.py:389
  14.9 25.1 %collective-permute-start.3 = (bf16[400,1024]{1,0:T(8,128)(2,1)}, bf16[400,1024]{1,0:T(8,128)(2,1)S(1)}, u32[]{:S(2)}, u32[]{:S(2)}) collective-permute-start(bf16[400,1024]{1,0:T(8,128)(2,1)} %get-tuple-element.24), channel_id=1, source_target_pairs={{0,48},{16,0},{32,16},{48,32},{1,49},{17,1},{33,17},{49,33},{2,50}... | collective-permute-start | bytes 2457608 | tf_op jit(solution)/shard_map/ppermute | solution.py:389
  16.4 10.9 %collective-permute-start.8 = (bf16[2,128,512]{2,1,0:T(8,128)(2,1)}, bf16[2,128,512]{2,1,0:T(8,128)(2,1)S(1)}, u32[]{:S(2)}, u32[]{:S(2)}) collective-permute-start(bf16[2,128,512]{2,1,0:T(8,128)(2,1)} %get-tuple-element.28.refs_8_), channel_id=1, source_target_pairs={{0,14},{2,0},{4,2},{6,4},{8,6},{10,8},{12,10},{14,12},{1,15},{3,1}... | collective-permute-start | bytes 786440 | tf_op jit(solution)/shard_map/ppermute | solution.py:333
  22.3 8.6 %collective-permute-start.11 = (bf16[2,128,512]{2,1,0:T(8,128)(2,1)}, bf16[2,128,512]{2,1,0:T(8,128)(2,1)S(1)}, u32[]{:S(2)}, u32[]{:S(2)}) collective-permute-start(bf16[2,128,512]{2,1,0:T(8,128)(2,1)} %get-tuple-element.28.refs_8_), channel_id=1, source_target_pairs={{0,2},{2,4},{4,6},{6,8},{8,10},{10,12},{12,14},{14,0},{1,3},{3,5},... | collective-permute-start | bytes 786440 | tf_op jit(solution)/shard_map/ppermute | solution.py:334
  27.3 12.6 %copy-start.7 = (bf16[2,128,512]{2,1,0:T(8,128)(2,1)}, bf16[2,128,512]{2,1,0:T(8,128)(2,1)S(1)}, u32[]{:S(2)}) copy-start(bf16[2,128,512]{2,1,0:T(8,128)(2,1)S(1)} %collective-permute-done.8.refs_9_) | copy-start | bytes 786436
  27.3 7.5 %collective-permute-start.9 = (bf16[2,128,512]{2,1,0:T(8,128)(2,1)S(1)}, bf16[2,128,512]{2,1,0:T(8,128)(2,1)S(1)}, u32[]{:S(2)}, u32[]{:S(2)}) collective-permute-start(bf16[2,128,512]{2,1,0:T(8,128)(2,1)S(1)} %collective-permute-done.8.refs_9_), channel_id=1, source_target_pairs={{0,14},{2,0},{4,2},{6,4},{8,6},{10,8},{12,10},{14,12},{1,15},{3,1}... | collective-permute-start | bytes 786440 | tf_op jit(solution)/shard_map/ppermute | solution.py:333
  30.9 9.0 %copy-start.8 = (bf16[2,128,512]{2,1,0:T(8,128)(2,1)}, bf16[2,128,512]{2,1,0:T(8,128)(2,1)S(1)}, u32[]{:S(2)}) copy-start(bf16[2,128,512]{2,1,0:T(8,128)(2,1)S(1)} %collective-permute-done.11.refs_14_) | copy-start | bytes 786436
  30.9 9.0 %collective-permute-start.12 = (bf16[2,128,512]{2,1,0:T(8,128)(2,1)S(1)}, bf16[2,128,512]{2,1,0:T(8,128)(2,1)S(1)}, u32[]{:S(2)}, u32[]{:S(2)}) collective-permute-start(bf16[2,128,512]{2,1,0:T(8,128)(2,1)S(1)} %collective-permute-done.11.refs_14_), channel_id=1, source_target_pairs={{0,2},{2,4},{4,6},{6,8},{8,10},{10,12},{12,14},{14,0},{1,3},{3,5},... | collective-permute-start | bytes 786440 | tf_op jit(solution)/shard_map/ppermute | solution.py:334
  34.8 21.0 %copy-start.9 = (bf16[2,128,512]{2,1,0:T(8,128)(2,1)}, bf16[2,128,512]{2,1,0:T(8,128)(2,1)S(1)}, u32[]{:S(2)}) copy-start(bf16[2,128,512]{2,1,0:T(8,128)(2,1)S(1)} %collective-permute-done.9.refs_10_) | copy-start | bytes 786436
  34.8 12.1 %collective-permute-start.10 = (bf16[2,128,512]{2,1,0:T(8,128)(2,1)S(1)}, bf16[2,128,512]{2,1,0:T(8,128)(2,1)S(1)}, u32[]{:S(2)}, u32[]{:S(2)}) collective-permute-start(bf16[2,128,512]{2,1,0:T(8,128)(2,1)S(1)} %collective-permute-done.9.refs_10_), channel_id=1, source_target_pairs={{0,14},{2,0},{4,2},{6,4},{8,6},{10,8},{12,10},{14,12},{1,15},{3,1}... | collective-permute-start | bytes 786440 | tf_op jit(solution)/shard_map/ppermute | solution.py:333
  38.5 8.4 %collective-permute-start.2 = (bf16[80,1024]{1,0:T(8,128)(2,1)}, bf16[80,1024]{1,0:T(8,128)(2,1)S(1)}, u32[]{:S(2)}, u32[]{:S(2)}) collective-permute-start(bf16[80,1024]{1,0:T(8,128)(2,1)} %get-tuple-element.23), channel_id=1, source_target_pairs={{0,32},{16,48},{32,0},{48,16},{1,33},{17,49},{33,1},{49,17},{2,34}... | collective-permute-start | bytes 491528 | tf_op jit(solution)/shard_map/ppermute | solution.py:389
  39.9 15.9 %copy-start.10 = (bf16[2,128,512]{2,1,0:T(8,128)(2,1)}, bf16[2,128,512]{2,1,0:T(8,128)(2,1)S(1)}, u32[]{:S(2)}) copy-start(bf16[2,128,512]{2,1,0:T(8,128)(2,1)S(1)} %collective-permute-done.12.refs_13_) | copy-start | bytes 786436
  39.9 7.6 %collective-permute-start.13 = (bf16[2,128,512]{2,1,0:T(8,128)(2,1)S(1)}, bf16[2,128,512]{2,1,0:T(8,128)(2,1)S(1)}, u32[]{:S(2)}, u32[]{:S(2)}) collective-permute-start(bf16[2,128,512]{2,1,0:T(8,128)(2,1)S(1)} %collective-permute-done.12.refs_13_), channel_id=1, source_target_pairs={{0,2},{2,4},{4,6},{6,8},{8,10},{10,12},{12,14},{14,0},{1,3},{3,5},... | collective-permute-start | bytes 786440 | tf_op jit(solution)/shard_map/ppermute | solution.py:334
  40.0 16.6 %copy-start = (bf16[400,1024]{1,0:T(8,128)(2,1)}, bf16[400,1024]{1,0:T(8,128)(2,1)S(1)}, u32[]{:S(2)}) copy-start(bf16[400,1024]{1,0:T(8,128)(2,1)S(1)} %collective-permute-done.1.before_ref.refs_1_) | copy-start | bytes 2457604
  40.0 16.6 %copy-start.1 = (bf16[400,1024]{1,0:T(8,128)(2,1)}, bf16[400,1024]{1,0:T(8,128)(2,1)S(1)}, u32[]{:S(2)}) copy-start(bf16[400,1024]{1,0:T(8,128)(2,1)S(1)} %collective-permute-done.3.after_ref.refs_3_) | copy-start | bytes 2457604
  40.1 15.0 %collective-permute-start.4 = (bf16[160,1024]{1,0:T(8,128)(2,1)S(1)}, bf16[160,1024]{1,0:T(8,128)(2,1)S(1)}, u32[]{:S(2)}, u32[]{:S(2)}) collective-permute-start(bf16[160,1024]{1,0:T(8,128)(2,1)S(1)} %get-tuple-element.25), channel_id=1, source_target_pairs={{0,16},{16,32},{32,48},{48,0},{1,17},{17,33},{33,49},{49,1},{2,18}... | collective-permute-start | bytes 983048 | tf_op jit(solution)/shard_map/ppermute | solution.py:392
  42.2 12.8 %collective-permute-start.5 = (bf16[160,1024]{1,0:T(8,128)(2,1)S(1)}, bf16[160,1024]{1,0:T(8,128)(2,1)S(1)}, u32[]{:S(2)}, u32[]{:S(2)}) collective-permute-start(bf16[160,1024]{1,0:T(8,128)(2,1)S(1)} %get-tuple-element.26), channel_id=1, source_target_pairs={{0,48},{16,0},{32,16},{48,32},{1,49},{17,1},{33,17},{49,33},{2,50}... | collective-permute-start | bytes 983048 | tf_op jit(solution)/shard_map/ppermute | solution.py:392
  46.9 9.0 %copy-start.12 = (bf16[80,1024]{1,0:T(8,128)(2,1)}, bf16[80,1024]{1,0:T(8,128)(2,1)S(1)}, u32[]{:S(2)}) copy-start(bf16[80,1024]{1,0:T(8,128)(2,1)S(1)} %collective-permute-done.2.refs_2_) | copy-start | bytes 491524
  46.9 1.4 %collective-permute-start.7 = (bf16[80,1024]{1,0:T(8,128)(2,1)S(1)}, bf16[80,1024]{1,0:T(8,128)(2,1)S(1)}, u32[]{:S(2)}, u32[]{:S(2)}) collective-permute-start(bf16[80,1024]{1,0:T(8,128)(2,1)S(1)} %collective-permute-done.2.refs_2_), channel_id=1, source_target_pairs={{0,64},{64,0},{1,65},{65,1},{2,66},{66,2},{3,67},{67,3},{4,68},{68... | collective-permute-start | bytes 491528 | tf_op jit(solution)/shard_map/ppermute | solution.py:393
  46.9 9.7 %copy-start.2 = (bf16[2,128,512]{2,1,0:T(8,128)(2,1)}, bf16[2,128,512]{2,1,0:T(8,128)(2,1)S(1)}, u32[]{:S(2)}) copy-start(bf16[2,128,512]{2,1,0:T(8,128)(2,1)S(1)} %collective-permute-done.10.up_ref.refs_11_) | copy-start | bytes 786436
  46.9 8.1 %collective-permute-start.6 = (bf16[128,1024]{1,0:T(8,128)(2,1)S(1)}, bf16[128,1024]{1,0:T(8,128)(2,1)S(1)}, u32[]{:S(2)}, u32[]{:S(2)}) collective-permute-start(bf16[128,1024]{1,0:T(8,128)(2,1)S(1)} %get-tuple-element.27), channel_id=1, source_target_pairs={{0,64},{64,0},{1,65},{65,1},{2,66},{66,2},{3,67},{67,3},{4,68},{68... | collective-permute-start | bytes 786440 | tf_op jit(solution)/shard_map/ppermute | solution.py:393
  47.5 0.7 copy-start.3
  48.2 5.4 %collective-permute-start.14 = (bf16[1,128,512]{2,1,0:T(8,128)(2,1)S(1)}, bf16[1,128,512]{2,1,0:T(8,128)(2,1)S(1)}, u32[]{:S(2)}, u32[]{:S(2)}) collective-permute-start(bf16[1,128,512]{2,1,0:T(8,128)(2,1)S(1)} %get-tuple-element.29), channel_id=1, source_target_pairs={{0,14},{2,0},{4,2},{6,4},{8,6},{10,8},{12,10},{14,12},{1,15},{3,1}... | collective-permute-start | bytes 393224 | tf_op jit(solution)/shard_map/ppermute | solution.py:336
  48.3 7.6 %copy-start.13 = (bf16[80,1024]{1,0:T(8,128)(2,1)}, bf16[80,1024]{1,0:T(8,128)(2,1)S(1)}, u32[]{:S(2)}) copy-start(bf16[80,1024]{1,0:T(8,128)(2,1)S(1)} %collective-permute-done.7.refs_7_) | copy-start | bytes 491524
  48.3 6.8 %collective-permute-start.15 = (bf16[1,128,512]{2,1,0:T(8,128)(2,1)S(1)}, bf16[1,128,512]{2,1,0:T(8,128)(2,1)S(1)}, u32[]{:S(2)}, u32[]{:S(2)}) collective-permute-start(bf16[1,128,512]{2,1,0:T(8,128)(2,1)S(1)} %get-tuple-element.30), channel_id=1, source_target_pairs={{0,2},{2,4},{4,6},{6,8},{8,10},{10,12},{12,14},{14,0},{1,3},{3,5},... | collective-permute-start | bytes 393224 | tf_op jit(solution)/shard_map/ppermute | solution.py:336
  53.6 3.0 %copy-start.14 = (bf16[1,128,512]{2,1,0:T(8,128)(2,1)}, bf16[1,128,512]{2,1,0:T(8,128)(2,1)S(1)}, u32[]{:S(2)}) copy-start(bf16[1,128,512]{2,1,0:T(8,128)(2,1)S(1)} %collective-permute-done.14.refs_15_) | copy-start | bytes 393220
  55.0 0.8 copy-start.15
  55.0 0.9 copy-start.11
  55.1 0.8 copy-start.5
  55.9 0.7 copy-start.6

commit v8 on v6

--- a/solution.py
+++ b/solution.py
@@ -76,8 +76,11 @@
     pairs = [(gate_out_hbm, out_ref.at[pl.ds(0, rank)]), (up_out_hbm, out_ref.at[pl.ds(rank, rank)])]
     for step, message in enumerate(messages, 1):
         start = pl.multiple_of(lax.rem(lax.axis_index("x") + step, NX) * width, width)
-        bottom = message.shape[0] - half - FOLD
-        pairs.append((down_hbm.at[pl.ds(core * half, half), pl.ds(start, width)], message.at[pl.ds(bottom, half)]))
+        columns = pl.ds(start, width)
+        if step == 2:
+            pairs.append((down_hbm.at[:, columns], message.at[pl.ds(0, hidden)]))
+        else:
+            pairs.append((down_hbm.at[pl.ds(core * half, half), columns], message.at[pl.ds(top, half)]))
     extra = [pltpu.make_async_copy(a, b, sems.at[count + k]) for k, (a, b) in enumerate(pairs)]
     for copy in extra:
         copy.start()
@@ -134,7 +137,7 @@
         lambda *refs: token_kernel(chunk, scale, *refs),
         out_shape=[
             jax.ShapeDtypeStruct((2 * hidden + hidden // 2 + rank + FOLD, rows), jnp.bfloat16),
-            jax.ShapeDtypeStruct((hidden // 2 + FOLD, rows), jnp.bfloat16),
+            jax.ShapeDtypeStruct((hidden + FOLD, rows), jnp.bfloat16),
             jax.ShapeDtypeStruct((2 * hidden + hidden // 2 + rank + FOLD, rows), jnp.bfloat16),
             jax.ShapeDtypeStruct((rows, 2 * rank), jnp.float32),
         ],
@@ -174,16 +177,37 @@
         out_shape=[shape, shape, swap],
         in_specs=[VMEM] * 2,
         out_specs=[VMEM] * 3,
-        compiler_params=pltpu.CompilerParams(vmem_limit_bytes=12 * MIB),
+        compiler_params=pltpu.CompilerParams(vmem_limit_bytes=8 * MIB),
         name="halves",
     )(before, after)
 
 
-def tail_kernel(weight_hbm, gate_out_ref, up_out_ref, down_out_hbm, right_ref, *refs):
-    messages, far_halves, swaps, blocks = refs[:NX], refs[NX : NX + 2], refs[NX + 2 : NX + 4], refs[NX + 4 : NX + 4 + NZ]
-    out_ref, weights, projs, grads, far_ref, total, sems = refs[NX + 4 + NZ :]
-    factors = [messages[0], messages[1], far_ref, messages[3]]
-    hidden, model_width = weight_hbm.shape
+def keep_kernel(message_ref, right_ref, pair_ref, factors_out, right_out, pair_out):
+    factors_out[...] = message_ref[: factors_out.shape[0], :]
+    right_out[...] = right_ref[...]
+    pair_out[...] = pair_ref[...]
+
+
+def keep(message, right, pair, rows):
+    return pl.pallas_call(
+        keep_kernel,
+        out_shape=[
+            jax.ShapeDtypeStruct((rows, message.shape[1]), message.dtype),
+            jax.ShapeDtypeStruct(right.shape, right.dtype),
+            jax.ShapeDtypeStruct(pair.shape, pair.dtype),
+        ],
+        in_specs=[VMEM] * 3,
+        out_specs=[VMEM] * 3,
+        compiler_params=pltpu.CompilerParams(vmem_limit_bytes=8 * MIB),
+        name="keep",
+    )(message, right, pair)
+
+
+def tail_kernel(weight_ref, gate_out_ref, up_out_ref, down_out_ref, right_ref, *refs):
+    own_ref, messages, far_halves, swap_ref = refs[0], refs[1:NX], refs[NX : NX + 2], refs[NX + 2]
+    blocks, far_block = refs[NX + 3 : NX + 2 + NZ], refs[NX + 2 + NZ : NX + 4 + NZ]
+    out_ref, weights, projs, grads = refs[NX + 4 + NZ :]
+    hidden, model_width = weight_ref.shape
     rank = gate_out_ref.shape[0]
     width = model_width // NX
     examples, both, seq_dev = blocks[0].shape
@@ -192,47 +216,51 @@
     x_at, z_at, y_at = lax.axis_index("x"), lax.axis_index("z"), lax.axis_index("yh")
 
     start = pl.multiple_of(x_at * width, width)
-    pairs = [
-        (weight_hbm.at[:, pl.ds(start, width)], weights.at[pl.ds(0, hidden)]),
-        (down_out_hbm.at[:, pl.ds(start, width)], weights.at[pl.ds(NX * hidden, rank)]),
-    ]
-    for step in range(1, NX):
-        bottom = messages[step].shape[0] - half - FOLD
-        mine = pl.ds(pl.multiple_of(step * hidden + core * half, half), half)
-        pairs.append((messages[step].at[pl.ds(bottom, half)], weights.at[mine]))
-        theirs = pl.ds(pl.multiple_of(step * hidden + (1 - core) * half, half), half)
-        swapped = swaps[1].at[pl.ds(0, half)] if step == 2 else swaps[0].at[pl.ds(step // 2 * half, half)]
-        pairs.append((swapped, weights.at[theirs]))
-    for index, part in enumerate(far_halves):
-        pairs.append((part, far_ref.at[pl.ds(index * part.shape[0], part.shape[0])]))
-    for step, block in enumerate(blocks):
-        base = lax.rem(z_at + step, NZ) * both
-        for kind, y_of in enumerate((y_at, 1 - y_at)):
-            rows = pl.ds(pl.multiple_of(base + y_of * piece, piece), piece)
-            pairs.append((block.at[:, pl.ds(kind * piece, piece)], grads.at[:, rows]))
-    copies = [pltpu.make_async_copy(a, b, sems.at[k]) for k, (a, b) in enumerate(pairs)]
-    for copy in copies:
-        copy.start()
+    weights[:hidden, :] = weight_ref[:, pl.ds(start, width)]
+    weights[NX * hidden :, :] = down_out_ref[:, pl.ds(start, width)]
     projs[:rank, :hidden] = gate_out_ref[...]
     projs[rank:, :hidden] = up_out_ref[...]
-    for step in range(1, NX):
+    for step, message in enumerate(messages, 1):
+        if step == 2:
+            weights[step * hidden : (step + 1) * hidden, :] = message[:hidden, :]
+        else:
+            mine = pl.ds(pl.multiple_of(step * hidden + core * half, half), half)
+            theirs = pl.ds(pl.multiple_of(step * hidden + (1 - core) * half, half), half)
+            weights[mine, :] = message[top : top + half, :]
+            weights[theirs, :] = swap_ref[step // 2 * half : (step // 2 + 1) * half, :]
         columns = slice(step * hidden, (step + 1) * hidden)
         for block in range(2 * rank // FOLD):
-            folded = messages[step][-FOLD:, block * hidden : (block + 1) * hidden]
+            folded = message[-FOLD:, block * hidden : (block + 1) * hidden]
             projs[block * FOLD : (block + 1) * FOLD, columns] = folded
-    for copy in copies:
-        copy.wait()
+
+    def factor_rows(step, first, last, columns):
+        if step != 2:
+            return (own_ref if step == 0 else messages[step - 1])[first:last, columns]
+        rows = far_halves[0].shape[0]
+        parts = [far_halves[0][first : min(last, rows), columns]] if first < rows else []
+        if last > rows:
+            parts.append(far_halves[1][max(first - rows, 0) : last - rows, columns])
+        return jnp.concatenate(parts, axis=0)
+
     for example in range(examples):
-        total[example] = jnp.dot(weights[...], grads[example], preferred_element_type=jnp.float32)
-    for example in range(examples):
+        for step in range(NZ):
+            if step == NZ // 2:
+                count = examples // 2
+                block = far_block[example // count][example % count]
+            else:
+                block = blocks[step if step < NZ // 2 else step - 1][example]
+            base = lax.rem(z_at + step, NZ) * both
+            for kind, y_of in enumerate((y_at, 1 - y_at)):
+                rows = pl.ds(pl.multiple_of(base + y_of * piece, piece), piece)
+                grads[rows, :] = block[kind * piece : (kind + 1) * piece]
         columns = slice(example * seq_dev, (example + 1) * seq_dev)
+        total = jnp.dot(weights[...], grads[...], preferred_element_type=jnp.float32)
         left = []
         for kind in range(2):
-            products = []
-            for step in range(NX):
-                factor = factors[step][kind * hidden : (kind + 1) * hidden, columns].astype(jnp.float32)
-                products.append(total[example, step * hidden : (step + 1) * hidden] * factor)
-            product = jnp.concatenate(products, axis=0)
+            factor = jnp.concatenate(
+                [factor_rows(step, kind * hidden, (kind + 1) * hidden, columns) for step in range(NX)], axis=0
+            )
+            product = total[: NX * hidden] * factor.astype(jnp.float32)
             high = product.astype(jnp.bfloat16)
             low = (product - high.astype(jnp.float32)).astype(jnp.bfloat16)
             proj = projs[kind * rank : (kind + 1) * rank, :]
@@ -246,39 +274,53 @@
             precision=lax.Precision.HIGHEST,
             preferred_element_type=jnp.float32,
         )
-        right_down = factors[0][2 * hidden : top, columns].astype(jnp.float32)
+        right_down = factor_rows(0, 2 * hidden, top, columns).astype(jnp.float32)
         for step in range(1, NX):
-            right_down = right_down + factors[step][2 * hidden : top, columns].astype(jnp.float32)
+            right_down = right_down + factor_rows(step, 2 * hidden, top, columns).astype(jnp.float32)
         out_ref[3 * example] = sides[:rank, :rank]
         out_ref[3 * example + 1] = sides[rank:, rank:]
         out_ref[3 * example + 2] = dot32(
-            total[example, NX * hidden :], right_down, ((1,), (1,)), precision=lax.Precision.HIGHEST
+            total[NX * hidden :], right_down, ((1,), (1,)), precision=lax.Precision.HIGHEST
         )
 
 
-def tail_stage(down_weight, gate_out, up_out, down_out, right, messages, far, swaps, blocks):
+def tail_stage(down_weight, gate_out, up_out, down_out, right, factors, messages, far, swap, blocks, far_block):
     hidden, model_width = down_weight.shape
     rank = gate_out.shape[0]
     examples, _, seq_dev = blocks[0].shape
     width = model_width // NX
-    operands = [down_weight, gate_out, up_out, down_out, right, *messages, *far, *swaps, *blocks]
+    operands = [down_weight, gate_out, up_out, down_out, right, factors, *messages, *far, swap, *blocks, *far_block]
     return pl.pallas_call(
         tail_kernel,
         out_shape=jax.ShapeDtypeStruct((examples * 3, rank, rank), jnp.float32),
-        in_specs=[HBM, VMEM, VMEM, HBM, VMEM] + [VMEM] * NX + [HBM] * (4 + NZ),
+        in_specs=[VMEM] * len(operands),
         out_specs=VMEM,
         scratch_shapes=[
             pltpu.VMEM((NX * hidden + rank, width), jnp.bfloat16),
             pltpu.VMEM((2 * rank, NX * hidden), jnp.bfloat16),
-            pltpu.VMEM((examples, width, seq_dev), jnp.bfloat16),
-            pltpu.VMEM((2 * far[0].shape[0], examples * seq_dev), jnp.bfloat16),
-            pltpu.VMEM((examples, NX * hidden + rank, seq_dev), jnp.float32),
-            pltpu.SemaphoreType.DMA((2 + 2 * NX + NZ * NY,)),
+            pltpu.VMEM((width, seq_dev), jnp.bfloat16),
         ],
-        compiler_params=pltpu.CompilerParams(vmem_limit_bytes=16 * MIB),
+        compiler_params=pltpu.CompilerParams(vmem_limit_bytes=20 * MIB),
         cost_estimate=pl.CostEstimate(flops=4 * 10**9, bytes_accessed=8 * MIB, transcendentals=0),
         name="tail_stage",
     )(*operands)
+
+
+def cut_kernel(up_ref, down_ref, first_ref, second_ref):
+    first_ref[...] = up_ref[: first_ref.shape[0]]
+    second_ref[...] = down_ref[first_ref.shape[0] :]
+
+
+def cut(up, down):
+    shape = jax.ShapeDtypeStruct((up.shape[0] // 2,) + up.shape[1:], up.dtype)
+    return pl.pallas_call(
+        cut_kernel,
+        out_shape=[shape] * 2,
+        in_specs=[VMEM] * 2,
+        out_specs=[VMEM] * 2,
+        compiler_params=pltpu.CompilerParams(vmem_limit_bytes=4 * MIB),
+        name="cut",
+    )(up, down)
 
 
 def ring_z(own):
@@ -286,7 +328,9 @@
     for _ in range(NZ // 2 - 1):
         up.append(lax.ppermute(up[-1], "z", shifted(NZ, -1)))
         down.append(lax.ppermute(down[-1], "z", shifted(NZ, 1)))
-    return up + [lax.ppermute(up[-1], "z", shifted(NZ, -1))] + down[:0:-1]
+    first, second = cut(up[-1], down[-1])
+    far = [lax.ppermute(first, "z", shifted(NZ, -1)), lax.ppermute(second, "z", shifted(NZ, 1))]
+    return up + down[:0:-1], far
 
 
 def sum_everywhere(partial):
@@ -338,13 +382,17 @@
     )
     sent, right = sent[: NX - 1], sent[NX - 1]
     pair, sent = pair_up(own_grad, other_grad, sent)
-    messages = [sent[0]] + [lax.ppermute(piece, "x", shifted(NX, step)) for step, piece in enumerate(sent, 1)]
+    messages = [lax.ppermute(piece, "x", shifted(NX, step)) for step, piece in enumerate(sent, 1)]
     hidden, rank = gate_weight.shape[1], gate_out.shape[0]
-    first, second, swap = halves(messages[1], messages[3], hidden + rank // 2, hidden // 2)
+    rows = 2 * hidden + rank
+    first, second, swap = halves(messages[0], messages[2], rows // 2, hidden // 2)
+    swap = lax.ppermute(swap, "sc", shifted(SEQ_PARTS[1], 1))
     far = [lax.ppermute(first, "x", shifted(NX, 1)), lax.ppermute(second, "x", shifted(NX, -1))]
-    swaps = [lax.ppermute(piece, "sc", shifted(SEQ_PARTS[1], 1)) for piece in (swap, messages[2])]
-    blocks = ring_z(pair)
-    products = tail_stage(down_weight, gate_out, up_out, proj_down_out.T, right, messages, far, swaps, blocks)
+    blocks, far_block = ring_z(pair)
+    factors, right, blocks[0] = keep(sent[0], right, pair, rows)
+    products = tail_stage(
+        down_weight, gate_out, up_out, proj_down_out.T, right, factors, messages, far, swap, blocks, far_block
+    )
     total = sum_everywhere(products.reshape(examples * 3, -1))
     return total.reshape(examples, 3, -1)
 

time: 101 us -> 94.6 us (0.937)
  starting transfers between devices: 27.8 us -> 22.6 us
  waiting for transfers between devices: 14.4 us -> 18.6 us
  blocking collectives: 36.9 us -> 33.8 us
  Pallas kernels: 17 us -> 14.4 us
    ppermute x3, starting transfers between devices: 4.03 us -> 0.68 us  [the longest x1 0.67 us: ring_z(): lax.ppermute(first, 'z', shifted(NZ, -1))]
    all_to_all x1, blocking collectives: 16.7 us -> 13.6 us  [sum_everywhere(): pieces = lax.all_to_all(pieces, ('sy', 'sc', 'z'), 0, 0, tiled=True)]
    ppermute x3, waiting for transfers between devices: 0.01 us -> 2.93 us  [the longest x1 2.93 us: ring_z(): lax.ppermute(second, 'z', shifted(NZ, 1))]
    pallas_call x1, Pallas kernels: 6.26 us -> 3.44 us  [tail_stage(): pl.pallas_call(tail_kernel, out_shape=jax.ShapeDtypeStruct((examples * 3,...]
    ppermute x3, starting transfers between devices: 1.92 us -> 0.01 us  [ring_z(): down.append(lax.ppermute(down[-1], 'z', shifted(NZ, 1)))]
    ppermute x3, waiting for transfers between devices: 7.52 us -> 9.14 us  [ring_z(): up.append(lax.ppermute(up[-1], 'z', shifted(NZ, -1)))]
    ppermute x3, waiting for transfers between devices: 6.15 us -> 5.09 us  [ring_z(): down.append(lax.ppermute(down[-1], 'z', shifted(NZ, 1)))]
  transfers between devices with their start and end apart: 15 -> 15, of which waited for: 5 -> 6; matrix products, arithmetic and copies ran while one was open for 0% -> 0% of each run, Pallas kernels for 9% -> 10%
where the time goes in v8:
time: 94.6 us; the launch traced here: 94.3 us
  blocking collectives  33.8 us (36%)
  starting transfers between devices  22.6 us (24%)
  waiting for transfers between devices  18.6 us (20%)
  Pallas kernels  14.4 us (15%)
  local copies, waits for them, and re-layouts  4.64 us (5%)
    all_to_all x1, blocking collectives, sum_everywhere(): blocks = lax.all_to_all(spread, ('x', 'z', 'yh'), 0, 0, tiled=True)  20.2 us
    all_to_all x1, blocking collectives, sum_everywhere(): pieces = lax.all_to_all(pieces, ('sy', 'sc', 'z'), 0, 0, tiled=True)  13.6 us
    ppermute x3, starting transfers between devices, ring_z(): up.append(lax.ppermute(up[-1], 'z', shifted(NZ, -1)))  13.1 us
    ppermute x3, waiting for transfers between devices, ring_z(): up.append(lax.ppermute(up[-1], 'z', shifted(NZ, -1)))  9.14 us
    pallas_call x1, Pallas kernels, token_stage(): pl.pallas_call(lambda *refs: token_kernel(chunk, scale, *refs), out_shape...  9.07 us
    ppermute x3, waiting for transfers between devices, ring_z(): down.append(lax.ppermute(down[-1], 'z', shifted(NZ, 1)))  5.09 us
    unnamed x17, local copies, waits for them, and re-layouts  3.81 us
    pallas_call x1, Pallas kernels, tail_stage(): pl.pallas_call(tail_kernel, out_shape=jax.ShapeDtypeStruct((examples * 3,...  3.44 us
  transfers between devices with their start and end apart: 15, of which 6 were waited for; matrix products, arithmetic and copies ran while one was open for 0% of the time, Pallas kernels for 10%

profile of v8, /device:TPU:6, one launch (start us, length us, event | category | flops | bytes accessed | tf_op | source)
XLA Modules:
  0.0 94.3 jit_solution(13930633784898249513)
XLA Ops:
  0.0 3.2 %collective-permute-start = (bf16[2,64,512]{2,1,0:T(8,128)(2,1)}, bf16[2,64,512]{2,1,0:T(8,128)(2,1)S(1)}, u32[]{:S(2)}, u32[]{:S(2)}) collective-permute-start(bf16[2,64,512]{2,1,0:T(8,128)(2,1)} %bitcast.22), channel_id=1, source_target_pairs={{0,1},{1,0},{2,3},{3,2},{4,5},{5,4},{6,7},{7,6},{8,9},{9,8},{10,11... | collective-permute-start | bytes 393224 | tf_op jit(solution)/shard_map/ppermute | solution.py:368
  3.2 0.0 copy-start.3
  3.2 0.0 copy-start.4
  3.2 0.0 copy-start.5
  3.2 0.0 copy-start.6
  3.2 9.1 %token_stage.1 = (bf16[400,1024]{1,0:T(8,128)(2,1)}, bf16[144,1024]{1,0:T(8,128)(2,1)}, bf16[400,1024]{1,0:T(8,128)(2,1)}, f32[1024,128]{1,0:T(8,128)}) custom-call(s32[2]{0:T(128)} %refs_0_.1, bf16[1024,4096]{1,0:T(8,128)(2,1)} %bitcast.25, bf16[4096,128]{1,0:T(8,128)(2,1)} %refs_2_.1, bf16[4096,128]{1,0:T(8,128)(2,1)} %refs_3_.1, ...), custom_call_target="tpu_custom_call" | custom-call | flops 4294967296 | bytes 16777216 | tf_op jit(solution)/shard_map/token_stage/pallas_call | solution.py:136
  12.3 0.0 collective-permute-done.other_ref
  12.3 0.0 copy-start.7
  12.3 0.7 copy-done.7
  13.0 1.7 %pair_up.1 = (bf16[400,1024]{1,0:T(8,128)(2,1)}, bf16[144,1024]{1,0:T(8,128)(2,1)}, bf16[400,1024]{1,0:T(8,128)(2,1)}, bf16[2,128,512]{2,1,0:T(8,128)(2,1)}) custom-call(bf16[2,64,512]{2,1,0:T(8,128)(2,1)} %bitcast.23, bf16[2,64,512]{2,1,0:T(8,128)(2,1)} %copy-done.7, ...), custom_call_target="tpu_custom_call", output_to_operand_aliasing={{0}: (2, {}), {1}: (3, {}), {2}: (4, {})} | custom-call | tf_op jit(solution)/shard_map/pair_up/pallas_call | solution.py:34
  14.7 0.5 collective-permute-start.1
  15.1 1.6 %collective-permute-start.3 = (bf16[400,1024]{1,0:T(8,128)(2,1)}, bf16[400,1024]{1,0:T(8,128)(2,1)S(1)}, u32[]{:S(2)}, u32[]{:S(2)}) collective-permute-start(bf16[400,1024]{1,0:T(8,128)(2,1)} %get-tuple-element.30), channel_id=1, source_target_pairs={{0,48},{16,0},{32,16},{48,32},{1,49},{17,1},{33,17},{49,33},{2,50}... | collective-permute-start | bytes 2457608 | tf_op jit(solution)/shard_map/ppermute | solution.py:385
  16.7 5.9 %collective-permute-start.7 = (bf16[2,128,512]{2,1,0:T(8,128)(2,1)}, bf16[2,128,512]{2,1,0:T(8,128)(2,1)S(1)}, u32[]{:S(2)}, u32[]{:S(2)}) collective-permute-start(bf16[2,128,512]{2,1,0:T(8,128)(2,1)} %get-tuple-element.26.pair_ref), channel_id=1, source_target_pairs={{0,14},{2,0},{4,2},{6,4},{8,6},{10,8},{12,10},{14,12},{1,15},{3,1}... | collective-permute-start | bytes 786440 | tf_op jit(solution)/shard_map/ppermute | solution.py:329
  22.5 0.0 collective-permute-start.10
  22.5 5.0 %collective-permute-done.7.refs_8_ = bf16[2,128,512]{2,1,0:T(8,128)(2,1)S(1)} collective-permute-done((bf16[2,128,512]{2,1,0:T(8,128)(2,1)}, bf16[2,128,512]{2,1,0:T(8,128)(2,1)S(1)}, u32[]{:S(2)}, u32[]{:S(2)}) %collective-permute-start.7) | collective-permute-done | bytes 262176 | tf_op jit(solution)/shard_map/ppermute | solution.py:329
  27.6 3.6 %collective-permute-start.8 = (bf16[2,128,512]{2,1,0:T(8,128)(2,1)S(1)}, bf16[2,128,512]{2,1,0:T(8,128)(2,1)S(1)}, u32[]{:S(2)}, u32[]{:S(2)}) collective-permute-start(bf16[2,128,512]{2,1,0:T(8,128)(2,1)S(1)} %collective-permute-done.7.refs_8_), channel_id=1, source_target_pairs={{0,14},{2,0},{4,2},{6,4},{8,6},{10,8},{12,10},{14,12},{1,15},{3,1}... | collective-permute-start | bytes 786440 | tf_op jit(solution)/shard_map/ppermute | solution.py:329
  31.2 0.0 collective-permute-done.10.refs_13_
  31.2 0.0 collective-permute-start.11
  31.2 3.9 %collective-permute-done.8.refs_9_ = bf16[2,128,512]{2,1,0:T(8,128)(2,1)S(1)} collective-permute-done((bf16[2,128,512]{2,1,0:T(8,128)(2,1)S(1)}, bf16[2,128,512]{2,1,0:T(8,128)(2,1)S(1)}, u32[]{:S(2)}, u32[]{:S(2)}) %collective-permute-start.8) | collective-permute-done | bytes 262176 | tf_op jit(solution)/shard_map/ppermute | solution.py:329
  35.1 3.7 %collective-permute-start.9 = (bf16[2,128,512]{2,1,0:T(8,128)(2,1)S(1)}, bf16[2,128,512]{2,1,0:T(8,128)(2,1)S(1)}, u32[]{:S(2)}, u32[]{:S(2)}) collective-permute-start(bf16[2,128,512]{2,1,0:T(8,128)(2,1)S(1)} %collective-permute-done.8.refs_9_), channel_id=1, source_target_pairs={{0,14},{2,0},{4,2},{6,4},{8,6},{10,8},{12,10},{14,12},{1,15},{3,1}... | collective-permute-start | bytes 786440 | tf_op jit(solution)/shard_map/ppermute | solution.py:329
  38.8 1.4 %collective-permute-start.2 = (bf16[144,1024]{1,0:T(8,128)(2,1)}, bf16[144,1024]{1,0:T(8,128)(2,1)S(1)}, u32[]{:S(2)}, u32[]{:S(2)}) collective-permute-start(bf16[144,1024]{1,0:T(8,128)(2,1)} %get-tuple-element.29), channel_id=1, source_target_pairs={{0,32},{16,48},{32,0},{48,16},{1,33},{17,49},{33,1},{49,17},{2,34}... | collective-permute-start | bytes 884744 | tf_op jit(solution)/shard_map/ppermute | solution.py:385
  40.1 0.0 collective-permute-done.11.refs_12_
  40.1 0.0 collective-permute-start.12
  40.2 0.0 collective-permute-done.1.before_ref.refs_1_
  40.2 0.0 collective-permute-done.3.after_ref.refs_3_
  40.2 0.1 halves.1
  40.2 2.2 %collective-permute-start.4 = (bf16[160,1024]{1,0:T(8,128)(2,1)S(1)}, bf16[160,1024]{1,0:T(8,128)(2,1)S(1)}, u32[]{:S(2)}, u32[]{:S(2)}) collective-permute-start(bf16[160,1024]{1,0:T(8,128)(2,1)S(1)} %get-tuple-element.31), channel_id=1, source_target_pairs={{0,16},{16,32},{32,48},{48,0},{1,17},{17,33},{33,49},{49,1},{2,18}... | collective-permute-start | bytes 983048 | tf_op jit(solution)/shard_map/ppermute | solution.py:390
  42.4 0.0 collective-permute-start.5
  42.4 0.2 collective-permute-done.9.up_ref.refs_10_
  42.6 0.0 collective-permute-start.6
  42.6 5.1 %collective-permute-done.12.down_ref.refs_11_ = bf16[2,128,512]{2,1,0:T(8,128)(2,1)S(1)} collective-permute-done((bf16[2,128,512]{2,1,0:T(8,128)(2,1)S(1)}, bf16[2,128,512]{2,1,0:T(8,128)(2,1)S(1)}, u32[]{:S(2)}, u32[]{:S(2)}) %collective-permute-start.12) | collective-permute-done | bytes 262176 | tf_op jit(solution)/shard_map/ppermute | solution.py:330
  47.8 0.7 collective-permute-start.13
  48.4 1.5 %collective-permute-done.2.refs_2_ = bf16[144,1024]{1,0:T(8,128)(2,1)S(1)} collective-permute-done((bf16[144,1024]{1,0:T(8,128)(2,1)}, bf16[144,1024]{1,0:T(8,128)(2,1)S(1)}, u32[]{:S(2)}, u32[]{:S(2)}) %collective-permute-start.2) | collective-permute-done | bytes 294944 | tf_op jit(solution)/shard_map/ppermute | solution.py:385
  49.9 0.0 collective-permute-start.14
  49.9 0.0 copy-start
  49.9 1.1 %copy-done = bf16[400,1024]{1,0:T(8,128)(2,1)S(1)} copy-done((bf16[400,1024]{1,0:T(8,128)(2,1)S(1)}, bf16[400,1024]{1,0:T(8,128)(2,1)}, u32[]{:S(2)}) %copy-start) | copy-done | bytes 819224
  51.0 0.0 copy-start.1
  51.0 1.0 %copy-done.1 = f32[1024,128]{1,0:T(8,128)S(1)} copy-done((f32[1024,128]{1,0:T(8,128)S(1)}, f32[1024,128]{1,0:T(8,128)}, u32[]{:S(2)}) %copy-start.1) | copy-done | bytes 524312
  52.1 0.0 copy-start.2
  52.1 0.9 %copy-done.2 = bf16[2,128,512]{2,1,0:T(8,128)(2,1)S(1)} copy-done((bf16[2,128,512]{2,1,0:T(8,128)(2,1)S(1)}, bf16[2,128,512]{2,1,0:T(8,128)(2,1)}, u32[]{:S(2)}) %copy-start.2) | copy-done | bytes 262168
  53.0 0.1 keep.1
  53.1 0.0 collective-permute-done.13.refs_14_
  53.1 2.9 %collective-permute-done.14.refs_15_ = bf16[1,128,512]{2,1,0:T(8,128)(2,1)S(1)} collective-permute-done((bf16[1,128,512]{2,1,0:T(8,128)(2,1)S(1)}, bf16[1,128,512]{2,1,0:T(8,128)(2,1)S(1)}, u32[]{:S(2)}, u32[]{:S(2)}) %collective-permute-start.14) | collective-permute-done | bytes 131104 | tf_op jit(solution)/shard_map/ppermute | solution.py:332
  56.1 0.0 collective-permute-done.6.refs_6_
  56.1 0.0 collective-permute-done.4.refs_4_
  56.1 0.0 collective-permute-done.5.refs_5_
  56.1 0.0 copy-done.3
  56.1 0.0 copy-done.4
  56.1 0.0 copy-done.5
  56.1 0.0 copy-done.6
  56.1 3.4 %tail_stage.1 = f32[6,64,64]{2,1,0:T(8,128)S(1)} custom-call(bf16[128,4096]{1,0:T(8,128)(2,1)S(1)} %copy-done.3, bf16[64,128]{1,0:T(8,128)(2,1)S(1)} %bitcast.17, bf16[64,128]{1,0:T(8,128)(2,1)S(1)} %bitcast.19, bf16[64,4096]{1,0:T(8,128)(2,1)S(1)} %bitcast.15, f32[1024,128]{1,0:T(8,128)S(1)} %get-tuple-element.27.right_ref, ...), custom_call_target="tpu_custom_call" | custom-call | flops 4000000000 | bytes 8388608 | tf_op jit(solution)/shard_map/tail_stage/pallas_call | solution.py:293
  59.6 0.1 reshape_reshape.6
  59.7 0.1 copy.33
  59.7 13.6 %all_to_all.10 = f32[32,6,128]{2,1,0:T(8,128)S(1)} all-to-all(f32[32,6,128]{2,1,0:T(8,128)S(1)} %bitcast.21), channel_id=1, replica_groups=mesh['sy'=2,'sc'=2,'x'=4,'z'=8,'yh'=2] {'sy','sc','z'}, dimensions={0} | all-to-all | bytes 196608 | tf_op jit(solution)/shard_map/all_to_all | solution.py:341
  73.4 20.2 %all_to_all.11 = f32[64,6,128]{2,1,0:T(8,128)S(1)} all-to-all(f32[64,6,128]{2,1,0:T(8,128)S(1)} %broadcast_in_dim.2), channel_id=1, replica_groups=mesh['sy'=2,'sc'=2,'x'=4,'z'=8,'yh'=2] {'x','z','yh'}, dimensions={0} | all-to-all | bytes 393216 | tf_op jit(solution)/shard_map/all_to_all | solution.py:344
  93.7 0.6 copy.27
  (6 shorter events, 0.1 us)
Async XLA Ops:
  0.0 12.3 %collective-permute-start = (bf16[2,64,512]{2,1,0:T(8,128)(2,1)}, bf16[2,64,512]{2,1,0:T(8,128)(2,1)S(1)}, u32[]{:S(2)}, u32[]{:S(2)}) collective-permute-start(bf16[2,64,512]{2,1,0:T(8,128)(2,1)} %bitcast.22), channel_id=1, source_target_pairs={{0,1},{1,0},{2,3},{3,2},{4,5},{5,4},{6,7},{7,6},{8,9},{9,8},{10,11... | collective-permute-start | bytes 393224 | tf_op jit(solution)/shard_map/ppermute | solution.py:368
  3.2 52.9 %copy-start.3 = (bf16[128,4096]{1,0:T(8,128)(2,1)S(1)}, bf16[128,4096]{1,0:T(8,128)(2,1)}, u32[]{:S(2)}) copy-start(bf16[128,4096]{1,0:T(8,128)(2,1)} %weight_ref.1) | copy-start | bytes 3145732
  3.2 52.9 %copy-start.4 = (bf16[4096,64]{0,1:T(8,128)(2,1)S(1)}, bf16[4096,64]{0,1:T(8,128)(2,1)}, u32[]{:S(2)}) copy-start(bf16[4096,64]{0,1:T(8,128)(2,1)} %param.22) | copy-start | bytes 1572868
  3.2 52.9 %copy-start.5 = (bf16[128,64]{0,1:T(8,128)(2,1)S(1)}, bf16[128,64]{0,1:T(8,128)(2,1)}, u32[]{:S(2)}) copy-start(bf16[128,64]{0,1:T(8,128)(2,1)} %param.18) | copy-start | bytes 49156
  3.2 52.9 %copy-start.6 = (bf16[128,64]{0,1:T(8,128)(2,1)S(1)}, bf16[128,64]{0,1:T(8,128)(2,1)}, u32[]{:S(2)}) copy-start(bf16[128,64]{0,1:T(8,128)(2,1)} %param.20) | copy-start | bytes 49156
  12.3 0.7 copy-start.7
  14.7 25.5 %collective-permute-start.1 = (bf16[400,1024]{1,0:T(8,128)(2,1)}, bf16[400,1024]{1,0:T(8,128)(2,1)S(1)}, u32[]{:S(2)}, u32[]{:S(2)}) collective-permute-start(bf16[400,1024]{1,0:T(8,128)(2,1)} %get-tuple-element.24.message_ref), channel_id=1, source_target_pairs={{0,16},{16,32},{32,48},{48,0},{1,17},{17,33},{33,49},{49,1},{2,18}... | collective-permute-start | bytes 2457608 | tf_op jit(solution)/shard_map/ppermute | solution.py:385
  15.1 25.0 %collective-permute-start.3 = (bf16[400,1024]{1,0:T(8,128)(2,1)}, bf16[400,1024]{1,0:T(8,128)(2,1)S(1)}, u32[]{:S(2)}, u32[]{:S(2)}) collective-permute-start(bf16[400,1024]{1,0:T(8,128)(2,1)} %get-tuple-element.30), channel_id=1, source_target_pairs={{0,48},{16,0},{32,16},{48,32},{1,49},{17,1},{33,17},{49,33},{2,50}... | collective-permute-start | bytes 2457608 | tf_op jit(solution)/shard_map/ppermute | solution.py:385
  16.7 10.9 %collective-permute-start.7 = (bf16[2,128,512]{2,1,0:T(8,128)(2,1)}, bf16[2,128,512]{2,1,0:T(8,128)(2,1)S(1)}, u32[]{:S(2)}, u32[]{:S(2)}) collective-permute-start(bf16[2,128,512]{2,1,0:T(8,128)(2,1)} %get-tuple-element.26.pair_ref), channel_id=1, source_target_pairs={{0,14},{2,0},{4,2},{6,4},{8,6},{10,8},{12,10},{14,12},{1,15},{3,1}... | collective-permute-start | bytes 786440 | tf_op jit(solution)/shard_map/ppermute | solution.py:329
  22.5 8.6 %collective-permute-start.10 = (bf16[2,128,512]{2,1,0:T(8,128)(2,1)}, bf16[2,128,512]{2,1,0:T(8,128)(2,1)S(1)}, u32[]{:S(2)}, u32[]{:S(2)}) collective-permute-start(bf16[2,128,512]{2,1,0:T(8,128)(2,1)} %get-tuple-element.26.pair_ref), channel_id=1, source_target_pairs={{0,2},{2,4},{4,6},{6,8},{8,10},{10,12},{12,14},{14,0},{1,3},{3,5},... | collective-permute-start | bytes 786440 | tf_op jit(solution)/shard_map/ppermute | solution.py:330
  27.6 7.5 %collective-permute-start.8 = (bf16[2,128,512]{2,1,0:T(8,128)(2,1)S(1)}, bf16[2,128,512]{2,1,0:T(8,128)(2,1)S(1)}, u32[]{:S(2)}, u32[]{:S(2)}) collective-permute-start(bf16[2,128,512]{2,1,0:T(8,128)(2,1)S(1)} %collective-permute-done.7.refs_8_), channel_id=1, source_target_pairs={{0,14},{2,0},{4,2},{6,4},{8,6},{10,8},{12,10},{14,12},{1,15},{3,1}... | collective-permute-start | bytes 786440 | tf_op jit(solution)/shard_map/ppermute | solution.py:329
  31.2 9.0 %collective-permute-start.11 = (bf16[2,128,512]{2,1,0:T(8,128)(2,1)S(1)}, bf16[2,128,512]{2,1,0:T(8,128)(2,1)S(1)}, u32[]{:S(2)}, u32[]{:S(2)}) collective-permute-start(bf16[2,128,512]{2,1,0:T(8,128)(2,1)S(1)} %collective-permute-done.10.refs_13_), channel_id=1, source_target_pairs={{0,2},{2,4},{4,6},{6,8},{8,10},{10,12},{12,14},{14,0},{1,3},{3,5},... | collective-permute-start | bytes 786440 | tf_op jit(solution)/shard_map/ppermute | solution.py:330
  35.1 7.6 %collective-permute-start.9 = (bf16[2,128,512]{2,1,0:T(8,128)(2,1)S(1)}, bf16[2,128,512]{2,1,0:T(8,128)(2,1)S(1)}, u32[]{:S(2)}, u32[]{:S(2)}) collective-permute-start(bf16[2,128,512]{2,1,0:T(8,128)(2,1)S(1)} %collective-permute-done.8.refs_9_), channel_id=1, source_target_pairs={{0,14},{2,0},{4,2},{6,4},{8,6},{10,8},{12,10},{14,12},{1,15},{3,1}... | collective-permute-start | bytes 786440 | tf_op jit(solution)/shard_map/ppermute | solution.py:329
  38.8 11.1 %collective-permute-start.2 = (bf16[144,1024]{1,0:T(8,128)(2,1)}, bf16[144,1024]{1,0:T(8,128)(2,1)S(1)}, u32[]{:S(2)}, u32[]{:S(2)}) collective-permute-start(bf16[144,1024]{1,0:T(8,128)(2,1)} %get-tuple-element.29), channel_id=1, source_target_pairs={{0,32},{16,48},{32,0},{48,16},{1,33},{17,49},{33,1},{49,17},{2,34}... | collective-permute-start | bytes 884744 | tf_op jit(solution)/shard_map/ppermute | solution.py:385
  40.1 7.6 %collective-permute-start.12 = (bf16[2,128,512]{2,1,0:T(8,128)(2,1)S(1)}, bf16[2,128,512]{2,1,0:T(8,128)(2,1)S(1)}, u32[]{:S(2)}, u32[]{:S(2)}) collective-permute-start(bf16[2,128,512]{2,1,0:T(8,128)(2,1)S(1)} %collective-permute-done.11.refs_12_), channel_id=1, source_target_pairs={{0,2},{2,4},{4,6},{6,8},{8,10},{10,12},{12,14},{14,0},{1,3},{3,5},... | collective-permute-start | bytes 786440 | tf_op jit(solution)/shard_map/ppermute | solution.py:330
  40.2 15.8 %collective-permute-start.4 = (bf16[160,1024]{1,0:T(8,128)(2,1)S(1)}, bf16[160,1024]{1,0:T(8,128)(2,1)S(1)}, u32[]{:S(2)}, u32[]{:S(2)}) collective-permute-start(bf16[160,1024]{1,0:T(8,128)(2,1)S(1)} %get-tuple-element.31), channel_id=1, source_target_pairs={{0,16},{16,32},{32,48},{48,0},{1,17},{17,33},{33,49},{49,1},{2,18}... | collective-permute-start | bytes 983048 | tf_op jit(solution)/shard_map/ppermute | solution.py:390
  42.4 13.7 %collective-permute-start.5 = (bf16[160,1024]{1,0:T(8,128)(2,1)S(1)}, bf16[160,1024]{1,0:T(8,128)(2,1)S(1)}, u32[]{:S(2)}, u32[]{:S(2)}) collective-permute-start(bf16[160,1024]{1,0:T(8,128)(2,1)S(1)} %get-tuple-element.32), channel_id=1, source_target_pairs={{0,48},{16,0},{32,16},{48,32},{1,49},{17,1},{33,17},{49,33},{2,50}... | collective-permute-start | bytes 983048 | tf_op jit(solution)/shard_map/ppermute | solution.py:390
  42.6 13.4 %collective-permute-start.6 = (bf16[128,1024]{1,0:T(8,128)(2,1)S(1)}, bf16[128,1024]{1,0:T(8,128)(2,1)S(1)}, u32[]{:S(2)}, u32[]{:S(2)}) collective-permute-start(bf16[128,1024]{1,0:T(8,128)(2,1)S(1)} %get-tuple-element.33), channel_id=1, source_target_pairs={{0,64},{64,0},{1,65},{65,1},{2,66},{66,2},{3,67},{67,3},{4,68},{68... | collective-permute-start | bytes 786440 | tf_op jit(solution)/shard_map/ppermute | solution.py:389
  47.8 5.4 %collective-permute-start.13 = (bf16[1,128,512]{2,1,0:T(8,128)(2,1)S(1)}, bf16[1,128,512]{2,1,0:T(8,128)(2,1)S(1)}, u32[]{:S(2)}, u32[]{:S(2)}) collective-permute-start(bf16[1,128,512]{2,1,0:T(8,128)(2,1)S(1)} %get-tuple-element.35), channel_id=1, source_target_pairs={{0,14},{2,0},{4,2},{6,4},{8,6},{10,8},{12,10},{14,12},{1,15},{3,1}... | collective-permute-start | bytes 393224 | tf_op jit(solution)/shard_map/ppermute | solution.py:332
  49.9 6.2 %collective-permute-start.14 = (bf16[1,128,512]{2,1,0:T(8,128)(2,1)S(1)}, bf16[1,128,512]{2,1,0:T(8,128)(2,1)S(1)}, u32[]{:S(2)}, u32[]{:S(2)}) collective-permute-start(bf16[1,128,512]{2,1,0:T(8,128)(2,1)S(1)} %get-tuple-element.36), channel_id=1, source_target_pairs={{0,2},{2,4},{4,6},{6,8},{8,10},{10,12},{12,14},{14,0},{1,3},{3,5},... | collective-permute-start | bytes 393224 | tf_op jit(solution)/shard_map/ppermute | solution.py:332
  49.9 1.1 %copy-start = (bf16[400,1024]{1,0:T(8,128)(2,1)S(1)}, bf16[400,1024]{1,0:T(8,128)(2,1)}, u32[]{:S(2)}) copy-start(bf16[400,1024]{1,0:T(8,128)(2,1)} %get-tuple-element.24.message_ref) | copy-start | bytes 2457604
  51.0 1.0 %copy-start.1 = (f32[1024,128]{1,0:T(8,128)S(1)}, f32[1024,128]{1,0:T(8,128)}, u32[]{:S(2)}) copy-start(f32[1024,128]{1,0:T(8,128)} %get-tuple-element.25.right_ref) | copy-start | bytes 1572868
  52.1 0.9 %copy-start.2 = (bf16[2,128,512]{2,1,0:T(8,128)(2,1)S(1)}, bf16[2,128,512]{2,1,0:T(8,128)(2,1)}, u32[]{:S(2)}) copy-start(bf16[2,128,512]{2,1,0:T(8,128)(2,1)} %get-tuple-element.26.pair_ref) | copy-start | bytes 786436

commit v9 on v8

--- a/solution.py
+++ b/solution.py
@@ -22,33 +22,32 @@
     return lax.dot_general(a, b, (dims, ((), ())), preferred_element_type=jnp.float32, precision=precision)
 
 
-def pair_kernel(own_ref, other_ref, *refs):
-    out_ref = refs[-1]
-    piece = own_ref.shape[1]
-    out_ref[:, :piece, :] = own_ref[...]
-    out_ref[:, piece:, :] = other_ref[...]
-
-
-def pair_up(own, other, messages):
-    examples, piece, seq_dev = own.shape
+def pair_kernel(other_hbm, own_hbm, *refs):
+    out_ref, sem = refs[-2:]
+    piece = other_hbm.shape[1]
+    copy = pltpu.make_async_copy(other_hbm, out_ref.at[:, pl.ds(piece, piece)], sem)
+    copy.start()
+    copy.wait()
+
+
+def pair_up(pair, other, messages):
+    arrays = [pair, *messages]
     *messages, pair = pl.pallas_call(
         pair_kernel,
-        out_shape=[
-            *[jax.ShapeDtypeStruct(message.shape, message.dtype) for message in messages],
-            jax.ShapeDtypeStruct((examples, NY * piece, seq_dev), own.dtype),
-        ],
-        in_specs=[VMEM, VMEM] + [HBM] * len(messages),
-        out_specs=[HBM] * len(messages) + [VMEM],
-        input_output_aliases={2 + index: index for index in range(len(messages))},
+        out_shape=[jax.ShapeDtypeStruct(array.shape, array.dtype) for array in [*messages, pair]],
+        in_specs=[HBM] * (1 + len(arrays)),
+        out_specs=[HBM] * len(arrays),
+        scratch_shapes=[pltpu.SemaphoreType.DMA],
+        input_output_aliases={1: len(messages)} | {2 + index: index for index in range(len(messages))},
         compiler_params=pltpu.CompilerParams(vmem_limit_bytes=62 * MIB),
         name="pair_up",
-    )(own, other, *messages)
+    )(other, *arrays)
     return pair, messages
 
 
-def token_kernel(chunk, scale, lengths_ref, tokens_hbm, gate_hbm, up_hbm, gate_in_hbm, up_in_hbm, down_in_hbm, down_hbm, gate_out_hbm, up_out_hbm, *refs):
-    messages, right_ref = refs[: NX - 1], refs[NX - 1]
-    tokens_ref, weight_ref, in_ref, down_in_ref, out_ref, total_ref, sems = refs[NX:]
+def token_kernel(chunk, scale, lengths_ref, tokens_hbm, gate_hbm, up_hbm, gate_in_hbm, up_in_hbm, down_in_hbm, down_hbm, gate_out_hbm, up_out_hbm, grad_hbm, *refs):
+    messages, (right_ref, pair_ref) = refs[: NX - 1], refs[NX - 1 : NX + 1]
+    tokens_ref, weight_ref, in_ref, down_in_ref, out_ref, total_ref, sems = refs[NX + 1 :]
     rows, model_width = tokens_hbm.shape
     hidden = gate_hbm.shape[1]
     rank = gate_in_hbm.shape[0]
@@ -74,13 +73,11 @@
     width, half = model_width // NX, hidden // 2
     core = lax.axis_index("sc")
     pairs = [(gate_out_hbm, out_ref.at[pl.ds(0, rank)]), (up_out_hbm, out_ref.at[pl.ds(rank, rank)])]
+    pairs.append((grad_hbm, pair_ref.at[:, pl.ds(0, grad_hbm.shape[1])]))
     for step, message in enumerate(messages, 1):
         start = pl.multiple_of(lax.rem(lax.axis_index("x") + step, NX) * width, width)
-        columns = pl.ds(start, width)
-        if step == 2:
-            pairs.append((down_hbm.at[:, columns], message.at[pl.ds(0, hidden)]))
-        else:
-            pairs.append((down_hbm.at[pl.ds(core * half, half), columns], message.at[pl.ds(top, half)]))
+        bottom = message.shape[0] - half - FOLD
+        pairs.append((down_hbm.at[pl.ds(core * half, half), pl.ds(start, width)], message.at[pl.ds(bottom, half)]))
     extra = [pltpu.make_async_copy(a, b, sems.at[count + k]) for k, (a, b) in enumerate(pairs)]
     for copy in extra:
         copy.start()
@@ -128,7 +125,7 @@
             message[-FOLD:, block * hidden : (block + 1) * hidden] = out_ref[rows_of, :]
 
 
-def token_stage(tokens, gate_weight, up_weight, gate_in, up_in, down_in, down_weight, gate_out, up_out, lengths, scale):
+def token_stage(tokens, gate_weight, up_weight, gate_in, up_in, down_in, down_weight, gate_out, up_out, own_grad, lengths, scale):
     rows, width = tokens.shape
     hidden = gate_weight.shape[1]
     rank = gate_in.shape[0]
@@ -137,12 +134,13 @@
         lambda *refs: token_kernel(chunk, scale, *refs),
         out_shape=[
             jax.ShapeDtypeStruct((2 * hidden + hidden // 2 + rank + FOLD, rows), jnp.bfloat16),
-            jax.ShapeDtypeStruct((hidden + FOLD, rows), jnp.bfloat16),
+            jax.ShapeDtypeStruct((hidden // 2 + FOLD, rows), jnp.bfloat16),
             jax.ShapeDtypeStruct((2 * hidden + hidden // 2 + rank + FOLD, rows), jnp.bfloat16),
             jax.ShapeDtypeStruct((rows, 2 * rank), jnp.float32),
+            jax.ShapeDtypeStruct((own_grad.shape[0], NY * own_grad.shape[1], own_grad.shape[2]), own_grad.dtype),
         ],
-        in_specs=[pl.BlockSpec(memory_space=pltpu.SMEM)] + [HBM] * 9,
-        out_specs=[VMEM] * NX,
+        in_specs=[pl.BlockSpec(memory_space=pltpu.SMEM)] + [HBM] * 10,
+        out_specs=[VMEM] * NX + [HBM],
         scratch_shapes=[
             pltpu.VMEM((rows, width), jnp.bfloat16),
             pltpu.VMEM((width, 2 * hidden), jnp.bfloat16),
@@ -150,36 +148,39 @@
             pltpu.VMEM((rank, hidden), jnp.bfloat16),
             pltpu.VMEM((2 * rank, hidden), jnp.bfloat16),
             pltpu.VMEM((rows, 2 * hidden), jnp.float32),
-            pltpu.SemaphoreType.DMA((5 * (width // chunk) + 2 + NX,)),
+            pltpu.SemaphoreType.DMA((5 * (width // chunk) + 3 + NX,)),
         ],
         compiler_params=pltpu.CompilerParams(vmem_limit_bytes=61 * MIB),
         cost_estimate=pl.CostEstimate(
             flops=2 * rows * width * 512, bytes_accessed=16 * MIB, transcendentals=rows * hidden
         ),
         name="token_stage",
-    )(lengths, tokens, gate_weight, up_weight, gate_in, up_in, down_in, down_weight, gate_out, up_out)
-
-
-def forward_kernel(before_ref, after_ref, first_ref, second_ref, swap_ref):
+    )(lengths, tokens, gate_weight, up_weight, gate_in, up_in, down_in, down_weight, gate_out, up_out, own_grad)
+
+
+def forward_kernel(*refs):
+    messages, (first_ref, second_ref, swap_ref) = refs[:-3], refs[-3:]
     rows = first_ref.shape[0]
-    half = swap_ref.shape[0] // 2
-    first_ref[...] = before_ref[:rows, :]
-    second_ref[...] = after_ref[rows : 2 * rows, :]
-    swap_ref[:half, :] = before_ref[2 * rows : 2 * rows + half, :]
-    swap_ref[half:, :] = after_ref[2 * rows : 2 * rows + half, :]
-
-
-def halves(before, after, rows, half):
-    shape = jax.ShapeDtypeStruct((rows, before.shape[1]), before.dtype)
-    swap = jax.ShapeDtypeStruct((2 * half, before.shape[1]), before.dtype)
+    half = swap_ref.shape[0] // len(messages)
+    first_ref[...] = messages[0][:rows, :]
+    second_ref[...] = messages[-1][rows : 2 * rows, :]
+    for index, message in enumerate(messages):
+        bottom = message.shape[0] - half - FOLD
+        swap_ref[index * half : (index + 1) * half, :] = message[bottom : bottom + half, :]
+
+
+def halves(messages, rows, half):
+    columns = messages[0].shape[1]
+    shape = jax.ShapeDtypeStruct((rows, columns), messages[0].dtype)
+    swap = jax.ShapeDtypeStruct((len(messages) * half, columns), messages[0].dtype)
     return pl.pallas_call(
         forward_kernel,
         out_shape=[shape, shape, swap],
-        in_specs=[VMEM] * 2,
+        in_specs=[VMEM] * len(messages),
         out_specs=[VMEM] * 3,
         compiler_params=pltpu.CompilerParams(vmem_limit_bytes=8 * MIB),
         name="halves",
-    )(before, after)
+    )(*messages)
 
 
 def keep_kernel(message_ref, right_ref, pair_ref, factors_out, right_out, pair_out):
@@ -221,13 +222,11 @@
     projs[:rank, :hidden] = gate_out_ref[...]
     projs[rank:, :hidden] = up_out_ref[...]
     for step, message in enumerate(messages, 1):
-        if step == 2:
-            weights[step * hidden : (step + 1) * hidden, :] = message[:hidden, :]
-        else:
-            mine = pl.ds(pl.multiple_of(step * hidden + core * half, half), half)
-            theirs = pl.ds(pl.multiple_of(step * hidden + (1 - core) * half, half), half)
-            weights[mine, :] = message[top : top + half, :]
-            weights[theirs, :] = swap_ref[step // 2 * half : (step // 2 + 1) * half, :]
+        bottom = message.shape[0] - half - FOLD
+        mine = pl.ds(pl.multiple_of(step * hidden + core * half, half), half)
+        theirs = pl.ds(pl.multiple_of(step * hidden + (1 - core) * half, half), half)
+        weights[mine, :] = message[bottom : bottom + half, :]
+        weights[theirs, :] = swap_ref[(step - 1) * half : step * half, :]
         columns = slice(step * hidden, (step + 1) * hidden)
         for block in range(2 * rank // FOLD):
             folded = message[-FOLD:, block * hidden : (block + 1) * hidden]
@@ -377,15 +376,16 @@
         down_weight,
         gate_out,
         up_out,
+        own_grad,
         lengths,
         scale,
     )
-    sent, right = sent[: NX - 1], sent[NX - 1]
-    pair, sent = pair_up(own_grad, other_grad, sent)
+    sent, (right, pair) = sent[: NX - 1], sent[NX - 1 :]
+    pair, sent = pair_up(pair, other_grad, sent)
     messages = [lax.ppermute(piece, "x", shifted(NX, step)) for step, piece in enumerate(sent, 1)]
     hidden, rank = gate_weight.shape[1], gate_out.shape[0]
     rows = 2 * hidden + rank
-    first, second, swap = halves(messages[0], messages[2], rows // 2, hidden // 2)
+    first, second, swap = halves(messages, rows // 2, hidden // 2)
     swap = lax.ppermute(swap, "sc", shifted(SEQ_PARTS[1], 1))
     far = [lax.ppermute(first, "x", shifted(NX, 1)), lax.ppermute(second, "x", shifted(NX, -1))]
     blocks, far_block = ring_z(pair)

time: 94.6 us -> 98.9 us (1.045)
  waiting for transfers between devices: 18.6 us -> 13.6 us
  Pallas kernels: 14.4 us -> 17.7 us
  starting transfers between devices: 22.6 us -> 25.7 us
  blocking collectives: 33.8 us -> 36.7 us
    ppermute x3, waiting for transfers between devices: 9.14 us -> 0.01 us  [ring_z(): up.append(lax.ppermute(up[-1], 'z', shifted(NZ, -1)))]
    ppermute x3, waiting for transfers between devices: 5.09 us -> 10.4 us  [ring_z(): down.append(lax.ppermute(down[-1], 'z', shifted(NZ, 1)))]
    ppermute x1, starting transfers between devices: 0.67 us -> 4.3 us  [ring_z(): lax.ppermute(first, 'z', shifted(NZ, -1))]
    pallas_call x1, Pallas kernels: 1.69 us -> 5.08 us  [pair_up(): pl.pallas_call(pair_kernel, out_shape=[jax.ShapeDtypeStruct(array.shape,...]
    all_to_all x1, blocking collectives: 13.6 us -> 16.5 us  [sum_everywhere(): pieces = lax.all_to_all(pieces, ('sy', 'sc', 'z'), 0, 0, tiled=True)]
    ppermute x3, starting transfers between devices: 13.1 us -> 10.4 us  [ring_z(): up.append(lax.ppermute(up[-1], 'z', shifted(NZ, -1)))]
    ppermute x3, starting transfers between devices: 0.01 us -> 1.92 us  [ring_z(): down.append(lax.ppermute(down[-1], 'z', shifted(NZ, 1)))]
    ppermute x3, waiting for transfers between devices: 1.46 us -> 0.26 us  [shards(): lax.ppermute(piece, 'x', shifted(NX, step))]
  transfers between devices with their start and end apart: 15 -> 15, of which waited for: 6 -> 6; matrix products, arithmetic and copies ran while one was open for 0% -> 0% of each run, Pallas kernels for 10% -> 9%
where the time goes in v9:
time: 98.9 us; the launch traced here: 98.6 us
  blocking collectives  36.7 us (37%)
  starting transfers between devices  25.7 us (26%)
  Pallas kernels  17.7 us (18%)
  waiting for transfers between devices  13.6 us (14%)
  local copies, waits for them, and re-layouts  4.63 us (5%)
    all_to_all x1, blocking collectives, sum_everywhere(): blocks = lax.all_to_all(spread, ('x', 'z', 'yh'), 0, 0, tiled=True)  20.2 us
    all_to_all x1, blocking collectives, sum_everywhere(): pieces = lax.all_to_all(pieces, ('sy', 'sc', 'z'), 0, 0, tiled=True)  16.5 us
    ppermute x3, waiting for transfers between devices, ring_z(): down.append(lax.ppermute(down[-1], 'z', shifted(NZ, 1)))  10.4 us
    ppermute x3, starting transfers between devices, ring_z(): up.append(lax.ppermute(up[-1], 'z', shifted(NZ, -1)))  10.4 us
    pallas_call x1, Pallas kernels, token_stage(): pl.pallas_call(lambda *refs: token_kernel(chunk, scale, *refs), out_shape...  9.03 us
    pallas_call x1, Pallas kernels, pair_up(): pl.pallas_call(pair_kernel, out_shape=[jax.ShapeDtypeStruct(array.shape,...  5.08 us
    ppermute x1, starting transfers between devices, ring_z(): lax.ppermute(first, 'z', shifted(NZ, -1))  4.3 us
    unnamed x17, local copies, waits for them, and re-layouts  3.8 us
  transfers between devices with their start and end apart: 15, of which 6 were waited for; matrix products, arithmetic and copies ran while one was open for 0% of the time, Pallas kernels for 9%

profile of v9, /device:TPU:6, one launch (start us, length us, event | category | flops | bytes accessed | tf_op | source)
XLA Modules:
  0.0 98.6 jit_solution(5460350853308084335)
XLA Ops:
  0.0 3.2 %collective-permute-start = (bf16[2,64,512]{2,1,0:T(8,128)(2,1)}, bf16[2,64,512]{2,1,0:T(8,128)(2,1)S(1)}, u32[]{:S(2)}, u32[]{:S(2)}) collective-permute-start(bf16[2,64,512]{2,1,0:T(8,128)(2,1)} %bitcast.26), channel_id=1, source_target_pairs={{0,1},{1,0},{2,3},{3,2},{4,5},{5,4},{6,7},{7,6},{8,9},{9,8},{10,11... | collective-permute-start | bytes 393224 | tf_op jit(solution)/shard_map/ppermute | solution.py:367
  3.2 0.0 copy-start.3
  3.2 0.0 copy-start.4
  3.2 0.0 copy-start.5
  3.2 0.0 copy-start.6
  3.2 9.0 %token_stage.1 = (bf16[400,1024]{1,0:T(8,128)(2,1)}, bf16[80,1024]{1,0:T(8,128)(2,1)}, bf16[400,1024]{1,0:T(8,128)(2,1)}, f32[1024,128]{1,0:T(8,128)}, bf16[2,128,512]{2,1,0:T(8,128)(2,1)}) custom-call(s32[2]{0:T(128)} %refs_0_.1, bf16[1024,4096]{1,0:T(8,128)(2,1)} %bitcast.23, bf16[4096,128]{1,0:T(8,128)(2,1)} %refs_2_.1, bf16[4096,128]{1,0:T(8,128)(2,1)} %refs_3_.1, ...), custom_call_target="tpu_custom_call" | custom-call | flops 4294967296 | bytes 16777216 | tf_op jit(solution)/shard_map/token_stage/pallas_call | solution.py:133
  12.2 0.0 collective-permute-done.other_hbm
  12.3 0.0 copy-start.7
  12.3 0.6 copy-done.7
  12.9 5.1 %pair_up.1 = (bf16[400,1024]{1,0:T(8,128)(2,1)}, bf16[80,1024]{1,0:T(8,128)(2,1)}, bf16[400,1024]{1,0:T(8,128)(2,1)}, bf16[2,128,512]{2,1,0:T(8,128)(2,1)}) custom-call(bf16[2,64,512]{2,1,0:T(8,128)(2,1)} %copy-done.7, bf16[2,128,512]{2,1,0:T(8,128)(2,1)} %get-tuple-element.22.own_hbm, ...), custom_call_target="tpu_custom_call", output_to_operand_aliasing={{3}: (1, {}), {0}: (2, {}), {1}: (3, {}), {2}: (4, {})} | custom-call | tf_op jit(solution)/shard_map/pair_up/pallas_call | solution.py:35
  18.0 0.5 collective-permute-start.1
  18.5 1.6 %collective-permute-start.3 = (bf16[400,1024]{1,0:T(8,128)(2,1)}, bf16[400,1024]{1,0:T(8,128)(2,1)S(1)}, u32[]{:S(2)}, u32[]{:S(2)}) collective-permute-start(bf16[400,1024]{1,0:T(8,128)(2,1)} %get-tuple-element.32), channel_id=1, source_target_pairs={{0,48},{16,0},{32,16},{48,32},{1,49},{17,1},{33,17},{49,33},{2,50}... | collective-permute-start | bytes 2457608 | tf_op jit(solution)/shard_map/ppermute | solution.py:385
  20.1 1.9 %collective-permute-start.10 = (bf16[2,128,512]{2,1,0:T(8,128)(2,1)}, bf16[2,128,512]{2,1,0:T(8,128)(2,1)S(1)}, u32[]{:S(2)}, u32[]{:S(2)}) collective-permute-start(bf16[2,128,512]{2,1,0:T(8,128)(2,1)} %get-tuple-element.28.pair_ref), channel_id=1, source_target_pairs={{0,2},{2,4},{4,6},{6,8},{8,10},{10,12},{12,14},{14,0},{1,3},{3,5},... | collective-permute-start | bytes 786440 | tf_op jit(solution)/shard_map/ppermute | solution.py:329
  22.0 3.9 %collective-permute-start.7 = (bf16[2,128,512]{2,1,0:T(8,128)(2,1)}, bf16[2,128,512]{2,1,0:T(8,128)(2,1)S(1)}, u32[]{:S(2)}, u32[]{:S(2)}) collective-permute-start(bf16[2,128,512]{2,1,0:T(8,128)(2,1)} %get-tuple-element.28.pair_ref), channel_id=1, source_target_pairs={{0,14},{2,0},{4,2},{6,4},{8,6},{10,8},{12,10},{14,12},{1,15},{3,1}... | collective-permute-start | bytes 786440 | tf_op jit(solution)/shard_map/ppermute | solution.py:328
  26.0 5.7 %collective-permute-done.10.refs_13_ = bf16[2,128,512]{2,1,0:T(8,128)(2,1)S(1)} collective-permute-done((bf16[2,128,512]{2,1,0:T(8,128)(2,1)}, bf16[2,128,512]{2,1,0:T(8,128)(2,1)S(1)}, u32[]{:S(2)}, u32[]{:S(2)}) %collective-permute-start.10) | collective-permute-done | bytes 262176 | tf_op jit(solution)/shard_map/ppermute | solution.py:329
  31.6 0.0 collective-permute-start.11
  31.6 0.0 collective-permute-done.7.refs_8_
  31.6 3.2 %collective-permute-start.8 = (bf16[2,128,512]{2,1,0:T(8,128)(2,1)S(1)}, bf16[2,128,512]{2,1,0:T(8,128)(2,1)S(1)}, u32[]{:S(2)}, u32[]{:S(2)}) collective-permute-start(bf16[2,128,512]{2,1,0:T(8,128)(2,1)S(1)} %collective-permute-done.7.refs_8_), channel_id=1, source_target_pairs={{0,14},{2,0},{4,2},{6,4},{8,6},{10,8},{12,10},{14,12},{1,15},{3,1}... | collective-permute-start | bytes 786440 | tf_op jit(solution)/shard_map/ppermute | solution.py:328
  34.9 1.4 %collective-permute-start.2 = (bf16[80,1024]{1,0:T(8,128)(2,1)}, bf16[80,1024]{1,0:T(8,128)(2,1)S(1)}, u32[]{:S(2)}, u32[]{:S(2)}) collective-permute-start(bf16[80,1024]{1,0:T(8,128)(2,1)} %get-tuple-element.31), channel_id=1, source_target_pairs={{0,32},{16,48},{32,0},{48,16},{1,33},{17,49},{33,1},{49,17},{2,34}... | collective-permute-start | bytes 491528 | tf_op jit(solution)/shard_map/ppermute | solution.py:385
  36.3 3.1 %collective-permute-done.11.refs_12_ = bf16[2,128,512]{2,1,0:T(8,128)(2,1)S(1)} collective-permute-done((bf16[2,128,512]{2,1,0:T(8,128)(2,1)S(1)}, bf16[2,128,512]{2,1,0:T(8,128)(2,1)S(1)}, u32[]{:S(2)}, u32[]{:S(2)}) %collective-permute-start.11) | collective-permute-done | bytes 262176 | tf_op jit(solution)/shard_map/ppermute | solution.py:329
  39.4 0.0 collective-permute-start.12
  39.4 0.0 collective-permute-done.8.refs_9_
  39.4 3.2 %collective-permute-start.9 = (bf16[2,128,512]{2,1,0:T(8,128)(2,1)S(1)}, bf16[2,128,512]{2,1,0:T(8,128)(2,1)S(1)}, u32[]{:S(2)}, u32[]{:S(2)}) collective-permute-start(bf16[2,128,512]{2,1,0:T(8,128)(2,1)S(1)} %collective-permute-done.8.refs_9_), channel_id=1, source_target_pairs={{0,14},{2,0},{4,2},{6,4},{8,6},{10,8},{12,10},{14,12},{1,15},{3,1}... | collective-permute-start | bytes 786440 | tf_op jit(solution)/shard_map/ppermute | solution.py:328
  42.6 0.1 collective-permute-done.2.refs_1_.refs_2_
  42.7 0.0 collective-permute-done.1.refs_0_.refs_1_
  42.7 0.2 collective-permute-done.3.refs_2_.refs_3_
  42.9 0.1 halves.1
  43.0 0.1 collective-permute-start.6
  43.1 1.7 %collective-permute-start.4 = (bf16[160,1024]{1,0:T(8,128)(2,1)S(1)}, bf16[160,1024]{1,0:T(8,128)(2,1)S(1)}, u32[]{:S(2)}, u32[]{:S(2)}) collective-permute-start(bf16[160,1024]{1,0:T(8,128)(2,1)S(1)} %get-tuple-element.33), channel_id=1, source_target_pairs={{0,16},{16,32},{32,48},{48,0},{1,17},{17,33},{33,49},{49,1},{2,18}... | collective-permute-start | bytes 983048 | tf_op jit(solution)/shard_map/ppermute | solution.py:390
  44.8 0.6 collective-permute-start.5
  45.4 1.6 %collective-permute-done.12.down_ref.refs_11_ = bf16[2,128,512]{2,1,0:T(8,128)(2,1)S(1)} collective-permute-done((bf16[2,128,512]{2,1,0:T(8,128)(2,1)S(1)}, bf16[2,128,512]{2,1,0:T(8,128)(2,1)S(1)}, u32[]{:S(2)}, u32[]{:S(2)}) %collective-permute-start.12) | collective-permute-done | bytes 262176 | tf_op jit(solution)/shard_map/ppermute | solution.py:329
  47.0 0.0 collective-permute-done.9.up_ref.refs_10_
  47.0 4.3 %collective-permute-start.13 = (bf16[1,128,512]{2,1,0:T(8,128)(2,1)S(1)}, bf16[1,128,512]{2,1,0:T(8,128)(2,1)S(1)}, u32[]{:S(2)}, u32[]{:S(2)}) collective-permute-start(bf16[1,128,512]{2,1,0:T(8,128)(2,1)S(1)} %get-tuple-element.37), channel_id=1, source_target_pairs={{0,14},{2,0},{4,2},{6,4},{8,6},{10,8},{12,10},{14,12},{1,15},{3,1}... | collective-permute-start | bytes 393224 | tf_op jit(solution)/shard_map/ppermute | solution.py:331
  51.3 0.0 collective-permute-start.14
  51.3 0.0 copy-start
  51.3 1.1 %copy-done = bf16[400,1024]{1,0:T(8,128)(2,1)S(1)} copy-done((bf16[400,1024]{1,0:T(8,128)(2,1)S(1)}, bf16[400,1024]{1,0:T(8,128)(2,1)}, u32[]{:S(2)}) %copy-start) | copy-done | bytes 819224
  52.5 0.0 copy-start.1
  52.5 0.9 copy-done.1
  53.4 0.0 copy-start.2
  53.4 1.0 %copy-done.2 = f32[1024,128]{1,0:T(8,128)S(1)} copy-done((f32[1024,128]{1,0:T(8,128)S(1)}, f32[1024,128]{1,0:T(8,128)}, u32[]{:S(2)}) %copy-start.2) | copy-done | bytes 524312
  54.5 0.1 keep.1
  54.6 0.0 collective-permute-done.13.refs_14_
  54.6 2.9 %collective-permute-done.14.refs_15_ = bf16[1,128,512]{2,1,0:T(8,128)(2,1)S(1)} collective-permute-done((bf16[1,128,512]{2,1,0:T(8,128)(2,1)S(1)}, bf16[1,128,512]{2,1,0:T(8,128)(2,1)S(1)}, u32[]{:S(2)}, u32[]{:S(2)}) %collective-permute-start.14) | collective-permute-done | bytes 131104 | tf_op jit(solution)/shard_map/ppermute | solution.py:331
  57.5 0.0 collective-permute-done.4.refs_4_
  57.5 0.0 collective-permute-done.5.refs_5_
  57.5 0.0 collective-permute-done.6.refs_6_
  57.5 0.0 copy-done.3
  57.5 0.0 copy-done.4
  57.5 0.0 copy-done.5
  57.5 0.0 copy-done.6
  57.5 3.4 %tail_stage.1 = f32[6,64,64]{2,1,0:T(8,128)S(1)} custom-call(bf16[128,4096]{1,0:T(8,128)(2,1)S(1)} %copy-done.3, bf16[64,128]{1,0:T(8,128)(2,1)S(1)} %bitcast.17, bf16[64,128]{1,0:T(8,128)(2,1)S(1)} %bitcast.19, bf16[64,4096]{1,0:T(8,128)(2,1)S(1)} %bitcast.15, f32[1024,128]{1,0:T(8,128)S(1)} %get-tuple-element.29.right_ref, ...), custom_call_target="tpu_custom_call" | custom-call | flops 4000000000 | bytes 8388608 | tf_op jit(solution)/shard_map/tail_stage/pallas_call | solution.py:292
  61.0 0.1 reshape_reshape.6
  61.1 0.1 copy.34
  61.2 16.5 %all_to_all.10 = f32[32,6,128]{2,1,0:T(8,128)S(1)} all-to-all(f32[32,6,128]{2,1,0:T(8,128)S(1)} %bitcast.21), channel_id=1, replica_groups=mesh['sy'=2,'sc'=2,'x'=4,'z'=8,'yh'=2] {'sy','sc','z'}, dimensions={0} | all-to-all | bytes 196608 | tf_op jit(solution)/shard_map/all_to_all | solution.py:340
  77.7 20.2 %all_to_all.11 = f32[64,6,128]{2,1,0:T(8,128)S(1)} all-to-all(f32[64,6,128]{2,1,0:T(8,128)S(1)} %broadcast_in_dim.2), channel_id=1, replica_groups=mesh['sy'=2,'sc'=2,'x'=4,'z'=8,'yh'=2] {'x','z','yh'}, dimensions={0} | all-to-all | bytes 393216 | tf_op jit(solution)/shard_map/all_to_all | solution.py:343
  97.9 0.6 copy.28
  (6 shorter events, 0.1 us)
Async XLA Ops:
  0.0 12.2 %collective-permute-start = (bf16[2,64,512]{2,1,0:T(8,128)(2,1)}, bf16[2,64,512]{2,1,0:T(8,128)(2,1)S(1)}, u32[]{:S(2)}, u32[]{:S(2)}) collective-permute-start(bf16[2,64,512]{2,1,0:T(8,128)(2,1)} %bitcast.26), channel_id=1, source_target_pairs={{0,1},{1,0},{2,3},{3,2},{4,5},{5,4},{6,7},{7,6},{8,9},{9,8},{10,11... | collective-permute-start | bytes 393224 | tf_op jit(solution)/shard_map/ppermute | solution.py:367
  3.2 54.3 %copy-start.3 = (bf16[128,4096]{1,0:T(8,128)(2,1)S(1)}, bf16[128,4096]{1,0:T(8,128)(2,1)}, u32[]{:S(2)}) copy-start(bf16[128,4096]{1,0:T(8,128)(2,1)} %weight_ref.1) | copy-start | bytes 3145732
  3.2 54.3 %copy-start.4 = (bf16[4096,64]{0,1:T(8,128)(2,1)S(1)}, bf16[4096,64]{0,1:T(8,128)(2,1)}, u32[]{:S(2)}) copy-start(bf16[4096,64]{0,1:T(8,128)(2,1)} %param.22) | copy-start | bytes 1572868
  3.2 54.3 %copy-start.5 = (bf16[128,64]{0,1:T(8,128)(2,1)S(1)}, bf16[128,64]{0,1:T(8,128)(2,1)}, u32[]{:S(2)}) copy-start(bf16[128,64]{0,1:T(8,128)(2,1)} %param.18) | copy-start | bytes 49156
  3.2 54.3 %copy-start.6 = (bf16[128,64]{0,1:T(8,128)(2,1)S(1)}, bf16[128,64]{0,1:T(8,128)(2,1)}, u32[]{:S(2)}) copy-start(bf16[128,64]{0,1:T(8,128)(2,1)} %param.20) | copy-start | bytes 49156
  12.3 0.7 copy-start.7
  18.0 24.7 %collective-permute-start.1 = (bf16[400,1024]{1,0:T(8,128)(2,1)}, bf16[400,1024]{1,0:T(8,128)(2,1)S(1)}, u32[]{:S(2)}, u32[]{:S(2)}) collective-permute-start(bf16[400,1024]{1,0:T(8,128)(2,1)} %get-tuple-element.26.message_ref), channel_id=1, source_target_pairs={{0,16},{16,32},{32,48},{48,0},{1,17},{17,33},{33,49},{49,1},{2,18}... | collective-permute-start | bytes 2457608 | tf_op jit(solution)/shard_map/ppermute | solution.py:385
  18.5 24.4 %collective-permute-start.3 = (bf16[400,1024]{1,0:T(8,128)(2,1)}, bf16[400,1024]{1,0:T(8,128)(2,1)S(1)}, u32[]{:S(2)}, u32[]{:S(2)}) collective-permute-start(bf16[400,1024]{1,0:T(8,128)(2,1)} %get-tuple-element.32), channel_id=1, source_target_pairs={{0,48},{16,0},{32,16},{48,32},{1,49},{17,1},{33,17},{49,33},{2,50}... | collective-permute-start | bytes 2457608 | tf_op jit(solution)/shard_map/ppermute | solution.py:385
  20.1 11.5 %collective-permute-start.10 = (bf16[2,128,512]{2,1,0:T(8,128)(2,1)}, bf16[2,128,512]{2,1,0:T(8,128)(2,1)S(1)}, u32[]{:S(2)}, u32[]{:S(2)}) collective-permute-start(bf16[2,128,512]{2,1,0:T(8,128)(2,1)} %get-tuple-element.28.pair_ref), channel_id=1, source_target_pairs={{0,2},{2,4},{4,6},{6,8},{8,10},{10,12},{12,14},{14,0},{1,3},{3,5},... | collective-permute-start | bytes 786440 | tf_op jit(solution)/shard_map/ppermute | solution.py:329
  22.0 9.6 %collective-permute-start.7 = (bf16[2,128,512]{2,1,0:T(8,128)(2,1)}, bf16[2,128,512]{2,1,0:T(8,128)(2,1)S(1)}, u32[]{:S(2)}, u32[]{:S(2)}) collective-permute-start(bf16[2,128,512]{2,1,0:T(8,128)(2,1)} %get-tuple-element.28.pair_ref), channel_id=1, source_target_pairs={{0,14},{2,0},{4,2},{6,4},{8,6},{10,8},{12,10},{14,12},{1,15},{3,1}... | collective-permute-start | bytes 786440 | tf_op jit(solution)/shard_map/ppermute | solution.py:328
  31.6 7.8 %collective-permute-start.11 = (bf16[2,128,512]{2,1,0:T(8,128)(2,1)S(1)}, bf16[2,128,512]{2,1,0:T(8,128)(2,1)S(1)}, u32[]{:S(2)}, u32[]{:S(2)}) collective-permute-start(bf16[2,128,512]{2,1,0:T(8,128)(2,1)S(1)} %collective-permute-done.10.refs_13_), channel_id=1, source_target_pairs={{0,2},{2,4},{4,6},{6,8},{8,10},{10,12},{12,14},{14,0},{1,3},{3,5},... | collective-permute-start | bytes 786440 | tf_op jit(solution)/shard_map/ppermute | solution.py:329
  31.6 7.8 %collective-permute-start.8 = (bf16[2,128,512]{2,1,0:T(8,128)(2,1)S(1)}, bf16[2,128,512]{2,1,0:T(8,128)(2,1)S(1)}, u32[]{:S(2)}, u32[]{:S(2)}) collective-permute-start(bf16[2,128,512]{2,1,0:T(8,128)(2,1)S(1)} %collective-permute-done.7.refs_8_), channel_id=1, source_target_pairs={{0,14},{2,0},{4,2},{6,4},{8,6},{10,8},{12,10},{14,12},{1,15},{3,1}... | collective-permute-start | bytes 786440 | tf_op jit(solution)/shard_map/ppermute | solution.py:328
  34.9 7.9 %collective-permute-start.2 = (bf16[80,1024]{1,0:T(8,128)(2,1)}, bf16[80,1024]{1,0:T(8,128)(2,1)S(1)}, u32[]{:S(2)}, u32[]{:S(2)}) collective-permute-start(bf16[80,1024]{1,0:T(8,128)(2,1)} %get-tuple-element.31), channel_id=1, source_target_pairs={{0,32},{16,48},{32,0},{48,16},{1,33},{17,49},{33,1},{49,17},{2,34}... | collective-permute-start | bytes 491528 | tf_op jit(solution)/shard_map/ppermute | solution.py:385
  39.4 7.6 %collective-permute-start.12 = (bf16[2,128,512]{2,1,0:T(8,128)(2,1)S(1)}, bf16[2,128,512]{2,1,0:T(8,128)(2,1)S(1)}, u32[]{:S(2)}, u32[]{:S(2)}) collective-permute-start(bf16[2,128,512]{2,1,0:T(8,128)(2,1)S(1)} %collective-permute-done.11.refs_12_), channel_id=1, source_target_pairs={{0,2},{2,4},{4,6},{6,8},{8,10},{10,12},{12,14},{14,0},{1,3},{3,5},... | collective-permute-start | bytes 786440 | tf_op jit(solution)/shard_map/ppermute | solution.py:329
  39.4 7.6 %collective-permute-start.9 = (bf16[2,128,512]{2,1,0:T(8,128)(2,1)S(1)}, bf16[2,128,512]{2,1,0:T(8,128)(2,1)S(1)}, u32[]{:S(2)}, u32[]{:S(2)}) collective-permute-start(bf16[2,128,512]{2,1,0:T(8,128)(2,1)S(1)} %collective-permute-done.8.refs_9_), channel_id=1, source_target_pairs={{0,14},{2,0},{4,2},{6,4},{8,6},{10,8},{12,10},{14,12},{1,15},{3,1}... | collective-permute-start | bytes 786440 | tf_op jit(solution)/shard_map/ppermute | solution.py:328
  43.0 14.5 %collective-permute-start.6 = (bf16[192,1024]{1,0:T(8,128)(2,1)S(1)}, bf16[192,1024]{1,0:T(8,128)(2,1)S(1)}, u32[]{:S(2)}, u32[]{:S(2)}) collective-permute-start(bf16[192,1024]{1,0:T(8,128)(2,1)S(1)} %get-tuple-element.35), channel_id=1, source_target_pairs={{0,64},{64,0},{1,65},{65,1},{2,66},{66,2},{3,67},{67,3},{4,68},{68... | collective-permute-start | bytes 1179656 | tf_op jit(solution)/shard_map/ppermute | solution.py:389
  43.1 14.4 %collective-permute-start.4 = (bf16[160,1024]{1,0:T(8,128)(2,1)S(1)}, bf16[160,1024]{1,0:T(8,128)(2,1)S(1)}, u32[]{:S(2)}, u32[]{:S(2)}) collective-permute-start(bf16[160,1024]{1,0:T(8,128)(2,1)S(1)} %get-tuple-element.33), channel_id=1, source_target_pairs={{0,16},{16,32},{32,48},{48,0},{1,17},{17,33},{33,49},{49,1},{2,18}... | collective-permute-start | bytes 983048 | tf_op jit(solution)/shard_map/ppermute | solution.py:390
  44.8 12.7 %collective-permute-start.5 = (bf16[160,1024]{1,0:T(8,128)(2,1)S(1)}, bf16[160,1024]{1,0:T(8,128)(2,1)S(1)}, u32[]{:S(2)}, u32[]{:S(2)}) collective-permute-start(bf16[160,1024]{1,0:T(8,128)(2,1)S(1)} %get-tuple-element.34), channel_id=1, source_target_pairs={{0,48},{16,0},{32,16},{48,32},{1,49},{17,1},{33,17},{49,33},{2,50}... | collective-permute-start | bytes 983048 | tf_op jit(solution)/shard_map/ppermute | solution.py:390
  47.0 7.5 %collective-permute-start.13 = (bf16[1,128,512]{2,1,0:T(8,128)(2,1)S(1)}, bf16[1,128,512]{2,1,0:T(8,128)(2,1)S(1)}, u32[]{:S(2)}, u32[]{:S(2)}) collective-permute-start(bf16[1,128,512]{2,1,0:T(8,128)(2,1)S(1)} %get-tuple-element.37), channel_id=1, source_target_pairs={{0,14},{2,0},{4,2},{6,4},{8,6},{10,8},{12,10},{14,12},{1,15},{3,1}... | collective-permute-start | bytes 393224 | tf_op jit(solution)/shard_map/ppermute | solution.py:331
  51.3 6.2 %collective-permute-start.14 = (bf16[1,128,512]{2,1,0:T(8,128)(2,1)S(1)}, bf16[1,128,512]{2,1,0:T(8,128)(2,1)S(1)}, u32[]{:S(2)}, u32[]{:S(2)}) collective-permute-start(bf16[1,128,512]{2,1,0:T(8,128)(2,1)S(1)} %get-tuple-element.38), channel_id=1, source_target_pairs={{0,2},{2,4},{4,6},{6,8},{8,10},{10,12},{12,14},{14,0},{1,3},{3,5},... | collective-permute-start | bytes 393224 | tf_op jit(solution)/shard_map/ppermute | solution.py:331
  51.3 1.1 %copy-start = (bf16[400,1024]{1,0:T(8,128)(2,1)S(1)}, bf16[400,1024]{1,0:T(8,128)(2,1)}, u32[]{:S(2)}) copy-start(bf16[400,1024]{1,0:T(8,128)(2,1)} %get-tuple-element.26.message_ref) | copy-start | bytes 2457604
  52.5 0.9 copy-start.1
  53.4 1.0 %copy-start.2 = (f32[1024,128]{1,0:T(8,128)S(1)}, f32[1024,128]{1,0:T(8,128)}, u32[]{:S(2)}) copy-start(f32[1024,128]{1,0:T(8,128)} %get-tuple-element.27.right_ref) | copy-start | bytes 1572868

commit v10 on v8

--- a/solution.py
+++ b/solution.py
@@ -22,28 +22,38 @@
     return lax.dot_general(a, b, (dims, ((), ())), preferred_element_type=jnp.float32, precision=precision)
 
 
-def pair_kernel(own_ref, other_ref, *refs):
-    out_ref = refs[-1]
+def hold_kernel(*refs):
+    pass
+
+
+def hold(arrays):
+    return pl.pallas_call(
+        hold_kernel,
+        out_shape=[jax.ShapeDtypeStruct(array.shape, array.dtype) for array in arrays],
+        in_specs=[HBM] * len(arrays),
+        out_specs=[HBM] * len(arrays),
+        input_output_aliases={index: index for index in range(len(arrays))},
+        compiler_params=pltpu.CompilerParams(vmem_limit_bytes=62 * MIB),
+        name="hold",
+    )(*arrays)
+
+
+def pair_kernel(own_ref, other_ref, out_ref):
     piece = own_ref.shape[1]
     out_ref[:, :piece, :] = own_ref[...]
     out_ref[:, piece:, :] = other_ref[...]
 
 
-def pair_up(own, other, messages):
+def pair_up(own, other):
     examples, piece, seq_dev = own.shape
-    *messages, pair = pl.pallas_call(
+    return pl.pallas_call(
         pair_kernel,
-        out_shape=[
-            *[jax.ShapeDtypeStruct(message.shape, message.dtype) for message in messages],
-            jax.ShapeDtypeStruct((examples, NY * piece, seq_dev), own.dtype),
-        ],
-        in_specs=[VMEM, VMEM] + [HBM] * len(messages),
-        out_specs=[HBM] * len(messages) + [VMEM],
-        input_output_aliases={2 + index: index for index in range(len(messages))},
-        compiler_params=pltpu.CompilerParams(vmem_limit_bytes=62 * MIB),
+        out_shape=jax.ShapeDtypeStruct((examples, NY * piece, seq_dev), own.dtype),
+        in_specs=[VMEM] * 2,
+        out_specs=VMEM,
+        compiler_params=pltpu.CompilerParams(vmem_limit_bytes=4 * MIB),
         name="pair_up",
-    )(own, other, *messages)
-    return pair, messages
+    )(own, other)
 
 
 def token_kernel(chunk, scale, lengths_ref, tokens_hbm, gate_hbm, up_hbm, gate_in_hbm, up_in_hbm, down_in_hbm, down_hbm, gate_out_hbm, up_out_hbm, *refs):
@@ -182,25 +192,23 @@
     )(before, after)
 
 
-def keep_kernel(message_ref, right_ref, pair_ref, factors_out, right_out, pair_out):
+def keep_kernel(message_ref, right_ref, factors_out, right_out):
     factors_out[...] = message_ref[: factors_out.shape[0], :]
     right_out[...] = right_ref[...]
-    pair_out[...] = pair_ref[...]
-
-
-def keep(message, right, pair, rows):
+
+
+def keep(message, right, rows):
     return pl.pallas_call(
         keep_kernel,
         out_shape=[
             jax.ShapeDtypeStruct((rows, message.shape[1]), message.dtype),
             jax.ShapeDtypeStruct(right.shape, right.dtype),
-            jax.ShapeDtypeStruct(pair.shape, pair.dtype),
         ],
-        in_specs=[VMEM] * 3,
-        out_specs=[VMEM] * 3,
+        in_specs=[VMEM] * 2,
+        out_specs=[VMEM] * 2,
         compiler_params=pltpu.CompilerParams(vmem_limit_bytes=8 * MIB),
         name="keep",
-    )(message, right, pair)
+    )(message, right)
 
 
 def tail_kernel(weight_ref, gate_out_ref, up_out_ref, down_out_ref, right_ref, *refs):
@@ -381,7 +389,8 @@
         scale,
     )
     sent, right = sent[: NX - 1], sent[NX - 1]
-    pair, sent = pair_up(own_grad, other_grad, sent)
+    *sent, _ = hold([*sent, other_grad])
+    pair = pair_up(own_grad, other_grad)
     messages = [lax.ppermute(piece, "x", shifted(NX, step)) for step, piece in enumerate(sent, 1)]
     hidden, rank = gate_weight.shape[1], gate_out.shape[0]
     rows = 2 * hidden + rank
@@ -389,7 +398,7 @@
     swap = lax.ppermute(swap, "sc", shifted(SEQ_PARTS[1], 1))
     far = [lax.ppermute(first, "x", shifted(NX, 1)), lax.ppermute(second, "x", shifted(NX, -1))]
     blocks, far_block = ring_z(pair)
-    factors, right, blocks[0] = keep(sent[0], right, pair, rows)
+    factors, right = keep(sent[0], right, rows)
     products = tail_stage(
         down_weight, gate_out, up_out, proj_down_out.T, right, factors, messages, far, swap, blocks, far_block
     )

time: 94.6 us -> 93.5 us (0.988)
  waiting for transfers between devices: 18.6 us -> 16.2 us
  starting transfers between devices: 22.6 us -> 25 us
  blocking collectives: 33.8 us -> 35.5 us
  Pallas kernels: 14.4 us -> 12.7 us
  local copies, waits for them, and re-layouts: 4.64 us -> 3.65 us
    ppermute x3, waiting for transfers between devices: 9.14 us -> 0.96 us  [ring_z(): up.append(lax.ppermute(up[-1], 'z', shifted(NZ, -1)))]
    ppermute x3, waiting for transfers between devices: 5.09 us -> 10.6 us  [ring_z(): down.append(lax.ppermute(down[-1], 'z', shifted(NZ, 1)))]
    ppermute x1, starting transfers between devices: 0.67 us -> 3.86 us  [ring_z(): lax.ppermute(first, 'z', shifted(NZ, -1))]
    ppermute x3, starting transfers between devices: 13.1 us -> 10.4 us  [ring_z(): up.append(lax.ppermute(up[-1], 'z', shifted(NZ, -1)))]
    ppermute x3, starting transfers between devices: 0.01 us -> 1.92 us  [ring_z(): down.append(lax.ppermute(down[-1], 'z', shifted(NZ, 1)))]
    pallas_call x1 -> x2, Pallas kernels: 1.69 us -> 0.02 us  [the longest x1 0.02 us: pair_up(): pl.pallas_call(pair_kernel, out_shape=jax.ShapeDtypeStruct((examples, NY...]
    ppermute x3, waiting for transfers between devices: 1.46 us -> 0.01 us  [shards(): lax.ppermute(piece, 'x', shifted(NX, step))]
    all_to_all x1, blocking collectives: 13.6 us -> 14.8 us  [sum_everywhere(): pieces = lax.all_to_all(pieces, ('sy', 'sc', 'z'), 0, 0, tiled=True)]
where the time goes in v10:
time: 93.5 us; the launch traced here: 93.2 us
  blocking collectives  35.5 us (38%)
  starting transfers between devices  25 us (27%)
  waiting for transfers between devices  16.2 us (17%)
  Pallas kernels  12.7 us (14%)
  local copies, waits for them, and re-layouts  3.65 us (4%)
    all_to_all x1, blocking collectives, sum_everywhere(): blocks = lax.all_to_all(spread, ('x', 'z', 'yh'), 0, 0, tiled=True)  20.7 us
    all_to_all x1, blocking collectives, sum_everywhere(): pieces = lax.all_to_all(pieces, ('sy', 'sc', 'z'), 0, 0, tiled=True)  14.8 us
    ppermute x3, waiting for transfers between devices, ring_z(): down.append(lax.ppermute(down[-1], 'z', shifted(NZ, 1)))  10.6 us
    ppermute x3, starting transfers between devices, ring_z(): up.append(lax.ppermute(up[-1], 'z', shifted(NZ, -1)))  10.4 us
    pallas_call x1, Pallas kernels, token_stage(): pl.pallas_call(lambda *refs: token_kernel(chunk, scale, *refs), out_shape...  9.08 us
    ppermute x1, starting transfers between devices, ring_z(): lax.ppermute(first, 'z', shifted(NZ, -1))  3.86 us
    pallas_call x1, Pallas kernels, tail_stage(): pl.pallas_call(tail_kernel, out_shape=jax.ShapeDtypeStruct((examples * 3,...  3.44 us
    ppermute x3, starting transfers between devices, shards(): lax.ppermute(piece, 'x', shifted(NX, step))  3.44 us
  transfers between devices with their start and end apart: 15, of which 6 were waited for; matrix products, arithmetic and copies ran while one was open for 0% of the time, Pallas kernels for 10%

profile of v10, /device:TPU:6, one launch (start us, length us, event | category | flops | bytes accessed | tf_op | source)
XLA Modules:
  0.0 93.2 jit_solution(15765379113565568277)
XLA Ops:
  0.0 0.0 copy-start.3
  0.0 3.2 %collective-permute-start = (bf16[2,64,512]{2,1,0:T(8,128)(2,1)}, bf16[2,64,512]{2,1,0:T(8,128)(2,1)S(1)}, u32[]{:S(2)}, u32[]{:S(2)}) collective-permute-start(bf16[2,64,512]{2,1,0:T(8,128)(2,1)} %bitcast.15), channel_id=1, source_target_pairs={{0,1},{1,0},{2,3},{3,2},{4,5},{5,4},{6,7},{7,6},{8,9},{9,8},{10,11... | collective-permute-start | bytes 393224 | tf_op jit(solution)/shard_map/ppermute | solution.py:376
  3.2 0.0 copy-start.4
  3.2 0.0 copy-start.5
  3.2 0.0 copy-start.6
  3.2 0.0 copy-start.7
  3.2 9.1 %token_stage.1 = (bf16[400,1024]{1,0:T(8,128)(2,1)}, bf16[144,1024]{1,0:T(8,128)(2,1)}, bf16[400,1024]{1,0:T(8,128)(2,1)}, f32[1024,128]{1,0:T(8,128)}) custom-call(s32[2]{0:T(128)} %refs_0_.1, bf16[1024,4096]{1,0:T(8,128)(2,1)} %bitcast.25, bf16[4096,128]{1,0:T(8,128)(2,1)} %refs_2_.1, bf16[4096,128]{1,0:T(8,128)(2,1)} %refs_3_.1, ...), custom_call_target="tpu_custom_call" | custom-call | flops 4294967296 | bytes 16777216 | tf_op jit(solution)/shard_map/token_stage/pallas_call | solution.py:146
  12.3 0.0 collective-permute-done.refs_3_.other_ref
  12.3 0.0 copy-done.3
  12.3 0.0 copy-start.1
  12.4 0.6 copy-done.1
  13.0 0.5 collective-permute-start.1
  13.4 1.6 %collective-permute-start.3 = (bf16[400,1024]{1,0:T(8,128)(2,1)}, bf16[400,1024]{1,0:T(8,128)(2,1)S(1)}, u32[]{:S(2)}, u32[]{:S(2)}) collective-permute-start(bf16[400,1024]{1,0:T(8,128)(2,1)} %get-tuple-element.27), channel_id=1, source_target_pairs={{0,48},{16,0},{32,16},{48,32},{1,49},{17,1},{33,17},{49,33},{2,50}... | collective-permute-start | bytes 2457608 | tf_op jit(solution)/shard_map/ppermute | solution.py:394
  15.0 1.9 %collective-permute-start.10 = (bf16[2,128,512]{2,1,0:T(8,128)(2,1)S(1)}, bf16[2,128,512]{2,1,0:T(8,128)(2,1)S(1)}, u32[]{:S(2)}, u32[]{:S(2)}) collective-permute-start(bf16[2,128,512]{2,1,0:T(8,128)(2,1)S(1)} %pair_up.1.refs_7_), channel_id=1, source_target_pairs={{0,2},{2,4},{4,6},{6,8},{8,10},{10,12},{12,14},{14,0},{1,3},{3,5},... | collective-permute-start | bytes 786440 | tf_op jit(solution)/shard_map/ppermute | solution.py:338
  16.9 3.9 %collective-permute-start.7 = (bf16[2,128,512]{2,1,0:T(8,128)(2,1)S(1)}, bf16[2,128,512]{2,1,0:T(8,128)(2,1)S(1)}, u32[]{:S(2)}, u32[]{:S(2)}) collective-permute-start(bf16[2,128,512]{2,1,0:T(8,128)(2,1)S(1)} %pair_up.1.refs_7_), channel_id=1, source_target_pairs={{0,14},{2,0},{4,2},{6,4},{8,6},{10,8},{12,10},{14,12},{1,15},{3,1}... | collective-permute-start | bytes 786440 | tf_op jit(solution)/shard_map/ppermute | solution.py:337
  20.8 5.5 %collective-permute-done.10.refs_13_ = bf16[2,128,512]{2,1,0:T(8,128)(2,1)S(1)} collective-permute-done((bf16[2,128,512]{2,1,0:T(8,128)(2,1)S(1)}, bf16[2,128,512]{2,1,0:T(8,128)(2,1)S(1)}, u32[]{:S(2)}, u32[]{:S(2)}) %collective-permute-start.10) | collective-permute-done | bytes 262176 | tf_op jit(solution)/shard_map/ppermute | solution.py:338
  26.3 0.0 collective-permute-start.11
  26.3 0.0 collective-permute-done.7.refs_8_
  26.3 3.2 %collective-permute-start.8 = (bf16[2,128,512]{2,1,0:T(8,128)(2,1)S(1)}, bf16[2,128,512]{2,1,0:T(8,128)(2,1)S(1)}, u32[]{:S(2)}, u32[]{:S(2)}) collective-permute-start(bf16[2,128,512]{2,1,0:T(8,128)(2,1)S(1)} %collective-permute-done.7.refs_8_), channel_id=1, source_target_pairs={{0,14},{2,0},{4,2},{6,4},{8,6},{10,8},{12,10},{14,12},{1,15},{3,1}... | collective-permute-start | bytes 786440 | tf_op jit(solution)/shard_map/ppermute | solution.py:337
  29.5 4.5 %collective-permute-done.11.refs_12_ = bf16[2,128,512]{2,1,0:T(8,128)(2,1)S(1)} collective-permute-done((bf16[2,128,512]{2,1,0:T(8,128)(2,1)S(1)}, bf16[2,128,512]{2,1,0:T(8,128)(2,1)S(1)}, u32[]{:S(2)}, u32[]{:S(2)}) %collective-permute-start.11) | collective-permute-done | bytes 262176 | tf_op jit(solution)/shard_map/ppermute | solution.py:338
  34.1 0.0 collective-permute-start.12
  34.1 1.4 %collective-permute-start.2 = (bf16[144,1024]{1,0:T(8,128)(2,1)}, bf16[144,1024]{1,0:T(8,128)(2,1)S(1)}, u32[]{:S(2)}, u32[]{:S(2)}) collective-permute-start(bf16[144,1024]{1,0:T(8,128)(2,1)} %get-tuple-element.26), channel_id=1, source_target_pairs={{0,32},{16,48},{32,0},{48,16},{1,33},{17,49},{33,1},{49,17},{2,34}... | collective-permute-start | bytes 884744 | tf_op jit(solution)/shard_map/ppermute | solution.py:394
  35.5 0.0 collective-permute-done.8.refs_9_
  35.5 3.2 %collective-permute-start.9 = (bf16[2,128,512]{2,1,0:T(8,128)(2,1)S(1)}, bf16[2,128,512]{2,1,0:T(8,128)(2,1)S(1)}, u32[]{:S(2)}, u32[]{:S(2)}) collective-permute-start(bf16[2,128,512]{2,1,0:T(8,128)(2,1)S(1)} %collective-permute-done.8.refs_9_), channel_id=1, source_target_pairs={{0,14},{2,0},{4,2},{6,4},{8,6},{10,8},{12,10},{14,12},{1,15},{3,1}... | collective-permute-start | bytes 786440 | tf_op jit(solution)/shard_map/ppermute | solution.py:337
  38.7 0.0 collective-permute-done.1.before_ref.refs_1_
  38.7 0.0 collective-permute-done.3.after_ref.refs_3_
  38.7 0.1 halves.1
  38.8 2.2 %collective-permute-start.4 = (bf16[160,1024]{1,0:T(8,128)(2,1)S(1)}, bf16[160,1024]{1,0:T(8,128)(2,1)S(1)}, u32[]{:S(2)}, u32[]{:S(2)}) collective-permute-start(bf16[160,1024]{1,0:T(8,128)(2,1)S(1)} %get-tuple-element.28), channel_id=1, source_target_pairs={{0,16},{16,32},{32,48},{48,0},{1,17},{17,33},{33,49},{49,1},{2,18}... | collective-permute-start | bytes 983048 | tf_op jit(solution)/shard_map/ppermute | solution.py:399
  41.0 0.0 collective-permute-start.5
  41.0 0.7 collective-permute-done.12.down_ref.refs_11_
  41.6 0.0 collective-permute-start.6
  41.7 1.0 %collective-permute-done.9.up_ref.refs_10_ = bf16[2,128,512]{2,1,0:T(8,128)(2,1)S(1)} collective-permute-done((bf16[2,128,512]{2,1,0:T(8,128)(2,1)S(1)}, bf16[2,128,512]{2,1,0:T(8,128)(2,1)S(1)}, u32[]{:S(2)}, u32[]{:S(2)}) %collective-permute-start.9) | collective-permute-done | bytes 262176 | tf_op jit(solution)/shard_map/ppermute | solution.py:337
  42.6 3.9 %collective-permute-start.13 = (bf16[1,128,512]{2,1,0:T(8,128)(2,1)S(1)}, bf16[1,128,512]{2,1,0:T(8,128)(2,1)S(1)}, u32[]{:S(2)}, u32[]{:S(2)}) collective-permute-start(bf16[1,128,512]{2,1,0:T(8,128)(2,1)S(1)} %get-tuple-element.31), channel_id=1, source_target_pairs={{0,14},{2,0},{4,2},{6,4},{8,6},{10,8},{12,10},{14,12},{1,15},{3,1}... | collective-permute-start | bytes 393224 | tf_op jit(solution)/shard_map/ppermute | solution.py:340
  46.5 0.0 collective-permute-done.2.refs_2_
  46.5 0.0 collective-permute-start.14
  46.5 0.0 copy-start
  46.5 1.1 %copy-done = bf16[400,1024]{1,0:T(8,128)(2,1)S(1)} copy-done((bf16[400,1024]{1,0:T(8,128)(2,1)S(1)}, bf16[400,1024]{1,0:T(8,128)(2,1)}, u32[]{:S(2)}) %copy-start) | copy-done | bytes 819224
  47.6 0.0 copy-start.2
  47.6 1.0 %copy-done.2 = f32[1024,128]{1,0:T(8,128)S(1)} copy-done((f32[1024,128]{1,0:T(8,128)S(1)}, f32[1024,128]{1,0:T(8,128)}, u32[]{:S(2)}) %copy-start.2) | copy-done | bytes 524312
  48.7 0.1 keep.1
  48.8 1.1 %collective-permute-done.13.refs_14_ = bf16[1,128,512]{2,1,0:T(8,128)(2,1)S(1)} collective-permute-done((bf16[1,128,512]{2,1,0:T(8,128)(2,1)S(1)}, bf16[1,128,512]{2,1,0:T(8,128)(2,1)S(1)}, u32[]{:S(2)}, u32[]{:S(2)}) %collective-permute-start.13) | collective-permute-done | bytes 131104 | tf_op jit(solution)/shard_map/ppermute | solution.py:340
  49.9 3.4 %collective-permute-done.14.refs_15_ = bf16[1,128,512]{2,1,0:T(8,128)(2,1)S(1)} collective-permute-done((bf16[1,128,512]{2,1,0:T(8,128)(2,1)S(1)}, bf16[1,128,512]{2,1,0:T(8,128)(2,1)S(1)}, u32[]{:S(2)}, u32[]{:S(2)}) %collective-permute-start.14) | collective-permute-done | bytes 131104 | tf_op jit(solution)/shard_map/ppermute | solution.py:340
  53.3 0.0 collective-permute-done.6.refs_6_
  53.3 0.0 collective-permute-done.4.refs_4_
  53.3 0.0 collective-permute-done.5.refs_5_
  53.3 0.0 copy-done.4
  53.4 0.0 copy-done.5
  53.4 0.0 copy-done.6
  53.4 0.0 copy-done.7
  53.4 3.4 %tail_stage.1 = f32[6,64,64]{2,1,0:T(8,128)S(1)} custom-call(bf16[128,4096]{1,0:T(8,128)(2,1)S(1)} %copy-done.4, bf16[64,128]{1,0:T(8,128)(2,1)S(1)} %bitcast.19, bf16[64,128]{1,0:T(8,128)(2,1)S(1)} %bitcast.21, bf16[64,4096]{1,0:T(8,128)(2,1)S(1)} %bitcast.17, f32[1024,128]{1,0:T(8,128)S(1)} %get-tuple-element.24.right_ref, ...), custom_call_target="tpu_custom_call" | custom-call | flops 4000000000 | bytes 8388608 | tf_op jit(solution)/shard_map/tail_stage/pallas_call | solution.py:301
  56.8 0.1 reshape_reshape.6
  56.9 0.1 copy.34
  57.0 14.8 %all_to_all.10 = f32[32,6,128]{2,1,0:T(8,128)S(1)} all-to-all(f32[32,6,128]{2,1,0:T(8,128)S(1)} %bitcast.23), channel_id=1, replica_groups=mesh['sy'=2,'sc'=2,'x'=4,'z'=8,'yh'=2] {'sy','sc','z'}, dimensions={0} | all-to-all | bytes 196608 | tf_op jit(solution)/shard_map/all_to_all | solution.py:349
  71.8 20.7 %all_to_all.11 = f32[64,6,128]{2,1,0:T(8,128)S(1)} all-to-all(f32[64,6,128]{2,1,0:T(8,128)S(1)} %broadcast_in_dim.2), channel_id=1, replica_groups=mesh['sy'=2,'sc'=2,'x'=4,'z'=8,'yh'=2] {'x','z','yh'}, dimensions={0} | all-to-all | bytes 393216 | tf_op jit(solution)/shard_map/all_to_all | solution.py:352
  92.6 0.6 copy.28
  (8 shorter events, 0.1 us)
Async XLA Ops:
  0.0 12.3 %copy-start.3 = (bf16[2,512,64]{1,2,0:T(8,128)(2,1)S(1)}, bf16[2,512,64]{1,2,0:T(8,128)(2,1)}, u32[]{:S(2)}) copy-start(bf16[2,512,64]{1,2,0:T(8,128)(2,1)} %param.13) | copy-start | bytes 393220
  0.0 12.3 %collective-permute-start = (bf16[2,64,512]{2,1,0:T(8,128)(2,1)}, bf16[2,64,512]{2,1,0:T(8,128)(2,1)S(1)}, u32[]{:S(2)}, u32[]{:S(2)}) collective-permute-start(bf16[2,64,512]{2,1,0:T(8,128)(2,1)} %bitcast.15), channel_id=1, source_target_pairs={{0,1},{1,0},{2,3},{3,2},{4,5},{5,4},{6,7},{7,6},{8,9},{9,8},{10,11... | collective-permute-start | bytes 393224 | tf_op jit(solution)/shard_map/ppermute | solution.py:376
  3.2 50.1 %copy-start.4 = (bf16[128,4096]{1,0:T(8,128)(2,1)S(1)}, bf16[128,4096]{1,0:T(8,128)(2,1)}, u32[]{:S(2)}) copy-start(bf16[128,4096]{1,0:T(8,128)(2,1)} %weight_ref.1) | copy-start | bytes 3145732
  3.2 50.2 %copy-start.5 = (bf16[4096,64]{0,1:T(8,128)(2,1)S(1)}, bf16[4096,64]{0,1:T(8,128)(2,1)}, u32[]{:S(2)}) copy-start(bf16[4096,64]{0,1:T(8,128)(2,1)} %param.22) | copy-start | bytes 1572868
  3.2 50.2 %copy-start.6 = (bf16[128,64]{0,1:T(8,128)(2,1)S(1)}, bf16[128,64]{0,1:T(8,128)(2,1)}, u32[]{:S(2)}) copy-start(bf16[128,64]{0,1:T(8,128)(2,1)} %param.18) | copy-start | bytes 49156
  3.2 50.2 %copy-start.7 = (bf16[128,64]{0,1:T(8,128)(2,1)S(1)}, bf16[128,64]{0,1:T(8,128)(2,1)}, u32[]{:S(2)}) copy-start(bf16[128,64]{0,1:T(8,128)(2,1)} %param.20) | copy-start | bytes 49156
  12.3 0.6 copy-start.1
  13.0 25.8 %collective-permute-start.1 = (bf16[400,1024]{1,0:T(8,128)(2,1)}, bf16[400,1024]{1,0:T(8,128)(2,1)S(1)}, u32[]{:S(2)}, u32[]{:S(2)}) collective-permute-start(bf16[400,1024]{1,0:T(8,128)(2,1)} %get-tuple-element.22.message_ref), channel_id=1, source_target_pairs={{0,16},{16,32},{32,48},{48,0},{1,17},{17,33},{33,49},{49,1},{2,18}... | collective-permute-start | bytes 2457608 | tf_op jit(solution)/shard_map/ppermute | solution.py:394
  13.4 25.3 %collective-permute-start.3 = (bf16[400,1024]{1,0:T(8,128)(2,1)}, bf16[400,1024]{1,0:T(8,128)(2,1)S(1)}, u32[]{:S(2)}, u32[]{:S(2)}) collective-permute-start(bf16[400,1024]{1,0:T(8,128)(2,1)} %get-tuple-element.27), channel_id=1, source_target_pairs={{0,48},{16,0},{32,16},{48,32},{1,49},{17,1},{33,17},{49,33},{2,50}... | collective-permute-start | bytes 2457608 | tf_op jit(solution)/shard_map/ppermute | solution.py:394
  15.0 11.3 %collective-permute-start.10 = (bf16[2,128,512]{2,1,0:T(8,128)(2,1)S(1)}, bf16[2,128,512]{2,1,0:T(8,128)(2,1)S(1)}, u32[]{:S(2)}, u32[]{:S(2)}) collective-permute-start(bf16[2,128,512]{2,1,0:T(8,128)(2,1)S(1)} %pair_up.1.refs_7_), channel_id=1, source_target_pairs={{0,2},{2,4},{4,6},{6,8},{8,10},{10,12},{12,14},{14,0},{1,3},{3,5},... | collective-permute-start | bytes 786440 | tf_op jit(solution)/shard_map/ppermute | solution.py:338
  16.9 9.4 %collective-permute-start.7 = (bf16[2,128,512]{2,1,0:T(8,128)(2,1)S(1)}, bf16[2,128,512]{2,1,0:T(8,128)(2,1)S(1)}, u32[]{:S(2)}, u32[]{:S(2)}) collective-permute-start(bf16[2,128,512]{2,1,0:T(8,128)(2,1)S(1)} %pair_up.1.refs_7_), channel_id=1, source_target_pairs={{0,14},{2,0},{4,2},{6,4},{8,6},{10,8},{12,10},{14,12},{1,15},{3,1}... | collective-permute-start | bytes 786440 | tf_op jit(solution)/shard_map/ppermute | solution.py:337
  26.3 7.8 %collective-permute-start.11 = (bf16[2,128,512]{2,1,0:T(8,128)(2,1)S(1)}, bf16[2,128,512]{2,1,0:T(8,128)(2,1)S(1)}, u32[]{:S(2)}, u32[]{:S(2)}) collective-permute-start(bf16[2,128,512]{2,1,0:T(8,128)(2,1)S(1)} %collective-permute-done.10.refs_13_), channel_id=1, source_target_pairs={{0,2},{2,4},{4,6},{6,8},{8,10},{10,12},{12,14},{14,0},{1,3},{3,5},... | collective-permute-start | bytes 786440 | tf_op jit(solution)/shard_map/ppermute | solution.py:338
  26.3 9.2 %collective-permute-start.8 = (bf16[2,128,512]{2,1,0:T(8,128)(2,1)S(1)}, bf16[2,128,512]{2,1,0:T(8,128)(2,1)S(1)}, u32[]{:S(2)}, u32[]{:S(2)}) collective-permute-start(bf16[2,128,512]{2,1,0:T(8,128)(2,1)S(1)} %collective-permute-done.7.refs_8_), channel_id=1, source_target_pairs={{0,14},{2,0},{4,2},{6,4},{8,6},{10,8},{12,10},{14,12},{1,15},{3,1}... | collective-permute-start | bytes 786440 | tf_op jit(solution)/shard_map/ppermute | solution.py:337
  34.1 7.6 %collective-permute-start.12 = (bf16[2,128,512]{2,1,0:T(8,128)(2,1)S(1)}, bf16[2,128,512]{2,1,0:T(8,128)(2,1)S(1)}, u32[]{:S(2)}, u32[]{:S(2)}) collective-permute-start(bf16[2,128,512]{2,1,0:T(8,128)(2,1)S(1)} %collective-permute-done.11.refs_12_), channel_id=1, source_target_pairs={{0,2},{2,4},{4,6},{6,8},{8,10},{10,12},{12,14},{14,0},{1,3},{3,5},... | collective-permute-start | bytes 786440 | tf_op jit(solution)/shard_map/ppermute | solution.py:338
  34.1 12.4 %collective-permute-start.2 = (bf16[144,1024]{1,0:T(8,128)(2,1)}, bf16[144,1024]{1,0:T(8,128)(2,1)S(1)}, u32[]{:S(2)}, u32[]{:S(2)}) collective-permute-start(bf16[144,1024]{1,0:T(8,128)(2,1)} %get-tuple-element.26), channel_id=1, source_target_pairs={{0,32},{16,48},{32,0},{48,16},{1,33},{17,49},{33,1},{49,17},{2,34}... | collective-permute-start | bytes 884744 | tf_op jit(solution)/shard_map/ppermute | solution.py:394
  35.5 7.1 %collective-permute-start.9 = (bf16[2,128,512]{2,1,0:T(8,128)(2,1)S(1)}, bf16[2,128,512]{2,1,0:T(8,128)(2,1)S(1)}, u32[]{:S(2)}, u32[]{:S(2)}) collective-permute-start(bf16[2,128,512]{2,1,0:T(8,128)(2,1)S(1)} %collective-permute-done.8.refs_9_), channel_id=1, source_target_pairs={{0,14},{2,0},{4,2},{6,4},{8,6},{10,8},{12,10},{14,12},{1,15},{3,1}... | collective-permute-start | bytes 786440 | tf_op jit(solution)/shard_map/ppermute | solution.py:337
  38.8 14.5 %collective-permute-start.4 = (bf16[160,1024]{1,0:T(8,128)(2,1)S(1)}, bf16[160,1024]{1,0:T(8,128)(2,1)S(1)}, u32[]{:S(2)}, u32[]{:S(2)}) collective-permute-start(bf16[160,1024]{1,0:T(8,128)(2,1)S(1)} %get-tuple-element.28), channel_id=1, source_target_pairs={{0,16},{16,32},{32,48},{48,0},{1,17},{17,33},{33,49},{49,1},{2,18}... | collective-permute-start | bytes 983048 | tf_op jit(solution)/shard_map/ppermute | solution.py:399
  41.0 12.4 %collective-permute-start.5 = (bf16[160,1024]{1,0:T(8,128)(2,1)S(1)}, bf16[160,1024]{1,0:T(8,128)(2,1)S(1)}, u32[]{:S(2)}, u32[]{:S(2)}) collective-permute-start(bf16[160,1024]{1,0:T(8,128)(2,1)S(1)} %get-tuple-element.29), channel_id=1, source_target_pairs={{0,48},{16,0},{32,16},{48,32},{1,49},{17,1},{33,17},{49,33},{2,50}... | collective-permute-start | bytes 983048 | tf_op jit(solution)/shard_map/ppermute | solution.py:399
  41.6 11.7 %collective-permute-start.6 = (bf16[128,1024]{1,0:T(8,128)(2,1)S(1)}, bf16[128,1024]{1,0:T(8,128)(2,1)S(1)}, u32[]{:S(2)}, u32[]{:S(2)}) collective-permute-start(bf16[128,1024]{1,0:T(8,128)(2,1)S(1)} %get-tuple-element.30), channel_id=1, source_target_pairs={{0,64},{64,0},{1,65},{65,1},{2,66},{66,2},{3,67},{67,3},{4,68},{68... | collective-permute-start | bytes 786440 | tf_op jit(solution)/shard_map/ppermute | solution.py:398
  42.6 7.3 %collective-permute-start.13 = (bf16[1,128,512]{2,1,0:T(8,128)(2,1)S(1)}, bf16[1,128,512]{2,1,0:T(8,128)(2,1)S(1)}, u32[]{:S(2)}, u32[]{:S(2)}) collective-permute-start(bf16[1,128,512]{2,1,0:T(8,128)(2,1)S(1)} %get-tuple-element.31), channel_id=1, source_target_pairs={{0,14},{2,0},{4,2},{6,4},{8,6},{10,8},{12,10},{14,12},{1,15},{3,1}... | collective-permute-start | bytes 393224 | tf_op jit(solution)/shard_map/ppermute | solution.py:340
  46.5 6.8 %collective-permute-start.14 = (bf16[1,128,512]{2,1,0:T(8,128)(2,1)S(1)}, bf16[1,128,512]{2,1,0:T(8,128)(2,1)S(1)}, u32[]{:S(2)}, u32[]{:S(2)}) collective-permute-start(bf16[1,128,512]{2,1,0:T(8,128)(2,1)S(1)} %get-tuple-element.32), channel_id=1, source_target_pairs={{0,2},{2,4},{4,6},{6,8},{8,10},{10,12},{12,14},{14,0},{1,3},{3,5},... | collective-permute-start | bytes 393224 | tf_op jit(solution)/shard_map/ppermute | solution.py:340
  46.5 1.1 %copy-start = (bf16[400,1024]{1,0:T(8,128)(2,1)S(1)}, bf16[400,1024]{1,0:T(8,128)(2,1)}, u32[]{:S(2)}) copy-start(bf16[400,1024]{1,0:T(8,128)(2,1)} %get-tuple-element.22.message_ref) | copy-start | bytes 2457604
  47.6 1.0 %copy-start.2 = (f32[1024,128]{1,0:T(8,128)S(1)}, f32[1024,128]{1,0:T(8,128)}, u32[]{:S(2)}) copy-start(f32[1024,128]{1,0:T(8,128)} %get-tuple-element.23.right_ref) | copy-start | bytes 1572868

commit v11 on v10

--- a/solution.py
+++ b/solution.py
@@ -192,58 +192,90 @@
     )(before, after)
 
 
-def keep_kernel(message_ref, right_ref, factors_out, right_out):
-    factors_out[...] = message_ref[: factors_out.shape[0], :]
-    right_out[...] = right_ref[...]
-
-
-def keep(message, right, rows):
-    return pl.pallas_call(
-        keep_kernel,
-        out_shape=[
-            jax.ShapeDtypeStruct((rows, message.shape[1]), message.dtype),
-            jax.ShapeDtypeStruct(right.shape, right.dtype),
-        ],
-        in_specs=[VMEM] * 2,
-        out_specs=[VMEM] * 2,
-        compiler_params=pltpu.CompilerParams(vmem_limit_bytes=8 * MIB),
-        name="keep",
-    )(message, right)
-
-
-def tail_kernel(weight_ref, gate_out_ref, up_out_ref, down_out_ref, right_ref, *refs):
-    own_ref, messages, far_halves, swap_ref = refs[0], refs[1:NX], refs[NX : NX + 2], refs[NX + 2]
-    blocks, far_block = refs[NX + 3 : NX + 2 + NZ], refs[NX + 2 + NZ : NX + 4 + NZ]
-    out_ref, weights, projs, grads = refs[NX + 4 + NZ :]
+def early_kernel(weight_ref, gate_out_ref, up_out_ref, down_out_ref, right_ref, own_ref, *refs):
+    messages, swap_ref, blocks = refs[: NX - 1], refs[NX - 1], refs[NX : NX + NZ - 1]
+    total_ref, far_ref, projs, right_out, factors_out, weights, grads = refs[NX + NZ - 1 :]
     hidden, model_width = weight_ref.shape
     rank = gate_out_ref.shape[0]
     width = model_width // NX
-    examples, both, seq_dev = blocks[0].shape
+    examples, both, _ = blocks[0].shape
     piece = both // NY
-    top, half, core = 2 * hidden + rank, hidden // 2, lax.axis_index("sc")
+    half, core = hidden // 2, lax.axis_index("sc")
     x_at, z_at, y_at = lax.axis_index("x"), lax.axis_index("z"), lax.axis_index("yh")
 
+    factors_out[...] = own_ref[: factors_out.shape[0], :]
+    right_out[...] = right_ref[...]
     start = pl.multiple_of(x_at * width, width)
     weights[:hidden, :] = weight_ref[:, pl.ds(start, width)]
     weights[NX * hidden :, :] = down_out_ref[:, pl.ds(start, width)]
     projs[:rank, :hidden] = gate_out_ref[...]
     projs[rank:, :hidden] = up_out_ref[...]
     for step, message in enumerate(messages, 1):
+        top = message.shape[0] - FOLD
         if step == 2:
-            weights[step * hidden : (step + 1) * hidden, :] = message[:hidden, :]
+            weights[step * hidden : (step + 1) * hidden, :] = message[top - hidden : top, :]
         else:
             mine = pl.ds(pl.multiple_of(step * hidden + core * half, half), half)
             theirs = pl.ds(pl.multiple_of(step * hidden + (1 - core) * half, half), half)
-            weights[mine, :] = message[top : top + half, :]
+            weights[mine, :] = message[top - half : top, :]
             weights[theirs, :] = swap_ref[step // 2 * half : (step // 2 + 1) * half, :]
         columns = slice(step * hidden, (step + 1) * hidden)
         for block in range(2 * rank // FOLD):
-            folded = message[-FOLD:, block * hidden : (block + 1) * hidden]
+            folded = message[top:, block * hidden : (block + 1) * hidden]
             projs[block * FOLD : (block + 1) * FOLD, columns] = folded
+    far_base = pl.multiple_of(lax.rem(z_at + NZ // 2, NZ) * both, both)
+    far_ref[...] = weights[:, pl.ds(far_base, both)]
+    for example in range(examples):
+        grads[example, pl.ds(far_base, both), :] = jnp.zeros((both, grads.shape[2]), grads.dtype)
+        for step, block in enumerate(blocks):
+            base = lax.rem(z_at + step + step // (NZ // 2), NZ) * both
+            for kind, y_of in enumerate((y_at, 1 - y_at)):
+                rows = pl.ds(pl.multiple_of(base + y_of * piece, piece), piece)
+                grads[example, rows, :] = block[example, kind * piece : (kind + 1) * piece]
+    for example in range(examples):
+        total_ref[example] = jnp.dot(weights[...], grads[example], preferred_element_type=jnp.float32)
+
+
+def early_stage(down_weight, gate_out, up_out, down_out, right, message, messages, swap, blocks):
+    hidden, model_width = down_weight.shape
+    rank = gate_out.shape[0]
+    examples, both, seq_dev = blocks[0].shape
+    width = model_width // NX
+    rows = NX * hidden + rank
+    operands = [down_weight, gate_out, up_out, down_out, right, message, *messages, swap, *blocks]
+    return pl.pallas_call(
+        early_kernel,
+        out_shape=[
+            jax.ShapeDtypeStruct((examples, rows, seq_dev), jnp.float32),
+            jax.ShapeDtypeStruct((rows, both), jnp.bfloat16),
+            jax.ShapeDtypeStruct((2 * rank, NX * hidden), jnp.bfloat16),
+            jax.ShapeDtypeStruct(right.shape, right.dtype),
+            jax.ShapeDtypeStruct((2 * hidden + rank, message.shape[1]), message.dtype),
+        ],
+        in_specs=[VMEM] * len(operands),
+        out_specs=[VMEM] * 5,
+        scratch_shapes=[
+            pltpu.VMEM((rows, width), jnp.bfloat16),
+            pltpu.VMEM((examples, width, seq_dev), jnp.bfloat16),
+        ],
+        compiler_params=pltpu.CompilerParams(vmem_limit_bytes=20 * MIB),
+        cost_estimate=pl.CostEstimate(flops=2 * 10**9, bytes_accessed=4 * MIB, transcendentals=0),
+        name="early_stage",
+    )(*operands)
+
+
+def tail_kernel(total_ref, far_ref, projs, right_ref, own_ref, *refs):
+    near, far_halves, far_block, (out_ref, grads) = refs[:2], refs[2:4], refs[4:6], refs[6:]
+    examples = total_ref.shape[0]
+    seq_dev = total_ref.shape[2]
+    rank, hidden = projs.shape[0] // 2, projs.shape[1] // NX
+    top = 2 * hidden + rank
+    piece = grads.shape[1] // NY
+    y_at = lax.axis_index("yh")
 
     def factor_rows(step, first, last, columns):
         if step != 2:
-            return (own_ref if step == 0 else messages[step - 1])[first:last, columns]
+            return (own_ref, near[0], None, near[1])[step][first:last, columns]
         rows = far_halves[0].shape[0]
         parts = [far_halves[0][first : min(last, rows), columns]] if first < rows else []
         if last > rows:
@@ -251,18 +283,13 @@
         return jnp.concatenate(parts, axis=0)
 
     for example in range(examples):
-        for step in range(NZ):
-            if step == NZ // 2:
-                count = examples // 2
-                block = far_block[example // count][example % count]
-            else:
-                block = blocks[step if step < NZ // 2 else step - 1][example]
-            base = lax.rem(z_at + step, NZ) * both
-            for kind, y_of in enumerate((y_at, 1 - y_at)):
-                rows = pl.ds(pl.multiple_of(base + y_of * piece, piece), piece)
-                grads[rows, :] = block[kind * piece : (kind + 1) * piece]
+        count = examples // 2
+        for kind, y_of in enumerate((y_at, 1 - y_at)):
+            rows = pl.ds(pl.multiple_of(y_of * piece, piece), piece)
+            grads[example, rows, :] = far_block[example // count][example % count, kind * piece : (kind + 1) * piece]
+    for example in range(examples):
         columns = slice(example * seq_dev, (example + 1) * seq_dev)
-        total = jnp.dot(weights[...], grads[...], preferred_element_type=jnp.float32)
+        total = total_ref[example] + jnp.dot(far_ref[...], grads[example], preferred_element_type=jnp.float32)
         left = []
         for kind in range(2):
             factor = jnp.concatenate(
@@ -292,24 +319,18 @@
         )
 
 
-def tail_stage(down_weight, gate_out, up_out, down_out, right, factors, messages, far, swap, blocks, far_block):
-    hidden, model_width = down_weight.shape
-    rank = gate_out.shape[0]
-    examples, _, seq_dev = blocks[0].shape
-    width = model_width // NX
-    operands = [down_weight, gate_out, up_out, down_out, right, factors, *messages, *far, swap, *blocks, *far_block]
+def tail_stage(total, far_weight, projs, right, factors, near, far, far_block):
+    examples, _, seq_dev = total.shape
+    rank = projs.shape[0] // 2
+    operands = [total, far_weight, projs, right, factors, *near, *far, *far_block]
     return pl.pallas_call(
         tail_kernel,
         out_shape=jax.ShapeDtypeStruct((examples * 3, rank, rank), jnp.float32),
         in_specs=[VMEM] * len(operands),
         out_specs=VMEM,
-        scratch_shapes=[
-            pltpu.VMEM((NX * hidden + rank, width), jnp.bfloat16),
-            pltpu.VMEM((2 * rank, NX * hidden), jnp.bfloat16),
-            pltpu.VMEM((width, seq_dev), jnp.bfloat16),
-        ],
-        compiler_params=pltpu.CompilerParams(vmem_limit_bytes=20 * MIB),
-        cost_estimate=pl.CostEstimate(flops=4 * 10**9, bytes_accessed=8 * MIB, transcendentals=0),
+        scratch_shapes=[pltpu.VMEM((examples, far_weight.shape[1], seq_dev), jnp.bfloat16)],
+        compiler_params=pltpu.CompilerParams(vmem_limit_bytes=16 * MIB),
+        cost_estimate=pl.CostEstimate(flops=2 * 10**9, bytes_accessed=4 * MIB, transcendentals=0),
         name="tail_stage",
     )(*operands)
 
@@ -398,10 +419,10 @@
     swap = lax.ppermute(swap, "sc", shifted(SEQ_PARTS[1], 1))
     far = [lax.ppermute(first, "x", shifted(NX, 1)), lax.ppermute(second, "x", shifted(NX, -1))]
     blocks, far_block = ring_z(pair)
-    factors, right = keep(sent[0], right, rows)
-    products = tail_stage(
-        down_weight, gate_out, up_out, proj_down_out.T, right, factors, messages, far, swap, blocks, far_block
+    total, far_weight, projs, right, factors = early_stage(
+        down_weight, gate_out, up_out, proj_down_out.T, right, sent[0], messages, swap, blocks
     )
+    products = tail_stage(total, far_weight, projs, right, factors, messages[::2], far, far_block)
     total = sum_everywhere(products.reshape(examples * 3, -1))
     return total.reshape(examples, 3, -1)
 

time: 93.5 us -> 94.4 us (level)
  starting transfers between devices: 25 us -> 28.7 us
  waiting for transfers between devices: 16.2 us -> 12.8 us
    ppermute x1, starting transfers between devices: 3.86 us -> 6.39 us  [ring_z(): lax.ppermute(first, 'z', shifted(NZ, -1))]
    pallas_call x1, Pallas kernels: 0.08 us -> 1.61 us  [early_stage(): pl.pallas_call(early_kernel, out_shape=[jax.ShapeDtypeStruct((examples, r...]
    ppermute x1, waiting for transfers between devices: 1.15 us -> 0.01 us  [ring_z(): lax.ppermute(first, 'z', shifted(NZ, -1))]
    ppermute x1, waiting for transfers between devices: 3.42 us -> 2.32 us  [ring_z(): lax.ppermute(second, 'z', shifted(NZ, 1))]
    pallas_call x1, Pallas kernels: 3.44 us -> 2.39 us  [tail_stage(): pl.pallas_call(tail_kernel, out_shape=jax.ShapeDtypeStruct((examples * 3,...]
  transfers between devices with their start and end apart: 15 -> 15, of which waited for: 6 -> 5; matrix products, arithmetic and copies ran while one was open for 0% -> 0% of each run, Pallas kernels for 10% -> 11%
where the time goes in v11:
time: 94.4 us; the launch traced here: 94.2 us
  blocking collectives  35.7 us (38%)
  starting transfers between devices  28.7 us (30%)
  Pallas kernels  13.2 us (14%)
  waiting for transfers between devices  12.8 us (14%)
  local copies, waits for them, and re-layouts  3.65 us (4%)
    all_to_all x1, blocking collectives, sum_everywhere(): blocks = lax.all_to_all(spread, ('x', 'z', 'yh'), 0, 0, tiled=True)  20.2 us
    all_to_all x1, blocking collectives, sum_everywhere(): pieces = lax.all_to_all(pieces, ('sy', 'sc', 'z'), 0, 0, tiled=True)  15.5 us
    ppermute x3, starting transfers between devices, ring_z(): up.append(lax.ppermute(up[-1], 'z', shifted(NZ, -1)))  10.4 us
    ppermute x3, waiting for transfers between devices, ring_z(): down.append(lax.ppermute(down[-1], 'z', shifted(NZ, 1)))  10.4 us
    pallas_call x1, Pallas kernels, token_stage(): pl.pallas_call(lambda *refs: token_kernel(chunk, scale, *refs), out_shape...  9.08 us
    ppermute x1, starting transfers between devices, ring_z(): lax.ppermute(first, 'z', shifted(NZ, -1))  6.39 us
    ppermute x3, starting transfers between devices, shards(): lax.ppermute(piece, 'x', shifted(NX, step))  3.44 us
    ppermute x1, starting transfers between devices, shards(): other_grad = lax.ppermute(own_grad, 'yh', shifted(NY, 1))  3.19 us
  transfers between devices with their start and end apart: 15, of which 5 were waited for; matrix products, arithmetic and copies ran while one was open for 0% of the time, Pallas kernels for 11%

profile of v11, /device:TPU:6, one launch (start us, length us, event | category | flops | bytes accessed | tf_op | source)
XLA Modules:
  0.0 94.2 jit_solution(8247305129544079754)
XLA Ops:
  0.0 0.0 copy-start.2
  0.0 3.2 %collective-permute-start = (bf16[2,64,512]{2,1,0:T(8,128)(2,1)}, bf16[2,64,512]{2,1,0:T(8,128)(2,1)S(1)}, u32[]{:S(2)}, u32[]{:S(2)}) collective-permute-start(bf16[2,64,512]{2,1,0:T(8,128)(2,1)} %bitcast.15), channel_id=1, source_target_pairs={{0,1},{1,0},{2,3},{3,2},{4,5},{5,4},{6,7},{7,6},{8,9},{9,8},{10,11... | collective-permute-start | bytes 393224 | tf_op jit(solution)/shard_map/ppermute | solution.py:397
  3.2 0.0 copy-start.3
  3.2 0.0 copy-start.4
  3.2 0.0 copy-start.5
  3.2 0.0 copy-start.6
  3.2 9.1 %token_stage.1 = (bf16[400,1024]{1,0:T(8,128)(2,1)}, bf16[144,1024]{1,0:T(8,128)(2,1)}, bf16[400,1024]{1,0:T(8,128)(2,1)}, f32[1024,128]{1,0:T(8,128)}) custom-call(s32[2]{0:T(128)} %refs_0_.1, bf16[1024,4096]{1,0:T(8,128)(2,1)} %bitcast.25, bf16[4096,128]{1,0:T(8,128)(2,1)} %refs_2_.1, bf16[4096,128]{1,0:T(8,128)(2,1)} %refs_3_.1, ...), custom_call_target="tpu_custom_call" | custom-call | flops 4294967296 | bytes 16777216 | tf_op jit(solution)/shard_map/token_stage/pallas_call | solution.py:146
  12.3 0.0 collective-permute-done.refs_3_.other_ref
  12.3 0.0 copy-done.2
  12.3 0.0 copy-start.1
  12.4 0.6 copy-done.1
  13.0 0.5 collective-permute-start.1
  13.4 1.6 %collective-permute-start.3 = (bf16[400,1024]{1,0:T(8,128)(2,1)}, bf16[400,1024]{1,0:T(8,128)(2,1)S(1)}, u32[]{:S(2)}, u32[]{:S(2)}) collective-permute-start(bf16[400,1024]{1,0:T(8,128)(2,1)} %get-tuple-element.28), channel_id=1, source_target_pairs={{0,48},{16,0},{32,16},{48,32},{1,49},{17,1},{33,17},{49,33},{2,50}... | collective-permute-start | bytes 2457608 | tf_op jit(solution)/shard_map/ppermute | solution.py:415
  15.0 1.9 %collective-permute-start.8 = (bf16[2,128,512]{2,1,0:T(8,128)(2,1)S(1)}, bf16[2,128,512]{2,1,0:T(8,128)(2,1)S(1)}, u32[]{:S(2)}, u32[]{:S(2)}) collective-permute-start(bf16[2,128,512]{2,1,0:T(8,128)(2,1)S(1)} %pair_up.1.refs_4_), channel_id=1, source_target_pairs={{0,2},{2,4},{4,6},{6,8},{8,10},{10,12},{12,14},{14,0},{1,3},{3,5},... | collective-permute-start | bytes 786440 | tf_op jit(solution)/shard_map/ppermute | solution.py:359
  16.9 3.9 %collective-permute-start.5 = (bf16[2,128,512]{2,1,0:T(8,128)(2,1)S(1)}, bf16[2,128,512]{2,1,0:T(8,128)(2,1)S(1)}, u32[]{:S(2)}, u32[]{:S(2)}) collective-permute-start(bf16[2,128,512]{2,1,0:T(8,128)(2,1)S(1)} %pair_up.1.refs_4_), channel_id=1, source_target_pairs={{0,14},{2,0},{4,2},{6,4},{8,6},{10,8},{12,10},{14,12},{1,15},{3,1}... | collective-permute-start | bytes 786440 | tf_op jit(solution)/shard_map/ppermute | solution.py:358
  20.8 5.5 %collective-permute-done.8.refs_10_ = bf16[2,128,512]{2,1,0:T(8,128)(2,1)S(1)} collective-permute-done((bf16[2,128,512]{2,1,0:T(8,128)(2,1)S(1)}, bf16[2,128,512]{2,1,0:T(8,128)(2,1)S(1)}, u32[]{:S(2)}, u32[]{:S(2)}) %collective-permute-start.8) | collective-permute-done | bytes 262176 | tf_op jit(solution)/shard_map/ppermute | solution.py:359
  26.3 0.0 collective-permute-start.9
  26.3 0.0 collective-permute-done.5.refs_5_
  26.3 3.2 %collective-permute-start.6 = (bf16[2,128,512]{2,1,0:T(8,128)(2,1)S(1)}, bf16[2,128,512]{2,1,0:T(8,128)(2,1)S(1)}, u32[]{:S(2)}, u32[]{:S(2)}) collective-permute-start(bf16[2,128,512]{2,1,0:T(8,128)(2,1)S(1)} %collective-permute-done.5.refs_5_), channel_id=1, source_target_pairs={{0,14},{2,0},{4,2},{6,4},{8,6},{10,8},{12,10},{14,12},{1,15},{3,1}... | collective-permute-start | bytes 786440 | tf_op jit(solution)/shard_map/ppermute | solution.py:358
  29.5 4.5 %collective-permute-done.9.refs_9_ = bf16[2,128,512]{2,1,0:T(8,128)(2,1)S(1)} collective-permute-done((bf16[2,128,512]{2,1,0:T(8,128)(2,1)S(1)}, bf16[2,128,512]{2,1,0:T(8,128)(2,1)S(1)}, u32[]{:S(2)}, u32[]{:S(2)}) %collective-permute-start.9) | collective-permute-done | bytes 262176 | tf_op jit(solution)/shard_map/ppermute | solution.py:359
  34.1 0.0 collective-permute-start.10
  34.1 1.4 %collective-permute-start.2 = (bf16[144,1024]{1,0:T(8,128)(2,1)}, bf16[144,1024]{1,0:T(8,128)(2,1)S(1)}, u32[]{:S(2)}, u32[]{:S(2)}) collective-permute-start(bf16[144,1024]{1,0:T(8,128)(2,1)} %get-tuple-element.27), channel_id=1, source_target_pairs={{0,32},{16,48},{32,0},{48,16},{1,33},{17,49},{33,1},{49,17},{2,34}... | collective-permute-start | bytes 884744 | tf_op jit(solution)/shard_map/ppermute | solution.py:415
  35.5 0.0 collective-permute-done.6.refs_6_
  35.5 3.2 %collective-permute-start.7 = (bf16[2,128,512]{2,1,0:T(8,128)(2,1)S(1)}, bf16[2,128,512]{2,1,0:T(8,128)(2,1)S(1)}, u32[]{:S(2)}, u32[]{:S(2)}) collective-permute-start(bf16[2,128,512]{2,1,0:T(8,128)(2,1)S(1)} %collective-permute-done.6.refs_6_), channel_id=1, source_target_pairs={{0,14},{2,0},{4,2},{6,4},{8,6},{10,8},{12,10},{14,12},{1,15},{3,1}... | collective-permute-start | bytes 786440 | tf_op jit(solution)/shard_map/ppermute | solution.py:358
  38.7 0.0 collective-permute-done.1.before_ref.refs_0_
  38.7 0.0 collective-permute-done.3.after_ref.refs_2_.refs_1_
  38.7 0.1 halves.1
  38.8 0.1 collective-permute-start.4
  38.9 2.4 %collective-permute-start.11 = (bf16[160,1024]{1,0:T(8,128)(2,1)S(1)}, bf16[160,1024]{1,0:T(8,128)(2,1)S(1)}, u32[]{:S(2)}, u32[]{:S(2)}) collective-permute-start(bf16[160,1024]{1,0:T(8,128)(2,1)S(1)} %get-tuple-element.35), channel_id=1, source_target_pairs={{0,16},{16,32},{32,48},{48,0},{1,17},{17,33},{33,49},{49,1},{2,18}... | collective-permute-start | bytes 983048 | tf_op jit(solution)/shard_map/ppermute | solution.py:420
  41.3 0.4 collective-permute-done.10.refs_8_.down_ref
  41.6 0.9 collective-permute-start.12
  42.5 0.1 collective-permute-done.7.refs_7_.up_ref
  42.6 6.4 %collective-permute-start.13 = (bf16[1,128,512]{2,1,0:T(8,128)(2,1)S(1)}, bf16[1,128,512]{2,1,0:T(8,128)(2,1)S(1)}, u32[]{:S(2)}, u32[]{:S(2)}) collective-permute-start(bf16[1,128,512]{2,1,0:T(8,128)(2,1)S(1)} %get-tuple-element.37), channel_id=1, source_target_pairs={{0,14},{2,0},{4,2},{6,4},{8,6},{10,8},{12,10},{14,12},{1,15},{3,1}... | collective-permute-start | bytes 393224 | tf_op jit(solution)/shard_map/ppermute | solution.py:361
  49.0 0.0 collective-permute-done.2.refs_1_
  49.0 0.0 collective-permute-start.14
  49.0 0.0 collective-permute-done.4.refs_3_
  49.0 0.0 copy-done.3
  49.0 0.0 copy-done.4
  49.0 0.0 copy-done.5
  49.1 0.0 copy-done.6
  49.1 0.0 copy-start
  49.1 1.1 %copy-done = bf16[400,1024]{1,0:T(8,128)(2,1)S(1)} copy-done((bf16[400,1024]{1,0:T(8,128)(2,1)S(1)}, bf16[400,1024]{1,0:T(8,128)(2,1)}, u32[]{:S(2)}) %copy-start) | copy-done | bytes 819224
  50.2 0.0 copy-start.7
  50.2 1.0 %copy-done.7 = f32[1024,128]{1,0:T(8,128)S(1)} copy-done((f32[1024,128]{1,0:T(8,128)S(1)}, f32[1024,128]{1,0:T(8,128)}, u32[]{:S(2)}) %copy-start.7) | copy-done | bytes 524312
  51.3 1.6 %early_stage.1 = (f32[2,576,512]{2,1,0:T(8,128)S(1)}, bf16[576,128]{1,0:T(8,128)(2,1)S(1)}, bf16[128,512]{1,0:T(8,128)(2,1)S(1)}, f32[1024,128]{1,0:T(8,128)S(1)}, bf16[320,1024]{1,0:T(8,128)(2,1)S(1)}) custom-call(bf16[128,4096]{1,0:T(8,128)(2,1)S(1)} %copy-done.3, bf16[64,128]{1,0:T(8,128)(2,1)S(1)} %bitcast.19, bf16[64,128]{1,0:T(8,128)(2,1)S(1)} %bitcast.21, ...), custom_call_target="tpu_custom_call" | custom-call | flops 2000000000 | bytes 4194304 | tf_op jit(solution)/shard_map/early_stage/pallas_call | solution.py:246
  52.9 0.0 collective-permute-done.13.refs_4_
  52.9 2.3 %collective-permute-done.14.refs_5_ = bf16[1,128,512]{2,1,0:T(8,128)(2,1)S(1)} collective-permute-done((bf16[1,128,512]{2,1,0:T(8,128)(2,1)S(1)}, bf16[1,128,512]{2,1,0:T(8,128)(2,1)S(1)}, u32[]{:S(2)}, u32[]{:S(2)}) %collective-permute-start.14) | collective-permute-done | bytes 131104 | tf_op jit(solution)/shard_map/ppermute | solution.py:361
  55.2 0.0 collective-permute-done.11.refs_2_
  55.2 0.0 collective-permute-done.12.refs_3_
  55.2 2.4 %tail_stage.1 = f32[6,64,64]{2,1,0:T(8,128)S(1)} custom-call(f32[2,576,512]{2,1,0:T(8,128)S(1)} %get-tuple-element.30.total_ref, bf16[576,128]{1,0:T(8,128)(2,1)S(1)} %get-tuple-element.31.far_ref, bf16[128,512]{1,0:T(8,128)(2,1)S(1)} %get-tuple-element.32.projs, f32[1024,128]{1,0:T(8,128)S(1)} %get-tuple-element.33.right_ref, ...), custom_call_target="tpu_custom_call" | custom-call | flops 2000000000 | bytes 4194304 | tf_op jit(solution)/shard_map/tail_stage/pallas_call | solution.py:326
  57.6 0.1 reshape_reshape.6
  57.7 0.1 copy.34
  57.8 15.5 %all_to_all.10 = f32[32,6,128]{2,1,0:T(8,128)S(1)} all-to-all(f32[32,6,128]{2,1,0:T(8,128)S(1)} %bitcast.23), channel_id=1, replica_groups=mesh['sy'=2,'sc'=2,'x'=4,'z'=8,'yh'=2] {'sy','sc','z'}, dimensions={0} | all-to-all | bytes 196608 | tf_op jit(solution)/shard_map/all_to_all | solution.py:370
  73.3 20.2 %all_to_all.11 = f32[64,6,128]{2,1,0:T(8,128)S(1)} all-to-all(f32[64,6,128]{2,1,0:T(8,128)S(1)} %broadcast_in_dim.2), channel_id=1, replica_groups=mesh['sy'=2,'sc'=2,'x'=4,'z'=8,'yh'=2] {'x','z','yh'}, dimensions={0} | all-to-all | bytes 393216 | tf_op jit(solution)/shard_map/all_to_all | solution.py:373
  93.6 0.6 copy.28
  (8 shorter events, 0.1 us)
Async XLA Ops:
  0.0 12.3 %copy-start.2 = (bf16[2,512,64]{1,2,0:T(8,128)(2,1)S(1)}, bf16[2,512,64]{1,2,0:T(8,128)(2,1)}, u32[]{:S(2)}) copy-start(bf16[2,512,64]{1,2,0:T(8,128)(2,1)} %param.13) | copy-start | bytes 393220
  0.0 12.3 %collective-permute-start = (bf16[2,64,512]{2,1,0:T(8,128)(2,1)}, bf16[2,64,512]{2,1,0:T(8,128)(2,1)S(1)}, u32[]{:S(2)}, u32[]{:S(2)}) collective-permute-start(bf16[2,64,512]{2,1,0:T(8,128)(2,1)} %bitcast.15), channel_id=1, source_target_pairs={{0,1},{1,0},{2,3},{3,2},{4,5},{5,4},{6,7},{7,6},{8,9},{9,8},{10,11... | collective-permute-start | bytes 393224 | tf_op jit(solution)/shard_map/ppermute | solution.py:397
  3.2 45.8 %copy-start.3 = (bf16[128,4096]{1,0:T(8,128)(2,1)S(1)}, bf16[128,4096]{1,0:T(8,128)(2,1)}, u32[]{:S(2)}) copy-start(bf16[128,4096]{1,0:T(8,128)(2,1)} %weight_ref.1) | copy-start | bytes 3145732
  3.2 45.8 %copy-start.4 = (bf16[4096,64]{0,1:T(8,128)(2,1)S(1)}, bf16[4096,64]{0,1:T(8,128)(2,1)}, u32[]{:S(2)}) copy-start(bf16[4096,64]{0,1:T(8,128)(2,1)} %param.22) | copy-start | bytes 1572868
  3.2 45.9 %copy-start.5 = (bf16[128,64]{0,1:T(8,128)(2,1)S(1)}, bf16[128,64]{0,1:T(8,128)(2,1)}, u32[]{:S(2)}) copy-start(bf16[128,64]{0,1:T(8,128)(2,1)} %param.18) | copy-start | bytes 49156
  3.2 45.9 %copy-start.6 = (bf16[128,64]{0,1:T(8,128)(2,1)S(1)}, bf16[128,64]{0,1:T(8,128)(2,1)}, u32[]{:S(2)}) copy-start(bf16[128,64]{0,1:T(8,128)(2,1)} %param.20) | copy-start | bytes 49156
  12.3 0.6 copy-start.1
  13.0 25.8 %collective-permute-start.1 = (bf16[400,1024]{1,0:T(8,128)(2,1)}, bf16[400,1024]{1,0:T(8,128)(2,1)S(1)}, u32[]{:S(2)}, u32[]{:S(2)}) collective-permute-start(bf16[400,1024]{1,0:T(8,128)(2,1)} %get-tuple-element.26.own_ref), channel_id=1, source_target_pairs={{0,16},{16,32},{32,48},{48,0},{1,17},{17,33},{33,49},{49,1},{2,18}... | collective-permute-start | bytes 2457608 | tf_op jit(solution)/shard_map/ppermute | solution.py:415
  13.4 25.3 %collective-permute-start.3 = (bf16[400,1024]{1,0:T(8,128)(2,1)}, bf16[400,1024]{1,0:T(8,128)(2,1)S(1)}, u32[]{:S(2)}, u32[]{:S(2)}) collective-permute-start(bf16[400,1024]{1,0:T(8,128)(2,1)} %get-tuple-element.28), channel_id=1, source_target_pairs={{0,48},{16,0},{32,16},{48,32},{1,49},{17,1},{33,17},{49,33},{2,50}... | collective-permute-start | bytes 2457608 | tf_op jit(solution)/shard_map/ppermute | solution.py:415
  15.0 11.3 %collective-permute-start.8 = (bf16[2,128,512]{2,1,0:T(8,128)(2,1)S(1)}, bf16[2,128,512]{2,1,0:T(8,128)(2,1)S(1)}, u32[]{:S(2)}, u32[]{:S(2)}) collective-permute-start(bf16[2,128,512]{2,1,0:T(8,128)(2,1)S(1)} %pair_up.1.refs_4_), channel_id=1, source_target_pairs={{0,2},{2,4},{4,6},{6,8},{8,10},{10,12},{12,14},{14,0},{1,3},{3,5},... | collective-permute-start | bytes 786440 | tf_op jit(solution)/shard_map/ppermute | solution.py:359
  16.9 9.4 %collective-permute-start.5 = (bf16[2,128,512]{2,1,0:T(8,128)(2,1)S(1)}, bf16[2,128,512]{2,1,0:T(8,128)(2,1)S(1)}, u32[]{:S(2)}, u32[]{:S(2)}) collective-permute-start(bf16[2,128,512]{2,1,0:T(8,128)(2,1)S(1)} %pair_up.1.refs_4_), channel_id=1, source_target_pairs={{0,14},{2,0},{4,2},{6,4},{8,6},{10,8},{12,10},{14,12},{1,15},{3,1}... | collective-permute-start | bytes 786440 | tf_op jit(solution)/shard_map/ppermute | solution.py:358
  26.3 7.8 %collective-permute-start.9 = (bf16[2,128,512]{2,1,0:T(8,128)(2,1)S(1)}, bf16[2,128,512]{2,1,0:T(8,128)(2,1)S(1)}, u32[]{:S(2)}, u32[]{:S(2)}) collective-permute-start(bf16[2,128,512]{2,1,0:T(8,128)(2,1)S(1)} %collective-permute-done.8.refs_10_), channel_id=1, source_target_pairs={{0,2},{2,4},{4,6},{6,8},{8,10},{10,12},{12,14},{14,0},{1,3},{3,5},... | collective-permute-start | bytes 786440 | tf_op jit(solution)/shard_map/ppermute | solution.py:359
  26.3 9.2 %collective-permute-start.6 = (bf16[2,128,512]{2,1,0:T(8,128)(2,1)S(1)}, bf16[2,128,512]{2,1,0:T(8,128)(2,1)S(1)}, u32[]{:S(2)}, u32[]{:S(2)}) collective-permute-start(bf16[2,128,512]{2,1,0:T(8,128)(2,1)S(1)} %collective-permute-done.5.refs_5_), channel_id=1, source_target_pairs={{0,14},{2,0},{4,2},{6,4},{8,6},{10,8},{12,10},{14,12},{1,15},{3,1}... | collective-permute-start | bytes 786440 | tf_op jit(solution)/shard_map/ppermute | solution.py:358
  34.1 7.6 %collective-permute-start.10 = (bf16[2,128,512]{2,1,0:T(8,128)(2,1)S(1)}, bf16[2,128,512]{2,1,0:T(8,128)(2,1)S(1)}, u32[]{:S(2)}, u32[]{:S(2)}) collective-permute-start(bf16[2,128,512]{2,1,0:T(8,128)(2,1)S(1)} %collective-permute-done.9.refs_9_), channel_id=1, source_target_pairs={{0,2},{2,4},{4,6},{6,8},{8,10},{10,12},{12,14},{14,0},{1,3},{3,5},... | collective-permute-start | bytes 786440 | tf_op jit(solution)/shard_map/ppermute | solution.py:359
  34.1 15.0 %collective-permute-start.2 = (bf16[144,1024]{1,0:T(8,128)(2,1)}, bf16[144,1024]{1,0:T(8,128)(2,1)S(1)}, u32[]{:S(2)}, u32[]{:S(2)}) collective-permute-start(bf16[144,1024]{1,0:T(8,128)(2,1)} %get-tuple-element.27), channel_id=1, source_target_pairs={{0,32},{16,48},{32,0},{48,16},{1,33},{17,49},{33,1},{49,17},{2,34}... | collective-permute-start | bytes 884744 | tf_op jit(solution)/shard_map/ppermute | solution.py:415
  35.5 7.1 %collective-permute-start.7 = (bf16[2,128,512]{2,1,0:T(8,128)(2,1)S(1)}, bf16[2,128,512]{2,1,0:T(8,128)(2,1)S(1)}, u32[]{:S(2)}, u32[]{:S(2)}) collective-permute-start(bf16[2,128,512]{2,1,0:T(8,128)(2,1)S(1)} %collective-permute-done.6.refs_6_), channel_id=1, source_target_pairs={{0,14},{2,0},{4,2},{6,4},{8,6},{10,8},{12,10},{14,12},{1,15},{3,1}... | collective-permute-start | bytes 786440 | tf_op jit(solution)/shard_map/ppermute | solution.py:358
  38.8 10.2 %collective-permute-start.4 = (bf16[128,1024]{1,0:T(8,128)(2,1)S(1)}, bf16[128,1024]{1,0:T(8,128)(2,1)S(1)}, u32[]{:S(2)}, u32[]{:S(2)}) collective-permute-start(bf16[128,1024]{1,0:T(8,128)(2,1)S(1)} %get-tuple-element.29), channel_id=1, source_target_pairs={{0,64},{64,0},{1,65},{65,1},{2,66},{66,2},{3,67},{67,3},{4,68},{68... | collective-permute-start | bytes 786440 | tf_op jit(solution)/shard_map/ppermute | solution.py:419
  38.9 16.3 %collective-permute-start.11 = (bf16[160,1024]{1,0:T(8,128)(2,1)S(1)}, bf16[160,1024]{1,0:T(8,128)(2,1)S(1)}, u32[]{:S(2)}, u32[]{:S(2)}) collective-permute-start(bf16[160,1024]{1,0:T(8,128)(2,1)S(1)} %get-tuple-element.35), channel_id=1, source_target_pairs={{0,16},{16,32},{32,48},{48,0},{1,17},{17,33},{33,49},{49,1},{2,18}... | collective-permute-start | bytes 983048 | tf_op jit(solution)/shard_map/ppermute | solution.py:420
  41.6 13.6 %collective-permute-start.12 = (bf16[160,1024]{1,0:T(8,128)(2,1)S(1)}, bf16[160,1024]{1,0:T(8,128)(2,1)S(1)}, u32[]{:S(2)}, u32[]{:S(2)}) collective-permute-start(bf16[160,1024]{1,0:T(8,128)(2,1)S(1)} %get-tuple-element.36), channel_id=1, source_target_pairs={{0,48},{16,0},{32,16},{48,32},{1,49},{17,1},{33,17},{49,33},{2,50}... | collective-permute-start | bytes 983048 | tf_op jit(solution)/shard_map/ppermute | solution.py:420
  42.6 10.2 %collective-permute-start.13 = (bf16[1,128,512]{2,1,0:T(8,128)(2,1)S(1)}, bf16[1,128,512]{2,1,0:T(8,128)(2,1)S(1)}, u32[]{:S(2)}, u32[]{:S(2)}) collective-permute-start(bf16[1,128,512]{2,1,0:T(8,128)(2,1)S(1)} %get-tuple-element.37), channel_id=1, source_target_pairs={{0,14},{2,0},{4,2},{6,4},{8,6},{10,8},{12,10},{14,12},{1,15},{3,1}... | collective-permute-start | bytes 393224 | tf_op jit(solution)/shard_map/ppermute | solution.py:361
  49.0 6.2 %collective-permute-start.14 = (bf16[1,128,512]{2,1,0:T(8,128)(2,1)S(1)}, bf16[1,128,512]{2,1,0:T(8,128)(2,1)S(1)}, u32[]{:S(2)}, u32[]{:S(2)}) collective-permute-start(bf16[1,128,512]{2,1,0:T(8,128)(2,1)S(1)} %get-tuple-element.38), channel_id=1, source_target_pairs={{0,2},{2,4},{4,6},{6,8},{8,10},{10,12},{12,14},{14,0},{1,3},{3,5},... | collective-permute-start | bytes 393224 | tf_op jit(solution)/shard_map/ppermute | solution.py:361
  49.1 1.1 %copy-start = (bf16[400,1024]{1,0:T(8,128)(2,1)S(1)}, bf16[400,1024]{1,0:T(8,128)(2,1)}, u32[]{:S(2)}) copy-start(bf16[400,1024]{1,0:T(8,128)(2,1)} %get-tuple-element.26.own_ref) | copy-start | bytes 2457604
  50.2 1.0 %copy-start.7 = (f32[1024,128]{1,0:T(8,128)S(1)}, f32[1024,128]{1,0:T(8,128)}, u32[]{:S(2)}) copy-start(f32[1024,128]{1,0:T(8,128)} %get-tuple-element.22.right_ref) | copy-start | bytes 1572868

commit v12 on v11

--- a/solution.py
+++ b/solution.py
@@ -170,23 +170,19 @@
     )(lengths, tokens, gate_weight, up_weight, gate_in, up_in, down_in, down_weight, gate_out, up_out)
 
 
-def forward_kernel(before_ref, after_ref, first_ref, second_ref, swap_ref):
+def forward_kernel(before_ref, after_ref, first_ref, second_ref):
     rows = first_ref.shape[0]
-    half = swap_ref.shape[0] // 2
     first_ref[...] = before_ref[:rows, :]
     second_ref[...] = after_ref[rows : 2 * rows, :]
-    swap_ref[:half, :] = before_ref[2 * rows : 2 * rows + half, :]
-    swap_ref[half:, :] = after_ref[2 * rows : 2 * rows + half, :]
-
-
-def halves(before, after, rows, half):
+
+
+def halves(before, after, rows):
     shape = jax.ShapeDtypeStruct((rows, before.shape[1]), before.dtype)
-    swap = jax.ShapeDtypeStruct((2 * half, before.shape[1]), before.dtype)
     return pl.pallas_call(
         forward_kernel,
-        out_shape=[shape, shape, swap],
+        out_shape=[shape] * 2,
         in_specs=[VMEM] * 2,
-        out_specs=[VMEM] * 3,
+        out_specs=[VMEM] * 2,
         compiler_params=pltpu.CompilerParams(vmem_limit_bytes=8 * MIB),
         name="halves",
     )(before, after)
@@ -335,31 +331,36 @@
     )(*operands)
 
 
-def cut_kernel(up_ref, down_ref, first_ref, second_ref):
+def cut_kernel(up_ref, down_ref, before_ref, after_ref, sent_ref, first_ref, second_ref, swap_ref):
     first_ref[...] = up_ref[: first_ref.shape[0]]
     second_ref[...] = down_ref[first_ref.shape[0] :]
-
-
-def cut(up, down):
+    half = swap_ref.shape[0] // 2
+    top = before_ref.shape[0] - FOLD
+    swap_ref[:half, :] = before_ref[top - half : top, :]
+    swap_ref[half:, :] = after_ref[top - half : top, :]
+
+
+def cut(up, down, before, after, sent, half):
     shape = jax.ShapeDtypeStruct((up.shape[0] // 2,) + up.shape[1:], up.dtype)
     return pl.pallas_call(
         cut_kernel,
-        out_shape=[shape] * 2,
-        in_specs=[VMEM] * 2,
-        out_specs=[VMEM] * 2,
-        compiler_params=pltpu.CompilerParams(vmem_limit_bytes=4 * MIB),
+        out_shape=[shape, shape, jax.ShapeDtypeStruct((2 * half, before.shape[1]), before.dtype)],
+        in_specs=[VMEM] * 5,
+        out_specs=[VMEM] * 3,
+        compiler_params=pltpu.CompilerParams(vmem_limit_bytes=8 * MIB),
         name="cut",
-    )(up, down)
-
-
-def ring_z(own):
+    )(up, down, before, after, sent)
+
+
+def ring_z(own, before, after, sent, half):
     up, down = [own], [own]
     for _ in range(NZ // 2 - 1):
         up.append(lax.ppermute(up[-1], "z", shifted(NZ, -1)))
         down.append(lax.ppermute(down[-1], "z", shifted(NZ, 1)))
-    first, second = cut(up[-1], down[-1])
+    first, second, swap = cut(up[-1], down[-1], before, after, sent, half)
+    swap = lax.ppermute(swap, "sc", shifted(SEQ_PARTS[1], 1))
     far = [lax.ppermute(first, "z", shifted(NZ, -1)), lax.ppermute(second, "z", shifted(NZ, 1))]
-    return up + down[:0:-1], far
+    return up + down[:0:-1], far, swap
 
 
 def sum_everywhere(partial):
@@ -415,10 +416,9 @@
     messages = [lax.ppermute(piece, "x", shifted(NX, step)) for step, piece in enumerate(sent, 1)]
     hidden, rank = gate_weight.shape[1], gate_out.shape[0]
     rows = 2 * hidden + rank
-    first, second, swap = halves(messages[0], messages[2], rows // 2, hidden // 2)
-    swap = lax.ppermute(swap, "sc", shifted(SEQ_PARTS[1], 1))
+    first, second = halves(messages[0], messages[2], rows // 2)
     far = [lax.ppermute(first, "x", shifted(NX, 1)), lax.ppermute(second, "x", shifted(NX, -1))]
-    blocks, far_block = ring_z(pair)
+    blocks, far_block, swap = ring_z(pair, messages[0], messages[2], first, hidden // 2)
     total, far_weight, projs, right, factors = early_stage(
         down_weight, gate_out, up_out, proj_down_out.T, right, sent[0], messages, swap, blocks
     )

time: 94.4 us -> 95.2 us (level)
  waiting for transfers between devices: 12.8 us -> 16.4 us
  starting transfers between devices: 28.7 us -> 25.8 us
    ppermute x3, waiting for transfers between devices: 10.4 us -> 14.1 us  [ring_z(): down.append(lax.ppermute(down[-1], 'z', shifted(NZ, 1)))]
    ppermute x1, starting transfers between devices: 6.39 us -> 3.27 us  [ring_z(): lax.ppermute(first, 'z', shifted(NZ, -1))]
  transfers between devices with their start and end apart: 15 -> 15, of which waited for: 5 -> 4; matrix products, arithmetic and copies ran while one was open for 0% -> 0% of each run, Pallas kernels for 11% -> 11%
where the time goes in v12:
time: 95.2 us; the launch traced here: 94.9 us
  blocking collectives  35.6 us (37%)
  starting transfers between devices  25.8 us (27%)
  waiting for transfers between devices  16.4 us (17%)
  Pallas kernels  13.2 us (14%)
  local copies, waits for them, and re-layouts  3.65 us (4%)
    all_to_all x1, blocking collectives, sum_everywhere(): blocks = lax.all_to_all(spread, ('x', 'z', 'yh'), 0, 0, tiled=True)  20.2 us
    all_to_all x1, blocking collectives, sum_everywhere(): pieces = lax.all_to_all(pieces, ('sy', 'sc', 'z'), 0, 0, tiled=True)  15.4 us
    ppermute x3, waiting for transfers between devices, ring_z(): down.append(lax.ppermute(down[-1], 'z', shifted(NZ, 1)))  14.1 us
    ppermute x3, starting transfers between devices, ring_z(): up.append(lax.ppermute(up[-1], 'z', shifted(NZ, -1)))  10.4 us
    pallas_call x1, Pallas kernels, token_stage(): pl.pallas_call(lambda *refs: token_kernel(chunk, scale, *refs), out_shape...  9.08 us
    ppermute x3, starting transfers between devices, shards(): lax.ppermute(piece, 'x', shifted(NX, step))  3.44 us
    ppermute x1, starting transfers between devices, ring_z(): lax.ppermute(first, 'z', shifted(NZ, -1))  3.27 us
    ppermute x1, starting transfers between devices, shards(): lax.ppermute(first, 'x', shifted(NX, 1))  3.22 us
  transfers between devices with their start and end apart: 15, of which 4 were waited for; matrix products, arithmetic and copies ran while one was open for 0% of the time, Pallas kernels for 11%

profile of v12, /device:TPU:6, one launch (start us, length us, event | category | flops | bytes accessed | tf_op | source)
XLA Modules:
  0.0 94.9 jit_solution(12460832311710507725)
XLA Ops:
  0.0 0.0 copy-start.2
  0.0 3.2 %collective-permute-start = (bf16[2,64,512]{2,1,0:T(8,128)(2,1)}, bf16[2,64,512]{2,1,0:T(8,128)(2,1)S(1)}, u32[]{:S(2)}, u32[]{:S(2)}) collective-permute-start(bf16[2,64,512]{2,1,0:T(8,128)(2,1)} %bitcast.15), channel_id=1, source_target_pairs={{0,1},{1,0},{2,3},{3,2},{4,5},{5,4},{6,7},{7,6},{8,9},{9,8},{10,11... | collective-permute-start | bytes 393224 | tf_op jit(solution)/shard_map/ppermute | solution.py:398
  3.2 0.0 copy-start.3
  3.2 0.0 copy-start.4
  3.2 0.0 copy-start.5
  3.2 0.0 copy-start.6
  3.2 9.1 %token_stage.1 = (bf16[400,1024]{1,0:T(8,128)(2,1)}, bf16[144,1024]{1,0:T(8,128)(2,1)}, bf16[400,1024]{1,0:T(8,128)(2,1)}, f32[1024,128]{1,0:T(8,128)}) custom-call(s32[2]{0:T(128)} %refs_0_.1, bf16[1024,4096]{1,0:T(8,128)(2,1)} %bitcast.25, bf16[4096,128]{1,0:T(8,128)(2,1)} %refs_2_.1, bf16[4096,128]{1,0:T(8,128)(2,1)} %refs_3_.1, ...), custom_call_target="tpu_custom_call" | custom-call | flops 4294967296 | bytes 16777216 | tf_op jit(solution)/shard_map/token_stage/pallas_call | solution.py:146
  12.3 0.0 collective-permute-done.refs_3_.other_ref
  12.3 0.0 copy-done.2
  12.3 0.0 copy-start.1
  12.4 0.6 copy-done.1
  13.0 0.8 collective-permute-start.3
  13.8 2.4 %collective-permute-start.1 = (bf16[400,1024]{1,0:T(8,128)(2,1)}, bf16[400,1024]{1,0:T(8,128)(2,1)S(1)}, u32[]{:S(2)}, u32[]{:S(2)}) collective-permute-start(bf16[400,1024]{1,0:T(8,128)(2,1)} %get-tuple-element.26.own_ref), channel_id=1, source_target_pairs={{0,16},{16,32},{32,48},{48,0},{1,17},{17,33},{33,49},{49,1},{2,18}... | collective-permute-start | bytes 2457608 | tf_op jit(solution)/shard_map/ppermute | solution.py:416
  16.2 1.9 %collective-permute-start.7 = (bf16[2,128,512]{2,1,0:T(8,128)(2,1)S(1)}, bf16[2,128,512]{2,1,0:T(8,128)(2,1)S(1)}, u32[]{:S(2)}, u32[]{:S(2)}) collective-permute-start(bf16[2,128,512]{2,1,0:T(8,128)(2,1)S(1)} %pair_up.1.refs_4_), channel_id=1, source_target_pairs={{0,2},{2,4},{4,6},{6,8},{8,10},{10,12},{12,14},{14,0},{1,3},{3,5},... | collective-permute-start | bytes 786440 | tf_op jit(solution)/shard_map/ppermute | solution.py:359
  18.1 3.9 %collective-permute-start.4 = (bf16[2,128,512]{2,1,0:T(8,128)(2,1)S(1)}, bf16[2,128,512]{2,1,0:T(8,128)(2,1)S(1)}, u32[]{:S(2)}, u32[]{:S(2)}) collective-permute-start(bf16[2,128,512]{2,1,0:T(8,128)(2,1)S(1)} %pair_up.1.refs_4_), channel_id=1, source_target_pairs={{0,14},{2,0},{4,2},{6,4},{8,6},{10,8},{12,10},{14,12},{1,15},{3,1}... | collective-permute-start | bytes 786440 | tf_op jit(solution)/shard_map/ppermute | solution.py:358
  22.1 5.5 %collective-permute-done.7.refs_10_ = bf16[2,128,512]{2,1,0:T(8,128)(2,1)S(1)} collective-permute-done((bf16[2,128,512]{2,1,0:T(8,128)(2,1)S(1)}, bf16[2,128,512]{2,1,0:T(8,128)(2,1)S(1)}, u32[]{:S(2)}, u32[]{:S(2)}) %collective-permute-start.7) | collective-permute-done | bytes 262176 | tf_op jit(solution)/shard_map/ppermute | solution.py:359
  27.5 0.0 collective-permute-start.8
  27.5 0.0 collective-permute-done.4.refs_5_
  27.5 3.2 %collective-permute-start.5 = (bf16[2,128,512]{2,1,0:T(8,128)(2,1)S(1)}, bf16[2,128,512]{2,1,0:T(8,128)(2,1)S(1)}, u32[]{:S(2)}, u32[]{:S(2)}) collective-permute-start(bf16[2,128,512]{2,1,0:T(8,128)(2,1)S(1)} %collective-permute-done.4.refs_5_), channel_id=1, source_target_pairs={{0,14},{2,0},{4,2},{6,4},{8,6},{10,8},{12,10},{14,12},{1,15},{3,1}... | collective-permute-start | bytes 786440 | tf_op jit(solution)/shard_map/ppermute | solution.py:358
  30.7 4.5 %collective-permute-done.8.refs_9_ = bf16[2,128,512]{2,1,0:T(8,128)(2,1)S(1)} collective-permute-done((bf16[2,128,512]{2,1,0:T(8,128)(2,1)S(1)}, bf16[2,128,512]{2,1,0:T(8,128)(2,1)S(1)}, u32[]{:S(2)}, u32[]{:S(2)}) %collective-permute-start.8) | collective-permute-done | bytes 262176 | tf_op jit(solution)/shard_map/ppermute | solution.py:359
  35.3 0.0 collective-permute-start.9
  35.3 0.0 collective-permute-done.5.refs_6_
  35.3 3.2 %collective-permute-start.6 = (bf16[2,128,512]{2,1,0:T(8,128)(2,1)S(1)}, bf16[2,128,512]{2,1,0:T(8,128)(2,1)S(1)}, u32[]{:S(2)}, u32[]{:S(2)}) collective-permute-start(bf16[2,128,512]{2,1,0:T(8,128)(2,1)S(1)} %collective-permute-done.5.refs_6_), channel_id=1, source_target_pairs={{0,14},{2,0},{4,2},{6,4},{8,6},{10,8},{12,10},{14,12},{1,15},{3,1}... | collective-permute-start | bytes 786440 | tf_op jit(solution)/shard_map/ppermute | solution.py:358
  38.5 0.2 collective-permute-start.2
  38.7 0.0 collective-permute-done.3.after_ref.refs_2_.refs_1_
  38.7 0.0 collective-permute-done.1.before_ref.refs_0_
  38.8 4.1 %collective-permute-done.9.down_ref.refs_8_ = bf16[2,128,512]{2,1,0:T(8,128)(2,1)S(1)} collective-permute-done((bf16[2,128,512]{2,1,0:T(8,128)(2,1)S(1)}, bf16[2,128,512]{2,1,0:T(8,128)(2,1)S(1)}, u32[]{:S(2)}, u32[]{:S(2)}) %collective-permute-start.9) | collective-permute-done | bytes 262176 | tf_op jit(solution)/shard_map/ppermute | solution.py:359
  42.9 0.0 collective-permute-done.6.up_ref.refs_7_
  42.9 0.1 collective-permute-start.10
  43.0 0.3 collective-permute-start.12
  43.3 3.2 %collective-permute-start.11 = (bf16[160,1024]{1,0:T(8,128)(2,1)S(1)}, bf16[160,1024]{1,0:T(8,128)(2,1)S(1)}, u32[]{:S(2)}, u32[]{:S(2)}) collective-permute-start(bf16[160,1024]{1,0:T(8,128)(2,1)S(1)} %get-tuple-element.29.sent_ref), channel_id=1, source_target_pairs={{0,16},{16,32},{32,48},{48,0},{1,17},{17,33},{33,49},{49,1},{2,18}... | collective-permute-start | bytes 983048 | tf_op jit(solution)/shard_map/ppermute | solution.py:420
  46.5 3.3 %collective-permute-start.13 = (bf16[1,128,512]{2,1,0:T(8,128)(2,1)S(1)}, bf16[1,128,512]{2,1,0:T(8,128)(2,1)S(1)}, u32[]{:S(2)}, u32[]{:S(2)}) collective-permute-start(bf16[1,128,512]{2,1,0:T(8,128)(2,1)S(1)} %get-tuple-element.37), channel_id=1, source_target_pairs={{0,14},{2,0},{4,2},{6,4},{8,6},{10,8},{12,10},{14,12},{1,15},{3,1}... | collective-permute-start | bytes 393224 | tf_op jit(solution)/shard_map/ppermute | solution.py:362
  49.8 0.0 collective-permute-done.2.refs_1_
  49.8 0.0 collective-permute-start.14
  49.8 0.0 collective-permute-done.10.refs_3_
  49.8 0.0 copy-done.3
  49.8 0.0 copy-done.4
  49.8 0.0 copy-done.5
  49.8 0.0 copy-done.6
  49.8 0.0 copy-start
  49.8 1.1 %copy-done = bf16[400,1024]{1,0:T(8,128)(2,1)S(1)} copy-done((bf16[400,1024]{1,0:T(8,128)(2,1)S(1)}, bf16[400,1024]{1,0:T(8,128)(2,1)}, u32[]{:S(2)}) %copy-start) | copy-done | bytes 819224
  51.0 0.0 copy-start.7
  51.0 1.0 %copy-done.7 = f32[1024,128]{1,0:T(8,128)S(1)} copy-done((f32[1024,128]{1,0:T(8,128)S(1)}, f32[1024,128]{1,0:T(8,128)}, u32[]{:S(2)}) %copy-start.7) | copy-done | bytes 524312
  52.0 1.6 %early_stage.1 = (f32[2,576,512]{2,1,0:T(8,128)S(1)}, bf16[576,128]{1,0:T(8,128)(2,1)S(1)}, bf16[128,512]{1,0:T(8,128)(2,1)S(1)}, f32[1024,128]{1,0:T(8,128)S(1)}, bf16[320,1024]{1,0:T(8,128)(2,1)S(1)}) custom-call(bf16[128,4096]{1,0:T(8,128)(2,1)S(1)} %copy-done.3, bf16[64,128]{1,0:T(8,128)(2,1)S(1)} %bitcast.19, bf16[64,128]{1,0:T(8,128)(2,1)S(1)} %bitcast.21, ...), custom_call_target="tpu_custom_call" | custom-call | flops 2000000000 | bytes 4194304 | tf_op jit(solution)/shard_map/early_stage/pallas_call | solution.py:242
  53.6 0.0 collective-permute-done.13.refs_4_
  53.6 2.3 %collective-permute-done.14.refs_5_ = bf16[1,128,512]{2,1,0:T(8,128)(2,1)S(1)} collective-permute-done((bf16[1,128,512]{2,1,0:T(8,128)(2,1)S(1)}, bf16[1,128,512]{2,1,0:T(8,128)(2,1)S(1)}, u32[]{:S(2)}, u32[]{:S(2)}) %collective-permute-start.14) | collective-permute-done | bytes 131104 | tf_op jit(solution)/shard_map/ppermute | solution.py:362
  56.0 0.0 collective-permute-done.12.refs_3_
  56.0 0.0 collective-permute-done.11.refs_2_
  56.0 2.4 %tail_stage.1 = f32[6,64,64]{2,1,0:T(8,128)S(1)} custom-call(f32[2,576,512]{2,1,0:T(8,128)S(1)} %get-tuple-element.31.total_ref, bf16[576,128]{1,0:T(8,128)(2,1)S(1)} %get-tuple-element.32.far_ref, bf16[128,512]{1,0:T(8,128)(2,1)S(1)} %get-tuple-element.33.projs, f32[1024,128]{1,0:T(8,128)S(1)} %get-tuple-element.34.right_ref, ...), custom_call_target="tpu_custom_call" | custom-call | flops 2000000000 | bytes 4194304 | tf_op jit(solution)/shard_map/tail_stage/pallas_call | solution.py:322
  58.4 0.1 reshape_reshape.6
  58.5 0.1 copy.34
  58.6 15.4 %all_to_all.10 = f32[32,6,128]{2,1,0:T(8,128)S(1)} all-to-all(f32[32,6,128]{2,1,0:T(8,128)S(1)} %bitcast.23), channel_id=1, replica_groups=mesh['sy'=2,'sc'=2,'x'=4,'z'=8,'yh'=2] {'sy','sc','z'}, dimensions={0} | all-to-all | bytes 196608 | tf_op jit(solution)/shard_map/all_to_all | solution.py:371
  74.1 20.2 %all_to_all.11 = f32[64,6,128]{2,1,0:T(8,128)S(1)} all-to-all(f32[64,6,128]{2,1,0:T(8,128)S(1)} %broadcast_in_dim.2), channel_id=1, replica_groups=mesh['sy'=2,'sc'=2,'x'=4,'z'=8,'yh'=2] {'x','z','yh'}, dimensions={0} | all-to-all | bytes 393216 | tf_op jit(solution)/shard_map/all_to_all | solution.py:374
  94.3 0.6 copy.28
  (9 shorter events, 0.2 us)
Async XLA Ops:
  0.0 12.3 %copy-start.2 = (bf16[2,512,64]{1,2,0:T(8,128)(2,1)S(1)}, bf16[2,512,64]{1,2,0:T(8,128)(2,1)}, u32[]{:S(2)}) copy-start(bf16[2,512,64]{1,2,0:T(8,128)(2,1)} %param.13) | copy-start | bytes 393220
  0.0 12.3 %collective-permute-start = (bf16[2,64,512]{2,1,0:T(8,128)(2,1)}, bf16[2,64,512]{2,1,0:T(8,128)(2,1)S(1)}, u32[]{:S(2)}, u32[]{:S(2)}) collective-permute-start(bf16[2,64,512]{2,1,0:T(8,128)(2,1)} %bitcast.15), channel_id=1, source_target_pairs={{0,1},{1,0},{2,3},{3,2},{4,5},{5,4},{6,7},{7,6},{8,9},{9,8},{10,11... | collective-permute-start | bytes 393224 | tf_op jit(solution)/shard_map/ppermute | solution.py:398
  3.2 46.6 %copy-start.3 = (bf16[128,4096]{1,0:T(8,128)(2,1)S(1)}, bf16[128,4096]{1,0:T(8,128)(2,1)}, u32[]{:S(2)}) copy-start(bf16[128,4096]{1,0:T(8,128)(2,1)} %weight_ref.1) | copy-start | bytes 3145732
  3.2 46.6 %copy-start.4 = (bf16[4096,64]{0,1:T(8,128)(2,1)S(1)}, bf16[4096,64]{0,1:T(8,128)(2,1)}, u32[]{:S(2)}) copy-start(bf16[4096,64]{0,1:T(8,128)(2,1)} %param.22) | copy-start | bytes 1572868
  3.2 46.6 %copy-start.5 = (bf16[128,64]{0,1:T(8,128)(2,1)S(1)}, bf16[128,64]{0,1:T(8,128)(2,1)}, u32[]{:S(2)}) copy-start(bf16[128,64]{0,1:T(8,128)(2,1)} %param.18) | copy-start | bytes 49156
  3.2 46.6 %copy-start.6 = (bf16[128,64]{0,1:T(8,128)(2,1)S(1)}, bf16[128,64]{0,1:T(8,128)(2,1)}, u32[]{:S(2)}) copy-start(bf16[128,64]{0,1:T(8,128)(2,1)} %param.20) | copy-start | bytes 49156
  12.3 0.6 copy-start.1
  13.0 25.8 %collective-permute-start.3 = (bf16[400,1024]{1,0:T(8,128)(2,1)}, bf16[400,1024]{1,0:T(8,128)(2,1)S(1)}, u32[]{:S(2)}, u32[]{:S(2)}) collective-permute-start(bf16[400,1024]{1,0:T(8,128)(2,1)} %get-tuple-element.28), channel_id=1, source_target_pairs={{0,48},{16,0},{32,16},{48,32},{1,49},{17,1},{33,17},{49,33},{2,50}... | collective-permute-start | bytes 2457608 | tf_op jit(solution)/shard_map/ppermute | solution.py:416
  13.8 24.9 %collective-permute-start.1 = (bf16[400,1024]{1,0:T(8,128)(2,1)}, bf16[400,1024]{1,0:T(8,128)(2,1)S(1)}, u32[]{:S(2)}, u32[]{:S(2)}) collective-permute-start(bf16[400,1024]{1,0:T(8,128)(2,1)} %get-tuple-element.26.own_ref), channel_id=1, source_target_pairs={{0,16},{16,32},{32,48},{48,0},{1,17},{17,33},{33,49},{49,1},{2,18}... | collective-permute-start | bytes 2457608 | tf_op jit(solution)/shard_map/ppermute | solution.py:416
  16.2 11.3 %collective-permute-start.7 = (bf16[2,128,512]{2,1,0:T(8,128)(2,1)S(1)}, bf16[2,128,512]{2,1,0:T(8,128)(2,1)S(1)}, u32[]{:S(2)}, u32[]{:S(2)}) collective-permute-start(bf16[2,128,512]{2,1,0:T(8,128)(2,1)S(1)} %pair_up.1.refs_4_), channel_id=1, source_target_pairs={{0,2},{2,4},{4,6},{6,8},{8,10},{10,12},{12,14},{14,0},{1,3},{3,5},... | collective-permute-start | bytes 786440 | tf_op jit(solution)/shard_map/ppermute | solution.py:359
  18.1 9.4 %collective-permute-start.4 = (bf16[2,128,512]{2,1,0:T(8,128)(2,1)S(1)}, bf16[2,128,512]{2,1,0:T(8,128)(2,1)S(1)}, u32[]{:S(2)}, u32[]{:S(2)}) collective-permute-start(bf16[2,128,512]{2,1,0:T(8,128)(2,1)S(1)} %pair_up.1.refs_4_), channel_id=1, source_target_pairs={{0,14},{2,0},{4,2},{6,4},{8,6},{10,8},{12,10},{14,12},{1,15},{3,1}... | collective-permute-start | bytes 786440 | tf_op jit(solution)/shard_map/ppermute | solution.py:358
  27.5 7.8 %collective-permute-start.8 = (bf16[2,128,512]{2,1,0:T(8,128)(2,1)S(1)}, bf16[2,128,512]{2,1,0:T(8,128)(2,1)S(1)}, u32[]{:S(2)}, u32[]{:S(2)}) collective-permute-start(bf16[2,128,512]{2,1,0:T(8,128)(2,1)S(1)} %collective-permute-done.7.refs_10_), channel_id=1, source_target_pairs={{0,2},{2,4},{4,6},{6,8},{8,10},{10,12},{12,14},{14,0},{1,3},{3,5},... | collective-permute-start | bytes 786440 | tf_op jit(solution)/shard_map/ppermute | solution.py:359
  27.5 7.8 %collective-permute-start.5 = (bf16[2,128,512]{2,1,0:T(8,128)(2,1)S(1)}, bf16[2,128,512]{2,1,0:T(8,128)(2,1)S(1)}, u32[]{:S(2)}, u32[]{:S(2)}) collective-permute-start(bf16[2,128,512]{2,1,0:T(8,128)(2,1)S(1)} %collective-permute-done.4.refs_5_), channel_id=1, source_target_pairs={{0,14},{2,0},{4,2},{6,4},{8,6},{10,8},{12,10},{14,12},{1,15},{3,1}... | collective-permute-start | bytes 786440 | tf_op jit(solution)/shard_map/ppermute | solution.py:358
  35.3 7.6 %collective-permute-start.9 = (bf16[2,128,512]{2,1,0:T(8,128)(2,1)S(1)}, bf16[2,128,512]{2,1,0:T(8,128)(2,1)S(1)}, u32[]{:S(2)}, u32[]{:S(2)}) collective-permute-start(bf16[2,128,512]{2,1,0:T(8,128)(2,1)S(1)} %collective-permute-done.8.refs_9_), channel_id=1, source_target_pairs={{0,2},{2,4},{4,6},{6,8},{8,10},{10,12},{12,14},{14,0},{1,3},{3,5},... | collective-permute-start | bytes 786440 | tf_op jit(solution)/shard_map/ppermute | solution.py:359
  35.3 7.6 %collective-permute-start.6 = (bf16[2,128,512]{2,1,0:T(8,128)(2,1)S(1)}, bf16[2,128,512]{2,1,0:T(8,128)(2,1)S(1)}, u32[]{:S(2)}, u32[]{:S(2)}) collective-permute-start(bf16[2,128,512]{2,1,0:T(8,128)(2,1)S(1)} %collective-permute-done.5.refs_6_), channel_id=1, source_target_pairs={{0,14},{2,0},{4,2},{6,4},{8,6},{10,8},{12,10},{14,12},{1,15},{3,1}... | collective-permute-start | bytes 786440 | tf_op jit(solution)/shard_map/ppermute | solution.py:358
  38.5 11.3 %collective-permute-start.2 = (bf16[144,1024]{1,0:T(8,128)(2,1)}, bf16[144,1024]{1,0:T(8,128)(2,1)S(1)}, u32[]{:S(2)}, u32[]{:S(2)}) collective-permute-start(bf16[144,1024]{1,0:T(8,128)(2,1)} %get-tuple-element.27), channel_id=1, source_target_pairs={{0,32},{16,48},{32,0},{48,16},{1,33},{17,49},{33,1},{49,17},{2,34}... | collective-permute-start | bytes 884744 | tf_op jit(solution)/shard_map/ppermute | solution.py:416
  42.9 6.9 %collective-permute-start.10 = (bf16[128,1024]{1,0:T(8,128)(2,1)S(1)}, bf16[128,1024]{1,0:T(8,128)(2,1)S(1)}, u32[]{:S(2)}, u32[]{:S(2)}) collective-permute-start(bf16[128,1024]{1,0:T(8,128)(2,1)S(1)} %get-tuple-element.30), channel_id=1, source_target_pairs={{0,64},{64,0},{1,65},{65,1},{2,66},{66,2},{3,67},{67,3},{4,68},{68... | collective-permute-start | bytes 786440 | tf_op jit(solution)/shard_map/ppermute | solution.py:361
  43.0 13.0 %collective-permute-start.12 = (bf16[160,1024]{1,0:T(8,128)(2,1)S(1)}, bf16[160,1024]{1,0:T(8,128)(2,1)S(1)}, u32[]{:S(2)}, u32[]{:S(2)}) collective-permute-start(bf16[160,1024]{1,0:T(8,128)(2,1)S(1)} %get-tuple-element.36), channel_id=1, source_target_pairs={{0,48},{16,0},{32,16},{48,32},{1,49},{17,1},{33,17},{49,33},{2,50}... | collective-permute-start | bytes 983048 | tf_op jit(solution)/shard_map/ppermute | solution.py:420
  43.3 12.7 %collective-permute-start.11 = (bf16[160,1024]{1,0:T(8,128)(2,1)S(1)}, bf16[160,1024]{1,0:T(8,128)(2,1)S(1)}, u32[]{:S(2)}, u32[]{:S(2)}) collective-permute-start(bf16[160,1024]{1,0:T(8,128)(2,1)S(1)} %get-tuple-element.29.sent_ref), channel_id=1, source_target_pairs={{0,16},{16,32},{32,48},{48,0},{1,17},{17,33},{33,49},{49,1},{2,18}... | collective-permute-start | bytes 983048 | tf_op jit(solution)/shard_map/ppermute | solution.py:420
  46.5 7.1 %collective-permute-start.13 = (bf16[1,128,512]{2,1,0:T(8,128)(2,1)S(1)}, bf16[1,128,512]{2,1,0:T(8,128)(2,1)S(1)}, u32[]{:S(2)}, u32[]{:S(2)}) collective-permute-start(bf16[1,128,512]{2,1,0:T(8,128)(2,1)S(1)} %get-tuple-element.37), channel_id=1, source_target_pairs={{0,14},{2,0},{4,2},{6,4},{8,6},{10,8},{12,10},{14,12},{1,15},{3,1}... | collective-permute-start | bytes 393224 | tf_op jit(solution)/shard_map/ppermute | solution.py:362
  49.8 6.2 %collective-permute-start.14 = (bf16[1,128,512]{2,1,0:T(8,128)(2,1)S(1)}, bf16[1,128,512]{2,1,0:T(8,128)(2,1)S(1)}, u32[]{:S(2)}, u32[]{:S(2)}) collective-permute-start(bf16[1,128,512]{2,1,0:T(8,128)(2,1)S(1)} %get-tuple-element.38), channel_id=1, source_target_pairs={{0,2},{2,4},{4,6},{6,8},{8,10},{10,12},{12,14},{14,0},{1,3},{3,5},... | collective-permute-start | bytes 393224 | tf_op jit(solution)/shard_map/ppermute | solution.py:362
  49.8 1.1 %copy-start = (bf16[400,1024]{1,0:T(8,128)(2,1)S(1)}, bf16[400,1024]{1,0:T(8,128)(2,1)}, u32[]{:S(2)}) copy-start(bf16[400,1024]{1,0:T(8,128)(2,1)} %get-tuple-element.26.own_ref) | copy-start | bytes 2457604
  51.0 1.0 %copy-start.7 = (f32[1024,128]{1,0:T(8,128)S(1)}, f32[1024,128]{1,0:T(8,128)}, u32[]{:S(2)}) copy-start(f32[1024,128]{1,0:T(8,128)} %get-tuple-element.22.right_ref) | copy-start | bytes 1572868

commit v13 on v10

--- a/solution.py
+++ b/solution.py
@@ -260,9 +260,10 @@
             base = lax.rem(z_at + step, NZ) * both
             for kind, y_of in enumerate((y_at, 1 - y_at)):
                 rows = pl.ds(pl.multiple_of(base + y_of * piece, piece), piece)
-                grads[rows, :] = block[kind * piece : (kind + 1) * piece]
+                grads[example, rows, :] = block[kind * piece : (kind + 1) * piece]
+    for example in range(examples):
         columns = slice(example * seq_dev, (example + 1) * seq_dev)
-        total = jnp.dot(weights[...], grads[...], preferred_element_type=jnp.float32)
+        total = jnp.dot(weights[...], grads[example], preferred_element_type=jnp.float32)
         left = []
         for kind in range(2):
             factor = jnp.concatenate(
@@ -306,7 +307,7 @@
         scratch_shapes=[
             pltpu.VMEM((NX * hidden + rank, width), jnp.bfloat16),
             pltpu.VMEM((2 * rank, NX * hidden), jnp.bfloat16),
-            pltpu.VMEM((width, seq_dev), jnp.bfloat16),
+            pltpu.VMEM((examples, width, seq_dev), jnp.bfloat16),
         ],
         compiler_params=pltpu.CompilerParams(vmem_limit_bytes=20 * MIB),
         cost_estimate=pl.CostEstimate(flops=4 * 10**9, bytes_accessed=8 * MIB, transcendentals=0),

time: 93.5 us -> 93.5 us (level)
  no operation moved by 1% of the time
where the time goes in v13:
time: 93.5 us; the launch traced here: 93.3 us
  blocking collectives  35.5 us (38%)
  starting transfers between devices  25 us (27%)
  waiting for transfers between devices  16.2 us (17%)
  Pallas kernels  12.7 us (14%)
  local copies, waits for them, and re-layouts  3.65 us (4%)
    all_to_all x1, blocking collectives, sum_everywhere(): blocks = lax.all_to_all(spread, ('x', 'z', 'yh'), 0, 0, tiled=True)  20.7 us
    all_to_all x1, blocking collectives, sum_everywhere(): pieces = lax.all_to_all(pieces, ('sy', 'sc', 'z'), 0, 0, tiled=True)  14.7 us
    ppermute x3, waiting for transfers between devices, ring_z(): down.append(lax.ppermute(down[-1], 'z', shifted(NZ, 1)))  10.6 us
    ppermute x3, starting transfers between devices, ring_z(): up.append(lax.ppermute(up[-1], 'z', shifted(NZ, -1)))  10.4 us
    pallas_call x1, Pallas kernels, token_stage(): pl.pallas_call(lambda *refs: token_kernel(chunk, scale, *refs), out_shape...  9.08 us
    ppermute x1, starting transfers between devices, ring_z(): lax.ppermute(first, 'z', shifted(NZ, -1))  3.86 us
    pallas_call x1, Pallas kernels, tail_stage(): pl.pallas_call(tail_kernel, out_shape=jax.ShapeDtypeStruct((examples * 3,...  3.48 us
    ppermute x3, starting transfers between devices, shards(): lax.ppermute(piece, 'x', shifted(NX, step))  3.44 us
  transfers between devices with their start and end apart: 15, of which 6 were waited for; matrix products, arithmetic and copies ran while one was open for 0% of the time, Pallas kernels for 10%

profile of v13, /device:TPU:6, one launch (start us, length us, event | category | flops | bytes accessed | tf_op | source)
XLA Modules:
  0.0 93.3 jit_solution(1646320307955826741)
XLA Ops:
  0.0 0.0 copy-start.3
  0.0 3.2 %collective-permute-start = (bf16[2,64,512]{2,1,0:T(8,128)(2,1)}, bf16[2,64,512]{2,1,0:T(8,128)(2,1)S(1)}, u32[]{:S(2)}, u32[]{:S(2)}) collective-permute-start(bf16[2,64,512]{2,1,0:T(8,128)(2,1)} %bitcast.15), channel_id=1, source_target_pairs={{0,1},{1,0},{2,3},{3,2},{4,5},{5,4},{6,7},{7,6},{8,9},{9,8},{10,11... | collective-permute-start | bytes 393224 | tf_op jit(solution)/shard_map/ppermute | solution.py:377
  3.2 0.0 copy-start.4
  3.2 0.0 copy-start.5
  3.2 0.0 copy-start.6
  3.2 0.0 copy-start.7
  3.2 9.1 %token_stage.1 = (bf16[400,1024]{1,0:T(8,128)(2,1)}, bf16[144,1024]{1,0:T(8,128)(2,1)}, bf16[400,1024]{1,0:T(8,128)(2,1)}, f32[1024,128]{1,0:T(8,128)}) custom-call(s32[2]{0:T(128)} %refs_0_.1, bf16[1024,4096]{1,0:T(8,128)(2,1)} %bitcast.25, bf16[4096,128]{1,0:T(8,128)(2,1)} %refs_2_.1, bf16[4096,128]{1,0:T(8,128)(2,1)} %refs_3_.1, ...), custom_call_target="tpu_custom_call" | custom-call | flops 4294967296 | bytes 16777216 | tf_op jit(solution)/shard_map/token_stage/pallas_call | solution.py:146
  12.3 0.0 collective-permute-done.refs_3_.other_ref
  12.3 0.0 copy-done.3
  12.3 0.0 copy-start.1
  12.4 0.6 copy-done.1
  13.0 0.5 collective-permute-start.1
  13.4 1.6 %collective-permute-start.3 = (bf16[400,1024]{1,0:T(8,128)(2,1)}, bf16[400,1024]{1,0:T(8,128)(2,1)S(1)}, u32[]{:S(2)}, u32[]{:S(2)}) collective-permute-start(bf16[400,1024]{1,0:T(8,128)(2,1)} %get-tuple-element.27), channel_id=1, source_target_pairs={{0,48},{16,0},{32,16},{48,32},{1,49},{17,1},{33,17},{49,33},{2,50}... | collective-permute-start | bytes 2457608 | tf_op jit(solution)/shard_map/ppermute | solution.py:395
  15.0 1.9 %collective-permute-start.10 = (bf16[2,128,512]{2,1,0:T(8,128)(2,1)S(1)}, bf16[2,128,512]{2,1,0:T(8,128)(2,1)S(1)}, u32[]{:S(2)}, u32[]{:S(2)}) collective-permute-start(bf16[2,128,512]{2,1,0:T(8,128)(2,1)S(1)} %pair_up.1.refs_7_), channel_id=1, source_target_pairs={{0,2},{2,4},{4,6},{6,8},{8,10},{10,12},{12,14},{14,0},{1,3},{3,5},... | collective-permute-start | bytes 786440 | tf_op jit(solution)/shard_map/ppermute | solution.py:339
  16.9 3.9 %collective-permute-start.7 = (bf16[2,128,512]{2,1,0:T(8,128)(2,1)S(1)}, bf16[2,128,512]{2,1,0:T(8,128)(2,1)S(1)}, u32[]{:S(2)}, u32[]{:S(2)}) collective-permute-start(bf16[2,128,512]{2,1,0:T(8,128)(2,1)S(1)} %pair_up.1.refs_7_), channel_id=1, source_target_pairs={{0,14},{2,0},{4,2},{6,4},{8,6},{10,8},{12,10},{14,12},{1,15},{3,1}... | collective-permute-start | bytes 786440 | tf_op jit(solution)/shard_map/ppermute | solution.py:338
  20.8 5.5 %collective-permute-done.10.refs_13_ = bf16[2,128,512]{2,1,0:T(8,128)(2,1)S(1)} collective-permute-done((bf16[2,128,512]{2,1,0:T(8,128)(2,1)S(1)}, bf16[2,128,512]{2,1,0:T(8,128)(2,1)S(1)}, u32[]{:S(2)}, u32[]{:S(2)}) %collective-permute-start.10) | collective-permute-done | bytes 262176 | tf_op jit(solution)/shard_map/ppermute | solution.py:339
  26.3 0.0 collective-permute-start.11
  26.3 0.0 collective-permute-done.7.refs_8_
  26.3 3.2 %collective-permute-start.8 = (bf16[2,128,512]{2,1,0:T(8,128)(2,1)S(1)}, bf16[2,128,512]{2,1,0:T(8,128)(2,1)S(1)}, u32[]{:S(2)}, u32[]{:S(2)}) collective-permute-start(bf16[2,128,512]{2,1,0:T(8,128)(2,1)S(1)} %collective-permute-done.7.refs_8_), channel_id=1, source_target_pairs={{0,14},{2,0},{4,2},{6,4},{8,6},{10,8},{12,10},{14,12},{1,15},{3,1}... | collective-permute-start | bytes 786440 | tf_op jit(solution)/shard_map/ppermute | solution.py:338
  29.5 4.5 %collective-permute-done.11.refs_12_ = bf16[2,128,512]{2,1,0:T(8,128)(2,1)S(1)} collective-permute-done((bf16[2,128,512]{2,1,0:T(8,128)(2,1)S(1)}, bf16[2,128,512]{2,1,0:T(8,128)(2,1)S(1)}, u32[]{:S(2)}, u32[]{:S(2)}) %collective-permute-start.11) | collective-permute-done | bytes 262176 | tf_op jit(solution)/shard_map/ppermute | solution.py:339
  34.1 0.0 collective-permute-start.12
  34.1 1.4 %collective-permute-start.2 = (bf16[144,1024]{1,0:T(8,128)(2,1)}, bf16[144,1024]{1,0:T(8,128)(2,1)S(1)}, u32[]{:S(2)}, u32[]{:S(2)}) collective-permute-start(bf16[144,1024]{1,0:T(8,128)(2,1)} %get-tuple-element.26), channel_id=1, source_target_pairs={{0,32},{16,48},{32,0},{48,16},{1,33},{17,49},{33,1},{49,17},{2,34}... | collective-permute-start | bytes 884744 | tf_op jit(solution)/shard_map/ppermute | solution.py:395
  35.5 0.0 collective-permute-done.8.refs_9_
  35.5 3.2 %collective-permute-start.9 = (bf16[2,128,512]{2,1,0:T(8,128)(2,1)S(1)}, bf16[2,128,512]{2,1,0:T(8,128)(2,1)S(1)}, u32[]{:S(2)}, u32[]{:S(2)}) collective-permute-start(bf16[2,128,512]{2,1,0:T(8,128)(2,1)S(1)} %collective-permute-done.8.refs_9_), channel_id=1, source_target_pairs={{0,14},{2,0},{4,2},{6,4},{8,6},{10,8},{12,10},{14,12},{1,15},{3,1}... | collective-permute-start | bytes 786440 | tf_op jit(solution)/shard_map/ppermute | solution.py:338
  38.7 0.0 collective-permute-done.1.before_ref.refs_1_
  38.7 0.0 collective-permute-done.3.after_ref.refs_3_
  38.7 0.1 halves.1
  38.8 2.2 %collective-permute-start.4 = (bf16[160,1024]{1,0:T(8,128)(2,1)S(1)}, bf16[160,1024]{1,0:T(8,128)(2,1)S(1)}, u32[]{:S(2)}, u32[]{:S(2)}) collective-permute-start(bf16[160,1024]{1,0:T(8,128)(2,1)S(1)} %get-tuple-element.28), channel_id=1, source_target_pairs={{0,16},{16,32},{32,48},{48,0},{1,17},{17,33},{33,49},{49,1},{2,18}... | collective-permute-start | bytes 983048 | tf_op jit(solution)/shard_map/ppermute | solution.py:400
  41.0 0.0 collective-permute-start.5
  41.0 0.7 collective-permute-done.12.down_ref.refs_11_
  41.6 0.0 collective-permute-start.6
  41.7 1.0 %collective-permute-done.9.up_ref.refs_10_ = bf16[2,128,512]{2,1,0:T(8,128)(2,1)S(1)} collective-permute-done((bf16[2,128,512]{2,1,0:T(8,128)(2,1)S(1)}, bf16[2,128,512]{2,1,0:T(8,128)(2,1)S(1)}, u32[]{:S(2)}, u32[]{:S(2)}) %collective-permute-start.9) | collective-permute-done | bytes 262176 | tf_op jit(solution)/shard_map/ppermute | solution.py:338
  42.6 3.9 %collective-permute-start.13 = (bf16[1,128,512]{2,1,0:T(8,128)(2,1)S(1)}, bf16[1,128,512]{2,1,0:T(8,128)(2,1)S(1)}, u32[]{:S(2)}, u32[]{:S(2)}) collective-permute-start(bf16[1,128,512]{2,1,0:T(8,128)(2,1)S(1)} %get-tuple-element.31), channel_id=1, source_target_pairs={{0,14},{2,0},{4,2},{6,4},{8,6},{10,8},{12,10},{14,12},{1,15},{3,1}... | collective-permute-start | bytes 393224 | tf_op jit(solution)/shard_map/ppermute | solution.py:341
  46.5 0.0 collective-permute-done.2.refs_2_
  46.5 0.0 collective-permute-start.14
  46.5 0.0 copy-start
  46.5 1.1 %copy-done = bf16[400,1024]{1,0:T(8,128)(2,1)S(1)} copy-done((bf16[400,1024]{1,0:T(8,128)(2,1)S(1)}, bf16[400,1024]{1,0:T(8,128)(2,1)}, u32[]{:S(2)}) %copy-start) | copy-done | bytes 819224
  47.6 0.0 copy-start.2
  47.6 1.0 %copy-done.2 = f32[1024,128]{1,0:T(8,128)S(1)} copy-done((f32[1024,128]{1,0:T(8,128)S(1)}, f32[1024,128]{1,0:T(8,128)}, u32[]{:S(2)}) %copy-start.2) | copy-done | bytes 524312
  48.7 0.1 keep.1
  48.8 1.1 %collective-permute-done.13.refs_14_ = bf16[1,128,512]{2,1,0:T(8,128)(2,1)S(1)} collective-permute-done((bf16[1,128,512]{2,1,0:T(8,128)(2,1)S(1)}, bf16[1,128,512]{2,1,0:T(8,128)(2,1)S(1)}, u32[]{:S(2)}, u32[]{:S(2)}) %collective-permute-start.13) | collective-permute-done | bytes 131104 | tf_op jit(solution)/shard_map/ppermute | solution.py:341
  49.9 3.4 %collective-permute-done.14.refs_15_ = bf16[1,128,512]{2,1,0:T(8,128)(2,1)S(1)} collective-permute-done((bf16[1,128,512]{2,1,0:T(8,128)(2,1)S(1)}, bf16[1,128,512]{2,1,0:T(8,128)(2,1)S(1)}, u32[]{:S(2)}, u32[]{:S(2)}) %collective-permute-start.14) | collective-permute-done | bytes 131104 | tf_op jit(solution)/shard_map/ppermute | solution.py:341
  53.3 0.0 collective-permute-done.6.refs_6_
  53.3 0.0 collective-permute-done.4.refs_4_
  53.3 0.0 collective-permute-done.5.refs_5_
  53.3 0.0 copy-done.4
  53.4 0.0 copy-done.5
  53.4 0.0 copy-done.6
  53.4 0.0 copy-done.7
  53.4 3.5 %tail_stage.1 = f32[6,64,64]{2,1,0:T(8,128)S(1)} custom-call(bf16[128,4096]{1,0:T(8,128)(2,1)S(1)} %copy-done.4, bf16[64,128]{1,0:T(8,128)(2,1)S(1)} %bitcast.19, bf16[64,128]{1,0:T(8,128)(2,1)S(1)} %bitcast.21, bf16[64,4096]{1,0:T(8,128)(2,1)S(1)} %bitcast.17, f32[1024,128]{1,0:T(8,128)S(1)} %get-tuple-element.24.right_ref, ...), custom_call_target="tpu_custom_call" | custom-call | flops 4000000000 | bytes 8388608 | tf_op jit(solution)/shard_map/tail_stage/pallas_call | solution.py:302
  56.9 0.1 reshape_reshape.6
  57.0 0.1 copy.34
  57.0 14.7 %all_to_all.10 = f32[32,6,128]{2,1,0:T(8,128)S(1)} all-to-all(f32[32,6,128]{2,1,0:T(8,128)S(1)} %bitcast.23), channel_id=1, replica_groups=mesh['sy'=2,'sc'=2,'x'=4,'z'=8,'yh'=2] {'sy','sc','z'}, dimensions={0} | all-to-all | bytes 196608 | tf_op jit(solution)/shard_map/all_to_all | solution.py:350
  71.8 20.7 %all_to_all.11 = f32[64,6,128]{2,1,0:T(8,128)S(1)} all-to-all(f32[64,6,128]{2,1,0:T(8,128)S(1)} %broadcast_in_dim.2), channel_id=1, replica_groups=mesh['sy'=2,'sc'=2,'x'=4,'z'=8,'yh'=2] {'x','z','yh'}, dimensions={0} | all-to-all | bytes 393216 | tf_op jit(solution)/shard_map/all_to_all | solution.py:353
  92.6 0.6 copy.28
  (8 shorter events, 0.1 us)
Async XLA Ops:
  0.0 12.3 %copy-start.3 = (bf16[2,512,64]{1,2,0:T(8,128)(2,1)S(1)}, bf16[2,512,64]{1,2,0:T(8,128)(2,1)}, u32[]{:S(2)}) copy-start(bf16[2,512,64]{1,2,0:T(8,128)(2,1)} %param.13) | copy-start | bytes 393220
  0.0 12.3 %collective-permute-start = (bf16[2,64,512]{2,1,0:T(8,128)(2,1)}, bf16[2,64,512]{2,1,0:T(8,128)(2,1)S(1)}, u32[]{:S(2)}, u32[]{:S(2)}) collective-permute-start(bf16[2,64,512]{2,1,0:T(8,128)(2,1)} %bitcast.15), channel_id=1, source_target_pairs={{0,1},{1,0},{2,3},{3,2},{4,5},{5,4},{6,7},{7,6},{8,9},{9,8},{10,11... | collective-permute-start | bytes 393224 | tf_op jit(solution)/shard_map/ppermute | solution.py:377
  3.2 50.1 %copy-start.4 = (bf16[128,4096]{1,0:T(8,128)(2,1)S(1)}, bf16[128,4096]{1,0:T(8,128)(2,1)}, u32[]{:S(2)}) copy-start(bf16[128,4096]{1,0:T(8,128)(2,1)} %weight_ref.1) | copy-start | bytes 3145732
  3.2 50.2 %copy-start.5 = (bf16[4096,64]{0,1:T(8,128)(2,1)S(1)}, bf16[4096,64]{0,1:T(8,128)(2,1)}, u32[]{:S(2)}) copy-start(bf16[4096,64]{0,1:T(8,128)(2,1)} %param.22) | copy-start | bytes 1572868
  3.2 50.2 %copy-start.6 = (bf16[128,64]{0,1:T(8,128)(2,1)S(1)}, bf16[128,64]{0,1:T(8,128)(2,1)}, u32[]{:S(2)}) copy-start(bf16[128,64]{0,1:T(8,128)(2,1)} %param.18) | copy-start | bytes 49156
  3.2 50.2 %copy-start.7 = (bf16[128,64]{0,1:T(8,128)(2,1)S(1)}, bf16[128,64]{0,1:T(8,128)(2,1)}, u32[]{:S(2)}) copy-start(bf16[128,64]{0,1:T(8,128)(2,1)} %param.20) | copy-start | bytes 49156
  12.3 0.6 copy-start.1
  13.0 25.8 %collective-permute-start.1 = (bf16[400,1024]{1,0:T(8,128)(2,1)}, bf16[400,1024]{1,0:T(8,128)(2,1)S(1)}, u32[]{:S(2)}, u32[]{:S(2)}) collective-permute-start(bf16[400,1024]{1,0:T(8,128)(2,1)} %get-tuple-element.22.message_ref), channel_id=1, source_target_pairs={{0,16},{16,32},{32,48},{48,0},{1,17},{17,33},{33,49},{49,1},{2,18}... | collective-permute-start | bytes 2457608 | tf_op jit(solution)/shard_map/ppermute | solution.py:395
  13.4 25.3 %collective-permute-start.3 = (bf16[400,1024]{1,0:T(8,128)(2,1)}, bf16[400,1024]{1,0:T(8,128)(2,1)S(1)}, u32[]{:S(2)}, u32[]{:S(2)}) collective-permute-start(bf16[400,1024]{1,0:T(8,128)(2,1)} %get-tuple-element.27), channel_id=1, source_target_pairs={{0,48},{16,0},{32,16},{48,32},{1,49},{17,1},{33,17},{49,33},{2,50}... | collective-permute-start | bytes 2457608 | tf_op jit(solution)/shard_map/ppermute | solution.py:395
  15.0 11.3 %collective-permute-start.10 = (bf16[2,128,512]{2,1,0:T(8,128)(2,1)S(1)}, bf16[2,128,512]{2,1,0:T(8,128)(2,1)S(1)}, u32[]{:S(2)}, u32[]{:S(2)}) collective-permute-start(bf16[2,128,512]{2,1,0:T(8,128)(2,1)S(1)} %pair_up.1.refs_7_), channel_id=1, source_target_pairs={{0,2},{2,4},{4,6},{6,8},{8,10},{10,12},{12,14},{14,0},{1,3},{3,5},... | collective-permute-start | bytes 786440 | tf_op jit(solution)/shard_map/ppermute | solution.py:339
  16.9 9.4 %collective-permute-start.7 = (bf16[2,128,512]{2,1,0:T(8,128)(2,1)S(1)}, bf16[2,128,512]{2,1,0:T(8,128)(2,1)S(1)}, u32[]{:S(2)}, u32[]{:S(2)}) collective-permute-start(bf16[2,128,512]{2,1,0:T(8,128)(2,1)S(1)} %pair_up.1.refs_7_), channel_id=1, source_target_pairs={{0,14},{2,0},{4,2},{6,4},{8,6},{10,8},{12,10},{14,12},{1,15},{3,1}... | collective-permute-start | bytes 786440 | tf_op jit(solution)/shard_map/ppermute | solution.py:338
  26.3 7.8 %collective-permute-start.11 = (bf16[2,128,512]{2,1,0:T(8,128)(2,1)S(1)}, bf16[2,128,512]{2,1,0:T(8,128)(2,1)S(1)}, u32[]{:S(2)}, u32[]{:S(2)}) collective-permute-start(bf16[2,128,512]{2,1,0:T(8,128)(2,1)S(1)} %collective-permute-done.10.refs_13_), channel_id=1, source_target_pairs={{0,2},{2,4},{4,6},{6,8},{8,10},{10,12},{12,14},{14,0},{1,3},{3,5},... | collective-permute-start | bytes 786440 | tf_op jit(solution)/shard_map/ppermute | solution.py:339
  26.3 9.2 %collective-permute-start.8 = (bf16[2,128,512]{2,1,0:T(8,128)(2,1)S(1)}, bf16[2,128,512]{2,1,0:T(8,128)(2,1)S(1)}, u32[]{:S(2)}, u32[]{:S(2)}) collective-permute-start(bf16[2,128,512]{2,1,0:T(8,128)(2,1)S(1)} %collective-permute-done.7.refs_8_), channel_id=1, source_target_pairs={{0,14},{2,0},{4,2},{6,4},{8,6},{10,8},{12,10},{14,12},{1,15},{3,1}... | collective-permute-start | bytes 786440 | tf_op jit(solution)/shard_map/ppermute | solution.py:338
  34.1 7.6 %collective-permute-start.12 = (bf16[2,128,512]{2,1,0:T(8,128)(2,1)S(1)}, bf16[2,128,512]{2,1,0:T(8,128)(2,1)S(1)}, u32[]{:S(2)}, u32[]{:S(2)}) collective-permute-start(bf16[2,128,512]{2,1,0:T(8,128)(2,1)S(1)} %collective-permute-done.11.refs_12_), channel_id=1, source_target_pairs={{0,2},{2,4},{4,6},{6,8},{8,10},{10,12},{12,14},{14,0},{1,3},{3,5},... | collective-permute-start | bytes 786440 | tf_op jit(solution)/shard_map/ppermute | solution.py:339
  34.1 12.4 %collective-permute-start.2 = (bf16[144,1024]{1,0:T(8,128)(2,1)}, bf16[144,1024]{1,0:T(8,128)(2,1)S(1)}, u32[]{:S(2)}, u32[]{:S(2)}) collective-permute-start(bf16[144,1024]{1,0:T(8,128)(2,1)} %get-tuple-element.26), channel_id=1, source_target_pairs={{0,32},{16,48},{32,0},{48,16},{1,33},{17,49},{33,1},{49,17},{2,34}... | collective-permute-start | bytes 884744 | tf_op jit(solution)/shard_map/ppermute | solution.py:395
  35.5 7.1 %collective-permute-start.9 = (bf16[2,128,512]{2,1,0:T(8,128)(2,1)S(1)}, bf16[2,128,512]{2,1,0:T(8,128)(2,1)S(1)}, u32[]{:S(2)}, u32[]{:S(2)}) collective-permute-start(bf16[2,128,512]{2,1,0:T(8,128)(2,1)S(1)} %collective-permute-done.8.refs_9_), channel_id=1, source_target_pairs={{0,14},{2,0},{4,2},{6,4},{8,6},{10,8},{12,10},{14,12},{1,15},{3,1}... | collective-permute-start | bytes 786440 | tf_op jit(solution)/shard_map/ppermute | solution.py:338
  38.8 14.5 %collective-permute-start.4 = (bf16[160,1024]{1,0:T(8,128)(2,1)S(1)}, bf16[160,1024]{1,0:T(8,128)(2,1)S(1)}, u32[]{:S(2)}, u32[]{:S(2)}) collective-permute-start(bf16[160,1024]{1,0:T(8,128)(2,1)S(1)} %get-tuple-element.28), channel_id=1, source_target_pairs={{0,16},{16,32},{32,48},{48,0},{1,17},{17,33},{33,49},{49,1},{2,18}... | collective-permute-start | bytes 983048 | tf_op jit(solution)/shard_map/ppermute | solution.py:400
  41.0 12.4 %collective-permute-start.5 = (bf16[160,1024]{1,0:T(8,128)(2,1)S(1)}, bf16[160,1024]{1,0:T(8,128)(2,1)S(1)}, u32[]{:S(2)}, u32[]{:S(2)}) collective-permute-start(bf16[160,1024]{1,0:T(8,128)(2,1)S(1)} %get-tuple-element.29), channel_id=1, source_target_pairs={{0,48},{16,0},{32,16},{48,32},{1,49},{17,1},{33,17},{49,33},{2,50}... | collective-permute-start | bytes 983048 | tf_op jit(solution)/shard_map/ppermute | solution.py:400
  41.6 11.7 %collective-permute-start.6 = (bf16[128,1024]{1,0:T(8,128)(2,1)S(1)}, bf16[128,1024]{1,0:T(8,128)(2,1)S(1)}, u32[]{:S(2)}, u32[]{:S(2)}) collective-permute-start(bf16[128,1024]{1,0:T(8,128)(2,1)S(1)} %get-tuple-element.30), channel_id=1, source_target_pairs={{0,64},{64,0},{1,65},{65,1},{2,66},{66,2},{3,67},{67,3},{4,68},{68... | collective-permute-start | bytes 786440 | tf_op jit(solution)/shard_map/ppermute | solution.py:399
  42.6 7.3 %collective-permute-start.13 = (bf16[1,128,512]{2,1,0:T(8,128)(2,1)S(1)}, bf16[1,128,512]{2,1,0:T(8,128)(2,1)S(1)}, u32[]{:S(2)}, u32[]{:S(2)}) collective-permute-start(bf16[1,128,512]{2,1,0:T(8,128)(2,1)S(1)} %get-tuple-element.31), channel_id=1, source_target_pairs={{0,14},{2,0},{4,2},{6,4},{8,6},{10,8},{12,10},{14,12},{1,15},{3,1}... | collective-permute-start | bytes 393224 | tf_op jit(solution)/shard_map/ppermute | solution.py:341
  46.5 6.8 %collective-permute-start.14 = (bf16[1,128,512]{2,1,0:T(8,128)(2,1)S(1)}, bf16[1,128,512]{2,1,0:T(8,128)(2,1)S(1)}, u32[]{:S(2)}, u32[]{:S(2)}) collective-permute-start(bf16[1,128,512]{2,1,0:T(8,128)(2,1)S(1)} %get-tuple-element.32), channel_id=1, source_target_pairs={{0,2},{2,4},{4,6},{6,8},{8,10},{10,12},{12,14},{14,0},{1,3},{3,5},... | collective-permute-start | bytes 393224 | tf_op jit(solution)/shard_map/ppermute | solution.py:341
  46.5 1.1 %copy-start = (bf16[400,1024]{1,0:T(8,128)(2,1)S(1)}, bf16[400,1024]{1,0:T(8,128)(2,1)}, u32[]{:S(2)}) copy-start(bf16[400,1024]{1,0:T(8,128)(2,1)} %get-tuple-element.22.message_ref) | copy-start | bytes 2457604
  47.6 1.0 %copy-start.2 = (f32[1024,128]{1,0:T(8,128)S(1)}, f32[1024,128]{1,0:T(8,128)}, u32[]{:S(2)}) copy-start(f32[1024,128]{1,0:T(8,128)} %get-tuple-element.23.right_ref) | copy-start | bytes 1572868

commit v14 on v13

--- a/solution.py
+++ b/solution.py
@@ -286,9 +286,9 @@
         right_down = factor_rows(0, 2 * hidden, top, columns).astype(jnp.float32)
         for step in range(1, NX):
             right_down = right_down + factor_rows(step, 2 * hidden, top, columns).astype(jnp.float32)
-        out_ref[3 * example] = sides[:rank, :rank]
-        out_ref[3 * example + 1] = sides[rank:, rank:]
-        out_ref[3 * example + 2] = dot32(
+        out_ref[example] = sides[:rank, :rank]
+        out_ref[1 * examples + example] = sides[rank:, rank:]
+        out_ref[2 * examples + example] = dot32(
             total[NX * hidden :], right_down, ((1,), (1,)), precision=lax.Precision.HIGHEST
         )
 
@@ -404,7 +404,7 @@
         down_weight, gate_out, up_out, proj_down_out.T, right, factors, messages, far, swap, blocks, far_block
     )
     total = sum_everywhere(products.reshape(examples * 3, -1))
-    return total.reshape(examples, 3, -1)
+    return total.reshape(3, examples, -1).transpose(1, 0, 2)
 
 
 def solution(mesh):

time: 93.5 us -> 93.5 us (level)
  no operation moved by 1% of the time
where the time goes in v14:
time: 93.5 us; the launch traced here: 93.2 us
  blocking collectives  35.5 us (38%)
  starting transfers between devices  25 us (27%)
  waiting for transfers between devices  16.2 us (17%)
  Pallas kernels  12.7 us (14%)
  local copies, waits for them, and re-layouts  3.64 us (4%)
    all_to_all x1, blocking collectives, sum_everywhere(): blocks = lax.all_to_all(spread, ('x', 'z', 'yh'), 0, 0, tiled=True)  20.7 us
    all_to_all x1, blocking collectives, sum_everywhere(): pieces = lax.all_to_all(pieces, ('sy', 'sc', 'z'), 0, 0, tiled=True)  14.7 us
    ppermute x3, waiting for transfers between devices, ring_z(): down.append(lax.ppermute(down[-1], 'z', shifted(NZ, 1)))  10.6 us
    ppermute x3, starting transfers between devices, ring_z(): up.append(lax.ppermute(up[-1], 'z', shifted(NZ, -1)))  10.4 us
    pallas_call x1, Pallas kernels, token_stage(): pl.pallas_call(lambda *refs: token_kernel(chunk, scale, *refs), out_shape...  9.08 us
    ppermute x1, starting transfers between devices, ring_z(): lax.ppermute(first, 'z', shifted(NZ, -1))  3.86 us
    pallas_call x1, Pallas kernels, tail_stage(): pl.pallas_call(tail_kernel, out_shape=jax.ShapeDtypeStruct((examples * 3,...  3.48 us
    ppermute x3, starting transfers between devices, shards(): lax.ppermute(piece, 'x', shifted(NX, step))  3.44 us
  transfers between devices with their start and end apart: 15, of which 6 were waited for; matrix products, arithmetic and copies ran while one was open for 0% of the time, Pallas kernels for 10%

profile of v14, /device:TPU:6, one launch (start us, length us, event | category | flops | bytes accessed | tf_op | source)
XLA Modules:
  0.0 93.2 jit_solution(6645253265742653752)
XLA Ops:
  0.0 0.0 copy-start.3
  0.0 3.2 %collective-permute-start = (bf16[2,64,512]{2,1,0:T(8,128)(2,1)}, bf16[2,64,512]{2,1,0:T(8,128)(2,1)S(1)}, u32[]{:S(2)}, u32[]{:S(2)}) collective-permute-start(bf16[2,64,512]{2,1,0:T(8,128)(2,1)} %bitcast.16), channel_id=1, source_target_pairs={{0,1},{1,0},{2,3},{3,2},{4,5},{5,4},{6,7},{7,6},{8,9},{9,8},{10,11... | collective-permute-start | bytes 393224 | tf_op jit(solution)/shard_map/ppermute | solution.py:377
  3.2 0.0 copy-start.4
  3.2 0.0 copy-start.5
  3.2 0.0 copy-start.6
  3.2 0.0 copy-start.7
  3.2 9.1 %token_stage.1 = (bf16[400,1024]{1,0:T(8,128)(2,1)}, bf16[144,1024]{1,0:T(8,128)(2,1)}, bf16[400,1024]{1,0:T(8,128)(2,1)}, f32[1024,128]{1,0:T(8,128)}) custom-call(s32[2]{0:T(128)} %refs_0_.1, bf16[1024,4096]{1,0:T(8,128)(2,1)} %bitcast.26, bf16[4096,128]{1,0:T(8,128)(2,1)} %refs_2_.1, bf16[4096,128]{1,0:T(8,128)(2,1)} %refs_3_.1, ...), custom_call_target="tpu_custom_call" | custom-call | flops 4294967296 | bytes 16777216 | tf_op jit(solution)/shard_map/token_stage/pallas_call | solution.py:146
  12.3 0.0 collective-permute-done.refs_3_.other_ref
  12.3 0.0 copy-done.3
  12.3 0.0 copy-start.1
  12.4 0.6 copy-done.1
  13.0 0.5 collective-permute-start.1
  13.4 1.6 %collective-permute-start.3 = (bf16[400,1024]{1,0:T(8,128)(2,1)}, bf16[400,1024]{1,0:T(8,128)(2,1)S(1)}, u32[]{:S(2)}, u32[]{:S(2)}) collective-permute-start(bf16[400,1024]{1,0:T(8,128)(2,1)} %get-tuple-element.27), channel_id=1, source_target_pairs={{0,48},{16,0},{32,16},{48,32},{1,49},{17,1},{33,17},{49,33},{2,50}... | collective-permute-start | bytes 2457608 | tf_op jit(solution)/shard_map/ppermute | solution.py:395
  15.0 1.9 %collective-permute-start.10 = (bf16[2,128,512]{2,1,0:T(8,128)(2,1)S(1)}, bf16[2,128,512]{2,1,0:T(8,128)(2,1)S(1)}, u32[]{:S(2)}, u32[]{:S(2)}) collective-permute-start(bf16[2,128,512]{2,1,0:T(8,128)(2,1)S(1)} %pair_up.1.refs_7_), channel_id=1, source_target_pairs={{0,2},{2,4},{4,6},{6,8},{8,10},{10,12},{12,14},{14,0},{1,3},{3,5},... | collective-permute-start | bytes 786440 | tf_op jit(solution)/shard_map/ppermute | solution.py:339
  16.9 3.9 %collective-permute-start.7 = (bf16[2,128,512]{2,1,0:T(8,128)(2,1)S(1)}, bf16[2,128,512]{2,1,0:T(8,128)(2,1)S(1)}, u32[]{:S(2)}, u32[]{:S(2)}) collective-permute-start(bf16[2,128,512]{2,1,0:T(8,128)(2,1)S(1)} %pair_up.1.refs_7_), channel_id=1, source_target_pairs={{0,14},{2,0},{4,2},{6,4},{8,6},{10,8},{12,10},{14,12},{1,15},{3,1}... | collective-permute-start | bytes 786440 | tf_op jit(solution)/shard_map/ppermute | solution.py:338
  20.8 5.5 %collective-permute-done.10.refs_13_ = bf16[2,128,512]{2,1,0:T(8,128)(2,1)S(1)} collective-permute-done((bf16[2,128,512]{2,1,0:T(8,128)(2,1)S(1)}, bf16[2,128,512]{2,1,0:T(8,128)(2,1)S(1)}, u32[]{:S(2)}, u32[]{:S(2)}) %collective-permute-start.10) | collective-permute-done | bytes 262176 | tf_op jit(solution)/shard_map/ppermute | solution.py:339
  26.3 0.0 collective-permute-start.11
  26.3 0.0 collective-permute-done.7.refs_8_
  26.3 3.2 %collective-permute-start.8 = (bf16[2,128,512]{2,1,0:T(8,128)(2,1)S(1)}, bf16[2,128,512]{2,1,0:T(8,128)(2,1)S(1)}, u32[]{:S(2)}, u32[]{:S(2)}) collective-permute-start(bf16[2,128,512]{2,1,0:T(8,128)(2,1)S(1)} %collective-permute-done.7.refs_8_), channel_id=1, source_target_pairs={{0,14},{2,0},{4,2},{6,4},{8,6},{10,8},{12,10},{14,12},{1,15},{3,1}... | collective-permute-start | bytes 786440 | tf_op jit(solution)/shard_map/ppermute | solution.py:338
  29.5 4.5 %collective-permute-done.11.refs_12_ = bf16[2,128,512]{2,1,0:T(8,128)(2,1)S(1)} collective-permute-done((bf16[2,128,512]{2,1,0:T(8,128)(2,1)S(1)}, bf16[2,128,512]{2,1,0:T(8,128)(2,1)S(1)}, u32[]{:S(2)}, u32[]{:S(2)}) %collective-permute-start.11) | collective-permute-done | bytes 262176 | tf_op jit(solution)/shard_map/ppermute | solution.py:339
  34.1 0.0 collective-permute-start.12
  34.1 1.4 %collective-permute-start.2 = (bf16[144,1024]{1,0:T(8,128)(2,1)}, bf16[144,1024]{1,0:T(8,128)(2,1)S(1)}, u32[]{:S(2)}, u32[]{:S(2)}) collective-permute-start(bf16[144,1024]{1,0:T(8,128)(2,1)} %get-tuple-element.26), channel_id=1, source_target_pairs={{0,32},{16,48},{32,0},{48,16},{1,33},{17,49},{33,1},{49,17},{2,34}... | collective-permute-start | bytes 884744 | tf_op jit(solution)/shard_map/ppermute | solution.py:395
  35.5 0.0 collective-permute-done.8.refs_9_
  35.5 3.2 %collective-permute-start.9 = (bf16[2,128,512]{2,1,0:T(8,128)(2,1)S(1)}, bf16[2,128,512]{2,1,0:T(8,128)(2,1)S(1)}, u32[]{:S(2)}, u32[]{:S(2)}) collective-permute-start(bf16[2,128,512]{2,1,0:T(8,128)(2,1)S(1)} %collective-permute-done.8.refs_9_), channel_id=1, source_target_pairs={{0,14},{2,0},{4,2},{6,4},{8,6},{10,8},{12,10},{14,12},{1,15},{3,1}... | collective-permute-start | bytes 786440 | tf_op jit(solution)/shard_map/ppermute | solution.py:338
  38.7 0.0 collective-permute-done.1.before_ref.refs_1_
  38.7 0.0 collective-permute-done.3.after_ref.refs_3_
  38.7 0.1 halves.1
  38.8 2.2 %collective-permute-start.4 = (bf16[160,1024]{1,0:T(8,128)(2,1)S(1)}, bf16[160,1024]{1,0:T(8,128)(2,1)S(1)}, u32[]{:S(2)}, u32[]{:S(2)}) collective-permute-start(bf16[160,1024]{1,0:T(8,128)(2,1)S(1)} %get-tuple-element.28), channel_id=1, source_target_pairs={{0,16},{16,32},{32,48},{48,0},{1,17},{17,33},{33,49},{49,1},{2,18}... | collective-permute-start | bytes 983048 | tf_op jit(solution)/shard_map/ppermute | solution.py:400
  41.0 0.0 collective-permute-start.5
  41.0 0.7 collective-permute-done.12.down_ref.refs_11_
  41.6 0.0 collective-permute-start.6
  41.7 1.0 %collective-permute-done.9.up_ref.refs_10_ = bf16[2,128,512]{2,1,0:T(8,128)(2,1)S(1)} collective-permute-done((bf16[2,128,512]{2,1,0:T(8,128)(2,1)S(1)}, bf16[2,128,512]{2,1,0:T(8,128)(2,1)S(1)}, u32[]{:S(2)}, u32[]{:S(2)}) %collective-permute-start.9) | collective-permute-done | bytes 262176 | tf_op jit(solution)/shard_map/ppermute | solution.py:338
  42.6 3.9 %collective-permute-start.13 = (bf16[1,128,512]{2,1,0:T(8,128)(2,1)S(1)}, bf16[1,128,512]{2,1,0:T(8,128)(2,1)S(1)}, u32[]{:S(2)}, u32[]{:S(2)}) collective-permute-start(bf16[1,128,512]{2,1,0:T(8,128)(2,1)S(1)} %get-tuple-element.31), channel_id=1, source_target_pairs={{0,14},{2,0},{4,2},{6,4},{8,6},{10,8},{12,10},{14,12},{1,15},{3,1}... | collective-permute-start | bytes 393224 | tf_op jit(solution)/shard_map/ppermute | solution.py:341
  46.5 0.0 collective-permute-done.2.refs_2_
  46.5 0.0 collective-permute-start.14
  46.5 0.0 copy-start
  46.5 1.1 %copy-done = bf16[400,1024]{1,0:T(8,128)(2,1)S(1)} copy-done((bf16[400,1024]{1,0:T(8,128)(2,1)S(1)}, bf16[400,1024]{1,0:T(8,128)(2,1)}, u32[]{:S(2)}) %copy-start) | copy-done | bytes 819224
  47.6 0.0 copy-start.2
  47.6 1.0 %copy-done.2 = f32[1024,128]{1,0:T(8,128)S(1)} copy-done((f32[1024,128]{1,0:T(8,128)S(1)}, f32[1024,128]{1,0:T(8,128)}, u32[]{:S(2)}) %copy-start.2) | copy-done | bytes 524312
  48.7 0.1 keep.1
  48.8 1.1 %collective-permute-done.13.refs_14_ = bf16[1,128,512]{2,1,0:T(8,128)(2,1)S(1)} collective-permute-done((bf16[1,128,512]{2,1,0:T(8,128)(2,1)S(1)}, bf16[1,128,512]{2,1,0:T(8,128)(2,1)S(1)}, u32[]{:S(2)}, u32[]{:S(2)}) %collective-permute-start.13) | collective-permute-done | bytes 131104 | tf_op jit(solution)/shard_map/ppermute | solution.py:341
  49.9 3.4 %collective-permute-done.14.refs_15_ = bf16[1,128,512]{2,1,0:T(8,128)(2,1)S(1)} collective-permute-done((bf16[1,128,512]{2,1,0:T(8,128)(2,1)S(1)}, bf16[1,128,512]{2,1,0:T(8,128)(2,1)S(1)}, u32[]{:S(2)}, u32[]{:S(2)}) %collective-permute-start.14) | collective-permute-done | bytes 131104 | tf_op jit(solution)/shard_map/ppermute | solution.py:341
  53.3 0.0 collective-permute-done.6.refs_6_
  53.3 0.0 collective-permute-done.4.refs_4_
  53.3 0.0 collective-permute-done.5.refs_5_
  53.3 0.0 copy-done.4
  53.4 0.0 copy-done.5
  53.4 0.0 copy-done.6
  53.4 0.0 copy-done.7
  53.4 3.5 %tail_stage.1 = f32[6,64,64]{2,1,0:T(8,128)S(1)} custom-call(bf16[128,4096]{1,0:T(8,128)(2,1)S(1)} %copy-done.4, bf16[64,128]{1,0:T(8,128)(2,1)S(1)} %bitcast.20, bf16[64,128]{1,0:T(8,128)(2,1)S(1)} %bitcast.22, bf16[64,4096]{1,0:T(8,128)(2,1)S(1)} %bitcast.18, f32[1024,128]{1,0:T(8,128)S(1)} %get-tuple-element.24.right_ref, ...), custom_call_target="tpu_custom_call" | custom-call | flops 4000000000 | bytes 8388608 | tf_op jit(solution)/shard_map/tail_stage/pallas_call | solution.py:302
  56.9 0.1 reshape_reshape.6
  57.0 0.1 copy.29
  57.0 14.7 %all_to_all.10 = f32[32,6,128]{2,1,0:T(8,128)S(1)} all-to-all(f32[32,6,128]{2,1,0:T(8,128)S(1)} %bitcast.24), channel_id=1, replica_groups=mesh['sy'=2,'sc'=2,'x'=4,'z'=8,'yh'=2] {'sy','sc','z'}, dimensions={0} | all-to-all | bytes 196608 | tf_op jit(solution)/shard_map/all_to_all | solution.py:350
  71.8 20.7 %all_to_all.11 = f32[64,6,128]{2,1,0:T(8,128)S(1)} all-to-all(f32[64,6,128]{2,1,0:T(8,128)S(1)} %broadcast_in_dim.2), channel_id=1, replica_groups=mesh['sy'=2,'sc'=2,'x'=4,'z'=8,'yh'=2] {'x','z','yh'}, dimensions={0} | all-to-all | bytes 393216 | tf_op jit(solution)/shard_map/all_to_all | solution.py:353
  92.6 0.6 reshape_reshape.7
  (7 shorter events, 0.1 us)
Async XLA Ops:
  0.0 12.3 %copy-start.3 = (bf16[2,512,64]{1,2,0:T(8,128)(2,1)S(1)}, bf16[2,512,64]{1,2,0:T(8,128)(2,1)}, u32[]{:S(2)}) copy-start(bf16[2,512,64]{1,2,0:T(8,128)(2,1)} %param.13) | copy-start | bytes 393220
  0.0 12.3 %collective-permute-start = (bf16[2,64,512]{2,1,0:T(8,128)(2,1)}, bf16[2,64,512]{2,1,0:T(8,128)(2,1)S(1)}, u32[]{:S(2)}, u32[]{:S(2)}) collective-permute-start(bf16[2,64,512]{2,1,0:T(8,128)(2,1)} %bitcast.16), channel_id=1, source_target_pairs={{0,1},{1,0},{2,3},{3,2},{4,5},{5,4},{6,7},{7,6},{8,9},{9,8},{10,11... | collective-permute-start | bytes 393224 | tf_op jit(solution)/shard_map/ppermute | solution.py:377
  3.2 50.1 %copy-start.4 = (bf16[128,4096]{1,0:T(8,128)(2,1)S(1)}, bf16[128,4096]{1,0:T(8,128)(2,1)}, u32[]{:S(2)}) copy-start(bf16[128,4096]{1,0:T(8,128)(2,1)} %weight_ref.1) | copy-start | bytes 3145732
  3.2 50.2 %copy-start.5 = (bf16[4096,64]{0,1:T(8,128)(2,1)S(1)}, bf16[4096,64]{0,1:T(8,128)(2,1)}, u32[]{:S(2)}) copy-start(bf16[4096,64]{0,1:T(8,128)(2,1)} %param.22) | copy-start | bytes 1572868
  3.2 50.2 %copy-start.6 = (bf16[128,64]{0,1:T(8,128)(2,1)S(1)}, bf16[128,64]{0,1:T(8,128)(2,1)}, u32[]{:S(2)}) copy-start(bf16[128,64]{0,1:T(8,128)(2,1)} %param.18) | copy-start | bytes 49156
  3.2 50.2 %copy-start.7 = (bf16[128,64]{0,1:T(8,128)(2,1)S(1)}, bf16[128,64]{0,1:T(8,128)(2,1)}, u32[]{:S(2)}) copy-start(bf16[128,64]{0,1:T(8,128)(2,1)} %param.20) | copy-start | bytes 49156
  12.3 0.6 copy-start.1
  13.0 25.8 %collective-permute-start.1 = (bf16[400,1024]{1,0:T(8,128)(2,1)}, bf16[400,1024]{1,0:T(8,128)(2,1)S(1)}, u32[]{:S(2)}, u32[]{:S(2)}) collective-permute-start(bf16[400,1024]{1,0:T(8,128)(2,1)} %get-tuple-element.22.message_ref), channel_id=1, source_target_pairs={{0,16},{16,32},{32,48},{48,0},{1,17},{17,33},{33,49},{49,1},{2,18}... | collective-permute-start | bytes 2457608 | tf_op jit(solution)/shard_map/ppermute | solution.py:395
  13.4 25.3 %collective-permute-start.3 = (bf16[400,1024]{1,0:T(8,128)(2,1)}, bf16[400,1024]{1,0:T(8,128)(2,1)S(1)}, u32[]{:S(2)}, u32[]{:S(2)}) collective-permute-start(bf16[400,1024]{1,0:T(8,128)(2,1)} %get-tuple-element.27), channel_id=1, source_target_pairs={{0,48},{16,0},{32,16},{48,32},{1,49},{17,1},{33,17},{49,33},{2,50}... | collective-permute-start | bytes 2457608 | tf_op jit(solution)/shard_map/ppermute | solution.py:395
  15.0 11.3 %collective-permute-start.10 = (bf16[2,128,512]{2,1,0:T(8,128)(2,1)S(1)}, bf16[2,128,512]{2,1,0:T(8,128)(2,1)S(1)}, u32[]{:S(2)}, u32[]{:S(2)}) collective-permute-start(bf16[2,128,512]{2,1,0:T(8,128)(2,1)S(1)} %pair_up.1.refs_7_), channel_id=1, source_target_pairs={{0,2},{2,4},{4,6},{6,8},{8,10},{10,12},{12,14},{14,0},{1,3},{3,5},... | collective-permute-start | bytes 786440 | tf_op jit(solution)/shard_map/ppermute | solution.py:339
  16.9 9.4 %collective-permute-start.7 = (bf16[2,128,512]{2,1,0:T(8,128)(2,1)S(1)}, bf16[2,128,512]{2,1,0:T(8,128)(2,1)S(1)}, u32[]{:S(2)}, u32[]{:S(2)}) collective-permute-start(bf16[2,128,512]{2,1,0:T(8,128)(2,1)S(1)} %pair_up.1.refs_7_), channel_id=1, source_target_pairs={{0,14},{2,0},{4,2},{6,4},{8,6},{10,8},{12,10},{14,12},{1,15},{3,1}... | collective-permute-start | bytes 786440 | tf_op jit(solution)/shard_map/ppermute | solution.py:338
  26.3 7.8 %collective-permute-start.11 = (bf16[2,128,512]{2,1,0:T(8,128)(2,1)S(1)}, bf16[2,128,512]{2,1,0:T(8,128)(2,1)S(1)}, u32[]{:S(2)}, u32[]{:S(2)}) collective-permute-start(bf16[2,128,512]{2,1,0:T(8,128)(2,1)S(1)} %collective-permute-done.10.refs_13_), channel_id=1, source_target_pairs={{0,2},{2,4},{4,6},{6,8},{8,10},{10,12},{12,14},{14,0},{1,3},{3,5},... | collective-permute-start | bytes 786440 | tf_op jit(solution)/shard_map/ppermute | solution.py:339
  26.3 9.2 %collective-permute-start.8 = (bf16[2,128,512]{2,1,0:T(8,128)(2,1)S(1)}, bf16[2,128,512]{2,1,0:T(8,128)(2,1)S(1)}, u32[]{:S(2)}, u32[]{:S(2)}) collective-permute-start(bf16[2,128,512]{2,1,0:T(8,128)(2,1)S(1)} %collective-permute-done.7.refs_8_), channel_id=1, source_target_pairs={{0,14},{2,0},{4,2},{6,4},{8,6},{10,8},{12,10},{14,12},{1,15},{3,1}... | collective-permute-start | bytes 786440 | tf_op jit(solution)/shard_map/ppermute | solution.py:338
  34.1 7.6 %collective-permute-start.12 = (bf16[2,128,512]{2,1,0:T(8,128)(2,1)S(1)}, bf16[2,128,512]{2,1,0:T(8,128)(2,1)S(1)}, u32[]{:S(2)}, u32[]{:S(2)}) collective-permute-start(bf16[2,128,512]{2,1,0:T(8,128)(2,1)S(1)} %collective-permute-done.11.refs_12_), channel_id=1, source_target_pairs={{0,2},{2,4},{4,6},{6,8},{8,10},{10,12},{12,14},{14,0},{1,3},{3,5},... | collective-permute-start | bytes 786440 | tf_op jit(solution)/shard_map/ppermute | solution.py:339
  34.1 12.4 %collective-permute-start.2 = (bf16[144,1024]{1,0:T(8,128)(2,1)}, bf16[144,1024]{1,0:T(8,128)(2,1)S(1)}, u32[]{:S(2)}, u32[]{:S(2)}) collective-permute-start(bf16[144,1024]{1,0:T(8,128)(2,1)} %get-tuple-element.26), channel_id=1, source_target_pairs={{0,32},{16,48},{32,0},{48,16},{1,33},{17,49},{33,1},{49,17},{2,34}... | collective-permute-start | bytes 884744 | tf_op jit(solution)/shard_map/ppermute | solution.py:395
  35.5 7.1 %collective-permute-start.9 = (bf16[2,128,512]{2,1,0:T(8,128)(2,1)S(1)}, bf16[2,128,512]{2,1,0:T(8,128)(2,1)S(1)}, u32[]{:S(2)}, u32[]{:S(2)}) collective-permute-start(bf16[2,128,512]{2,1,0:T(8,128)(2,1)S(1)} %collective-permute-done.8.refs_9_), channel_id=1, source_target_pairs={{0,14},{2,0},{4,2},{6,4},{8,6},{10,8},{12,10},{14,12},{1,15},{3,1}... | collective-permute-start | bytes 786440 | tf_op jit(solution)/shard_map/ppermute | solution.py:338
  38.8 14.5 %collective-permute-start.4 = (bf16[160,1024]{1,0:T(8,128)(2,1)S(1)}, bf16[160,1024]{1,0:T(8,128)(2,1)S(1)}, u32[]{:S(2)}, u32[]{:S(2)}) collective-permute-start(bf16[160,1024]{1,0:T(8,128)(2,1)S(1)} %get-tuple-element.28), channel_id=1, source_target_pairs={{0,16},{16,32},{32,48},{48,0},{1,17},{17,33},{33,49},{49,1},{2,18}... | collective-permute-start | bytes 983048 | tf_op jit(solution)/shard_map/ppermute | solution.py:400
  41.0 12.4 %collective-permute-start.5 = (bf16[160,1024]{1,0:T(8,128)(2,1)S(1)}, bf16[160,1024]{1,0:T(8,128)(2,1)S(1)}, u32[]{:S(2)}, u32[]{:S(2)}) collective-permute-start(bf16[160,1024]{1,0:T(8,128)(2,1)S(1)} %get-tuple-element.29), channel_id=1, source_target_pairs={{0,48},{16,0},{32,16},{48,32},{1,49},{17,1},{33,17},{49,33},{2,50}... | collective-permute-start | bytes 983048 | tf_op jit(solution)/shard_map/ppermute | solution.py:400
  41.6 11.7 %collective-permute-start.6 = (bf16[128,1024]{1,0:T(8,128)(2,1)S(1)}, bf16[128,1024]{1,0:T(8,128)(2,1)S(1)}, u32[]{:S(2)}, u32[]{:S(2)}) collective-permute-start(bf16[128,1024]{1,0:T(8,128)(2,1)S(1)} %get-tuple-element.30), channel_id=1, source_target_pairs={{0,64},{64,0},{1,65},{65,1},{2,66},{66,2},{3,67},{67,3},{4,68},{68... | collective-permute-start | bytes 786440 | tf_op jit(solution)/shard_map/ppermute | solution.py:399
  42.6 7.3 %collective-permute-start.13 = (bf16[1,128,512]{2,1,0:T(8,128)(2,1)S(1)}, bf16[1,128,512]{2,1,0:T(8,128)(2,1)S(1)}, u32[]{:S(2)}, u32[]{:S(2)}) collective-permute-start(bf16[1,128,512]{2,1,0:T(8,128)(2,1)S(1)} %get-tuple-element.31), channel_id=1, source_target_pairs={{0,14},{2,0},{4,2},{6,4},{8,6},{10,8},{12,10},{14,12},{1,15},{3,1}... | collective-permute-start | bytes 393224 | tf_op jit(solution)/shard_map/ppermute | solution.py:341
  46.5 6.8 %collective-permute-start.14 = (bf16[1,128,512]{2,1,0:T(8,128)(2,1)S(1)}, bf16[1,128,512]{2,1,0:T(8,128)(2,1)S(1)}, u32[]{:S(2)}, u32[]{:S(2)}) collective-permute-start(bf16[1,128,512]{2,1,0:T(8,128)(2,1)S(1)} %get-tuple-element.32), channel_id=1, source_target_pairs={{0,2},{2,4},{4,6},{6,8},{8,10},{10,12},{12,14},{14,0},{1,3},{3,5},... | collective-permute-start | bytes 393224 | tf_op jit(solution)/shard_map/ppermute | solution.py:341
  46.5 1.1 %copy-start = (bf16[400,1024]{1,0:T(8,128)(2,1)S(1)}, bf16[400,1024]{1,0:T(8,128)(2,1)}, u32[]{:S(2)}) copy-start(bf16[400,1024]{1,0:T(8,128)(2,1)} %get-tuple-element.22.message_ref) | copy-start | bytes 2457604
  47.6 1.0 %copy-start.2 = (f32[1024,128]{1,0:T(8,128)S(1)}, f32[1024,128]{1,0:T(8,128)}, u32[]{:S(2)}) copy-start(f32[1024,128]{1,0:T(8,128)} %get-tuple-element.23.right_ref) | copy-start | bytes 1572868
